TPU v7x, 32 devices: a whole 2x2x4 slice. The times are simulated.
32 devices in a mesh: rep: 2 (over y), cell: 4 (over x, core), gene: 4 (over z).
Axes of the slice: x: 2, y: 2, z: 4, core: 2. Of those that a mesh axis runs over, the one named last changes fastest.
Arguments:
- counts: int32 [4096, 5120], P('cell', 'gene'), may hold values from 0 to 63
- usage_init: float32 [8192, 200], P(('rep', 'cell')), parts along dimension 0, may hold values from 0.05 to 1
- program_init: float32 [400, 5120], P('rep', 'gene'), parts along dimension 0, may hold values from 0.05 to 1
Outputs:
- usage: float32 [8192, 200], P(('rep', 'cell')), parts along dimension 0
- program: float32 [400, 5120], P('rep', 'gene'), parts along dimension 0
There are 2 independent parts, one for each index of `rep`. A program takes and returns all parts, laid end to end along the dimension named above; an argument that names none is the same for every part. Nothing has to cross between parts.
All inputs are finite; a program needn't handle non-finite values.
Results may differ from a plain program's by a relative error of at most 0.0001.
Values sent between devices are 32-bit elements; how exact they have to be, the bound alone decides.
No kernel may reach another device: no remote copies, remote signals or barrier semaphores. Data moves between devices by JAX's collectives and lax.ppermute only.
A program may use at most 64 MiB of HBM per device.

v0:
```python
import jax
import jax.numpy as jnp
from jax import lax
from jax.sharding import PartitionSpec as P

ITERS = 2


highest = lax.Precision.HIGHEST


def contract(left, right, left_dim, right_dim):
    return lax.dot_general(
        left,
        right,
        (((left_dim,), (right_dim,)), ((), ())),
        precision=highest,
        preferred_element_type=jnp.float32,
    )


def update_usage(expression, usage, program):
    usage_top = contract(expression, program, 1, 1)
    program_gram = contract(program, program, 1, 1)
    usage_top, program_gram = lax.psum((usage_top, program_gram), "gene")
    return usage * usage_top / jnp.dot(usage, program_gram, precision=highest)


def update_program(expression, usage, program):
    program_top = contract(usage, expression, 0, 0)
    usage_gram = contract(usage, usage, 0, 0)
    program_top, usage_gram = lax.psum((program_top, usage_gram), "cell")
    return program * program_top / jnp.dot(usage_gram, program, precision=highest)


def body(counts, usage_init, program_init):
    expression = counts.astype(jnp.float32)
    usage = usage_init
    program = program_init
    for iteration in range(ITERS):
        usage = update_usage(expression, usage, program)
        program = update_program(expression, usage, program)
    return (usage, program)


def solution(mesh):
    return jax.shard_map(
        body,
        mesh=mesh,
        in_specs=(P("cell", "gene"), P(("rep", "cell"), None), P("rep", "gene")),
        out_specs=(P(("rep", "cell"), None), P("rep", "gene")),
        check_vma=False,
    )
```

profile of v0, /device:TPU:0, one launch (start us, length us, event | category | flops | bytes accessed | tf_op | source)
XLA Modules:
  0.0 245.1 jit_solution(8099532930881843260)
XLA Ops:
  7.2 0.0 copy-start.2
  7.2 0.0 all-reduce.11.cloned.1.call-start
  7.2 3.3 %fusion.12 = f32[200,200]{1,0:T(8,128)} fusion(f32[200,1280]{1,0:T(8,128)} %param.5), kind=kOutput, calls=%fused_computation.14 | convolution fusion | flops 614400000 | bytes 1184000 | tf_op jit(solution)/shard_map/dot_general | solution.py:13
  10.5 9.0 %fusion.6 = f32[1024,200]{0,1:T(8,128)} fusion(f32[200,1280]{1,0:T(8,128)} %param.5, s32[1024,1280]{1,0:T(8,128)} %param.3), kind=kOutput, calls=%fused_computation.6 | convolution fusion | flops 3147038720 | bytes 7086080 | tf_op jit(solution)/shard_map/dot_general | solution.py:13
  19.5 0.0 all-reduce.11.cloned.1.call-update
  19.5 0.0 all-reduce.15.cloned.1.call-start
  19.5 54.7 %all-reduce.11.cloned.1.call-done = (f32[200,200]{1,0:T(8,128)}, f32[1024,200]{0,1:T(8,128)}) async-done(((f32[200,200]{1,0:T(8,128)}, f32[1024,200]{0,1:T(8,128)}), (f32[200,200]{1,0:T(8,128)}, f32[1024,200]{0,1:T(8,128)})) %all-reduce.11.cloned.1.call-update) | async-done | bytes 979216 | tf_op jit(solution)/shard_map/psum | solution.py:25
  74.2 0.0 copy-done.2
  74.2 2.2 fusion.8
  76.4 0.0 copy-start
  76.4 1.5 fusion.13
  77.9 6.5 %fusion.4 = f32[200,1280]{1,0:T(8,128)} fusion(f32[1024,200]{0,1:T(8,128)S(1)} %fusion.8, s32[1024,1280]{1,0:T(8,128)} %param.3), kind=kOutput, calls=%fused_computation.4 | convolution fusion | flops 3147038720 | bytes 7086080 | tf_op jit(solution)/shard_map/dot_general | solution.py:13
  84.5 0.0 all-reduce.15.cloned.1.call-update
  84.5 0.2 all-reduce.9.cloned.1.call-start
  84.7 37.5 %all-reduce.15.cloned.1.call-done = (f32[200,200]{1,0:T(8,128)}, f32[200,1280]{1,0:T(8,128)}) async-done(((f32[200,200]{1,0:T(8,128)}, f32[200,1280]{1,0:T(8,128)}), (f32[200,200]{1,0:T(8,128)}, f32[200,1280]{1,0:T(8,128)})) %all-reduce.15.cloned.1.call-update) | async-done | bytes 1184016 | tf_op jit(solution)/shard_map/psum | solution.py:32
  122.2 0.0 copy-done
  122.2 2.4 convolution_divide_fusion.1
  124.6 1.7 fusion.14
  126.3 8.7 %fusion.9 = f32[1024,200]{0,1:T(8,128)} fusion(f32[200,1280]{1,0:T(8,128)S(1)} %convolution_divide_fusion.1, s32[1024,1280]{1,0:T(8,128)} %param.3), kind=kOutput, calls=%fused_computation.13 | convolution fusion | flops 3147038720 | bytes 7086080 | tf_op jit(solution)/shard_map/dot_general | solution.py:13
  135.0 0.0 all-reduce.9.cloned.1.call-update
  135.0 0.0 all-reduce.13.cloned.1.call-start
  135.1 52.0 %all-reduce.9.cloned.1.call-done = (f32[200,200]{1,0:T(8,128)}, f32[1024,200]{0,1:T(8,128)}) async-done(((f32[200,200]{1,0:T(8,128)}, f32[1024,200]{0,1:T(8,128)}), (f32[200,200]{1,0:T(8,128)}, f32[1024,200]{0,1:T(8,128)})) %all-reduce.9.cloned.1.call-update) | async-done | bytes 979216 | tf_op jit(solution)/shard_map/psum | solution.py:25
  187.1 2.2 convolution_divide_fusion.2
  189.3 0.0 copy-start.1
  189.3 1.5 fusion.15
  190.8 6.5 %fusion = f32[200,1280]{1,0:T(8,128)} fusion(f32[1024,200]{0,1:T(8,128)S(1)} %convolution_divide_fusion.2, s32[1024,1280]{1,0:T(8,128)} %param.3), kind=kOutput, calls=%fused_computation | convolution fusion | flops 3147038720 | bytes 7086080 | tf_op jit(solution)/shard_map/dot_general | solution.py:13
  197.4 0.0 all-reduce.13.cloned.1.call-update
  197.4 37.7 %all-reduce.13.cloned.1.call-done = (f32[200,200]{1,0:T(8,128)}, f32[200,1280]{1,0:T(8,128)}) async-done(((f32[200,200]{1,0:T(8,128)}, f32[200,1280]{1,0:T(8,128)}), (f32[200,200]{1,0:T(8,128)}, f32[200,1280]{1,0:T(8,128)})) %all-reduce.13.cloned.1.call-update) | async-done | bytes 1184016 | tf_op jit(solution)/shard_map/psum | solution.py:32
  235.1 3.4 %convolution_divide_fusion = f32[200,1280]{1,0:T(8,128)} fusion(f32[200,200]{1,0:T(8,128)} %get-tuple-element.6, f32[200,1280]{1,0:T(8,128)S(1)} %convolution_divide_fusion.1, f32[200,1280]{1,0:T(8,128)} %get-tuple-element.7), kind=kOutput, calls=%fused_computation.8 | convolution fusion | flops 614912000 | bytes 3232000 | tf_op jit(solution)/shard_map/dot_general | solution.py:33
  238.5 0.0 copy-done.1
Async XLA Ops:
  7.2 67.1 %copy-start.2 = (f32[1024,200]{0,1:T(8,128)S(1)}, f32[1024,200]{0,1:T(8,128)}, u32[]{:S(2)}) copy-start(f32[1024,200]{0,1:T(8,128)} %param.4) | copy-start | bytes 2457604
  7.2 67.0 %all-reduce.11.cloned.1.call-start = ((), (), s32[]{:S(2)}) async-start(), calls=%async_computation.1 | async-start | bytes 2048000 | tf_op jit(solution)/shard_map/psum | solution.py:25
  19.5 102.7 %all-reduce.15.cloned.1.call-start = ((), (), s32[]{:S(2)}) async-start(), calls=%async_computation.3 | async-start | bytes 2457600 | tf_op jit(solution)/shard_map/psum | solution.py:32
  76.4 45.8 %copy-start = (f32[200,1280]{1,0:T(8,128)S(1)}, f32[200,1280]{1,0:T(8,128)}, u32[]{:S(2)}) copy-start(f32[200,1280]{1,0:T(8,128)} %param.5) | copy-start | bytes 3072004
  84.5 102.6 %all-reduce.9.cloned.1.call-start = ((), (), s32[]{:S(2)}) async-start(), calls=%async_computation | async-start | bytes 2048000 | tf_op jit(solution)/shard_map/psum | solution.py:25
  135.0 100.1 %all-reduce.13.cloned.1.call-start = ((), (), s32[]{:S(2)}) async-start(), calls=%async_computation.2 | async-start | bytes 2457600 | tf_op jit(solution)/shard_map/psum | solution.py:32
  189.3 49.2 %copy-start.1 = (f32[1024,200]{0,1:T(8,128)}, f32[1024,200]{0,1:T(8,128)S(1)}, u32[]{:S(2)}) copy-start(f32[1024,200]{0,1:T(8,128)S(1)} %convolution_divide_fusion.2) | copy-start | bytes 2457604
Sparse Core Ops, SparseCore 0:
  19.6 54.5 all-reduce.10
  84.6 37.5 all-reduce.14
  135.1 51.9 all-reduce.8
  197.5 37.5 all-reduce.12
where the time goes:
time: 245 us
  waiting for transfers between devices  182 us (74%)
  matrix products  48.9 us (20%)
  between operations  13.8 us (6%)
    psum x2, waiting for transfers between devices, update_usage(): usage_top, program_gram = lax.psum((usage_top, program_gram), 'gene')  107 us
    psum x2, waiting for transfers between devices, update_program(): program_top, usage_gram = lax.psum((program_top, usage_gram), 'cell')  75.3 us
    dot_general x8, matrix products, contract(): lax.dot_general(left, right, (((left_dim,), (right_dim,)), ((), ())), pre...  38.8 us
    dot_general x2, matrix products, update_program(): jnp.dot(usage_gram, program, precision=highest)  5.74 us
  transfers between devices with their start and end apart: 4, of which 4 were waited for; matrix products, arithmetic and copies ran while one was open for 0% of the time, Pallas kernels for 0%

commit v1 on v0

v1 whole, which is shorter than its diff:
```python
import functools

import jax
import jax.numpy as jnp
from jax import lax
from jax.experimental import pallas as pl
from jax.experimental.pallas import tpu as pltpu
from jax.sharding import PartitionSpec as P

ITERS = 2
VMEM = pl.BlockSpec(memory_space=pltpu.VMEM)
SMEM = pl.BlockSpec(memory_space=pltpu.SMEM)
PARAMS = pltpu.CompilerParams(vmem_limit_bytes=32 * 1024 * 1024)
F32 = jnp.float32
BF16 = jnp.bfloat16


def split(a):
    high = a.astype(BF16)
    return high, (a - high.astype(F32)).astype(BF16)


def dot(a, b, a_dim, b_dim):
    return lax.dot_general(a, b, (((a_dim,), (b_dim,)), ((), ())), preferred_element_type=F32)


def dot3(a, b, a_dim, b_dim):
    ah, al = split(a)
    bh, bl = split(b)
    return dot(ah, bh, a_dim, b_dim) + (dot(al, bh, a_dim, b_dim) + dot(ah, bl, a_dim, b_dim))


def call(body, outs, *args, flops):
    specs = [SMEM if a.dtype == jnp.int32 and a.ndim == 1 else VMEM for a in args]
    shapes = [jax.ShapeDtypeStruct(s, F32) for s in outs]
    moved = sum(a.size * a.dtype.itemsize for a in args) + sum(s.size * 4 for s in shapes)
    return pl.pallas_call(
        body,
        out_shape=shapes,
        in_specs=specs,
        out_specs=[VMEM] * len(outs),
        compiler_params=PARAMS,
        cost_estimate=pl.CostEstimate(flops=flops, bytes_accessed=moved, transcendentals=0),
    )(*args)


def gram_rows(a, start, rows):
    def body(start_ref, a_ref, g_ref):
        part = a_ref[pl.ds(pl.multiple_of(start_ref[0], 8), rows), :]
        g_ref[...] = dot3(part, a_ref[...], 1, 1)

    k, n = a.shape
    return call(body, [(rows, k)], start, a, flops=6 * rows * k * n)[0]


def usage_top(program, x, start, rows):
    def body(start_ref, p_ref, x_ref, t_ref):
        ph, plo = split(p_ref[...])
        part = x_ref[pl.ds(pl.multiple_of(start_ref[0], 16), rows), :]
        t_ref[...] = dot(ph, part, 1, 1) + dot(plo, part, 1, 1)

    k, n = program.shape
    return call(body, [(k, rows)], start, program, x, flops=4 * rows * k * n)[0]


def usage_update(gram, usage, top_a, top_b):
    def body(g_ref, u_ref, a_ref, b_ref, o_ref):
        u = u_ref[...]
        o_ref[...] = u * (a_ref[...] + b_ref[...]) / dot3(g_ref[...], u, 1, 0)

    k, n = usage.shape
    return call(body, [(k, n)], gram, usage, top_a, top_b, flops=6 * k * k * n)[0]


def program_top(usage, x, start, column, columns):
    def body(start_ref, column_ref, u_ref, x_ref, t_ref):
        uh, ul = split(u_ref[...])
        rows = pl.ds(pl.multiple_of(start_ref[0], 16), u_ref.shape[1])
        part = x_ref[rows, pl.ds(pl.multiple_of(column_ref[0], 128), columns)]
        t_ref[...] = dot(uh, part, 1, 0) + dot(ul, part, 1, 0)

    if columns % 128:
        x = lax.dynamic_slice_in_dim(x, column[0], columns, 1)
        column = jnp.zeros_like(column)
    k, n = usage.shape
    return call(body, [(k, columns)], start, column, usage, x, flops=4 * k * n * columns)[0]


def exchange(a, axis, size, flip):
    return lax.ppermute(a, axis, [(i, i ^ flip) for i in range(size)])


def body(genes, cells, counts, usage_init, program_init):
    x = counts.astype(BF16)
    cell, gene = lax.axis_index("cell"), lax.axis_index("gene")
    core = cell % 2
    half = (gene ^ (gene >> 1)) % 2
    n_cells, n_genes = counts.shape
    k = program_init.shape[0]
    rows, columns = n_cells // 2, n_genes // 2
    grows = -(-k // 16) * 8
    usage_t = usage_init.T

    def at(index):
        return jnp.full((1,), index, jnp.int32)

    own, other = at(half * rows), at((1 - half) * rows)
    own_col, other_col = at(core * columns), at((1 - core) * columns)
    grow, other_grow = at(core * (k - grows)), at((1 - core) * (k - grows))

    def join(mine, theirs, which, axis):
        first = jnp.where(which == 0, mine, theirs)
        second = jnp.where(which == 0, theirs, mine)
        return first, second, jnp.concatenate([first, second], axis)

    def whole_gram(mine):
        theirs = exchange(mine, "cell", cells, 1)
        first, second, _ = join(mine, theirs, core, 0)
        return jnp.concatenate([first, second[2 * grows - k :]], 0)

    usage = lax.dynamic_slice_in_dim(usage_t, half * rows, rows, 1)
    program = program_init
    program_half = lax.dynamic_slice_in_dim(program_init, core * columns, columns, 1)
    for _ in range(ITERS):
        gram = gram_rows(program, grow, grows)
        send = usage_top(program, x, other, rows)
        gram = gram + exchange(gram, "gene", genes, 1)
        near = exchange(send, "gene", genes, 1)
        keep = usage_top(program, x, own, rows)
        top = keep + near
        step = 2
        while step < genes:
            gram = gram + exchange(gram, "gene", genes, 2 * step - 1)
            step *= 2
        gram = whole_gram(gram)
        step = 2
        while step < genes:
            add = exchange(top, "gene", genes, 2 * step - 1)
            step *= 2
            if step < genes:
                top = top + add
        usage = usage_update(gram, usage, top, add)
        usage_other = exchange(usage, "gene", genes, 1)
        usage_first, usage_second, usage_t = join(usage, usage_other, half, 1)

        zero = at(0)
        send = program_top(usage_t, x, zero, other_col, columns)
        near = exchange(send, "cell", cells, 1)
        gram_send = gram_rows(usage_t, other_grow, grows)
        gram_near = exchange(gram_send, "cell", cells, 1)
        gram_keep = gram_rows(usage_t, grow, grows)
        keep = program_top(usage_t, x, zero, own_col, columns)
        top = keep + near
        gram = gram_keep + gram_near
        step = 2
        while step < cells:
            gram = gram + exchange(gram, "cell", cells, step)
            step *= 2
        gram = whole_gram(gram)
        step = 2
        while step < cells:
            add = exchange(top, "cell", cells, step)
            step *= 2
            if step < cells:
                top = top + add
        program_half = usage_update(gram, program_half, top, add)
        program_other = exchange(program_half, "cell", cells, 1)
        _, _, program = join(program_half, program_other, core, 1)
    return usage_t.T, program


def solution(mesh):
    return jax.shard_map(
        functools.partial(body, mesh.shape["gene"], mesh.shape["cell"]),
        mesh=mesh,
        in_specs=(P("cell", "gene"), P(("rep", "cell"), None), P("rep", "gene")),
        out_specs=(P(("rep", "cell"), None), P("rep", "gene")),
        check_vma=False,
    )
```

time: 245 us -> 186 us (0.76)
  waiting for transfers between devices: 182 us -> 104 us
  matrix products: 48.9 us -> 0 us
  starting transfers between devices: 0.34 us -> 43 us
  Pallas kernels: 0 us -> 15.8 us
  between operations: 13.8 us -> 1.09 us
  other arithmetic: 0 us -> 11.9 us
  local copies, waits for them, and re-layouts: 0.02 us -> 9.86 us
    psum x4 -> x0, waiting for transfers between devices: 182 us -> none  [the longest x2 107 us: update_usage(): usage_top, program_gram = lax.psum((usage_top, program_gram), 'gene')]
    ppermute x0 -> x24, waiting for transfers between devices: none -> 104 us  [exchange(): return lax.ppermute(a, axis, [(i, i ^ flip) for i in range(size)])]
    dot_general x12 -> x0, matrix products: 48.9 us -> none  [the longest x8 38.8 us: contract(): lax.dot_general(left, right, (((left_dim,), (right_dim,)), ((), ())), pre...]
    ppermute x0 -> x24, starting transfers between devices: none -> 43 us  [exchange(): return lax.ppermute(a, axis, [(i, i ^ flip) for i in range(size)])]
    pallas_call x0 -> x18, Pallas kernels: none -> 15.8 us  [call(): pl.pallas_call(body, out_shape=shapes, in_specs=specs, out_specs=[VMEM] *...]
    unnamed x6 -> x20, local copies, waits for them, and re-layouts: 0.02 us -> 7.98 us
    add x0 -> x12, other arithmetic: none -> 4.28 us  [the longest x4 2.32 us: body(): top = keep + near]
    convert_element_type x0 -> x1, other arithmetic: none -> 2.95 us  [body(): x = counts.astype(BF16)]
  transfers between devices with their start and end apart: 4 -> 24, of which waited for: 4 -> 15; matrix products, arithmetic and copies ran while one was open for 0% -> 4% of each run, Pallas kernels for 0% -> 4%
where the time goes in v1:
time: 186 us
  waiting for transfers between devices  104 us (56%)
  starting transfers between devices  43 us (23%)
  Pallas kernels  15.8 us (8%)
  other arithmetic  11.9 us (6%)
  local copies, waits for them, and re-layouts  9.86 us (5%)
    ppermute x24, waiting for transfers between devices, exchange(): return lax.ppermute(a, axis, [(i, i ^ flip) for i in range(size)])  104 us
    ppermute x24, starting transfers between devices, exchange(): return lax.ppermute(a, axis, [(i, i ^ flip) for i in range(size)])  43 us
    pallas_call x18, Pallas kernels, call(): pl.pallas_call(body, out_shape=shapes, in_specs=specs, out_specs=[VMEM] *...  15.8 us
    unnamed x20, local copies, waits for them, and re-layouts  7.98 us
  transfers between devices with their start and end apart: 24, of which 15 were waited for; matrix products, arithmetic and copies ran while one was open for 4% of the time, Pallas kernels for 4%

profile of v1, /device:TPU:0, one launch (start us, length us, event | category | flops | bytes accessed | tf_op | source)
XLA Modules:
  0.0 185.8 jit_solution(5314478573371205017)
XLA Ops:
  0.7 2.9 %convert_element_type.3.x_ref = bf16[1024,1280]{1,0:T(8,128)(2,1)S(1)} convert(s32[1024,1280]{1,0:T(8,128)} %param.3) | non-fusion elementwise | flops 1310720 | bytes 7864320 | tf_op jit(solution)/shard_map/convert_element_type | solution.py:94
  3.6 1.2 copy-done.5
  4.8 1.7 shard_map.52
  6.6 3.0 %collective-permute-start.3 = (f32[200,512]{1,0:T(8,128)}, f32[200,512]{1,0:T(8,128)}, u32[]{:S(2)}, u32[]{:S(2)}) collective-permute-start(f32[200,512]{1,0:T(8,128)} %shard_map.52), channel_id=1, source_target_pairs={{0,1},{1,0},{2,3},{3,2},{4,5},{5,4},{6,7},{7,6},{8,9},{9,8},{10,11... | collective-permute-start | bytes 1228808 | tf_op jit(solution)/shard_map/ppermute | solution.py:90
  9.6 1.2 copy-done.6
  10.8 0.7 shard_map.50
  11.6 10.0 %collective-permute-done = f32[104,200]{1,0:T(8,128)S(1)} collective-permute-done((f32[104,200]{1,0:T(8,128)S(1)}, f32[104,200]{1,0:T(8,128)S(1)}, u32[]{:S(2)}, u32[]{:S(2)}) %collective-permute-start) | collective-permute-done | bytes 83232 | tf_op jit(solution)/shard_map/ppermute | solution.py:90
  21.6 3.8 %collective-permute-start.1 = (f32[104,200]{1,0:T(8,128)S(1)}, f32[104,200]{1,0:T(8,128)}, u32[]{:S(2)}, u32[]{:S(2)}) collective-permute-start(f32[104,200]{1,0:T(8,128)S(1)} %add.51), channel_id=1, source_target_pairs={{0,3},{1,2},{2,1},{3,0},{4,7},{5,6},{6,5},{7,4},{8,11},{9,10},{10,... | collective-permute-start | bytes 249608 | tf_op jit(solution)/shard_map/ppermute | solution.py:90
  25.4 2.9 %collective-permute-done.1 = f32[104,200]{1,0:T(8,128)} collective-permute-done((f32[104,200]{1,0:T(8,128)S(1)}, f32[104,200]{1,0:T(8,128)}, u32[]{:S(2)}, u32[]{:S(2)}) %collective-permute-start.1) | collective-permute-done | bytes 83232 | tf_op jit(solution)/shard_map/ppermute | solution.py:90
  28.3 1.0 add.52
  29.4 0.8 dynamic-slice_bitcast_fusion.u_ref
  30.2 1.2 copy-done.7
  31.4 1.0 shard_map.51
  32.4 1.1 add.54.a_ref
  33.4 3.9 %collective-permute-start.4 = (f32[200,512]{1,0:T(8,128)S(1)}, f32[200,512]{1,0:T(8,128)S(1)}, u32[]{:S(2)}, u32[]{:S(2)}) collective-permute-start(f32[200,512]{1,0:T(8,128)S(1)} %add.54.a_ref), channel_id=1, source_target_pairs={{0,3},{1,2},{2,1},{3,0},{4,7},{5,6},{6,5},{7,4},{8,11},{9,10},{10,... | collective-permute-start | bytes 1228808 | tf_op jit(solution)/shard_map/ppermute | solution.py:90
  37.3 0.9 slice_select_fusion.3
  38.3 9.3 %collective-permute-done.4.b_ref = f32[200,512]{1,0:T(8,128)S(1)} collective-permute-done((f32[200,512]{1,0:T(8,128)S(1)}, f32[200,512]{1,0:T(8,128)S(1)}, u32[]{:S(2)}, u32[]{:S(2)}) %collective-permute-start.4) | collective-permute-done | bytes 409632 | tf_op jit(solution)/shard_map/ppermute | solution.py:90
  47.5 1.1 shard_map.53.u_ref
  48.7 8.6 %collective-permute-start.5 = (f32[200,512]{1,0:T(8,128)}, f32[200,512]{1,0:T(8,128)}, u32[]{:S(2)}, u32[]{:S(2)}) collective-permute-start(f32[200,512]{1,0:T(8,128)} %shard_map.53.u_ref), channel_id=1, source_target_pairs={{0,1},{1,0},{2,3},{3,2},{4,5},{5,4},{6,7},{7,6},{8,9},{9,8},{10,11... | collective-permute-start | bytes 1228808 | tf_op jit(solution)/shard_map/ppermute | solution.py:90
  57.2 9.8 %collective-permute-done.5 = f32[200,512]{1,0:T(8,128)} collective-permute-done((f32[200,512]{1,0:T(8,128)}, f32[200,512]{1,0:T(8,128)}, u32[]{:S(2)}, u32[]{:S(2)}) %collective-permute-start.5) | collective-permute-done | bytes 409632 | tf_op jit(solution)/shard_map/ppermute | solution.py:90
  67.1 1.2 broadcast_select_fusion.7
  68.4 1.7 shard_map.57
  70.0 0.9 copy-done.1
  70.9 1.1 copy-done.2
  72.1 0.6 shard_map.55
  72.6 0.6 collective-permute-start.6
  73.2 1.1 copy-done.3
  74.3 0.5 shard_map.54
  74.9 1.6 collective-permute-start.7
  76.5 3.5 %collective-permute-done.7 = f32[104,200]{1,0:T(8,128)} collective-permute-done((f32[104,200]{1,0:T(8,128)S(1)}, f32[104,200]{1,0:T(8,128)}, u32[]{:S(2)}, u32[]{:S(2)}) %collective-permute-start.7) | collective-permute-done | bytes 83232 | tf_op jit(solution)/shard_map/ppermute | solution.py:90
  80.0 0.9 add.56
  81.0 1.1 constant_dynamic-slice_fusion.u_ref
  82.1 1.1 copy-done.4
  83.2 0.8 shard_map.56
  84.1 1.1 add.58.a_ref
  85.2 1.6 collective-permute-start.10
  86.8 12.5 %collective-permute-done.10.b_ref = f32[200,640]{1,0:T(8,128)S(1)} collective-permute-done((f32[200,640]{1,0:T(8,128)S(1)}, f32[200,640]{1,0:T(8,128)S(1)}, u32[]{:S(2)}, u32[]{:S(2)}) %collective-permute-start.10) | collective-permute-done | bytes 512032 | tf_op jit(solution)/shard_map/ppermute | solution.py:90
  99.3 0.4 shard_map.58.u_ref
  99.9 1.9 %collective-permute-done.11 = f32[200,640]{1,0:T(8,128)S(1)} collective-permute-done((f32[200,640]{1,0:T(8,128)S(1)}, f32[200,640]{1,0:T(8,128)S(1)}, u32[]{:S(2)}, u32[]{:S(2)}) %collective-permute-start.11) | collective-permute-done | bytes 512032 | tf_op jit(solution)/shard_map/ppermute | solution.py:90
  101.9 1.0 shard_map.61
  102.9 1.8 collective-permute-start.15
  104.7 0.7 shard_map.59
  105.7 11.0 %collective-permute-done.12 = f32[104,200]{1,0:T(8,128)S(1)} collective-permute-done((f32[104,200]{1,0:T(8,128)S(1)}, f32[104,200]{1,0:T(8,128)S(1)}, u32[]{:S(2)}, u32[]{:S(2)}) %collective-permute-start.12) | collective-permute-done | bytes 83232 | tf_op jit(solution)/shard_map/ppermute | solution.py:90
  116.8 2.5 %collective-permute-start.13 = (f32[104,200]{1,0:T(8,128)S(1)}, f32[104,200]{1,0:T(8,128)S(1)}, u32[]{:S(2)}, u32[]{:S(2)}) collective-permute-start(f32[104,200]{1,0:T(8,128)S(1)} %add.59), channel_id=1, source_target_pairs={{0,3},{1,2},{2,1},{3,0},{4,7},{5,6},{6,5},{7,4},{8,11},{9,10},{10,... | collective-permute-start | bytes 249608 | tf_op jit(solution)/shard_map/ppermute | solution.py:90
  119.3 4.1 %collective-permute-done.13 = f32[104,200]{1,0:T(8,128)S(1)} collective-permute-done((f32[104,200]{1,0:T(8,128)S(1)}, f32[104,200]{1,0:T(8,128)S(1)}, u32[]{:S(2)}, u32[]{:S(2)}) %collective-permute-start.13) | collective-permute-done | bytes 83232 | tf_op jit(solution)/shard_map/ppermute | solution.py:90
  123.5 1.0 shard_map.60
  124.5 2.5 %collective-permute-start.16 = (f32[200,512]{1,0:T(8,128)S(1)}, f32[200,512]{1,0:T(8,128)S(1)}, u32[]{:S(2)}, u32[]{:S(2)}) collective-permute-start(f32[200,512]{1,0:T(8,128)S(1)} %add.61.a_ref), channel_id=1, source_target_pairs={{0,3},{1,2},{2,1},{3,0},{4,7},{5,6},{6,5},{7,4},{8,11},{9,10},{10,... | collective-permute-start | bytes 1228808 | tf_op jit(solution)/shard_map/ppermute | solution.py:90
  127.1 11.3 %collective-permute-done.16.b_ref = f32[200,512]{1,0:T(8,128)S(1)} collective-permute-done((f32[200,512]{1,0:T(8,128)S(1)}, f32[200,512]{1,0:T(8,128)S(1)}, u32[]{:S(2)}, u32[]{:S(2)}) %collective-permute-start.16) | collective-permute-done | bytes 409632 | tf_op jit(solution)/shard_map/ppermute | solution.py:90
  138.4 1.4 shard_map.62
  139.7 8.6 %collective-permute-start.17 = (f32[200,512]{1,0:T(8,128)S(1)}, f32[200,512]{1,0:T(8,128)S(1)}, u32[]{:S(2)}, u32[]{:S(2)}) collective-permute-start(f32[200,512]{1,0:T(8,128)S(1)} %shard_map.62), channel_id=1, source_target_pairs={{0,1},{1,0},{2,3},{3,2},{4,5},{5,4},{6,7},{7,6},{8,9},{9,8},{10,11... | collective-permute-start | bytes 1228808 | tf_op jit(solution)/shard_map/ppermute | solution.py:90
  148.4 9.3 %collective-permute-done.17 = f32[200,512]{1,0:T(8,128)S(1)} collective-permute-done((f32[200,512]{1,0:T(8,128)S(1)}, f32[200,512]{1,0:T(8,128)S(1)}, u32[]{:S(2)}, u32[]{:S(2)}) %collective-permute-start.17) | collective-permute-done | bytes 409632 | tf_op jit(solution)/shard_map/ppermute | solution.py:90
  157.8 1.0 pad_maximum_fusion.3
  158.8 0.9 shard_map.66
  159.7 0.6 shard_map.64
  160.3 0.6 collective-permute-start.18
  160.8 0.6 shard_map.63
  161.8 1.6 collective-permute-start.19
  163.4 3.7 %collective-permute-done.19 = f32[104,200]{1,0:T(8,128)S(1)} collective-permute-done((f32[104,200]{1,0:T(8,128)S(1)}, f32[104,200]{1,0:T(8,128)S(1)}, u32[]{:S(2)}, u32[]{:S(2)}) %collective-permute-start.19) | collective-permute-done | bytes 83232 | tf_op jit(solution)/shard_map/ppermute | solution.py:90
  167.2 0.9 shard_map.65
  168.1 1.6 collective-permute-start.22
  169.8 12.5 %collective-permute-done.22.b_ref = f32[200,640]{1,0:T(8,128)S(1)} collective-permute-done((f32[200,640]{1,0:T(8,128)S(1)}, f32[200,640]{1,0:T(8,128)S(1)}, u32[]{:S(2)}, u32[]{:S(2)}) %collective-permute-start.22) | collective-permute-done | bytes 512032 | tf_op jit(solution)/shard_map/ppermute | solution.py:90
  182.3 0.5 shard_map.67
  182.8 1.9 %collective-permute-done.23 = f32[200,640]{1,0:T(8,128)S(1)} collective-permute-done((f32[200,640]{1,0:T(8,128)S(1)}, f32[200,640]{1,0:T(8,128)S(1)}, u32[]{:S(2)}, u32[]{:S(2)}) %collective-permute-start.23) | collective-permute-done | bytes 512032 | tf_op jit(solution)/shard_map/ppermute | solution.py:90
  184.8 1.0 pad_maximum_fusion.1
  (57 shorter events, 2.1 us)
Async XLA Ops:
  0.6 28.7 %copy-start = (f32[1024,200]{0,1:T(8,128)S(1)}, f32[1024,200]{0,1:T(8,128)}, u32[]{:S(2)}) copy-start(f32[1024,200]{0,1:T(8,128)} %param.4) | copy-start | bytes 2457604
  3.6 1.2 copy-start.5
  6.6 25.8 %collective-permute-start.3 = (f32[200,512]{1,0:T(8,128)}, f32[200,512]{1,0:T(8,128)}, u32[]{:S(2)}, u32[]{:S(2)}) collective-permute-start(f32[200,512]{1,0:T(8,128)} %shard_map.52), channel_id=1, source_target_pairs={{0,1},{1,0},{2,3},{3,2},{4,5},{5,4},{6,7},{7,6},{8,9},{9,8},{10,11... | collective-permute-start | bytes 1228808 | tf_op jit(solution)/shard_map/ppermute | solution.py:90
  9.6 1.2 copy-start.6
  11.5 10.1 %collective-permute-start = (f32[104,200]{1,0:T(8,128)S(1)}, f32[104,200]{1,0:T(8,128)S(1)}, u32[]{:S(2)}, u32[]{:S(2)}) collective-permute-start(f32[104,200]{1,0:T(8,128)S(1)} %shard_map.50), channel_id=1, source_target_pairs={{0,1},{1,0},{2,3},{3,2},{4,5},{5,4},{6,7},{7,6},{8,9},{9,8},{10,11... | collective-permute-start | bytes 249608 | tf_op jit(solution)/shard_map/ppermute | solution.py:90
  21.6 3.9 %copy-start.9 = (f32[104,200]{1,0:T(8,128)}, f32[104,200]{1,0:T(8,128)S(1)}, u32[]{:S(2)}) copy-start(f32[104,200]{1,0:T(8,128)S(1)} %add.51) | copy-start | bytes 249604
  21.6 6.7 %collective-permute-start.1 = (f32[104,200]{1,0:T(8,128)S(1)}, f32[104,200]{1,0:T(8,128)}, u32[]{:S(2)}, u32[]{:S(2)}) collective-permute-start(f32[104,200]{1,0:T(8,128)S(1)} %add.51), channel_id=1, source_target_pairs={{0,3},{1,2},{2,1},{3,0},{4,7},{5,6},{6,5},{7,4},{8,11},{9,10},{10,... | collective-permute-start | bytes 249608 | tf_op jit(solution)/shard_map/ppermute | solution.py:90
  29.3 8.0 %collective-permute-start.2 = (f32[104,200]{1,0:T(8,128)S(1)}, f32[104,200]{1,0:T(8,128)}, u32[]{:S(2)}, u32[]{:S(2)}) collective-permute-start(f32[104,200]{1,0:T(8,128)S(1)} %add.52), channel_id=1, source_target_pairs={{0,4},{4,0},{8,12},{12,8},{1,5},{5,1},{9,13},{13,9},{2,6},{6,2},{1... | collective-permute-start | bytes 249608 | tf_op jit(solution)/shard_map/ppermute | solution.py:90
  30.2 1.2 copy-start.7
  31.4 16.2 %copy-start.8 = (f32[200,512]{1,0:T(8,128)S(1)}, f32[200,512]{1,0:T(8,128)}, u32[]{:S(2)}) copy-start(f32[200,512]{1,0:T(8,128)} %dynamic-slice_bitcast_fusion.u_ref) | copy-start | bytes 1228804
  33.4 14.1 %collective-permute-start.4 = (f32[200,512]{1,0:T(8,128)S(1)}, f32[200,512]{1,0:T(8,128)S(1)}, u32[]{:S(2)}, u32[]{:S(2)}) collective-permute-start(f32[200,512]{1,0:T(8,128)S(1)} %add.54.a_ref), channel_id=1, source_target_pairs={{0,3},{1,2},{2,1},{3,0},{4,7},{5,6},{6,5},{7,4},{8,11},{9,10},{10,... | collective-permute-start | bytes 1228808 | tf_op jit(solution)/shard_map/ppermute | solution.py:90
  48.7 18.4 %collective-permute-start.5 = (f32[200,512]{1,0:T(8,128)}, f32[200,512]{1,0:T(8,128)}, u32[]{:S(2)}, u32[]{:S(2)}) collective-permute-start(f32[200,512]{1,0:T(8,128)} %shard_map.53.u_ref), channel_id=1, source_target_pairs={{0,1},{1,0},{2,3},{3,2},{4,5},{5,4},{6,7},{7,6},{8,9},{9,8},{10,11... | collective-permute-start | bytes 1228808 | tf_op jit(solution)/shard_map/ppermute | solution.py:90
  70.0 0.9 copy-start.1
  70.9 13.1 %collective-permute-start.9 = (f32[200,640]{1,0:T(8,128)}, f32[200,640]{1,0:T(8,128)}, u32[]{:S(2)}, u32[]{:S(2)}) collective-permute-start(f32[200,640]{1,0:T(8,128)} %shard_map.57), channel_id=1, source_target_pairs={{0,4},{4,0},{8,12},{12,8},{1,5},{5,1},{9,13},{13,9},{2,6},{6,2},{1... | collective-permute-start | bytes 1536008 | tf_op jit(solution)/shard_map/ppermute | solution.py:90
  70.9 1.1 copy-start.2
  72.6 2.3 %collective-permute-start.6 = (f32[104,200]{1,0:T(8,128)S(1)}, f32[104,200]{1,0:T(8,128)S(1)}, u32[]{:S(2)}, u32[]{:S(2)}) collective-permute-start(f32[104,200]{1,0:T(8,128)S(1)} %shard_map.55), channel_id=1, source_target_pairs={{0,4},{4,0},{8,12},{12,8},{1,5},{5,1},{9,13},{13,9},{2,6},{6,2},{1... | collective-permute-start | bytes 249608 | tf_op jit(solution)/shard_map/ppermute | solution.py:90
  73.2 1.1 copy-start.3
  74.9 5.1 %collective-permute-start.7 = (f32[104,200]{1,0:T(8,128)S(1)}, f32[104,200]{1,0:T(8,128)}, u32[]{:S(2)}, u32[]{:S(2)}) collective-permute-start(f32[104,200]{1,0:T(8,128)S(1)} %add.55), channel_id=1, source_target_pairs={{0,8},{4,12},{8,0},{12,4},{1,9},{5,13},{9,1},{13,5},{2,10},{6,14},... | collective-permute-start | bytes 249608 | tf_op jit(solution)/shard_map/ppermute | solution.py:90
  80.9 5.8 %collective-permute-start.8 = (f32[104,200]{1,0:T(8,128)S(1)}, f32[104,200]{1,0:T(8,128)S(1)}, u32[]{:S(2)}, u32[]{:S(2)}) collective-permute-start(f32[104,200]{1,0:T(8,128)S(1)} %add.56), channel_id=1, source_target_pairs={{0,4},{4,0},{8,12},{12,8},{1,5},{5,1},{9,13},{13,9},{2,6},{6,2},{1... | collective-permute-start | bytes 249608 | tf_op jit(solution)/shard_map/ppermute | solution.py:90
  82.1 1.1 copy-start.4
  85.2 14.1 %collective-permute-start.10 = (f32[200,640]{1,0:T(8,128)S(1)}, f32[200,640]{1,0:T(8,128)S(1)}, u32[]{:S(2)}, u32[]{:S(2)}) collective-permute-start(f32[200,640]{1,0:T(8,128)S(1)} %add.58.a_ref), channel_id=1, source_target_pairs={{0,8},{4,12},{8,0},{12,4},{1,9},{5,13},{9,1},{13,5},{2,10},{6,14},... | collective-permute-start | bytes 1536008 | tf_op jit(solution)/shard_map/ppermute | solution.py:90
  99.8 2.0 %collective-permute-start.11 = (f32[200,640]{1,0:T(8,128)S(1)}, f32[200,640]{1,0:T(8,128)S(1)}, u32[]{:S(2)}, u32[]{:S(2)}) collective-permute-start(f32[200,640]{1,0:T(8,128)S(1)} %shard_map.58.u_ref), channel_id=1, source_target_pairs={{0,4},{4,0},{8,12},{12,8},{1,5},{5,1},{9,13},{13,9},{2,6},{6,2},{1... | collective-permute-start | bytes 1536008 | tf_op jit(solution)/shard_map/ppermute | solution.py:90
  102.9 21.6 %collective-permute-start.15 = (f32[200,512]{1,0:T(8,128)S(1)}, f32[200,512]{1,0:T(8,128)S(1)}, u32[]{:S(2)}, u32[]{:S(2)}) collective-permute-start(f32[200,512]{1,0:T(8,128)S(1)} %shard_map.61), channel_id=1, source_target_pairs={{0,1},{1,0},{2,3},{3,2},{4,5},{5,4},{6,7},{7,6},{8,9},{9,8},{10,11... | collective-permute-start | bytes 1228808 | tf_op jit(solution)/shard_map/ppermute | solution.py:90
  105.3 11.4 %collective-permute-start.12 = (f32[104,200]{1,0:T(8,128)S(1)}, f32[104,200]{1,0:T(8,128)S(1)}, u32[]{:S(2)}, u32[]{:S(2)}) collective-permute-start(f32[104,200]{1,0:T(8,128)S(1)} %shard_map.59), channel_id=1, source_target_pairs={{0,1},{1,0},{2,3},{3,2},{4,5},{5,4},{6,7},{7,6},{8,9},{9,8},{10,11... | collective-permute-start | bytes 249608 | tf_op jit(solution)/shard_map/ppermute | solution.py:90
  116.8 6.6 %collective-permute-start.13 = (f32[104,200]{1,0:T(8,128)S(1)}, f32[104,200]{1,0:T(8,128)S(1)}, u32[]{:S(2)}, u32[]{:S(2)}) collective-permute-start(f32[104,200]{1,0:T(8,128)S(1)} %add.59), channel_id=1, source_target_pairs={{0,3},{1,2},{2,1},{3,0},{4,7},{5,6},{6,5},{7,4},{8,11},{9,10},{10,... | collective-permute-start | bytes 249608 | tf_op jit(solution)/shard_map/ppermute | solution.py:90
  123.4 3.6 %collective-permute-start.14 = (f32[104,200]{1,0:T(8,128)S(1)}, f32[104,200]{1,0:T(8,128)S(1)}, u32[]{:S(2)}, u32[]{:S(2)}) collective-permute-start(f32[104,200]{1,0:T(8,128)S(1)} %add.60), channel_id=1, source_target_pairs={{0,4},{4,0},{8,12},{12,8},{1,5},{5,1},{9,13},{13,9},{2,6},{6,2},{1... | collective-permute-start | bytes 249608 | tf_op jit(solution)/shard_map/ppermute | solution.py:90
  124.5 13.8 %collective-permute-start.16 = (f32[200,512]{1,0:T(8,128)S(1)}, f32[200,512]{1,0:T(8,128)S(1)}, u32[]{:S(2)}, u32[]{:S(2)}) collective-permute-start(f32[200,512]{1,0:T(8,128)S(1)} %add.61.a_ref), channel_id=1, source_target_pairs={{0,3},{1,2},{2,1},{3,0},{4,7},{5,6},{6,5},{7,4},{8,11},{9,10},{10,... | collective-permute-start | bytes 1228808 | tf_op jit(solution)/shard_map/ppermute | solution.py:90
  139.7 17.9 %collective-permute-start.17 = (f32[200,512]{1,0:T(8,128)S(1)}, f32[200,512]{1,0:T(8,128)S(1)}, u32[]{:S(2)}, u32[]{:S(2)}) collective-permute-start(f32[200,512]{1,0:T(8,128)S(1)} %shard_map.62), channel_id=1, source_target_pairs={{0,1},{1,0},{2,3},{3,2},{4,5},{5,4},{6,7},{7,6},{8,9},{9,8},{10,11... | collective-permute-start | bytes 1228808 | tf_op jit(solution)/shard_map/ppermute | solution.py:90
  159.6 8.4 %collective-permute-start.21 = (f32[200,640]{1,0:T(8,128)S(1)}, f32[200,640]{1,0:T(8,128)S(1)}, u32[]{:S(2)}, u32[]{:S(2)}) collective-permute-start(f32[200,640]{1,0:T(8,128)S(1)} %shard_map.66), channel_id=1, source_target_pairs={{0,4},{4,0},{8,12},{12,8},{1,5},{5,1},{9,13},{13,9},{2,6},{6,2},{1... | collective-permute-start | bytes 1536008 | tf_op jit(solution)/shard_map/ppermute | solution.py:90
  160.3 1.5 collective-permute-start.18
  161.8 5.3 %collective-permute-start.19 = (f32[104,200]{1,0:T(8,128)S(1)}, f32[104,200]{1,0:T(8,128)S(1)}, u32[]{:S(2)}, u32[]{:S(2)}) collective-permute-start(f32[104,200]{1,0:T(8,128)S(1)} %add.62), channel_id=1, source_target_pairs={{0,8},{4,12},{8,0},{12,4},{1,9},{5,13},{9,1},{13,5},{2,10},{6,14},... | collective-permute-start | bytes 249608 | tf_op jit(solution)/shard_map/ppermute | solution.py:90
  167.1 2.6 %collective-permute-start.20 = (f32[104,200]{1,0:T(8,128)S(1)}, f32[104,200]{1,0:T(8,128)S(1)}, u32[]{:S(2)}, u32[]{:S(2)}) collective-permute-start(f32[104,200]{1,0:T(8,128)S(1)} %add.63), channel_id=1, source_target_pairs={{0,4},{4,0},{8,12},{12,8},{1,5},{5,1},{9,13},{13,9},{2,6},{6,2},{1... | collective-permute-start | bytes 249608 | tf_op jit(solution)/shard_map/ppermute | solution.py:90
  168.1 14.1 %collective-permute-start.22 = (f32[200,640]{1,0:T(8,128)S(1)}, f32[200,640]{1,0:T(8,128)S(1)}, u32[]{:S(2)}, u32[]{:S(2)}) collective-permute-start(f32[200,640]{1,0:T(8,128)S(1)} %add.64.a_ref), channel_id=1, source_target_pairs={{0,8},{4,12},{8,0},{12,4},{1,9},{5,13},{9,1},{13,5},{2,10},{6,14},... | collective-permute-start | bytes 1536008 | tf_op jit(solution)/shard_map/ppermute | solution.py:90
  182.7 2.0 %collective-permute-start.23 = (f32[200,640]{1,0:T(8,128)S(1)}, f32[200,640]{1,0:T(8,128)S(1)}, u32[]{:S(2)}, u32[]{:S(2)}) collective-permute-start(f32[200,640]{1,0:T(8,128)S(1)} %shard_map.67), channel_id=1, source_target_pairs={{0,4},{4,0},{8,12},{12,8},{1,5},{5,1},{9,13},{13,9},{2,6},{6,2},{1... | collective-permute-start | bytes 1536008 | tf_op jit(solution)/shard_map/ppermute | solution.py:90

commit v2 on v1

--- a/solution.py
+++ b/solution.py
@@ -10,7 +10,7 @@
 ITERS = 2
 VMEM = pl.BlockSpec(memory_space=pltpu.VMEM)
 SMEM = pl.BlockSpec(memory_space=pltpu.SMEM)
-PARAMS = pltpu.CompilerParams(vmem_limit_bytes=32 * 1024 * 1024)
+PARAMS = pltpu.CompilerParams(vmem_limit_bytes=12 * 1024 * 1024)
 F32 = jnp.float32
 BF16 = jnp.bfloat16
 
@@ -63,13 +63,14 @@
     return call(body, [(k, rows)], start, program, x, flops=4 * rows * k * n)[0]
 
 
-def usage_update(gram, usage, top_a, top_b):
+def update(gram, factor, first, rows, top_a, top_b):
     def body(g_ref, u_ref, a_ref, b_ref, o_ref):
         u = u_ref[...]
-        o_ref[...] = u * (a_ref[...] + b_ref[...]) / dot3(g_ref[...], u, 1, 0)
+        part = u_ref[first : first + rows, :]
+        o_ref[...] = part * (a_ref[...] + b_ref[...]) / dot3(g_ref[first : first + rows, :], u, 1, 0)
 
-    k, n = usage.shape
-    return call(body, [(k, n)], gram, usage, top_a, top_b, flops=6 * k * k * n)[0]
+    k, n = factor.shape
+    return call(body, [(rows, n)], gram, factor, top_a, top_b, flops=6 * rows * k * n)[0]
 
 
 def program_top(usage, x, start, column, columns):
@@ -91,7 +92,6 @@
 
 
 def body(genes, cells, counts, usage_init, program_init):
-    x = counts.astype(BF16)
     cell, gene = lax.axis_index("cell"), lax.axis_index("gene")
     core = cell % 2
     half = (gene ^ (gene >> 1)) % 2
@@ -99,7 +99,7 @@
     k = program_init.shape[0]
     rows, columns = n_cells // 2, n_genes // 2
     grows = -(-k // 16) * 8
-    usage_t = usage_init.T
+    chunks = [(0, grows), (grows, k - grows)]
 
     def at(index):
         return jnp.full((1,), index, jnp.int32)
@@ -107,66 +107,60 @@
     own, other = at(half * rows), at((1 - half) * rows)
     own_col, other_col = at(core * columns), at((1 - core) * columns)
     grow, other_grow = at(core * (k - grows)), at((1 - core) * (k - grows))
+    zero = at(0)
 
     def join(mine, theirs, which, axis):
         first = jnp.where(which == 0, mine, theirs)
         second = jnp.where(which == 0, theirs, mine)
-        return first, second, jnp.concatenate([first, second], axis)
+        return jnp.concatenate([first, second], axis)
 
     def whole_gram(mine):
         theirs = exchange(mine, "cell", cells, 1)
-        first, second, _ = join(mine, theirs, core, 0)
+        first = jnp.where(core == 0, mine, theirs)
+        second = jnp.where(core == 0, theirs, mine)
         return jnp.concatenate([first, second[2 * grows - k :]], 0)
 
-    usage = lax.dynamic_slice_in_dim(usage_t, half * rows, rows, 1)
+    def far(a, axis, size, mirrored):
+        step = 2
+        add = jnp.zeros_like(a)
+        while step < size:
+            if step > 2:
+                a = a + add
+            add = exchange(a, axis, size, 2 * step - 1 if mirrored else step)
+            step *= 2
+        return a, add
+
+    x = counts.astype(BF16)
     program = program_init
+    parts = [program_init[f : f + n] for f, n in chunks]
+    usage_half = lax.dynamic_slice_in_dim(usage_init.T, half * rows, rows, 1)
     program_half = lax.dynamic_slice_in_dim(program_init, core * columns, columns, 1)
     for _ in range(ITERS):
         gram = gram_rows(program, grow, grows)
-        send = usage_top(program, x, other, rows)
         gram = gram + exchange(gram, "gene", genes, 1)
-        near = exchange(send, "gene", genes, 1)
-        keep = usage_top(program, x, own, rows)
-        top = keep + near
-        step = 2
-        while step < genes:
-            gram = gram + exchange(gram, "gene", genes, 2 * step - 1)
-            step *= 2
-        gram = whole_gram(gram)
-        step = 2
-        while step < genes:
-            add = exchange(top, "gene", genes, 2 * step - 1)
-            step *= 2
-            if step < genes:
-                top = top + add
-        usage = usage_update(gram, usage, top, add)
-        usage_other = exchange(usage, "gene", genes, 1)
-        usage_first, usage_second, usage_t = join(usage, usage_other, half, 1)
+        gram, add = far(gram, "gene", genes, True)
+        gram = whole_gram(gram + add)
+        tops = []
+        for part in parts:
+            near = exchange(usage_top(part, x, other, rows), "gene", genes, 1)
+            tops.append(far(usage_top(part, x, own, rows) + near, "gene", genes, True))
+        new = [update(gram, usage_half, f, n, *top) for (f, n), top in zip(chunks, tops)]
+        usage_half = jnp.concatenate(new, 0)
+        usages = [join(part, exchange(part, "gene", genes, 1), half, 1) for part in new]
+        usage = jnp.concatenate(usages, 0)
 
-        zero = at(0)
-        send = program_top(usage_t, x, zero, other_col, columns)
-        near = exchange(send, "cell", cells, 1)
-        gram_send = gram_rows(usage_t, other_grow, grows)
-        gram_near = exchange(gram_send, "cell", cells, 1)
-        gram_keep = gram_rows(usage_t, grow, grows)
-        keep = program_top(usage_t, x, zero, own_col, columns)
-        top = keep + near
-        gram = gram_keep + gram_near
-        step = 2
-        while step < cells:
-            gram = gram + exchange(gram, "cell", cells, step)
-            step *= 2
-        gram = whole_gram(gram)
-        step = 2
-        while step < cells:
-            add = exchange(top, "cell", cells, step)
-            step *= 2
-            if step < cells:
-                top = top + add
-        program_half = usage_update(gram, program_half, top, add)
-        program_other = exchange(program_half, "cell", cells, 1)
-        _, _, program = join(program_half, program_other, core, 1)
-    return usage_t.T, program
+        gram_near = exchange(gram_rows(usage, other_grow, grows), "cell", cells, 1)
+        gram, add = far(gram_rows(usage, grow, grows) + gram_near, "cell", cells, False)
+        gram = whole_gram(gram + add)
+        tops = []
+        for part in usages:
+            near = exchange(program_top(part, x, zero, other_col, columns), "cell", cells, 1)
+            tops.append(far(program_top(part, x, zero, own_col, columns) + near, "cell", cells, False))
+        new = [update(gram, program_half, f, n, *top) for (f, n), top in zip(chunks, tops)]
+        program_half = jnp.concatenate(new, 0)
+        parts = [join(part, exchange(part, "cell", cells, 1), core, 1) for part in new]
+        program = jnp.concatenate(parts, 0)
+    return usage.T, program
 
 
 def solution(mesh):

time: 186 us -> 157 us (0.84)
  waiting for transfers between devices: 104 us -> 60.7 us
  starting transfers between devices: 43 us -> 51 us
  Pallas kernels: 15.8 us -> 21.4 us
    ppermute x24 -> x36, waiting for transfers between devices: 104 us -> 60.7 us  [exchange(): return lax.ppermute(a, axis, [(i, i ^ flip) for i in range(size)])]
    ppermute x24 -> x36, starting transfers between devices: 43 us -> 51 us  [exchange(): return lax.ppermute(a, axis, [(i, i ^ flip) for i in range(size)])]
    pallas_call x18 -> x30, Pallas kernels: 15.8 us -> 21.4 us  [call(): pl.pallas_call(body, out_shape=shapes, in_specs=specs, out_specs=[VMEM] *...]
    slice x0 -> x2, local copies, waits for them, and re-layouts: none -> 1.89 us  [body(): parts = [program_init[f:f + n] for f, n in chunks]]
    unnamed x20 -> x22, local copies, waits for them, and re-layouts: 7.98 us -> 7.22 us
    add x10 -> x14, other arithmetic: 4.25 us -> 3.8 us  [the longest x4 2.65 us: body(): tops.append(far(usage_top(part, x, own, rows) + near, 'gene', genes, True))]
  transfers between devices with their start and end apart: 24 -> 36, of which waited for: 15 -> 17; matrix products, arithmetic and copies ran while one was open for 4% -> 8% of each run, Pallas kernels for 4% -> 12%
where the time goes in v2:
time: 157 us
  waiting for transfers between devices  60.7 us (39%)
  starting transfers between devices  51 us (32%)
  Pallas kernels  21.4 us (14%)
  other arithmetic  13.2 us (8%)
  local copies, waits for them, and re-layouts  9.18 us (6%)
    ppermute x36, waiting for transfers between devices, exchange(): return lax.ppermute(a, axis, [(i, i ^ flip) for i in range(size)])  60.7 us
    ppermute x36, starting transfers between devices, exchange(): return lax.ppermute(a, axis, [(i, i ^ flip) for i in range(size)])  51 us
    pallas_call x30, Pallas kernels, call(): pl.pallas_call(body, out_shape=shapes, in_specs=specs, out_specs=[VMEM] *...  21.4 us
    unnamed x22, local copies, waits for them, and re-layouts  7.22 us
  transfers between devices with their start and end apart: 36, of which 17 were waited for; matrix products, arithmetic and copies ran while one was open for 8% of the time, Pallas kernels for 12%

profile of v2, /device:TPU:0, one launch (start us, length us, event | category | flops | bytes accessed | tf_op | source)
XLA Modules:
  0.0 156.7 jit_solution(14020347475747010554)
XLA Ops:
  0.7 1.3 copy-done.1
  2.6 3.1 %collective-permute-start = (f32[104,200]{1,0:T(8,128)S(1)}, f32[104,200]{1,0:T(8,128)}, u32[]{:S(2)}, u32[]{:S(2)}) collective-permute-start(f32[104,200]{1,0:T(8,128)S(1)} %shard_map.50), channel_id=1, source_target_pairs={{0,1},{1,0},{2,3},{3,2},{4,5},{5,4},{6,7},{7,6},{8,9},{9,8},{10,11... | collective-permute-start | bytes 249608 | tf_op jit(solution)/shard_map/ppermute | solution.py:91
  5.7 0.8 slice.19.p_ref
  6.5 2.9 %convert_element_type.3.x_ref = bf16[1024,1280]{1,0:T(8,128)(2,1)S(1)} convert(s32[1024,1280]{1,0:T(8,128)} %param.3) | non-fusion elementwise | flops 1310720 | bytes 7864320 | tf_op jit(solution)/shard_map/convert_element_type | solution.py:133
  9.4 1.0 copy-done.3
  10.5 1.6 %shard_map.52 = f32[104,512]{1,0:T(8,128)} custom-call(s32[1]{0:T(128)} %bitcast.3.start_ref, f32[104,1280]{1,0:T(8,128)S(1)} %copy-done.3, bf16[1024,1280]{1,0:T(8,128)(2,1)S(1)} %convert_element_type.3.x_ref), custom_call_target="tpu_custom_call" | custom-call | flops 272629760 | bytes 3366916 | tf_op jit(solution)/shard_map/pallas_call | solution.py:37
  12.1 1.1 slice.20.p_ref
  13.2 1.6 add.63
  14.8 4.0 %collective-permute-start.1 = (f32[104,200]{1,0:T(8,128)}, f32[104,200]{1,0:T(8,128)S(1)}, u32[]{:S(2)}, u32[]{:S(2)}) collective-permute-start(f32[104,200]{1,0:T(8,128)} %add.63), channel_id=1, source_target_pairs={{0,3},{1,2},{2,1},{3,0},{4,7},{5,6},{6,5},{7,4},{8,11},{9,10},{10,... | collective-permute-start | bytes 249608 | tf_op jit(solution)/shard_map/ppermute | solution.py:91
  18.8 1.6 %shard_map.55 = f32[96,512]{1,0:T(8,128)} custom-call(s32[1]{0:T(128)} %bitcast.3.start_ref, f32[96,1280]{1,0:T(8,128)S(1)} %slice.20.p_ref, bf16[1024,1280]{1,0:T(8,128)(2,1)S(1)} %convert_element_type.3.x_ref), custom_call_target="tpu_custom_call" | custom-call | flops 251658240 | bytes 3309572 | tf_op jit(solution)/shard_map/pallas_call | solution.py:37
  20.4 0.8 copy-done.5
  21.2 1.0 copy-done.6
  22.2 0.9 shard_map.54
  23.2 1.0 copy-done.4
  24.2 0.9 shard_map.51
  25.2 0.9 add.64
  26.2 2.0 %collective-permute-done.6 = f32[96,512]{1,0:T(8,128)} collective-permute-done((f32[96,512]{1,0:T(8,128)}, f32[96,512]{1,0:T(8,128)}, u32[]{:S(2)}, u32[]{:S(2)}) %collective-permute-start.6) | collective-permute-done | bytes 196640 | tf_op jit(solution)/shard_map/ppermute | solution.py:91
  28.2 1.0 add.67.a_ref
  29.1 1.3 collective-permute-start.7
  30.4 1.6 %add.66.a_ref = f32[104,512]{1,0:T(8,128)} add(f32[104,512]{1,0:T(8,128)S(1)} %shard_map.51, f32[104,512]{1,0:T(8,128)} %collective-permute-done.3) | non-fusion elementwise | flops 53248 | bytes 638976 | tf_op jit(solution)/shard_map/add | solution.py:146
  32.0 2.6 %collective-permute-start.4 = (f32[104,512]{1,0:T(8,128)}, f32[104,512]{1,0:T(8,128)}, u32[]{:S(2)}, u32[]{:S(2)}) collective-permute-start(f32[104,512]{1,0:T(8,128)} %add.66.a_ref), channel_id=1, source_target_pairs={{0,3},{1,2},{2,1},{3,0},{4,7},{5,6},{6,5},{7,4},{8,11},{9,10},{10,... | collective-permute-start | bytes 638984 | tf_op jit(solution)/shard_map/ppermute | solution.py:91
  34.8 3.0 %collective-permute-done.7.b_ref = f32[96,512]{1,0:T(8,128)S(1)} collective-permute-done((f32[96,512]{1,0:T(8,128)S(1)}, f32[96,512]{1,0:T(8,128)S(1)}, u32[]{:S(2)}, u32[]{:S(2)}) %collective-permute-start.7) | collective-permute-done | bytes 196640 | tf_op jit(solution)/shard_map/ppermute | solution.py:91
  37.8 1.0 shard_map.56
  38.7 8.1 %collective-permute-start.8 = (f32[96,512]{1,0:T(8,128)}, f32[96,512]{1,0:T(8,128)}, u32[]{:S(2)}, u32[]{:S(2)}) collective-permute-start(f32[96,512]{1,0:T(8,128)} %shard_map.56), channel_id=1, source_target_pairs={{0,1},{1,0},{2,3},{3,2},{4,5},{5,4},{6,7},{7,6},{8,9},{9,8},{10,11... | collective-permute-start | bytes 589832 | tf_op jit(solution)/shard_map/ppermute | solution.py:91
  46.9 1.1 copy-done.8
  48.0 0.9 copy-done.10
  48.9 1.3 shard_map.53
  50.2 3.3 %collective-permute-start.5 = (f32[104,512]{1,0:T(8,128)S(1)}, f32[104,512]{1,0:T(8,128)S(1)}, u32[]{:S(2)}, u32[]{:S(2)}) collective-permute-start(f32[104,512]{1,0:T(8,128)S(1)} %shard_map.53), channel_id=1, source_target_pairs={{0,1},{1,0},{2,3},{3,2},{4,5},{5,4},{6,7},{7,6},{8,9},{9,8},{10,11... | collective-permute-start | bytes 638984 | tf_op jit(solution)/shard_map/ppermute | solution.py:91
  53.5 1.1 broadcast_select_fusion.15
  54.5 4.1 %collective-permute-done.5 = f32[104,512]{1,0:T(8,128)S(1)} collective-permute-done((f32[104,512]{1,0:T(8,128)S(1)}, f32[104,512]{1,0:T(8,128)S(1)}, u32[]{:S(2)}, u32[]{:S(2)}) %collective-permute-start.5) | collective-permute-done | bytes 213024 | tf_op jit(solution)/shard_map/ppermute | solution.py:91
  61.1 1.6 collective-permute-start.10
  63.3 2.8 %collective-permute-done.10 = f32[104,200]{1,0:T(8,128)S(1)} collective-permute-done((f32[104,200]{1,0:T(8,128)S(1)}, f32[104,200]{1,0:T(8,128)S(1)}, u32[]{:S(2)}, u32[]{:S(2)}) %collective-permute-start.10) | collective-permute-done | bytes 83232 | tf_op jit(solution)/shard_map/ppermute | solution.py:91
  68.0 1.6 collective-permute-start.16
  70.3 6.6 %collective-permute-done.16.b_ref = f32[96,640]{1,0:T(8,128)S(1)} collective-permute-done((f32[96,640]{1,0:T(8,128)S(1)}, f32[96,640]{1,0:T(8,128)S(1)}, u32[]{:S(2)}, u32[]{:S(2)}) %collective-permute-start.16) | collective-permute-done | bytes 245792 | tf_op jit(solution)/shard_map/ppermute | solution.py:91
  77.3 4.4 %collective-permute-done.13.b_ref = f32[104,640]{1,0:T(8,128)S(1)} collective-permute-done((f32[104,640]{1,0:T(8,128)S(1)}, f32[104,640]{1,0:T(8,128)S(1)}, u32[]{:S(2)}, u32[]{:S(2)}) %collective-permute-start.13) | collective-permute-done | bytes 266272 | tf_op jit(solution)/shard_map/ppermute | solution.py:91
  82.1 1.5 collective-permute-done.14
  84.4 1.8 %collective-permute-start.18 = (f32[104,200]{1,0:T(8,128)S(1)}, f32[104,200]{1,0:T(8,128)S(1)}, u32[]{:S(2)}, u32[]{:S(2)}) collective-permute-start(f32[104,200]{1,0:T(8,128)S(1)} %shard_map.65), channel_id=1, source_target_pairs={{0,1},{1,0},{2,3},{3,2},{4,5},{5,4},{6,7},{7,6},{8,9},{9,8},{10,11... | collective-permute-start | bytes 249608 | tf_op jit(solution)/shard_map/ppermute | solution.py:91
  86.2 3.2 %collective-permute-done.18 = f32[104,200]{1,0:T(8,128)S(1)} collective-permute-done((f32[104,200]{1,0:T(8,128)S(1)}, f32[104,200]{1,0:T(8,128)S(1)}, u32[]{:S(2)}, u32[]{:S(2)}) %collective-permute-start.18) | collective-permute-done | bytes 83232 | tf_op jit(solution)/shard_map/ppermute | solution.py:91
  89.5 1.2 collective-permute-start.19
  90.7 0.9 shard_map.67
  91.6 0.9 collective-permute-start.21
  92.6 0.9 shard_map.70
  93.5 1.2 collective-permute-start.24
  94.7 2.5 %collective-permute-done.19 = f32[104,200]{1,0:T(8,128)S(1)} collective-permute-done((f32[104,200]{1,0:T(8,128)S(1)}, f32[104,200]{1,0:T(8,128)S(1)}, u32[]{:S(2)}, u32[]{:S(2)}) %collective-permute-start.19) | collective-permute-done | bytes 83232 | tf_op jit(solution)/shard_map/ppermute | solution.py:91
  97.3 1.0 pad_maximum_fusion.5.u_ref
  98.3 0.9 shard_map.69
  99.2 0.9 shard_map.66
  100.2 4.2 %collective-permute-done.24 = f32[96,512]{1,0:T(8,128)S(1)} collective-permute-done((f32[96,512]{1,0:T(8,128)S(1)}, f32[96,512]{1,0:T(8,128)S(1)}, u32[]{:S(2)}, u32[]{:S(2)}) %collective-permute-start.24) | collective-permute-done | bytes 196640 | tf_op jit(solution)/shard_map/ppermute | solution.py:91
  104.4 1.6 %collective-permute-start.25 = (f32[96,512]{1,0:T(8,128)S(1)}, f32[96,512]{1,0:T(8,128)S(1)}, u32[]{:S(2)}, u32[]{:S(2)}) collective-permute-start(f32[96,512]{1,0:T(8,128)S(1)} %add.76.a_ref), channel_id=1, source_target_pairs={{0,3},{1,2},{2,1},{3,0},{4,7},{5,6},{6,5},{7,4},{8,11},{9,10},{10,... | collective-permute-start | bytes 589832 | tf_op jit(solution)/shard_map/ppermute | solution.py:91
  106.1 2.3 %collective-permute-start.22 = (f32[104,512]{1,0:T(8,128)S(1)}, f32[104,512]{1,0:T(8,128)S(1)}, u32[]{:S(2)}, u32[]{:S(2)}) collective-permute-start(f32[104,512]{1,0:T(8,128)S(1)} %add.75.a_ref), channel_id=1, source_target_pairs={{0,3},{1,2},{2,1},{3,0},{4,7},{5,6},{6,5},{7,4},{8,11},{9,10},{10,... | collective-permute-start | bytes 638984 | tf_op jit(solution)/shard_map/ppermute | solution.py:91
  108.5 5.7 %collective-permute-done.25.b_ref = f32[96,512]{1,0:T(8,128)S(1)} collective-permute-done((f32[96,512]{1,0:T(8,128)S(1)}, f32[96,512]{1,0:T(8,128)S(1)}, u32[]{:S(2)}, u32[]{:S(2)}) %collective-permute-start.25) | collective-permute-done | bytes 196640 | tf_op jit(solution)/shard_map/ppermute | solution.py:91
  114.4 6.8 %collective-permute-start.26 = (f32[96,512]{1,0:T(8,128)S(1)}, f32[96,512]{1,0:T(8,128)S(1)}, u32[]{:S(2)}, u32[]{:S(2)}) collective-permute-start(f32[96,512]{1,0:T(8,128)S(1)} %shard_map.71), channel_id=1, source_target_pairs={{0,1},{1,0},{2,3},{3,2},{4,5},{5,4},{6,7},{7,6},{8,9},{9,8},{10,11... | collective-permute-start | bytes 589832 | tf_op jit(solution)/shard_map/ppermute | solution.py:91
  121.5 2.4 %collective-permute-start.23 = (f32[104,512]{1,0:T(8,128)S(1)}, f32[104,512]{1,0:T(8,128)S(1)}, u32[]{:S(2)}, u32[]{:S(2)}) collective-permute-start(f32[104,512]{1,0:T(8,128)S(1)} %shard_map.68), channel_id=1, source_target_pairs={{0,1},{1,0},{2,3},{3,2},{4,5},{5,4},{6,7},{7,6},{8,9},{9,8},{10,11... | collective-permute-start | bytes 638984 | tf_op jit(solution)/shard_map/ppermute | solution.py:91
  123.9 2.8 %collective-permute-done.26 = f32[96,512]{1,0:T(8,128)S(1)} collective-permute-done((f32[96,512]{1,0:T(8,128)S(1)}, f32[96,512]{1,0:T(8,128)S(1)}, u32[]{:S(2)}, u32[]{:S(2)}) %collective-permute-start.26) | collective-permute-done | bytes 196640 | tf_op jit(solution)/shard_map/ppermute | solution.py:91
  126.7 2.7 %collective-permute-done.23 = f32[104,512]{1,0:T(8,128)S(1)} collective-permute-done((f32[104,512]{1,0:T(8,128)S(1)}, f32[104,512]{1,0:T(8,128)S(1)}, u32[]{:S(2)}, u32[]{:S(2)}) %collective-permute-start.23) | collective-permute-done | bytes 213024 | tf_op jit(solution)/shard_map/ppermute | solution.py:91
  129.4 1.1 maximum_maximum_fusion.3
  130.5 0.7 shard_map.73
  133.1 1.5 collective-permute-start.28
  135.3 2.8 %collective-permute-done.28 = f32[104,200]{1,0:T(8,128)S(1)} collective-permute-done((f32[104,200]{1,0:T(8,128)S(1)}, f32[104,200]{1,0:T(8,128)S(1)}, u32[]{:S(2)}, u32[]{:S(2)}) %collective-permute-start.28) | collective-permute-done | bytes 83232 | tf_op jit(solution)/shard_map/ppermute | solution.py:91
  140.0 1.5 collective-permute-start.34
  142.2 6.6 %collective-permute-done.34.b_ref = f32[96,640]{1,0:T(8,128)S(1)} collective-permute-done((f32[96,640]{1,0:T(8,128)S(1)}, f32[96,640]{1,0:T(8,128)S(1)}, u32[]{:S(2)}, u32[]{:S(2)}) %collective-permute-start.34) | collective-permute-done | bytes 245792 | tf_op jit(solution)/shard_map/ppermute | solution.py:91
  149.3 4.4 %collective-permute-done.31.b_ref = f32[104,640]{1,0:T(8,128)S(1)} collective-permute-done((f32[104,640]{1,0:T(8,128)S(1)}, f32[104,640]{1,0:T(8,128)S(1)}, u32[]{:S(2)}, u32[]{:S(2)}) %collective-permute-start.31) | collective-permute-done | bytes 266272 | tf_op jit(solution)/shard_map/ppermute | solution.py:91
  154.1 1.5 collective-permute-done.32
  155.7 1.0 maximum_maximum_fusion.1
  (113 shorter events, 15.0 us)
Async XLA Ops:
  0.6 25.5 %copy-start = (f32[1024,200]{0,1:T(8,128)S(1)}, f32[1024,200]{0,1:T(8,128)}, u32[]{:S(2)}) copy-start(f32[1024,200]{0,1:T(8,128)} %param.4) | copy-start | bytes 2457604
  0.7 1.3 copy-start.1
  2.6 10.6 %collective-permute-start = (f32[104,200]{1,0:T(8,128)S(1)}, f32[104,200]{1,0:T(8,128)}, u32[]{:S(2)}, u32[]{:S(2)}) collective-permute-start(f32[104,200]{1,0:T(8,128)S(1)} %shard_map.50), channel_id=1, source_target_pairs={{0,1},{1,0},{2,3},{3,2},{4,5},{5,4},{6,7},{7,6},{8,9},{9,8},{10,11... | collective-permute-start | bytes 249608 | tf_op jit(solution)/shard_map/ppermute | solution.py:91
  9.4 1.0 copy-start.3
  12.1 18.3 %collective-permute-start.3 = (f32[104,512]{1,0:T(8,128)}, f32[104,512]{1,0:T(8,128)}, u32[]{:S(2)}, u32[]{:S(2)}) collective-permute-start(f32[104,512]{1,0:T(8,128)} %shard_map.52), channel_id=1, source_target_pairs={{0,1},{1,0},{2,3},{3,2},{4,5},{5,4},{6,7},{7,6},{8,9},{9,8},{10,11... | collective-permute-start | bytes 638984 | tf_op jit(solution)/shard_map/ppermute | solution.py:91
  14.8 10.4 %collective-permute-start.1 = (f32[104,200]{1,0:T(8,128)}, f32[104,200]{1,0:T(8,128)S(1)}, u32[]{:S(2)}, u32[]{:S(2)}) collective-permute-start(f32[104,200]{1,0:T(8,128)} %add.63), channel_id=1, source_target_pairs={{0,3},{1,2},{2,1},{3,0},{4,7},{5,6},{6,5},{7,4},{8,11},{9,10},{10,... | collective-permute-start | bytes 249608 | tf_op jit(solution)/shard_map/ppermute | solution.py:91
  20.4 0.8 copy-start.5
  21.2 7.0 %collective-permute-start.6 = (f32[96,512]{1,0:T(8,128)}, f32[96,512]{1,0:T(8,128)}, u32[]{:S(2)}, u32[]{:S(2)}) collective-permute-start(f32[96,512]{1,0:T(8,128)} %shard_map.55), channel_id=1, source_target_pairs={{0,1},{1,0},{2,3},{3,2},{4,5},{5,4},{6,7},{7,6},{8,9},{9,8},{10,11... | collective-permute-start | bytes 589832 | tf_op jit(solution)/shard_map/ppermute | solution.py:91
  21.2 1.0 copy-start.6
  23.2 1.1 copy-start.4
  26.1 8.6 %collective-permute-start.2 = (f32[104,200]{1,0:T(8,128)S(1)}, f32[104,200]{1,0:T(8,128)S(1)}, u32[]{:S(2)}, u32[]{:S(2)}) collective-permute-start(f32[104,200]{1,0:T(8,128)S(1)} %add.64), channel_id=1, source_target_pairs={{0,4},{4,0},{8,12},{12,8},{1,5},{5,1},{9,13},{13,9},{2,6},{6,2},{1... | collective-permute-start | bytes 249608 | tf_op jit(solution)/shard_map/ppermute | solution.py:91
  26.2 11.6 %copy-start.7 = (f32[200,512]{1,0:T(8,128)}, f32[200,512]{1,0:T(8,128)S(1)}, u32[]{:S(2)}) copy-start(f32[200,512]{1,0:T(8,128)S(1)} %dynamic-slice_bitcast_fusion.u_ref) | copy-start | bytes 1228804
  29.1 8.6 %collective-permute-start.7 = (f32[96,512]{1,0:T(8,128)S(1)}, f32[96,512]{1,0:T(8,128)S(1)}, u32[]{:S(2)}, u32[]{:S(2)}) collective-permute-start(f32[96,512]{1,0:T(8,128)S(1)} %add.67.a_ref), channel_id=1, source_target_pairs={{0,3},{1,2},{2,1},{3,0},{4,7},{5,6},{6,5},{7,4},{8,11},{9,10},{10,... | collective-permute-start | bytes 589832 | tf_op jit(solution)/shard_map/ppermute | solution.py:91
  32.0 14.8 %collective-permute-start.4 = (f32[104,512]{1,0:T(8,128)}, f32[104,512]{1,0:T(8,128)}, u32[]{:S(2)}, u32[]{:S(2)}) collective-permute-start(f32[104,512]{1,0:T(8,128)} %add.66.a_ref), channel_id=1, source_target_pairs={{0,3},{1,2},{2,1},{3,0},{4,7},{5,6},{6,5},{7,4},{8,11},{9,10},{10,... | collective-permute-start | bytes 638984 | tf_op jit(solution)/shard_map/ppermute | solution.py:91
  34.7 4.0 %copy-start.9 = (f32[200,200]{1,0:T(8,128)}, f32[200,200]{1,0:T(8,128)S(1)}, u32[]{:S(2)}) copy-start(f32[200,200]{1,0:T(8,128)S(1)} %pad_maximum_fusion.8.g_ref) | copy-start | bytes 480004
  38.7 14.7 %collective-permute-start.8 = (f32[96,512]{1,0:T(8,128)}, f32[96,512]{1,0:T(8,128)}, u32[]{:S(2)}, u32[]{:S(2)}) collective-permute-start(f32[96,512]{1,0:T(8,128)} %shard_map.56), channel_id=1, source_target_pairs={{0,1},{1,0},{2,3},{3,2},{4,5},{5,4},{6,7},{7,6},{8,9},{9,8},{10,11... | collective-permute-start | bytes 589832 | tf_op jit(solution)/shard_map/ppermute | solution.py:91
  46.9 15.8 %copy-start.2 = (f32[200,1280]{1,0:T(8,128)S(1)}, f32[200,1280]{1,0:T(8,128)}, u32[]{:S(2)}) copy-start(f32[200,1280]{1,0:T(8,128)} %a_ref.1) | copy-start | bytes 3072004
  46.9 1.1 copy-start.8
  48.0 0.9 copy-start.10
  50.2 8.4 %collective-permute-start.5 = (f32[104,512]{1,0:T(8,128)S(1)}, f32[104,512]{1,0:T(8,128)S(1)}, u32[]{:S(2)}, u32[]{:S(2)}) collective-permute-start(f32[104,512]{1,0:T(8,128)S(1)} %shard_map.53), channel_id=1, source_target_pairs={{0,1},{1,0},{2,3},{3,2},{4,5},{5,4},{6,7},{7,6},{8,9},{9,8},{10,11... | collective-permute-start | bytes 638984 | tf_op jit(solution)/shard_map/ppermute | solution.py:91
  59.3 1.8 %collective-permute-start.9 = (f32[104,200]{1,0:T(8,128)S(1)}, f32[104,200]{1,0:T(8,128)S(1)}, u32[]{:S(2)}, u32[]{:S(2)}) collective-permute-start(f32[104,200]{1,0:T(8,128)S(1)} %shard_map.58), channel_id=1, source_target_pairs={{0,4},{4,0},{8,12},{12,8},{1,5},{5,1},{9,13},{13,9},{2,6},{6,2},{1... | collective-permute-start | bytes 249608 | tf_op jit(solution)/shard_map/ppermute | solution.py:91
  60.0 8.0 %collective-permute-start.15 = (f32[96,640]{1,0:T(8,128)S(1)}, f32[96,640]{1,0:T(8,128)S(1)}, u32[]{:S(2)}, u32[]{:S(2)}) collective-permute-start(f32[96,640]{1,0:T(8,128)S(1)} %shard_map.63), channel_id=1, source_target_pairs={{0,4},{4,0},{8,12},{12,8},{1,5},{5,1},{9,13},{13,9},{2,6},{6,2},{1... | collective-permute-start | bytes 737288 | tf_op jit(solution)/shard_map/ppermute | solution.py:91
  61.1 5.0 %collective-permute-start.10 = (f32[104,200]{1,0:T(8,128)S(1)}, f32[104,200]{1,0:T(8,128)S(1)}, u32[]{:S(2)}, u32[]{:S(2)}) collective-permute-start(f32[104,200]{1,0:T(8,128)S(1)} %add.68), channel_id=1, source_target_pairs={{0,8},{4,12},{8,0},{12,4},{1,9},{5,13},{9,1},{13,5},{2,10},{6,14},... | collective-permute-start | bytes 249608 | tf_op jit(solution)/shard_map/ppermute | solution.py:91
  66.1 3.4 %collective-permute-start.11 = (f32[104,200]{1,0:T(8,128)S(1)}, f32[104,200]{1,0:T(8,128)S(1)}, u32[]{:S(2)}, u32[]{:S(2)}) collective-permute-start(f32[104,200]{1,0:T(8,128)S(1)} %add.69), channel_id=1, source_target_pairs={{0,4},{4,0},{8,12},{12,8},{1,5},{5,1},{9,13},{13,9},{2,6},{6,2},{1... | collective-permute-start | bytes 249608 | tf_op jit(solution)/shard_map/ppermute | solution.py:91
  66.8 2.8 %collective-permute-start.12 = (f32[104,640]{1,0:T(8,128)S(1)}, f32[104,640]{1,0:T(8,128)S(1)}, u32[]{:S(2)}, u32[]{:S(2)}) collective-permute-start(f32[104,640]{1,0:T(8,128)S(1)} %shard_map.60), channel_id=1, source_target_pairs={{0,4},{4,0},{8,12},{12,8},{1,5},{5,1},{9,13},{13,9},{2,6},{6,2},{1... | collective-permute-start | bytes 798728 | tf_op jit(solution)/shard_map/ppermute | solution.py:91
  68.0 8.9 %collective-permute-start.16 = (f32[96,640]{1,0:T(8,128)S(1)}, f32[96,640]{1,0:T(8,128)S(1)}, u32[]{:S(2)}, u32[]{:S(2)}) collective-permute-start(f32[96,640]{1,0:T(8,128)S(1)} %add.72.a_ref), channel_id=1, source_target_pairs={{0,8},{4,12},{8,0},{12,4},{1,9},{5,13},{9,1},{13,5},{2,10},{6,14},... | collective-permute-start | bytes 737288 | tf_op jit(solution)/shard_map/ppermute | solution.py:91
  69.6 12.0 %collective-permute-start.13 = (f32[104,640]{1,0:T(8,128)S(1)}, f32[104,640]{1,0:T(8,128)S(1)}, u32[]{:S(2)}, u32[]{:S(2)}) collective-permute-start(f32[104,640]{1,0:T(8,128)S(1)} %add.71.a_ref), channel_id=1, source_target_pairs={{0,8},{4,12},{8,0},{12,4},{1,9},{5,13},{9,1},{13,5},{2,10},{6,14},... | collective-permute-start | bytes 798728 | tf_op jit(solution)/shard_map/ppermute | solution.py:91
  77.2 4.9 %collective-permute-start.17 = (f32[96,640]{1,0:T(8,128)S(1)}, f32[96,640]{1,0:T(8,128)S(1)}, u32[]{:S(2)}, u32[]{:S(2)}) collective-permute-start(f32[96,640]{1,0:T(8,128)S(1)} %shard_map.64), channel_id=1, source_target_pairs={{0,4},{4,0},{8,12},{12,8},{1,5},{5,1},{9,13},{13,9},{2,6},{6,2},{1... | collective-permute-start | bytes 737288 | tf_op jit(solution)/shard_map/ppermute | solution.py:91
  82.0 1.6 %collective-permute-start.14 = (f32[104,640]{1,0:T(8,128)S(1)}, f32[104,640]{1,0:T(8,128)S(1)}, u32[]{:S(2)}, u32[]{:S(2)}) collective-permute-start(f32[104,640]{1,0:T(8,128)S(1)} %shard_map.61), channel_id=1, source_target_pairs={{0,4},{4,0},{8,12},{12,8},{1,5},{5,1},{9,13},{13,9},{2,6},{6,2},{1... | collective-permute-start | bytes 798728 | tf_op jit(solution)/shard_map/ppermute | solution.py:91
  84.4 5.1 %collective-permute-start.18 = (f32[104,200]{1,0:T(8,128)S(1)}, f32[104,200]{1,0:T(8,128)S(1)}, u32[]{:S(2)}, u32[]{:S(2)}) collective-permute-start(f32[104,200]{1,0:T(8,128)S(1)} %shard_map.65), channel_id=1, source_target_pairs={{0,1},{1,0},{2,3},{3,2},{4,5},{5,4},{6,7},{7,6},{8,9},{9,8},{10,11... | collective-permute-start | bytes 249608 | tf_op jit(solution)/shard_map/ppermute | solution.py:91
  89.5 7.7 %collective-permute-start.19 = (f32[104,200]{1,0:T(8,128)S(1)}, f32[104,200]{1,0:T(8,128)S(1)}, u32[]{:S(2)}, u32[]{:S(2)}) collective-permute-start(f32[104,200]{1,0:T(8,128)S(1)} %add.73), channel_id=1, source_target_pairs={{0,3},{1,2},{2,1},{3,0},{4,7},{5,6},{6,5},{7,4},{8,11},{9,10},{10,... | collective-permute-start | bytes 249608 | tf_op jit(solution)/shard_map/ppermute | solution.py:91
  91.6 14.4 %collective-permute-start.21 = (f32[104,512]{1,0:T(8,128)S(1)}, f32[104,512]{1,0:T(8,128)S(1)}, u32[]{:S(2)}, u32[]{:S(2)}) collective-permute-start(f32[104,512]{1,0:T(8,128)S(1)} %shard_map.67), channel_id=1, source_target_pairs={{0,1},{1,0},{2,3},{3,2},{4,5},{5,4},{6,7},{7,6},{8,9},{9,8},{10,11... | collective-permute-start | bytes 638984 | tf_op jit(solution)/shard_map/ppermute | solution.py:91
  93.5 10.9 %collective-permute-start.24 = (f32[96,512]{1,0:T(8,128)S(1)}, f32[96,512]{1,0:T(8,128)S(1)}, u32[]{:S(2)}, u32[]{:S(2)}) collective-permute-start(f32[96,512]{1,0:T(8,128)S(1)} %shard_map.70), channel_id=1, source_target_pairs={{0,1},{1,0},{2,3},{3,2},{4,5},{5,4},{6,7},{7,6},{8,9},{9,8},{10,11... | collective-permute-start | bytes 589832 | tf_op jit(solution)/shard_map/ppermute | solution.py:91
  97.2 11.2 %collective-permute-start.20 = (f32[104,200]{1,0:T(8,128)S(1)}, f32[104,200]{1,0:T(8,128)S(1)}, u32[]{:S(2)}, u32[]{:S(2)}) collective-permute-start(f32[104,200]{1,0:T(8,128)S(1)} %add.74), channel_id=1, source_target_pairs={{0,4},{4,0},{8,12},{12,8},{1,5},{5,1},{9,13},{13,9},{2,6},{6,2},{1... | collective-permute-start | bytes 249608 | tf_op jit(solution)/shard_map/ppermute | solution.py:91
  104.4 9.8 %collective-permute-start.25 = (f32[96,512]{1,0:T(8,128)S(1)}, f32[96,512]{1,0:T(8,128)S(1)}, u32[]{:S(2)}, u32[]{:S(2)}) collective-permute-start(f32[96,512]{1,0:T(8,128)S(1)} %add.76.a_ref), channel_id=1, source_target_pairs={{0,3},{1,2},{2,1},{3,0},{4,7},{5,6},{6,5},{7,4},{8,11},{9,10},{10,... | collective-permute-start | bytes 589832 | tf_op jit(solution)/shard_map/ppermute | solution.py:91
  106.1 15.1 %collective-permute-start.22 = (f32[104,512]{1,0:T(8,128)S(1)}, f32[104,512]{1,0:T(8,128)S(1)}, u32[]{:S(2)}, u32[]{:S(2)}) collective-permute-start(f32[104,512]{1,0:T(8,128)S(1)} %add.75.a_ref), channel_id=1, source_target_pairs={{0,3},{1,2},{2,1},{3,0},{4,7},{5,6},{6,5},{7,4},{8,11},{9,10},{10,... | collective-permute-start | bytes 638984 | tf_op jit(solution)/shard_map/ppermute | solution.py:91
  114.4 12.2 %collective-permute-start.26 = (f32[96,512]{1,0:T(8,128)S(1)}, f32[96,512]{1,0:T(8,128)S(1)}, u32[]{:S(2)}, u32[]{:S(2)}) collective-permute-start(f32[96,512]{1,0:T(8,128)S(1)} %shard_map.71), channel_id=1, source_target_pairs={{0,1},{1,0},{2,3},{3,2},{4,5},{5,4},{6,7},{7,6},{8,9},{9,8},{10,11... | collective-permute-start | bytes 589832 | tf_op jit(solution)/shard_map/ppermute | solution.py:91
  121.5 7.9 %collective-permute-start.23 = (f32[104,512]{1,0:T(8,128)S(1)}, f32[104,512]{1,0:T(8,128)S(1)}, u32[]{:S(2)}, u32[]{:S(2)}) collective-permute-start(f32[104,512]{1,0:T(8,128)S(1)} %shard_map.68), channel_id=1, source_target_pairs={{0,1},{1,0},{2,3},{3,2},{4,5},{5,4},{6,7},{7,6},{8,9},{9,8},{10,11... | collective-permute-start | bytes 638984 | tf_op jit(solution)/shard_map/ppermute | solution.py:91
  131.3 1.8 %collective-permute-start.27 = (f32[104,200]{1,0:T(8,128)S(1)}, f32[104,200]{1,0:T(8,128)S(1)}, u32[]{:S(2)}, u32[]{:S(2)}) collective-permute-start(f32[104,200]{1,0:T(8,128)S(1)} %shard_map.73), channel_id=1, source_target_pairs={{0,4},{4,0},{8,12},{12,8},{1,5},{5,1},{9,13},{13,9},{2,6},{6,2},{1... | collective-permute-start | bytes 249608 | tf_op jit(solution)/shard_map/ppermute | solution.py:91
  132.0 7.9 %collective-permute-start.33 = (f32[96,640]{1,0:T(8,128)S(1)}, f32[96,640]{1,0:T(8,128)S(1)}, u32[]{:S(2)}, u32[]{:S(2)}) collective-permute-start(f32[96,640]{1,0:T(8,128)S(1)} %shard_map.78), channel_id=1, source_target_pairs={{0,4},{4,0},{8,12},{12,8},{1,5},{5,1},{9,13},{13,9},{2,6},{6,2},{1... | collective-permute-start | bytes 737288 | tf_op jit(solution)/shard_map/ppermute | solution.py:91
  133.1 5.0 %collective-permute-start.28 = (f32[104,200]{1,0:T(8,128)S(1)}, f32[104,200]{1,0:T(8,128)S(1)}, u32[]{:S(2)}, u32[]{:S(2)}) collective-permute-start(f32[104,200]{1,0:T(8,128)S(1)} %add.77), channel_id=1, source_target_pairs={{0,8},{4,12},{8,0},{12,4},{1,9},{5,13},{9,1},{13,5},{2,10},{6,14},... | collective-permute-start | bytes 249608 | tf_op jit(solution)/shard_map/ppermute | solution.py:91
  138.1 3.4 %collective-permute-start.29 = (f32[104,200]{1,0:T(8,128)S(1)}, f32[104,200]{1,0:T(8,128)S(1)}, u32[]{:S(2)}, u32[]{:S(2)}) collective-permute-start(f32[104,200]{1,0:T(8,128)S(1)} %add.78), channel_id=1, source_target_pairs={{0,4},{4,0},{8,12},{12,8},{1,5},{5,1},{9,13},{13,9},{2,6},{6,2},{1... | collective-permute-start | bytes 249608 | tf_op jit(solution)/shard_map/ppermute | solution.py:91
  138.8 2.7 %collective-permute-start.30 = (f32[104,640]{1,0:T(8,128)S(1)}, f32[104,640]{1,0:T(8,128)S(1)}, u32[]{:S(2)}, u32[]{:S(2)}) collective-permute-start(f32[104,640]{1,0:T(8,128)S(1)} %shard_map.75), channel_id=1, source_target_pairs={{0,4},{4,0},{8,12},{12,8},{1,5},{5,1},{9,13},{13,9},{2,6},{6,2},{1... | collective-permute-start | bytes 798728 | tf_op jit(solution)/shard_map/ppermute | solution.py:91
  140.0 8.9 %collective-permute-start.34 = (f32[96,640]{1,0:T(8,128)S(1)}, f32[96,640]{1,0:T(8,128)S(1)}, u32[]{:S(2)}, u32[]{:S(2)}) collective-permute-start(f32[96,640]{1,0:T(8,128)S(1)} %add.80.a_ref), channel_id=1, source_target_pairs={{0,8},{4,12},{8,0},{12,4},{1,9},{5,13},{9,1},{13,5},{2,10},{6,14},... | collective-permute-start | bytes 737288 | tf_op jit(solution)/shard_map/ppermute | solution.py:91
  141.6 12.1 %collective-permute-start.31 = (f32[104,640]{1,0:T(8,128)S(1)}, f32[104,640]{1,0:T(8,128)S(1)}, u32[]{:S(2)}, u32[]{:S(2)}) collective-permute-start(f32[104,640]{1,0:T(8,128)S(1)} %add.79.a_ref), channel_id=1, source_target_pairs={{0,8},{4,12},{8,0},{12,4},{1,9},{5,13},{9,1},{13,5},{2,10},{6,14},... | collective-permute-start | bytes 798728 | tf_op jit(solution)/shard_map/ppermute | solution.py:91
  149.2 4.9 %collective-permute-start.35 = (f32[96,640]{1,0:T(8,128)S(1)}, f32[96,640]{1,0:T(8,128)S(1)}, u32[]{:S(2)}, u32[]{:S(2)}) collective-permute-start(f32[96,640]{1,0:T(8,128)S(1)} %shard_map.79), channel_id=1, source_target_pairs={{0,4},{4,0},{8,12},{12,8},{1,5},{5,1},{9,13},{13,9},{2,6},{6,2},{1... | collective-permute-start | bytes 737288 | tf_op jit(solution)/shard_map/ppermute | solution.py:91
  154.0 1.6 %collective-permute-start.32 = (f32[104,640]{1,0:T(8,128)S(1)}, f32[104,640]{1,0:T(8,128)S(1)}, u32[]{:S(2)}, u32[]{:S(2)}) collective-permute-start(f32[104,640]{1,0:T(8,128)S(1)} %shard_map.76), channel_id=1, source_target_pairs={{0,4},{4,0},{8,12},{12,8},{1,5},{5,1},{9,13},{13,9},{2,6},{6,2},{1... | collective-permute-start | bytes 798728 | tf_op jit(solution)/shard_map/ppermute | solution.py:91

commit v3 on v0

v3 whole, which is shorter than its diff:
```python
import functools

import jax
import jax.numpy as jnp
from jax import lax
from jax.experimental import pallas as pl
from jax.experimental.pallas import tpu as pltpu
from jax.sharding import PartitionSpec as P

ITERS = 2
FIRST_ROWS = 104
GRAM_AT = 1
WEIGHT = 12
VMEM = pl.BlockSpec(memory_space=pltpu.VMEM)
SMEM = pl.BlockSpec(memory_space=pltpu.SMEM)
ANY = pl.BlockSpec(memory_space=pl.ANY)
HBM = pl.BlockSpec(memory_space=pltpu.HBM)
PARAMS = pltpu.CompilerParams(vmem_limit_bytes=16 * 1024 * 1024)
F32 = jnp.float32
BF16 = jnp.bfloat16


def split(a):
    high = a.astype(BF16)
    return high, (a - high.astype(F32)).astype(BF16)


def dot(a, b, a_dim, b_dim):
    return lax.dot_general(a, b, (((a_dim,), (b_dim,)), ((), ())), preferred_element_type=F32)


def dot2(a, b, a_dim, b_dim):
    high, low = split(a)
    return dot(high, b, a_dim, b_dim) + dot(low, b, a_dim, b_dim)


def dot3(a, b, a_dim, b_dim):
    ah, al = split(a)
    bh, bl = split(b)
    return dot(ah, bh, a_dim, b_dim) + (dot(al, bh, a_dim, b_dim) + dot(ah, bl, a_dim, b_dim))


class Chain:
    def __init__(self):
        self.last = None

    def __call__(self, body, outs, *args, flops=0, any_args=(), scratch=()):
        specs = [
            SMEM if a.dtype == jnp.int32 and a.ndim == 1 else HBM if i in any_args else VMEM
            for i, a in enumerate(args)
        ]
        shapes = [s if isinstance(s, jax.ShapeDtypeStruct) else jax.ShapeDtypeStruct(s, F32) for s in outs]
        moved = sum(a.size * a.dtype.itemsize for a in args) + sum(s.size * 4 for s in shapes)
        tail = [] if self.last is None else [self.last]
        n_args = len(args)

        def run(*refs):
            body(*refs[:n_args], *refs[n_args + len(tail) :])

        result = pl.pallas_call(
            run,
            out_shape=[pltpu.VMEM(s.shape, s.dtype) for s in shapes],
            in_specs=specs + [ANY] * len(tail),
            out_specs=[VMEM] * len(outs),
            scratch_shapes=scratch,
            compiler_params=PARAMS,
            cost_estimate=pl.CostEstimate(flops=flops, bytes_accessed=moved, transcendentals=0),
        )(*args, *tail)
        self.last = result[0]
        return result


def exchange(a, axis, size, flip):
    return lax.ppermute(a, axis, [(i, i ^ flip) for i in range(size)])


def body(genes, cells, counts, usage_init, program_init):
    cell, gene = lax.axis_index("cell"), lax.axis_index("gene")
    core = cell % 2
    half = (gene ^ (gene >> 1)) % 2
    n_cells, n_genes = counts.shape
    k = program_init.shape[0]
    rows, columns = n_cells // 2, n_genes // 2
    grows = -(-k // 16) * 8
    first_size = FIRST_ROWS if k > FIRST_ROWS else grows
    sizes = [first_size, k - first_size]
    where = jnp.stack([core, half]).astype(jnp.int32)
    chain = Chain()

    def stacked(refs):
        return jnp.concatenate([r[...] for r in refs], 0)

    def whole_gram(parts):
        return sum(dot3(a, a, 1, 1) for a in parts)

    def share(g, first):
        return jnp.where(first, g[:grows], g[k - grows :])

    def gram(factor_a, factor_b, both):
        def kernel(where_ref, a0, a1, b0, b1, *outs):
            g = whole_gram([stacked((a0, a1)), stacked((b0, b1))])
            first = where_ref[0] == 0
            if both:
                outs[0][...] = share(g, jnp.logical_not(first))
            outs[-1][...] = share(g, first)

        n = factor_a[0].shape[1] + factor_b[0].shape[1]
        return chain(kernel, [(grows, k)] * (1 + both), where, *factor_a, *factor_b, flops=6 * k * k * n)

    def product(a, b, xa, xb, dim):
        parts = len(a)

        def kernel(*refs):
            a_refs, b_refs, (xa_ref, xb_ref, o_ref) = refs[:parts], refs[parts : 2 * parts], refs[2 * parts :]
            o_ref[...] = dot2(stacked(a_refs), xa_ref[...], 1, dim) + dot2(stacked(b_refs), xb_ref[...], 1, dim)

        n, m = sum(r.shape[0] for r in a), xa.shape[1 - dim]
        return chain(kernel, [(n, m)], *a, *b, xa, xb, flops=8 * n * a[0].shape[1] * m)[0]

    def add(a, b):
        def kernel(a_ref, b_ref, o_ref):
            o_ref[...] = a_ref[...] + b_ref[...]

        return chain(kernel, [a.shape], a, b)[0]

    def update(index, mine, theirs, factor, tops, weight=1):
        first = index * sizes[0]

        def rows_of(a):
            return a if a.shape[0] == sizes[index] else a[first : first + sizes[index]]

        def kernel(where_ref, m_ref, t_ref, f0, f1, *refs):
            *top_refs, o_ref = refs
            own = where_ref[0] == 0
            upper = jnp.where(own, m_ref[...], t_ref[...])
            lower = jnp.where(own, t_ref[...], m_ref[...])
            g = rows_of(jnp.concatenate([upper, lower[2 * grows - k :]], 0))
            f = stacked((f0, f1))
            part = (f0, f1)[index][...]
            top = sum(rows_of(ref[...]) for ref in top_refs)
            o_ref[...] = part * top / dot3(g, f, 1, 0)

        n, m = factor[index].shape
        return chain(kernel, [(n, m)], where, mine, theirs, *factor, *tops, flops=6 * n * k * m * weight)[0]

    def far(a, axis, size, mirrored):
        step = 2
        other = jnp.zeros_like(a)
        while step < size:
            if step > 2:
                a = a + other
            other = exchange(a, axis, size, 2 * step - 1 if mirrored else step)
            step *= 2
        return a, other

    if columns % 128 == 0 and rows % 32 == 0:
        pieces = 4
        piece = rows // pieces

        def halves(a, which, size):
            first, second = a[:, :size], a[:, size:]
            return jnp.where(which, second, first), jnp.where(which, first, second)

        def load(start, counts_ref, buffer, sems):
            copies = [
                pltpu.make_async_copy(
                    counts_ref.at[pl.ds(pl.multiple_of(start + i * piece, 8), piece)], buffer.at[i], sems.at[i]
                )
                for i in range(pieces)
            ]
            for copy in copies:
                copy.start()
            return copies

        def convert(copies, swap, x_refs, buffer):
            for i, copy in enumerate(copies):
                copy.wait()
                at = slice(i * piece, (i + 1) * piece)
                own, other = halves(buffer[i].astype(F32), swap, columns)
                x_refs[0][at, :], x_refs[1][at, :] = own.astype(BF16), other.astype(BF16)

        def prepare(where_ref, p_ref, counts_ref, g_ref, s0, s1, a0, a1, b0, b1, x0, x1, p, buffer, p_sem, sems):
            copy = pltpu.make_async_copy(p_ref, p, p_sem)
            copy.start()
            copies = load((1 - where_ref[1]) * rows, counts_ref, buffer, sems)
            copy.wait()
            own, other = halves(p[...], where_ref[0] == 1, columns)
            for part, refs in ((own, (a0, a1)), (other, (b0, b1))):
                refs[0][...], refs[1][...] = part[: sizes[0]], part[sizes[0] :]
            g_ref[...] = share(whole_gram([own, other]), where_ref[0] == 0)
            convert(copies, where_ref[0] == 1, (x0, x1), buffer)
            s = dot2(own, x0[...], 1, 1) + dot2(other, x1[...], 1, 1)
            s0[...], s1[...] = s[: sizes[0]], s[sizes[0] :]

        def load_own(where_ref, counts_ref, a0, a1, b0, b1, u_ref, k0, k1, x0, x1, u0, u1, buffer, sems):
            copies = load(where_ref[1] * rows, counts_ref, buffer, sems)
            mine, _ = halves(u_ref[...], where_ref[1] == 1, rows)
            u0[...], u1[...] = mine[: sizes[0]], mine[sizes[0] :]
            convert(copies, where_ref[0] == 1, (x0, x1), buffer)
            keep = dot2(stacked((a0, a1)), x0[...], 1, 1) + dot2(stacked((b0, b1)), x1[...], 1, 1)
            k0[...], k1[...] = keep[: sizes[0]], keep[sizes[0] :]

        half_x = [jax.ShapeDtypeStruct((rows, columns), BF16)] * 2
        buffer = pltpu.VMEM((pieces, piece, n_genes), jnp.int32)
        sems = pltpu.SemaphoreType.DMA((pieces,))
        flops = 4 * k * rows * n_genes
        gram_p, s0, s1, *rest = chain(
            prepare,
            [(grows, k)] + [(n, rows) for n in sizes] + [(n, columns) for n in sizes] * 2 + half_x,
            where,
            program_init,
            pltpu.with_memory_space_constraint(counts, pltpu.HBM),
            flops=flops,
            any_args=(1, 2),
            scratch=[pltpu.VMEM(program_init.shape, F32), buffer, pltpu.SemaphoreType.DMA, sems],
        )
        program_own, program_other, x_other = list(rest[:2]), list(rest[2:4]), list(rest[4:])
        gram_near = exchange(gram_p, "gene", genes, 1)
        nears = [exchange(a, "gene", genes, 1) for a in (s0, s1)]
        keep0, keep1, x0, x1, u0, u1 = chain(
            load_own,
            [(n, rows) for n in sizes] + half_x + [(n, rows) for n in sizes],
            where,
            pltpu.with_memory_space_constraint(counts, pltpu.HBM),
            *program_own,
            *program_other,
            usage_init.T,
            flops=flops,
            any_args=(1,),
            scratch=[buffer, sems],
        )
        x = [[x0, x1], x_other]
        usage_own = [u0, u1]
        keeps = [keep0, keep1]
    else:

        def at(a, which, axis):
            size = a.shape[axis] // 2
            return [lax.dynamic_slice_in_dim(a, i * size, size, axis) for i in (which, 1 - which)]

        def chunked(a):
            return [a[:first_size], a[first_size:]]

        x = [at(part, core, 1) for part in at(counts.astype(BF16), half, 0)]
        program_own, program_other = [chunked(a) for a in at(program_init, core, 1)]
        usage_own = chunked(at(usage_init.T, half, 1)[0])
        gram_p = gram(program_own, program_other, False)[0]
        gram_near = exchange(gram_p, "gene", genes, 1)
        nears, keeps = [], []
        for i in range(2):
            a, b = program_own[i : i + 1], program_other[i : i + 1]
            nears.append(exchange(product(a, b, *x[1], 1), "gene", genes, 1))
            keeps.append(product(a, b, *x[0], 1))

    for iteration in range(ITERS):
        if iteration:
            nears, keeps = [], []
            for i in range(2):
                a, b = program_own[i : i + 1], program_other[i : i + 1]
                if i == GRAM_AT:
                    gram_p = gram(program_own, program_other, False)[0]
                    gram_near = exchange(gram_p, "gene", genes, 1)
                nears.append(exchange(product(a, b, *x[1], 1), "gene", genes, 1))
                keeps.append(product(a, b, *x[0], 1))
        gram_top = far(add(gram_p, gram_near), "gene", genes, True)
        tops = [far(add(keep, near), "gene", genes, True) for keep, near in zip(keeps, nears)]
        mine = add(*gram_top)
        theirs = exchange(mine, "cell", cells, 1)
        new, other = [], []
        for i in range(2):
            new.append(update(i, mine, theirs, usage_own, tops[i], weight=WEIGHT if i else 1))
            other.append(exchange(new[i], "gene", genes, 1))
        usage_own, usage_other = new, other

        sends = [exchange(product(new[:1], other[:1], x[0][1], x[1][1], 0), "cell", cells, 1)]
        keeps = [product(new[:1], other[:1], x[0][0], x[1][0], 0)]
        tops = [far(add(keeps[0], sends[0]), "cell", cells, False)]
        gram_send, gram_keep = gram(usage_own, usage_other, True)
        gram_near = exchange(gram_send, "cell", cells, 1)
        send = product(new[1:], other[1:], x[0][1], x[1][1], 0)
        sends.append(exchange(send, "cell", cells, 1))
        keeps.append(product(new[1:], other[1:], x[0][0], x[1][0], 0))
        tops[0] = (add(*tops[0]),)
        gram_top = far(add(gram_keep, gram_near), "cell", cells, False)
        tops.append(far(add(keeps[1], sends[1]), "cell", cells, False))
        mine = add(*gram_top)
        theirs = exchange(mine, "cell", cells, 1)
        new, other = [], []
        for i in range(2):
            new.append(update(i, mine, theirs, program_own, tops[i]))
            other.append(exchange(new[i], "cell", cells, 1))
        program_own, program_other = new, other

    def join(mine, theirs, which):
        mine, theirs = jnp.concatenate(mine, 0), jnp.concatenate(theirs, 0)
        return jnp.concatenate([jnp.where(which == 0, mine, theirs), jnp.where(which == 0, theirs, mine)], 1)

    return join(usage_own, usage_other, half).T, join(program_own, program_other, core)


def solution(mesh):
    return jax.shard_map(
        functools.partial(body, mesh.shape["gene"], mesh.shape["cell"]),
        mesh=mesh,
        in_specs=(P("cell", "gene"), P(("rep", "cell"), None), P("rep", "gene")),
        out_specs=(P(("rep", "cell"), None), P("rep", "gene")),
        check_vma=False,
    )
```

time: 245 us -> 134 us (0.55)
  waiting for transfers between devices: 182 us -> 58.5 us
  matrix products: 48.9 us -> 0 us
  starting transfers between devices: 0.34 us -> 41.7 us
  Pallas kernels: 0 us -> 28.7 us
  between operations: 13.8 us -> 1.07 us
    psum x4 -> x0, waiting for transfers between devices: 182 us -> none  [the longest x2 107 us: update_usage(): usage_top, program_gram = lax.psum((usage_top, program_gram), 'gene')]
    ppermute x0 -> x36, waiting for transfers between devices: none -> 58.5 us  [exchange(): return lax.ppermute(a, axis, [(i, i ^ flip) for i in range(size)])]
    dot_general x12 -> x0, matrix products: 48.9 us -> none  [the longest x8 38.8 us: contract(): lax.dot_general(left, right, (((left_dim,), (right_dim,)), ((), ())), pre...]
    ppermute x0 -> x36, starting transfers between devices: none -> 41.7 us  [exchange(): return lax.ppermute(a, axis, [(i, i ^ flip) for i in range(size)])]
    pallas_call x0 -> x43, Pallas kernels: none -> 28.7 us  [__call__(): pl.pallas_call(run, out_shape=[pltpu.VMEM(s.shape, s.dtype) for s in shap...]
  transfers between devices with their start and end apart: 4 -> 36, of which waited for: 4 -> 18; matrix products, arithmetic and copies ran while one was open for 0% -> 1% of each run, Pallas kernels for 0% -> 18%
where the time goes in v3:
time: 134 us; the launch traced here: 133 us
  waiting for transfers between devices  58.5 us (44%)
  starting transfers between devices  41.7 us (31%)
  Pallas kernels  28.7 us (21%)
  other arithmetic  2.19 us (2%)
    ppermute x36, waiting for transfers between devices, exchange(): return lax.ppermute(a, axis, [(i, i ^ flip) for i in range(size)])  58.5 us
    ppermute x36, starting transfers between devices, exchange(): return lax.ppermute(a, axis, [(i, i ^ flip) for i in range(size)])  41.7 us
    pallas_call x43, Pallas kernels, __call__(): pl.pallas_call(run, out_shape=[pltpu.VMEM(s.shape, s.dtype) for s in shap...  28.7 us
  transfers between devices with their start and end apart: 36, of which 18 were waited for; matrix products, arithmetic and copies ran while one was open for 1% of the time, Pallas kernels for 18%

profile of v3, /device:TPU:0, one launch (start us, length us, event | category | flops | bytes accessed | tf_op | source)
XLA Modules:
  0.0 133.4 jit_solution(5612334456498783723)
XLA Ops:
  0.7 1.2 copy-done
  2.0 4.1 %shard_map.50 = (f32[104,200]{1,0:T(8,128)S(1)}, f32[104,512]{1,0:T(8,128)S(1)}, f32[96,512]{1,0:T(8,128)S(1)}, f32[104,640]{1,0:T(8,128)S(1)}, f32[96,640]{1,0:...) custom-call(s32[2]{0:T(128)S(1)} %pad_add_fusion.refs_0_, ...), custom_call_target="tpu_custom_call" | custom-call | flops 524288000 | bytes 10405128 | tf_op jit(solution)/shard_map/pallas_call | solution.py:60
  6.0 3.1 %collective-permute-start.3 = (f32[104,512]{1,0:T(8,128)S(1)}, f32[104,512]{1,0:T(8,128)S(1)}, u32[]{:S(2)}, u32[]{:S(2)}) collective-permute-start(f32[104,512]{1,0:T(8,128)S(1)} %get-tuple-element.29), channel_id=1, source_target_pairs={{0,1},{1,0},{2,3},{3,2},{4,5},{5,4},{6,7},{7,6},{8,9},{9,8},{10,11... | collective-permute-start | bytes 638984 | tf_op jit(solution)/shard_map/ppermute | solution.py:74
  9.2 1.9 %collective-permute-start.2 = (f32[96,512]{1,0:T(8,128)S(1)}, f32[96,512]{1,0:T(8,128)S(1)}, u32[]{:S(2)}, u32[]{:S(2)}) collective-permute-start(f32[96,512]{1,0:T(8,128)S(1)} %get-tuple-element.28), channel_id=1, source_target_pairs={{0,1},{1,0},{2,3},{3,2},{4,5},{5,4},{6,7},{7,6},{8,9},{9,8},{10,11... | collective-permute-start | bytes 589832 | tf_op jit(solution)/shard_map/ppermute | solution.py:74
  11.1 3.3 %shard_map.51 = (f32[104,512]{1,0:T(8,128)S(1)}, f32[96,512]{1,0:T(8,128)S(1)}, bf16[512,640]{1,0:T(8,128)(2,1)S(1)}, bf16[512,640]{1,0:T(8,128)(2,1)S(1)}, f32[...) custom-call(s32[2]{0:T(128)S(1)} %pad_add_fusion.refs_0_, s32[1024,1280]{1,0:T(8,128)} %refs_1_.3, ...), custom_call_target="tpu_custom_call" | custom-call | flops 524288000 | bytes 10526728 | tf_op jit(solution)/shard_map/pallas_call | solution.py:60
  14.5 3.0 %collective-permute-done.refs_1_ = f32[104,200]{1,0:T(8,128)S(1)} collective-permute-done((f32[104,200]{1,0:T(8,128)S(1)}, f32[104,200]{1,0:T(8,128)S(1)}, u32[]{:S(2)}, u32[]{:S(2)}) %collective-permute-start) | collective-permute-done | bytes 83232 | tf_op jit(solution)/shard_map/ppermute | solution.py:74
  17.5 4.2 %collective-permute-start.5 = (f32[104,512]{1,0:T(8,128)S(1)}, f32[104,512]{1,0:T(8,128)S(1)}, u32[]{:S(2)}, u32[]{:S(2)}) collective-permute-start(f32[104,512]{1,0:T(8,128)S(1)} %shard_map.53.refs_2_.refs_5_), channel_id=1, source_target_pairs={{0,3},{1,2},{2,1},{3,0},{4,7},{5,6},{6,5},{7,4},{8,11},{9,10},{10,... | collective-permute-start | bytes 638984 | tf_op jit(solution)/shard_map/ppermute | solution.py:74
  21.8 8.2 %collective-permute-done.1.refs_1_ = f32[104,200]{1,0:T(8,128)S(1)} collective-permute-done((f32[104,200]{1,0:T(8,128)S(1)}, f32[104,200]{1,0:T(8,128)S(1)}, u32[]{:S(2)}, u32[]{:S(2)}) %collective-permute-start.1) | collective-permute-done | bytes 83232 | tf_op jit(solution)/shard_map/ppermute | solution.py:74
  30.1 1.6 %collective-permute-start.6 = (f32[96,512]{1,0:T(8,128)S(1)}, f32[96,512]{1,0:T(8,128)S(1)}, u32[]{:S(2)}, u32[]{:S(2)}) collective-permute-start(f32[96,512]{1,0:T(8,128)S(1)} %shard_map.54.refs_2_.refs_5_), channel_id=1, source_target_pairs={{0,3},{1,2},{2,1},{3,0},{4,7},{5,6},{6,5},{7,4},{8,11},{9,10},{10,... | collective-permute-start | bytes 589832 | tf_op jit(solution)/shard_map/ppermute | solution.py:74
  31.7 0.8 shard_map.56.refs_7_.refs_0_.refs_1_.refs_3_
  32.5 3.9 %collective-permute-start.7 = (f32[104,512]{1,0:T(8,128)S(1)}, f32[104,512]{1,0:T(8,128)S(1)}, u32[]{:S(2)}, u32[]{:S(2)}) collective-permute-start(f32[104,512]{1,0:T(8,128)S(1)} %shard_map.56.refs_7_.refs_0_.refs_1_.refs_3_), channel_id=1, source_target_pairs={{0,1},{1,0},{2,3},{3,2},{4,5},{5,4},{6,7},{7,6},{8,9},{9,8},{10,11... | collective-permute-start | bytes 638984 | tf_op jit(solution)/shard_map/ppermute | solution.py:74
  36.4 3.0 %collective-permute-done.6.refs_6_ = f32[96,512]{1,0:T(8,128)S(1)} collective-permute-done((f32[96,512]{1,0:T(8,128)S(1)}, f32[96,512]{1,0:T(8,128)S(1)}, u32[]{:S(2)}, u32[]{:S(2)}) %collective-permute-start.6) | collective-permute-done | bytes 196640 | tf_op jit(solution)/shard_map/ppermute | solution.py:74
  39.4 0.8 shard_map.57.refs_4_.refs_2_.refs_0_
  40.2 3.6 %collective-permute-done.7.refs_1_.refs_3_ = f32[104,512]{1,0:T(8,128)S(1)} collective-permute-done((f32[104,512]{1,0:T(8,128)S(1)}, f32[104,512]{1,0:T(8,128)S(1)}, u32[]{:S(2)}, u32[]{:S(2)}) %collective-permute-start.7) | collective-permute-done | bytes 213024 | tf_op jit(solution)/shard_map/ppermute | solution.py:74
  43.9 0.6 shard_map.58.refs_4_
  44.6 1.0 collective-permute-start.8
  46.2 1.6 %collective-permute-start.11 = (f32[104,640]{1,0:T(8,128)S(1)}, f32[104,640]{1,0:T(8,128)S(1)}, u32[]{:S(2)}, u32[]{:S(2)}) collective-permute-start(f32[104,640]{1,0:T(8,128)S(1)} %shard_map.60.refs_5_.refs_0_), channel_id=1, source_target_pairs={{0,8},{4,12},{8,0},{12,4},{1,9},{5,13},{9,1},{13,5},{2,10},{6,14},... | collective-permute-start | bytes 798728 | tf_op jit(solution)/shard_map/ppermute | solution.py:74
  47.8 4.1 %collective-permute-done.8.refs_4_.refs_1_ = f32[96,512]{1,0:T(8,128)S(1)} collective-permute-done((f32[96,512]{1,0:T(8,128)S(1)}, f32[96,512]{1,0:T(8,128)S(1)}, u32[]{:S(2)}, u32[]{:S(2)}) %collective-permute-start.8) | collective-permute-done | bytes 196640 | tf_op jit(solution)/shard_map/ppermute | solution.py:74
  51.9 1.1 shard_map.61
  52.9 0.6 shard_map.62.refs_4_
  54.1 0.6 shard_map.63.refs_2_.refs_0_
  55.3 1.6 %collective-permute-start.12 = (f32[104,200]{1,0:T(8,128)S(1)}, f32[104,200]{1,0:T(8,128)S(1)}, u32[]{:S(2)}, u32[]{:S(2)}) collective-permute-start(f32[104,200]{1,0:T(8,128)S(1)} %shard_map.65.refs_2_.refs_0_), channel_id=1, source_target_pairs={{0,8},{4,12},{8,0},{12,4},{1,9},{5,13},{9,1},{13,5},{2,10},{6,14},... | collective-permute-start | bytes 249608 | tf_op jit(solution)/shard_map/ppermute | solution.py:74
  56.9 0.6 collective-permute-start.15
  57.5 3.7 %collective-permute-done.12.refs_1_ = f32[104,200]{1,0:T(8,128)S(1)} collective-permute-done((f32[104,200]{1,0:T(8,128)S(1)}, f32[104,200]{1,0:T(8,128)S(1)}, u32[]{:S(2)}, u32[]{:S(2)}) %collective-permute-start.12) | collective-permute-done | bytes 83232 | tf_op jit(solution)/shard_map/ppermute | solution.py:74
  61.2 1.3 collective-permute-done.14.refs_2_
  62.5 0.9 shard_map.68.refs_7_.refs_0_.refs_1_.refs_3_
  63.6 2.0 %collective-permute-done.15.refs_6_ = f32[96,640]{1,0:T(8,128)S(1)} collective-permute-done((f32[96,640]{1,0:T(8,128)S(1)}, f32[96,640]{1,0:T(8,128)S(1)}, u32[]{:S(2)}, u32[]{:S(2)}) %collective-permute-start.15) | collective-permute-done | bytes 245792 | tf_op jit(solution)/shard_map/ppermute | solution.py:74
  65.6 0.8 shard_map.69.refs_4_.refs_2_.refs_0_
  66.6 0.9 shard_map.70.refs_4_
  67.5 1.0 collective-permute-start.21
  68.6 0.9 shard_map.71.refs_5_.refs_0_
  69.5 1.2 shard_map.72.refs_4_.refs_0_
  70.8 1.1 collective-permute-start.18
  71.9 0.9 shard_map.73.refs_4_
  72.8 1.0 collective-permute-start.20
  73.8 0.9 shard_map.74.refs_2_.refs_0_
  74.8 3.2 %collective-permute-done.18.refs_1_ = f32[104,200]{1,0:T(8,128)S(1)} collective-permute-done((f32[104,200]{1,0:T(8,128)S(1)}, f32[104,200]{1,0:T(8,128)S(1)}, u32[]{:S(2)}, u32[]{:S(2)}) %collective-permute-start.18) | collective-permute-done | bytes 83232 | tf_op jit(solution)/shard_map/ppermute | solution.py:74
  78.0 1.6 %collective-permute-start.23 = (f32[104,512]{1,0:T(8,128)S(1)}, f32[104,512]{1,0:T(8,128)S(1)}, u32[]{:S(2)}, u32[]{:S(2)}) collective-permute-start(f32[104,512]{1,0:T(8,128)S(1)} %shard_map.76.refs_2_.refs_5_), channel_id=1, source_target_pairs={{0,3},{1,2},{2,1},{3,0},{4,7},{5,6},{6,5},{7,4},{8,11},{9,10},{10,... | collective-permute-start | bytes 638984 | tf_op jit(solution)/shard_map/ppermute | solution.py:74
  79.6 2.3 %collective-permute-start.19 = (f32[104,200]{1,0:T(8,128)S(1)}, f32[104,200]{1,0:T(8,128)S(1)}, u32[]{:S(2)}, u32[]{:S(2)}) collective-permute-start(f32[104,200]{1,0:T(8,128)S(1)} %shard_map.75.refs_2_.refs_0_), channel_id=1, source_target_pairs={{0,3},{1,2},{2,1},{3,0},{4,7},{5,6},{6,5},{7,4},{8,11},{9,10},{10,... | collective-permute-start | bytes 249608 | tf_op jit(solution)/shard_map/ppermute | solution.py:74
  81.9 7.2 %collective-permute-done.19.refs_1_ = f32[104,200]{1,0:T(8,128)S(1)} collective-permute-done((f32[104,200]{1,0:T(8,128)S(1)}, f32[104,200]{1,0:T(8,128)S(1)}, u32[]{:S(2)}, u32[]{:S(2)}) %collective-permute-start.19) | collective-permute-done | bytes 83232 | tf_op jit(solution)/shard_map/ppermute | solution.py:74
  89.2 2.4 %collective-permute-start.24 = (f32[96,512]{1,0:T(8,128)S(1)}, f32[96,512]{1,0:T(8,128)S(1)}, u32[]{:S(2)}, u32[]{:S(2)}) collective-permute-start(f32[96,512]{1,0:T(8,128)S(1)} %shard_map.77.refs_2_.refs_5_), channel_id=1, source_target_pairs={{0,3},{1,2},{2,1},{3,0},{4,7},{5,6},{6,5},{7,4},{8,11},{9,10},{10,... | collective-permute-start | bytes 589832 | tf_op jit(solution)/shard_map/ppermute | solution.py:74
  91.6 0.8 shard_map.79.refs_7_.refs_0_.refs_1_
  92.5 4.4 %collective-permute-start.25 = (f32[104,512]{1,0:T(8,128)S(1)}, f32[104,512]{1,0:T(8,128)S(1)}, u32[]{:S(2)}, u32[]{:S(2)}) collective-permute-start(f32[104,512]{1,0:T(8,128)S(1)} %shard_map.79.refs_7_.refs_0_.refs_1_), channel_id=1, source_target_pairs={{0,1},{1,0},{2,3},{3,2},{4,5},{5,4},{6,7},{7,6},{8,9},{9,8},{10,11... | collective-permute-start | bytes 638984 | tf_op jit(solution)/shard_map/ppermute | solution.py:74
  96.9 1.6 %collective-permute-done.24.refs_6_ = f32[96,512]{1,0:T(8,128)S(1)} collective-permute-done((f32[96,512]{1,0:T(8,128)S(1)}, f32[96,512]{1,0:T(8,128)S(1)}, u32[]{:S(2)}, u32[]{:S(2)}) %collective-permute-start.24) | collective-permute-done | bytes 196640 | tf_op jit(solution)/shard_map/ppermute | solution.py:74
  98.5 0.8 shard_map.80.refs_4_.refs_2_.refs_0_
  99.3 3.6 %collective-permute-done.25.refs_1_.refs_3_ = f32[104,512]{1,0:T(8,128)S(1)} collective-permute-done((f32[104,512]{1,0:T(8,128)S(1)}, f32[104,512]{1,0:T(8,128)S(1)}, u32[]{:S(2)}, u32[]{:S(2)}) %collective-permute-start.25) | collective-permute-done | bytes 213024 | tf_op jit(solution)/shard_map/ppermute | solution.py:74
  103.6 1.3 collective-permute-start.26
  104.9 0.6 shard_map.82.refs_0_.refs_2_
  105.5 1.6 %collective-permute-start.29 = (f32[104,640]{1,0:T(8,128)S(1)}, f32[104,640]{1,0:T(8,128)S(1)}, u32[]{:S(2)}, u32[]{:S(2)}) collective-permute-start(f32[104,640]{1,0:T(8,128)S(1)} %shard_map.83.refs_5_.refs_0_), channel_id=1, source_target_pairs={{0,8},{4,12},{8,0},{12,4},{1,9},{5,13},{9,1},{13,5},{2,10},{6,14},... | collective-permute-start | bytes 798728 | tf_op jit(solution)/shard_map/ppermute | solution.py:74
  107.2 3.8 %collective-permute-done.26.refs_4_.refs_1_ = f32[96,512]{1,0:T(8,128)S(1)} collective-permute-done((f32[96,512]{1,0:T(8,128)S(1)}, f32[96,512]{1,0:T(8,128)S(1)}, u32[]{:S(2)}, u32[]{:S(2)}) %collective-permute-start.26) | collective-permute-done | bytes 196640 | tf_op jit(solution)/shard_map/ppermute | solution.py:74
  110.9 1.7 %shard_map.84 = (f32[104,200]{1,0:T(8,128)}, f32[104,200]{1,0:T(8,128)S(1)}) custom-call(s32[2]{0:T(128)S(1)} %pad_add_fusion.refs_0_, f32[104,512]{1,0:T(8,128)S(1)} %shard_map.79.refs_7_.refs_0_.refs_1_, f32[96,512]{1,0:T(8,128)S(1)} %shard_map.80.refs_4_.refs_2_.refs_0_, f32[104,512]{1,0:T(8,128)S(1)} %collective-permute-done.25.refs_1_.refs_3_, ...), custom_call_target="tpu_custom_call" | custom-call | flops 245760000 | bytes 985608 | tf_op jit(solution)/shard_map/pallas_call | solution.py:60
  112.7 0.6 shard_map.85.refs_4_
  113.8 0.6 shard_map.86.refs_2_.refs_0_
  114.5 0.8 collective-permute-done.28.refs_1_
  115.3 0.9 shard_map.88.refs_2_.refs_0_
  116.2 1.6 %collective-permute-start.30 = (f32[104,200]{1,0:T(8,128)S(1)}, f32[104,200]{1,0:T(8,128)S(1)}, u32[]{:S(2)}, u32[]{:S(2)}) collective-permute-start(f32[104,200]{1,0:T(8,128)S(1)} %shard_map.88.refs_2_.refs_0_), channel_id=1, source_target_pairs={{0,8},{4,12},{8,0},{12,4},{1,9},{5,13},{9,1},{13,5},{2,10},{6,14},... | collective-permute-start | bytes 249608 | tf_op jit(solution)/shard_map/ppermute | solution.py:74
  117.8 1.0 shard_map.89.refs_2_.refs_5_
  118.8 2.5 %collective-permute-done.30.refs_1_ = f32[104,200]{1,0:T(8,128)S(1)} collective-permute-done((f32[104,200]{1,0:T(8,128)S(1)}, f32[104,200]{1,0:T(8,128)S(1)}, u32[]{:S(2)}, u32[]{:S(2)}) %collective-permute-start.30) | collective-permute-done | bytes 83232 | tf_op jit(solution)/shard_map/ppermute | solution.py:74
  121.4 1.6 %collective-permute-start.33 = (f32[96,640]{1,0:T(8,128)S(1)}, f32[96,640]{1,0:T(8,128)S(1)}, u32[]{:S(2)}, u32[]{:S(2)}) collective-permute-start(f32[96,640]{1,0:T(8,128)S(1)} %shard_map.89.refs_2_.refs_5_), channel_id=1, source_target_pairs={{0,8},{4,12},{8,0},{12,4},{1,9},{5,13},{9,1},{13,5},{2,10},{6,14},... | collective-permute-start | bytes 737288 | tf_op jit(solution)/shard_map/ppermute | solution.py:74
  123.0 0.9 shard_map.91.refs_7_
  124.2 5.6 %collective-permute-done.33.refs_6_ = f32[96,640]{1,0:T(8,128)S(1)} collective-permute-done((f32[96,640]{1,0:T(8,128)S(1)}, f32[96,640]{1,0:T(8,128)S(1)}, u32[]{:S(2)}, u32[]{:S(2)}) %collective-permute-start.33) | collective-permute-done | bytes 245792 | tf_op jit(solution)/shard_map/ppermute | solution.py:74
  129.9 0.8 shard_map.92
  130.8 0.9 maximum_bitcast_fusion
  132.4 1.0 pad_maximum_fusion
  (64 shorter events, 5.3 us)
Async XLA Ops:
  0.7 1.2 copy-start
  1.9 9.2 %copy-start.1 = (f32[1024,200]{0,1:T(8,128)S(1)}, f32[1024,200]{0,1:T(8,128)}, u32[]{:S(2)}) copy-start(f32[1024,200]{0,1:T(8,128)} %param.4) | copy-start | bytes 2457604
  6.0 11.5 %collective-permute-start.3 = (f32[104,512]{1,0:T(8,128)S(1)}, f32[104,512]{1,0:T(8,128)S(1)}, u32[]{:S(2)}, u32[]{:S(2)}) collective-permute-start(f32[104,512]{1,0:T(8,128)S(1)} %get-tuple-element.29), channel_id=1, source_target_pairs={{0,1},{1,0},{2,3},{3,2},{4,5},{5,4},{6,7},{7,6},{8,9},{9,8},{10,11... | collective-permute-start | bytes 638984 | tf_op jit(solution)/shard_map/ppermute | solution.py:74
  9.1 8.4 %collective-permute-start = (f32[104,200]{1,0:T(8,128)S(1)}, f32[104,200]{1,0:T(8,128)S(1)}, u32[]{:S(2)}, u32[]{:S(2)}) collective-permute-start(f32[104,200]{1,0:T(8,128)S(1)} %get-tuple-element.21.refs_7_.refs_0_), channel_id=1, source_target_pairs={{0,1},{1,0},{2,3},{3,2},{4,5},{5,4},{6,7},{7,6},{8,9},{9,8},{10,11... | collective-permute-start | bytes 249608 | tf_op jit(solution)/shard_map/ppermute | solution.py:74
  9.2 12.6 %collective-permute-start.2 = (f32[96,512]{1,0:T(8,128)S(1)}, f32[96,512]{1,0:T(8,128)S(1)}, u32[]{:S(2)}, u32[]{:S(2)}) collective-permute-start(f32[96,512]{1,0:T(8,128)S(1)} %get-tuple-element.28), channel_id=1, source_target_pairs={{0,1},{1,0},{2,3},{3,2},{4,5},{5,4},{6,7},{7,6},{8,9},{9,8},{10,11... | collective-permute-start | bytes 589832 | tf_op jit(solution)/shard_map/ppermute | solution.py:74
  17.5 14.1 %collective-permute-start.5 = (f32[104,512]{1,0:T(8,128)S(1)}, f32[104,512]{1,0:T(8,128)S(1)}, u32[]{:S(2)}, u32[]{:S(2)}) collective-permute-start(f32[104,512]{1,0:T(8,128)S(1)} %shard_map.53.refs_2_.refs_5_), channel_id=1, source_target_pairs={{0,3},{1,2},{2,1},{3,0},{4,7},{5,6},{6,5},{7,4},{8,11},{9,10},{10,... | collective-permute-start | bytes 638984 | tf_op jit(solution)/shard_map/ppermute | solution.py:74
  21.7 8.3 %collective-permute-start.1 = (f32[104,200]{1,0:T(8,128)S(1)}, f32[104,200]{1,0:T(8,128)S(1)}, u32[]{:S(2)}, u32[]{:S(2)}) collective-permute-start(f32[104,200]{1,0:T(8,128)S(1)} %shard_map.52.refs_2_.refs_0_), channel_id=1, source_target_pairs={{0,3},{1,2},{2,1},{3,0},{4,7},{5,6},{6,5},{7,4},{8,11},{9,10},{10,... | collective-permute-start | bytes 249608 | tf_op jit(solution)/shard_map/ppermute | solution.py:74
  30.0 1.7 %collective-permute-start.4 = (f32[104,200]{1,0:T(8,128)S(1)}, f32[104,200]{1,0:T(8,128)S(1)}, u32[]{:S(2)}, u32[]{:S(2)}) collective-permute-start(f32[104,200]{1,0:T(8,128)S(1)} %shard_map.55.refs_1_.refs_7_), channel_id=1, source_target_pairs={{0,4},{4,0},{8,12},{12,8},{1,5},{5,1},{9,13},{13,9},{2,6},{6,2},{1... | collective-permute-start | bytes 249608 | tf_op jit(solution)/shard_map/ppermute | solution.py:74
  30.1 9.3 %collective-permute-start.6 = (f32[96,512]{1,0:T(8,128)S(1)}, f32[96,512]{1,0:T(8,128)S(1)}, u32[]{:S(2)}, u32[]{:S(2)}) collective-permute-start(f32[96,512]{1,0:T(8,128)S(1)} %shard_map.54.refs_2_.refs_5_), channel_id=1, source_target_pairs={{0,3},{1,2},{2,1},{3,0},{4,7},{5,6},{6,5},{7,4},{8,11},{9,10},{10,... | collective-permute-start | bytes 589832 | tf_op jit(solution)/shard_map/ppermute | solution.py:74
  32.5 11.4 %collective-permute-start.7 = (f32[104,512]{1,0:T(8,128)S(1)}, f32[104,512]{1,0:T(8,128)S(1)}, u32[]{:S(2)}, u32[]{:S(2)}) collective-permute-start(f32[104,512]{1,0:T(8,128)S(1)} %shard_map.56.refs_7_.refs_0_.refs_1_.refs_3_), channel_id=1, source_target_pairs={{0,1},{1,0},{2,3},{3,2},{4,5},{5,4},{6,7},{7,6},{8,9},{9,8},{10,11... | collective-permute-start | bytes 638984 | tf_op jit(solution)/shard_map/ppermute | solution.py:74
  44.5 1.7 %collective-permute-start.9 = (f32[104,640]{1,0:T(8,128)S(1)}, f32[104,640]{1,0:T(8,128)S(1)}, u32[]{:S(2)}, u32[]{:S(2)}) collective-permute-start(f32[104,640]{1,0:T(8,128)S(1)} %shard_map.58.refs_4_), channel_id=1, source_target_pairs={{0,4},{4,0},{8,12},{12,8},{1,5},{5,1},{9,13},{13,9},{2,6},{6,2},{1... | collective-permute-start | bytes 798728 | tf_op jit(solution)/shard_map/ppermute | solution.py:74
  44.6 7.3 %collective-permute-start.8 = (f32[96,512]{1,0:T(8,128)S(1)}, f32[96,512]{1,0:T(8,128)S(1)}, u32[]{:S(2)}, u32[]{:S(2)}) collective-permute-start(f32[96,512]{1,0:T(8,128)S(1)} %shard_map.57.refs_4_.refs_2_.refs_0_), channel_id=1, source_target_pairs={{0,1},{1,0},{2,3},{3,2},{4,5},{5,4},{6,7},{7,6},{8,9},{9,8},{10,11... | collective-permute-start | bytes 589832 | tf_op jit(solution)/shard_map/ppermute | solution.py:74
  46.2 8.5 %collective-permute-start.11 = (f32[104,640]{1,0:T(8,128)S(1)}, f32[104,640]{1,0:T(8,128)S(1)}, u32[]{:S(2)}, u32[]{:S(2)}) collective-permute-start(f32[104,640]{1,0:T(8,128)S(1)} %shard_map.60.refs_5_.refs_0_), channel_id=1, source_target_pairs={{0,8},{4,12},{8,0},{12,4},{1,9},{5,13},{9,1},{13,5},{2,10},{6,14},... | collective-permute-start | bytes 798728 | tf_op jit(solution)/shard_map/ppermute | solution.py:74
  53.5 3.3 %collective-permute-start.13 = (f32[96,640]{1,0:T(8,128)S(1)}, f32[96,640]{1,0:T(8,128)S(1)}, u32[]{:S(2)}, u32[]{:S(2)}) collective-permute-start(f32[96,640]{1,0:T(8,128)S(1)} %shard_map.62.refs_4_), channel_id=1, source_target_pairs={{0,4},{4,0},{8,12},{12,8},{1,5},{5,1},{9,13},{13,9},{2,6},{6,2},{1... | collective-permute-start | bytes 737288 | tf_op jit(solution)/shard_map/ppermute | solution.py:74
  53.6 1.7 %collective-permute-start.10 = (f32[104,200]{1,0:T(8,128)S(1)}, f32[104,200]{1,0:T(8,128)S(1)}, u32[]{:S(2)}, u32[]{:S(2)}) collective-permute-start(f32[104,200]{1,0:T(8,128)S(1)} %get-tuple-element.37.refs_4_), channel_id=1, source_target_pairs={{0,4},{4,0},{8,12},{12,8},{1,5},{5,1},{9,13},{13,9},{2,6},{6,2},{1... | collective-permute-start | bytes 249608 | tf_op jit(solution)/shard_map/ppermute | solution.py:74
  55.3 5.9 %collective-permute-start.12 = (f32[104,200]{1,0:T(8,128)S(1)}, f32[104,200]{1,0:T(8,128)S(1)}, u32[]{:S(2)}, u32[]{:S(2)}) collective-permute-start(f32[104,200]{1,0:T(8,128)S(1)} %shard_map.65.refs_2_.refs_0_), channel_id=1, source_target_pairs={{0,8},{4,12},{8,0},{12,4},{1,9},{5,13},{9,1},{13,5},{2,10},{6,14},... | collective-permute-start | bytes 249608 | tf_op jit(solution)/shard_map/ppermute | solution.py:74
  56.9 8.7 %collective-permute-start.15 = (f32[96,640]{1,0:T(8,128)S(1)}, f32[96,640]{1,0:T(8,128)S(1)}, u32[]{:S(2)}, u32[]{:S(2)}) collective-permute-start(f32[96,640]{1,0:T(8,128)S(1)} %shard_map.66.refs_2_.refs_5_), channel_id=1, source_target_pairs={{0,8},{4,12},{8,0},{12,4},{1,9},{5,13},{9,1},{13,5},{2,10},{6,14},... | collective-permute-start | bytes 737288 | tf_op jit(solution)/shard_map/ppermute | solution.py:74
  61.2 1.4 %collective-permute-start.14 = (f32[104,200]{1,0:T(8,128)S(1)}, f32[104,200]{1,0:T(8,128)S(1)}, u32[]{:S(2)}, u32[]{:S(2)}) collective-permute-start(f32[104,200]{1,0:T(8,128)S(1)} %shard_map.67.refs_1_.refs_6_), channel_id=1, source_target_pairs={{0,4},{4,0},{8,12},{12,8},{1,5},{5,1},{9,13},{13,9},{2,6},{6,2},{1... | collective-permute-start | bytes 249608 | tf_op jit(solution)/shard_map/ppermute | solution.py:74
  63.4 3.2 %collective-permute-start.16 = (f32[104,640]{1,0:T(8,128)S(1)}, f32[104,640]{1,0:T(8,128)S(1)}, u32[]{:S(2)}, u32[]{:S(2)}) collective-permute-start(f32[104,640]{1,0:T(8,128)S(1)} %shard_map.68.refs_7_.refs_0_.refs_1_.refs_3_), channel_id=1, source_target_pairs={{0,4},{4,0},{8,12},{12,8},{1,5},{5,1},{9,13},{13,9},{2,6},{6,2},{1... | collective-permute-start | bytes 798728 | tf_op jit(solution)/shard_map/ppermute | solution.py:74
  66.5 3.0 %collective-permute-start.17 = (f32[96,640]{1,0:T(8,128)S(1)}, f32[96,640]{1,0:T(8,128)S(1)}, u32[]{:S(2)}, u32[]{:S(2)}) collective-permute-start(f32[96,640]{1,0:T(8,128)S(1)} %shard_map.69.refs_4_.refs_2_.refs_0_), channel_id=1, source_target_pairs={{0,4},{4,0},{8,12},{12,8},{1,5},{5,1},{9,13},{13,9},{2,6},{6,2},{1... | collective-permute-start | bytes 737288 | tf_op jit(solution)/shard_map/ppermute | solution.py:74
  67.5 10.4 %collective-permute-start.21 = (f32[104,512]{1,0:T(8,128)S(1)}, f32[104,512]{1,0:T(8,128)S(1)}, u32[]{:S(2)}, u32[]{:S(2)}) collective-permute-start(f32[104,512]{1,0:T(8,128)S(1)} %shard_map.70.refs_4_), channel_id=1, source_target_pairs={{0,1},{1,0},{2,3},{3,2},{4,5},{5,4},{6,7},{7,6},{8,9},{9,8},{10,11... | collective-permute-start | bytes 638984 | tf_op jit(solution)/shard_map/ppermute | solution.py:74
  70.8 7.2 %collective-permute-start.18 = (f32[104,200]{1,0:T(8,128)S(1)}, f32[104,200]{1,0:T(8,128)S(1)}, u32[]{:S(2)}, u32[]{:S(2)}) collective-permute-start(f32[104,200]{1,0:T(8,128)S(1)} %shard_map.72.refs_4_.refs_0_), channel_id=1, source_target_pairs={{0,1},{1,0},{2,3},{3,2},{4,5},{5,4},{6,7},{7,6},{8,9},{9,8},{10,11... | collective-permute-start | bytes 249608 | tf_op jit(solution)/shard_map/ppermute | solution.py:74
  72.8 9.1 %collective-permute-start.20 = (f32[96,512]{1,0:T(8,128)S(1)}, f32[96,512]{1,0:T(8,128)S(1)}, u32[]{:S(2)}, u32[]{:S(2)}) collective-permute-start(f32[96,512]{1,0:T(8,128)S(1)} %shard_map.73.refs_4_), channel_id=1, source_target_pairs={{0,1},{1,0},{2,3},{3,2},{4,5},{5,4},{6,7},{7,6},{8,9},{9,8},{10,11... | collective-permute-start | bytes 589832 | tf_op jit(solution)/shard_map/ppermute | solution.py:74
  78.0 13.6 %collective-permute-start.23 = (f32[104,512]{1,0:T(8,128)S(1)}, f32[104,512]{1,0:T(8,128)S(1)}, u32[]{:S(2)}, u32[]{:S(2)}) collective-permute-start(f32[104,512]{1,0:T(8,128)S(1)} %shard_map.76.refs_2_.refs_5_), channel_id=1, source_target_pairs={{0,3},{1,2},{2,1},{3,0},{4,7},{5,6},{6,5},{7,4},{8,11},{9,10},{10,... | collective-permute-start | bytes 638984 | tf_op jit(solution)/shard_map/ppermute | solution.py:74
  79.6 9.6 %collective-permute-start.19 = (f32[104,200]{1,0:T(8,128)S(1)}, f32[104,200]{1,0:T(8,128)S(1)}, u32[]{:S(2)}, u32[]{:S(2)}) collective-permute-start(f32[104,200]{1,0:T(8,128)S(1)} %shard_map.75.refs_2_.refs_0_), channel_id=1, source_target_pairs={{0,3},{1,2},{2,1},{3,0},{4,7},{5,6},{6,5},{7,4},{8,11},{9,10},{10,... | collective-permute-start | bytes 249608 | tf_op jit(solution)/shard_map/ppermute | solution.py:74
  89.2 2.5 %collective-permute-start.22 = (f32[104,200]{1,0:T(8,128)S(1)}, f32[104,200]{1,0:T(8,128)S(1)}, u32[]{:S(2)}, u32[]{:S(2)}) collective-permute-start(f32[104,200]{1,0:T(8,128)S(1)} %shard_map.78.refs_1_.refs_7_), channel_id=1, source_target_pairs={{0,4},{4,0},{8,12},{12,8},{1,5},{5,1},{9,13},{13,9},{2,6},{6,2},{1... | collective-permute-start | bytes 249608 | tf_op jit(solution)/shard_map/ppermute | solution.py:74
  89.2 9.3 %collective-permute-start.24 = (f32[96,512]{1,0:T(8,128)S(1)}, f32[96,512]{1,0:T(8,128)S(1)}, u32[]{:S(2)}, u32[]{:S(2)}) collective-permute-start(f32[96,512]{1,0:T(8,128)S(1)} %shard_map.77.refs_2_.refs_5_), channel_id=1, source_target_pairs={{0,3},{1,2},{2,1},{3,0},{4,7},{5,6},{6,5},{7,4},{8,11},{9,10},{10,... | collective-permute-start | bytes 589832 | tf_op jit(solution)/shard_map/ppermute | solution.py:74
  92.5 10.5 %collective-permute-start.25 = (f32[104,512]{1,0:T(8,128)S(1)}, f32[104,512]{1,0:T(8,128)S(1)}, u32[]{:S(2)}, u32[]{:S(2)}) collective-permute-start(f32[104,512]{1,0:T(8,128)S(1)} %shard_map.79.refs_7_.refs_0_.refs_1_), channel_id=1, source_target_pairs={{0,1},{1,0},{2,3},{3,2},{4,5},{5,4},{6,7},{7,6},{8,9},{9,8},{10,11... | collective-permute-start | bytes 638984 | tf_op jit(solution)/shard_map/ppermute | solution.py:74
  103.6 1.9 %collective-permute-start.27 = (f32[104,640]{1,0:T(8,128)S(1)}, f32[104,640]{1,0:T(8,128)S(1)}, u32[]{:S(2)}, u32[]{:S(2)}) collective-permute-start(f32[104,640]{1,0:T(8,128)S(1)} %shard_map.81.refs_4_), channel_id=1, source_target_pairs={{0,4},{4,0},{8,12},{12,8},{1,5},{5,1},{9,13},{13,9},{2,6},{6,2},{1... | collective-permute-start | bytes 798728 | tf_op jit(solution)/shard_map/ppermute | solution.py:74
  103.6 7.3 %collective-permute-start.26 = (f32[96,512]{1,0:T(8,128)S(1)}, f32[96,512]{1,0:T(8,128)S(1)}, u32[]{:S(2)}, u32[]{:S(2)}) collective-permute-start(f32[96,512]{1,0:T(8,128)S(1)} %shard_map.80.refs_4_.refs_2_.refs_0_), channel_id=1, source_target_pairs={{0,1},{1,0},{2,3},{3,2},{4,5},{5,4},{6,7},{7,6},{8,9},{9,8},{10,11... | collective-permute-start | bytes 589832 | tf_op jit(solution)/shard_map/ppermute | solution.py:74
  105.5 8.9 %collective-permute-start.29 = (f32[104,640]{1,0:T(8,128)S(1)}, f32[104,640]{1,0:T(8,128)S(1)}, u32[]{:S(2)}, u32[]{:S(2)}) collective-permute-start(f32[104,640]{1,0:T(8,128)S(1)} %shard_map.83.refs_5_.refs_0_), channel_id=1, source_target_pairs={{0,8},{4,12},{8,0},{12,4},{1,9},{5,13},{9,1},{13,5},{2,10},{6,14},... | collective-permute-start | bytes 798728 | tf_op jit(solution)/shard_map/ppermute | solution.py:74
  113.2 4.6 %collective-permute-start.31 = (f32[96,640]{1,0:T(8,128)S(1)}, f32[96,640]{1,0:T(8,128)}, u32[]{:S(2)}, u32[]{:S(2)}) collective-permute-start(f32[96,640]{1,0:T(8,128)S(1)} %shard_map.85.refs_4_), channel_id=1, source_target_pairs={{0,4},{4,0},{8,12},{12,8},{1,5},{5,1},{9,13},{13,9},{2,6},{6,2},{1... | collective-permute-start | bytes 737288 | tf_op jit(solution)/shard_map/ppermute | solution.py:74
  113.3 2.0 %collective-permute-start.28 = (f32[104,200]{1,0:T(8,128)}, f32[104,200]{1,0:T(8,128)}, u32[]{:S(2)}, u32[]{:S(2)}) collective-permute-start(f32[104,200]{1,0:T(8,128)} %get-tuple-element.39.refs_4_), channel_id=1, source_target_pairs={{0,4},{4,0},{8,12},{12,8},{1,5},{5,1},{9,13},{13,9},{2,6},{6,2},{1... | collective-permute-start | bytes 249608 | tf_op jit(solution)/shard_map/ppermute | solution.py:74
  116.2 5.1 %collective-permute-start.30 = (f32[104,200]{1,0:T(8,128)S(1)}, f32[104,200]{1,0:T(8,128)S(1)}, u32[]{:S(2)}, u32[]{:S(2)}) collective-permute-start(f32[104,200]{1,0:T(8,128)S(1)} %shard_map.88.refs_2_.refs_0_), channel_id=1, source_target_pairs={{0,8},{4,12},{8,0},{12,4},{1,9},{5,13},{9,1},{13,5},{2,10},{6,14},... | collective-permute-start | bytes 249608 | tf_op jit(solution)/shard_map/ppermute | solution.py:74
  121.3 1.7 %collective-permute-start.32 = (f32[104,200]{1,0:T(8,128)S(1)}, f32[104,200]{1,0:T(8,128)S(1)}, u32[]{:S(2)}, u32[]{:S(2)}) collective-permute-start(f32[104,200]{1,0:T(8,128)S(1)} %shard_map.90.refs_1_.refs_6_), channel_id=1, source_target_pairs={{0,4},{4,0},{8,12},{12,8},{1,5},{5,1},{9,13},{13,9},{2,6},{6,2},{1... | collective-permute-start | bytes 249608 | tf_op jit(solution)/shard_map/ppermute | solution.py:74
  121.4 8.4 %collective-permute-start.33 = (f32[96,640]{1,0:T(8,128)S(1)}, f32[96,640]{1,0:T(8,128)S(1)}, u32[]{:S(2)}, u32[]{:S(2)}) collective-permute-start(f32[96,640]{1,0:T(8,128)S(1)} %shard_map.89.refs_2_.refs_5_), channel_id=1, source_target_pairs={{0,8},{4,12},{8,0},{12,4},{1,9},{5,13},{9,1},{13,5},{2,10},{6,14},... | collective-permute-start | bytes 737288 | tf_op jit(solution)/shard_map/ppermute | solution.py:74
  123.9 7.9 %collective-permute-start.34 = (f32[104,640]{1,0:T(8,128)S(1)}, f32[104,640]{1,0:T(8,128)S(1)}, u32[]{:S(2)}, u32[]{:S(2)}) collective-permute-start(f32[104,640]{1,0:T(8,128)S(1)} %shard_map.91.refs_7_), channel_id=1, source_target_pairs={{0,4},{4,0},{8,12},{12,8},{1,5},{5,1},{9,13},{13,9},{2,6},{6,2},{1... | collective-permute-start | bytes 798728 | tf_op jit(solution)/shard_map/ppermute | solution.py:74
  130.7 1.6 %collective-permute-start.35 = (f32[96,640]{1,0:T(8,128)S(1)}, f32[96,640]{1,0:T(8,128)S(1)}, u32[]{:S(2)}, u32[]{:S(2)}) collective-permute-start(f32[96,640]{1,0:T(8,128)S(1)} %shard_map.92), channel_id=1, source_target_pairs={{0,4},{4,0},{8,12},{12,8},{1,5},{5,1},{9,13},{13,9},{2,6},{6,2},{1... | collective-permute-start | bytes 737288 | tf_op jit(solution)/shard_map/ppermute | solution.py:74

commit v4 on v3

--- a/solution.py
+++ b/solution.py
@@ -11,6 +11,7 @@
 FIRST_ROWS = 104
 GRAM_AT = 1
 WEIGHT = 12
+LAST_WEIGHT = 12
 VMEM = pl.BlockSpec(memory_space=pltpu.VMEM)
 SMEM = pl.BlockSpec(memory_space=pltpu.SMEM)
 ANY = pl.BlockSpec(memory_space=pl.ANY)
@@ -107,21 +108,28 @@
         n = factor_a[0].shape[1] + factor_b[0].shape[1]
         return chain(kernel, [(grows, k)] * (1 + both), where, *factor_a, *factor_b, flops=6 * k * k * n)
 
-    def product(a, b, xa, xb, dim):
+    def product(a, b, xa, xb, dim, cut=0):
         parts = len(a)
 
         def kernel(*refs):
-            a_refs, b_refs, (xa_ref, xb_ref, o_ref) = refs[:parts], refs[parts : 2 * parts], refs[2 * parts :]
-            o_ref[...] = dot2(stacked(a_refs), xa_ref[...], 1, dim) + dot2(stacked(b_refs), xb_ref[...], 1, dim)
+            a_refs, b_refs, (xa_ref, xb_ref, *o_refs) = refs[:parts], refs[parts : 2 * parts], refs[2 * parts :]
+            o = dot2(stacked(a_refs), xa_ref[...], 1, dim) + dot2(stacked(b_refs), xb_ref[...], 1, dim)
+            if cut:
+                o_refs[0][...], o_refs[1][...] = o[:cut], o[cut:]
+            else:
+                o_refs[0][...] = o
 
         n, m = sum(r.shape[0] for r in a), xa.shape[1 - dim]
-        return chain(kernel, [(n, m)], *a, *b, xa, xb, flops=8 * n * a[0].shape[1] * m)[0]
-
-    def add(a, b):
-        def kernel(a_ref, b_ref, o_ref):
-            o_ref[...] = a_ref[...] + b_ref[...]
-
-        return chain(kernel, [a.shape], a, b)[0]
+        outs = [(cut, m), (n - cut, m)] if cut else [(n, m)]
+        result = chain(kernel, outs, *a, *b, xa, xb, flops=8 * n * a[0].shape[1] * m)
+        return result if cut else result[0]
+
+    def add(a, *b):
+        def kernel(a_ref, *refs):
+            *b_refs, o_ref = refs
+            o_ref[...] = a_ref[...] + stacked(b_refs)
+
+        return chain(kernel, [a.shape], a, *b)[0]
 
     def update(index, mine, theirs, factor, tops, weight=1):
         first = index * sizes[0]
@@ -142,6 +150,20 @@
 
         n, m = factor[index].shape
         return chain(kernel, [(n, m)], where, mine, theirs, *factor, *tops, flops=6 * n * k * m * weight)[0]
+
+    def join(mine, theirs, index, which):
+        size = mine[0].shape[1]
+        if size % 128:
+            mine, theirs = jnp.concatenate(mine, 0), jnp.concatenate(theirs, 0)
+            return jnp.concatenate([jnp.where(which == 0, mine, theirs), jnp.where(which == 0, theirs, mine)], 1)
+
+        def kernel(where_ref, m0, m1, t0, t1, o_ref):
+            first = where_ref[index] == 0
+            for a, b, rows_at in ((m0, t0, slice(0, sizes[0])), (m1, t1, slice(sizes[0], k))):
+                o_ref[rows_at, :size] = jnp.where(first, a[...], b[...])
+                o_ref[rows_at, size:] = jnp.where(first, b[...], a[...])
+
+        return chain(kernel, [(k, 2 * size)], where, *mine, *theirs)[0]
 
     def far(a, axis, size, mirrored):
         step = 2
@@ -272,30 +294,30 @@
             other.append(exchange(new[i], "gene", genes, 1))
         usage_own, usage_other = new, other
 
-        sends = [exchange(product(new[:1], other[:1], x[0][1], x[1][1], 0), "cell", cells, 1)]
+        cut = sizes[0] // 16 * 8
+        send = product(new[:1], other[:1], x[0][1], x[1][1], 0, cut)
+        sends = [[exchange(a, "cell", cells, 1) for a in send]]
         keeps = [product(new[:1], other[:1], x[0][0], x[1][0], 0)]
-        tops = [far(add(keeps[0], sends[0]), "cell", cells, False)]
+        tops = [far(add(keeps[0], *sends[0]), "cell", cells, False)]
         gram_send, gram_keep = gram(usage_own, usage_other, True)
         gram_near = exchange(gram_send, "cell", cells, 1)
         send = product(new[1:], other[1:], x[0][1], x[1][1], 0)
         sends.append(exchange(send, "cell", cells, 1))
         keeps.append(product(new[1:], other[1:], x[0][0], x[1][0], 0))
+        if iteration == ITERS - 1:
+            usage = join(usage_own, usage_other, 1, half)
+        gram_top = far(add(gram_keep, gram_near), "cell", cells, False)
         tops[0] = (add(*tops[0]),)
-        gram_top = far(add(gram_keep, gram_near), "cell", cells, False)
         tops.append(far(add(keeps[1], sends[1]), "cell", cells, False))
         mine = add(*gram_top)
         theirs = exchange(mine, "cell", cells, 1)
         new, other = [], []
         for i in range(2):
-            new.append(update(i, mine, theirs, program_own, tops[i]))
+            new.append(update(i, mine, theirs, program_own, tops[i], weight=LAST_WEIGHT if i == 0 and iteration == ITERS - 1 else 1))
             other.append(exchange(new[i], "cell", cells, 1))
         program_own, program_other = new, other
 
-    def join(mine, theirs, which):
-        mine, theirs = jnp.concatenate(mine, 0), jnp.concatenate(theirs, 0)
-        return jnp.concatenate([jnp.where(which == 0, mine, theirs), jnp.where(which == 0, theirs, mine)], 1)
-
-    return join(usage_own, usage_other, half).T, join(program_own, program_other, core)
+    return usage.T, join(program_own, program_other, 0, core)
 
 
 def solution(mesh):

time: 134 us -> 126 us (0.940)
  waiting for transfers between devices: 58.5 us -> 43 us
  starting transfers between devices: 41.7 us -> 51.2 us
  other arithmetic: 2.19 us -> 0.08 us
  local copies, waits for them, and re-layouts: 1.29 us -> 3.07 us
    ppermute x36 -> x38, waiting for transfers between devices: 58.5 us -> 43 us  [exchange(): return lax.ppermute(a, axis, [(i, i ^ flip) for i in range(size)])]
    ppermute x36 -> x38, starting transfers between devices: 41.7 us -> 51.2 us  [exchange(): return lax.ppermute(a, axis, [(i, i ^ flip) for i in range(size)])]
    unnamed x6, local copies, waits for them, and re-layouts: 1.25 us -> 3.07 us
    pallas_call x43 -> x45, Pallas kernels: 28.7 us -> 27.5 us  [__call__(): pl.pallas_call(run, out_shape=[pltpu.VMEM(s.shape, s.dtype) for s in shap...]
  transfers between devices with their start and end apart: 36 -> 38, of which waited for: 18 -> 20; matrix products, arithmetic and copies ran while one was open for 1% -> 1% of each run, Pallas kernels for 18% -> 18%
where the time goes in v4:
time: 126 us
  starting transfers between devices  51.2 us (41%)
  waiting for transfers between devices  43 us (34%)
  Pallas kernels  27.5 us (22%)
  local copies, waits for them, and re-layouts  3.07 us (2%)
    ppermute x38, starting transfers between devices, exchange(): return lax.ppermute(a, axis, [(i, i ^ flip) for i in range(size)])  51.2 us
    ppermute x38, waiting for transfers between devices, exchange(): return lax.ppermute(a, axis, [(i, i ^ flip) for i in range(size)])  43 us
    pallas_call x45, Pallas kernels, __call__(): pl.pallas_call(run, out_shape=[pltpu.VMEM(s.shape, s.dtype) for s in shap...  27.5 us
    unnamed x6, local copies, waits for them, and re-layouts  3.07 us
  transfers between devices with their start and end apart: 38, of which 20 were waited for; matrix products, arithmetic and copies ran while one was open for 1% of the time, Pallas kernels for 18%

profile of v4, /device:TPU:0, one launch (start us, length us, event | category | flops | bytes accessed | tf_op | source)
XLA Modules:
  0.0 125.9 jit_solution(12729091871063890957)
XLA Ops:
  0.7 1.2 copy-done
  2.0 4.1 %shard_map.50 = (f32[104,200]{1,0:T(8,128)S(1)}, f32[104,512]{1,0:T(8,128)S(1)}, f32[96,512]{1,0:T(8,128)S(1)}, f32[104,640]{1,0:T(8,128)S(1)}, f32[96,640]{1,0:...) custom-call(s32[2]{0:T(128)S(1)} %pad_add_fusion.refs_0_, ...), custom_call_target="tpu_custom_call" | custom-call | flops 524288000 | bytes 10405128 | tf_op jit(solution)/shard_map/pallas_call | solution.py:61
  6.0 3.1 %collective-permute-start.3 = (f32[104,512]{1,0:T(8,128)S(1)}, f32[104,512]{1,0:T(8,128)S(1)}, u32[]{:S(2)}, u32[]{:S(2)}) collective-permute-start(f32[104,512]{1,0:T(8,128)S(1)} %get-tuple-element.33), channel_id=1, source_target_pairs={{0,1},{1,0},{2,3},{3,2},{4,5},{5,4},{6,7},{7,6},{8,9},{9,8},{10,11... | collective-permute-start | bytes 638984 | tf_op jit(solution)/shard_map/ppermute | solution.py:75
  9.2 1.9 %collective-permute-start.2 = (f32[96,512]{1,0:T(8,128)S(1)}, f32[96,512]{1,0:T(8,128)S(1)}, u32[]{:S(2)}, u32[]{:S(2)}) collective-permute-start(f32[96,512]{1,0:T(8,128)S(1)} %get-tuple-element.32), channel_id=1, source_target_pairs={{0,1},{1,0},{2,3},{3,2},{4,5},{5,4},{6,7},{7,6},{8,9},{9,8},{10,11... | collective-permute-start | bytes 589832 | tf_op jit(solution)/shard_map/ppermute | solution.py:75
  11.2 3.4 %shard_map.51 = (f32[104,512]{1,0:T(8,128)S(1)}, f32[96,512]{1,0:T(8,128)S(1)}, bf16[512,640]{1,0:T(8,128)(2,1)S(1)}, bf16[512,640]{1,0:T(8,128)(2,1)S(1)}, f32[...) custom-call(s32[2]{0:T(128)S(1)} %pad_add_fusion.refs_0_, s32[1024,1280]{1,0:T(8,128)} %refs_1_.3, ...), custom_call_target="tpu_custom_call" | custom-call | flops 524288000 | bytes 10526728 | tf_op jit(solution)/shard_map/pallas_call | solution.py:61
  14.5 3.0 %collective-permute-done.refs_1_ = f32[104,200]{1,0:T(8,128)S(1)} collective-permute-done((f32[104,200]{1,0:T(8,128)S(1)}, f32[104,200]{1,0:T(8,128)S(1)}, u32[]{:S(2)}, u32[]{:S(2)}) %collective-permute-start) | collective-permute-done | bytes 83232 | tf_op jit(solution)/shard_map/ppermute | solution.py:75
  17.5 4.1 %collective-permute-start.5 = (f32[104,512]{1,0:T(8,128)S(1)}, f32[104,512]{1,0:T(8,128)S(1)}, u32[]{:S(2)}, u32[]{:S(2)}) collective-permute-start(f32[104,512]{1,0:T(8,128)S(1)} %shard_map.53.refs_2_.refs_5_), channel_id=1, source_target_pairs={{0,3},{1,2},{2,1},{3,0},{4,7},{5,6},{6,5},{7,4},{8,11},{9,10},{10,... | collective-permute-start | bytes 638984 | tf_op jit(solution)/shard_map/ppermute | solution.py:75
  21.8 8.2 %collective-permute-done.1.refs_1_ = f32[104,200]{1,0:T(8,128)S(1)} collective-permute-done((f32[104,200]{1,0:T(8,128)S(1)}, f32[104,200]{1,0:T(8,128)S(1)}, u32[]{:S(2)}, u32[]{:S(2)}) %collective-permute-start.1) | collective-permute-done | bytes 83232 | tf_op jit(solution)/shard_map/ppermute | solution.py:75
  30.1 1.6 %collective-permute-start.6 = (f32[96,512]{1,0:T(8,128)S(1)}, f32[96,512]{1,0:T(8,128)S(1)}, u32[]{:S(2)}, u32[]{:S(2)}) collective-permute-start(f32[96,512]{1,0:T(8,128)S(1)} %shard_map.54.refs_2_.refs_5_), channel_id=1, source_target_pairs={{0,3},{1,2},{2,1},{3,0},{4,7},{5,6},{6,5},{7,4},{8,11},{9,10},{10,... | collective-permute-start | bytes 589832 | tf_op jit(solution)/shard_map/ppermute | solution.py:75
  31.7 0.8 shard_map.56.refs_7_.refs_0_.refs_1_.refs_3_
  32.5 3.9 %collective-permute-start.7 = (f32[104,512]{1,0:T(8,128)S(1)}, f32[104,512]{1,0:T(8,128)S(1)}, u32[]{:S(2)}, u32[]{:S(2)}) collective-permute-start(f32[104,512]{1,0:T(8,128)S(1)} %shard_map.56.refs_7_.refs_0_.refs_1_.refs_3_), channel_id=1, source_target_pairs={{0,1},{1,0},{2,3},{3,2},{4,5},{5,4},{6,7},{7,6},{8,9},{9,8},{10,11... | collective-permute-start | bytes 638984 | tf_op jit(solution)/shard_map/ppermute | solution.py:75
  36.4 3.0 %collective-permute-done.6.refs_6_ = f32[96,512]{1,0:T(8,128)S(1)} collective-permute-done((f32[96,512]{1,0:T(8,128)S(1)}, f32[96,512]{1,0:T(8,128)S(1)}, u32[]{:S(2)}, u32[]{:S(2)}) %collective-permute-start.6) | collective-permute-done | bytes 196640 | tf_op jit(solution)/shard_map/ppermute | solution.py:75
  39.4 0.8 shard_map.57.refs_4_.refs_2_.refs_0_
  40.2 4.6 %collective-permute-start.8 = (f32[96,512]{1,0:T(8,128)S(1)}, f32[96,512]{1,0:T(8,128)S(1)}, u32[]{:S(2)}, u32[]{:S(2)}) collective-permute-start(f32[96,512]{1,0:T(8,128)S(1)} %shard_map.57.refs_4_.refs_2_.refs_0_), channel_id=1, source_target_pairs={{0,1},{1,0},{2,3},{3,2},{4,5},{5,4},{6,7},{7,6},{8,9},{9,8},{10,11... | collective-permute-start | bytes 589832 | tf_op jit(solution)/shard_map/ppermute | solution.py:75
  46.0 0.6 shard_map.59.refs_0_.refs_3_
  47.1 1.6 %collective-permute-start.14 = (f32[104,640]{1,0:T(8,128)S(1)}, f32[104,640]{1,0:T(8,128)S(1)}, u32[]{:S(2)}, u32[]{:S(2)}) collective-permute-start(f32[104,640]{1,0:T(8,128)S(1)} %shard_map.60.refs_5_.refs_0_), channel_id=1, source_target_pairs={{0,8},{4,12},{8,0},{12,4},{1,9},{5,13},{9,1},{13,5},{2,10},{6,14},... | collective-permute-start | bytes 798728 | tf_op jit(solution)/shard_map/ppermute | solution.py:75
  48.7 1.4 %collective-permute-done.8.refs_4_.refs_1_ = f32[96,512]{1,0:T(8,128)S(1)} collective-permute-done((f32[96,512]{1,0:T(8,128)S(1)}, f32[96,512]{1,0:T(8,128)S(1)}, u32[]{:S(2)}, u32[]{:S(2)}) %collective-permute-start.8) | collective-permute-done | bytes 196640 | tf_op jit(solution)/shard_map/ppermute | solution.py:75
  50.0 1.1 shard_map.61
  51.1 0.6 shard_map.62.refs_4_
  52.3 0.6 shard_map.63.refs_2_.refs_0_
  53.4 1.6 %collective-permute-start.12 = (f32[104,200]{1,0:T(8,128)S(1)}, f32[104,200]{1,0:T(8,128)S(1)}, u32[]{:S(2)}, u32[]{:S(2)}) collective-permute-start(f32[104,200]{1,0:T(8,128)S(1)} %shard_map.64.refs_2_.refs_0_), channel_id=1, source_target_pairs={{0,8},{4,12},{8,0},{12,4},{1,9},{5,13},{9,1},{13,5},{2,10},{6,14},... | collective-permute-start | bytes 249608 | tf_op jit(solution)/shard_map/ppermute | solution.py:75
  55.0 0.8 collective-permute-done.14.refs_1_
  55.9 1.6 %collective-permute-start.16 = (f32[96,640]{1,0:T(8,128)S(1)}, f32[96,640]{1,0:T(8,128)S(1)}, u32[]{:S(2)}, u32[]{:S(2)}) collective-permute-start(f32[96,640]{1,0:T(8,128)S(1)} %shard_map.66.refs_2_.refs_5_), channel_id=1, source_target_pairs={{0,8},{4,12},{8,0},{12,4},{1,9},{5,13},{9,1},{13,5},{2,10},{6,14},... | collective-permute-start | bytes 737288 | tf_op jit(solution)/shard_map/ppermute | solution.py:75
  57.4 1.7 %collective-permute-done.12.refs_1_ = f32[104,200]{1,0:T(8,128)S(1)} collective-permute-done((f32[104,200]{1,0:T(8,128)S(1)}, f32[104,200]{1,0:T(8,128)S(1)}, u32[]{:S(2)}, u32[]{:S(2)}) %collective-permute-start.12) | collective-permute-done | bytes 83232 | tf_op jit(solution)/shard_map/ppermute | solution.py:75
  59.2 1.3 %collective-permute-done.15.refs_2_ = f32[104,200]{1,0:T(8,128)S(1)} collective-permute-done((f32[104,200]{1,0:T(8,128)S(1)}, f32[104,200]{1,0:T(8,128)S(1)}, u32[]{:S(2)}, u32[]{:S(2)}) %collective-permute-start.15) | collective-permute-done | bytes 83232 | tf_op jit(solution)/shard_map/ppermute | solution.py:75
  60.5 0.8 shard_map.68.refs_7_.refs_0_.refs_1_.refs_3_
  61.6 2.3 %collective-permute-done.16.refs_6_ = f32[96,640]{1,0:T(8,128)S(1)} collective-permute-done((f32[96,640]{1,0:T(8,128)S(1)}, f32[96,640]{1,0:T(8,128)S(1)}, u32[]{:S(2)}, u32[]{:S(2)}) %collective-permute-start.16) | collective-permute-done | bytes 245792 | tf_op jit(solution)/shard_map/ppermute | solution.py:75
  63.8 0.9 shard_map.69.refs_4_.refs_2_.refs_0_
  64.8 0.9 shard_map.70.refs_4_
  65.7 1.8 %collective-permute-start.22 = (f32[104,512]{1,0:T(8,128)S(1)}, f32[104,512]{1,0:T(8,128)S(1)}, u32[]{:S(2)}, u32[]{:S(2)}) collective-permute-start(f32[104,512]{1,0:T(8,128)S(1)} %shard_map.70.refs_4_), channel_id=1, source_target_pairs={{0,1},{1,0},{2,3},{3,2},{4,5},{5,4},{6,7},{7,6},{8,9},{9,8},{10,11... | collective-permute-start | bytes 638984 | tf_op jit(solution)/shard_map/ppermute | solution.py:75
  67.5 0.9 shard_map.71.refs_5_.refs_0_
  68.5 1.2 shard_map.72.refs_4_.refs_0_
  70.1 0.9 shard_map.73.refs_4_
  71.0 1.8 %collective-permute-start.21 = (f32[96,512]{1,0:T(8,128)S(1)}, f32[96,512]{1,0:T(8,128)S(1)}, u32[]{:S(2)}, u32[]{:S(2)}) collective-permute-start(f32[96,512]{1,0:T(8,128)S(1)} %shard_map.73.refs_4_), channel_id=1, source_target_pairs={{0,1},{1,0},{2,3},{3,2},{4,5},{5,4},{6,7},{7,6},{8,9},{9,8},{10,11... | collective-permute-start | bytes 589832 | tf_op jit(solution)/shard_map/ppermute | solution.py:75
  72.8 0.9 shard_map.74.refs_2_.refs_0_
  73.7 2.4 %collective-permute-done.19.refs_1_ = f32[104,200]{1,0:T(8,128)S(1)} collective-permute-done((f32[104,200]{1,0:T(8,128)S(1)}, f32[104,200]{1,0:T(8,128)S(1)}, u32[]{:S(2)}, u32[]{:S(2)}) %collective-permute-start.19) | collective-permute-done | bytes 83232 | tf_op jit(solution)/shard_map/ppermute | solution.py:75
  76.2 1.6 %collective-permute-start.24 = (f32[104,512]{1,0:T(8,128)S(1)}, f32[104,512]{1,0:T(8,128)S(1)}, u32[]{:S(2)}, u32[]{:S(2)}) collective-permute-start(f32[104,512]{1,0:T(8,128)S(1)} %shard_map.76.refs_2_.refs_5_), channel_id=1, source_target_pairs={{0,3},{1,2},{2,1},{3,0},{4,7},{5,6},{6,5},{7,4},{8,11},{9,10},{10,... | collective-permute-start | bytes 638984 | tf_op jit(solution)/shard_map/ppermute | solution.py:75
  77.7 2.3 %collective-permute-start.20 = (f32[104,200]{1,0:T(8,128)S(1)}, f32[104,200]{1,0:T(8,128)S(1)}, u32[]{:S(2)}, u32[]{:S(2)}) collective-permute-start(f32[104,200]{1,0:T(8,128)S(1)} %shard_map.75.refs_2_.refs_0_), channel_id=1, source_target_pairs={{0,3},{1,2},{2,1},{3,0},{4,7},{5,6},{6,5},{7,4},{8,11},{9,10},{10,... | collective-permute-start | bytes 249608 | tf_op jit(solution)/shard_map/ppermute | solution.py:75
  80.1 8.0 %collective-permute-done.20.refs_1_ = f32[104,200]{1,0:T(8,128)S(1)} collective-permute-done((f32[104,200]{1,0:T(8,128)S(1)}, f32[104,200]{1,0:T(8,128)S(1)}, u32[]{:S(2)}, u32[]{:S(2)}) %collective-permute-start.20) | collective-permute-done | bytes 83232 | tf_op jit(solution)/shard_map/ppermute | solution.py:75
  88.2 2.4 %collective-permute-start.25 = (f32[96,512]{1,0:T(8,128)S(1)}, f32[96,512]{1,0:T(8,128)S(1)}, u32[]{:S(2)}, u32[]{:S(2)}) collective-permute-start(f32[96,512]{1,0:T(8,128)S(1)} %shard_map.77.refs_2_.refs_5_), channel_id=1, source_target_pairs={{0,3},{1,2},{2,1},{3,0},{4,7},{5,6},{6,5},{7,4},{8,11},{9,10},{10,... | collective-permute-start | bytes 589832 | tf_op jit(solution)/shard_map/ppermute | solution.py:75
  90.6 0.8 shard_map.79.refs_7_.refs_0_.refs_1_
  91.4 4.4 %collective-permute-start.26 = (f32[104,512]{1,0:T(8,128)S(1)}, f32[104,512]{1,0:T(8,128)S(1)}, u32[]{:S(2)}, u32[]{:S(2)}) collective-permute-start(f32[104,512]{1,0:T(8,128)S(1)} %shard_map.79.refs_7_.refs_0_.refs_1_), channel_id=1, source_target_pairs={{0,1},{1,0},{2,3},{3,2},{4,5},{5,4},{6,7},{7,6},{8,9},{9,8},{10,11... | collective-permute-start | bytes 638984 | tf_op jit(solution)/shard_map/ppermute | solution.py:75
  95.8 1.6 %collective-permute-done.25.refs_6_ = f32[96,512]{1,0:T(8,128)S(1)} collective-permute-done((f32[96,512]{1,0:T(8,128)S(1)}, f32[96,512]{1,0:T(8,128)S(1)}, u32[]{:S(2)}, u32[]{:S(2)}) %collective-permute-start.25) | collective-permute-done | bytes 196640 | tf_op jit(solution)/shard_map/ppermute | solution.py:75
  97.5 0.8 shard_map.80.refs_4_.refs_2_.refs_0_
  98.3 4.7 %collective-permute-start.27 = (f32[96,512]{1,0:T(8,128)S(1)}, f32[96,512]{1,0:T(8,128)S(1)}, u32[]{:S(2)}, u32[]{:S(2)}) collective-permute-start(f32[96,512]{1,0:T(8,128)S(1)} %shard_map.80.refs_4_.refs_2_.refs_0_), channel_id=1, source_target_pairs={{0,1},{1,0},{2,3},{3,2},{4,5},{5,4},{6,7},{7,6},{8,9},{9,8},{10,11... | collective-permute-start | bytes 589832 | tf_op jit(solution)/shard_map/ppermute | solution.py:75
  104.1 0.6 shard_map.82.refs_0_.refs_3_
  105.2 1.6 %collective-permute-start.33 = (f32[104,640]{1,0:T(8,128)S(1)}, f32[104,640]{1,0:T(8,128)S(1)}, u32[]{:S(2)}, u32[]{:S(2)}) collective-permute-start(f32[104,640]{1,0:T(8,128)S(1)} %shard_map.83.refs_5_.refs_0_), channel_id=1, source_target_pairs={{0,8},{4,12},{8,0},{12,4},{1,9},{5,13},{9,1},{13,5},{2,10},{6,14},... | collective-permute-start | bytes 798728 | tf_op jit(solution)/shard_map/ppermute | solution.py:75
  106.7 1.3 %collective-permute-done.27.refs_4_.refs_1_ = f32[96,512]{1,0:T(8,128)S(1)} collective-permute-done((f32[96,512]{1,0:T(8,128)S(1)}, f32[96,512]{1,0:T(8,128)S(1)}, u32[]{:S(2)}, u32[]{:S(2)}) %collective-permute-start.27) | collective-permute-done | bytes 196640 | tf_op jit(solution)/shard_map/ppermute | solution.py:75
  108.1 1.1 shard_map.84
  109.2 0.6 shard_map.85.refs_4_
  110.3 0.6 shard_map.86.refs_5_.refs_0_
  110.9 0.6 shard_map.87.refs_2_
  111.6 1.6 %collective-permute-start.31 = (f32[104,200]{1,0:T(8,128)S(1)}, f32[104,200]{1,0:T(8,128)S(1)}, u32[]{:S(2)}, u32[]{:S(2)}) collective-permute-start(f32[104,200]{1,0:T(8,128)S(1)} %shard_map.88.refs_2_.refs_0_), channel_id=1, source_target_pairs={{0,8},{4,12},{8,0},{12,4},{1,9},{5,13},{9,1},{13,5},{2,10},{6,14},... | collective-permute-start | bytes 249608 | tf_op jit(solution)/shard_map/ppermute | solution.py:75
  113.1 0.7 collective-permute-done.33.refs_1_
  113.9 1.6 %collective-permute-start.35 = (f32[96,640]{1,0:T(8,128)S(1)}, f32[96,640]{1,0:T(8,128)S(1)}, u32[]{:S(2)}, u32[]{:S(2)}) collective-permute-start(f32[96,640]{1,0:T(8,128)S(1)} %shard_map.90.refs_2_.refs_5_), channel_id=1, source_target_pairs={{0,8},{4,12},{8,0},{12,4},{1,9},{5,13},{9,1},{13,5},{2,10},{6,14},... | collective-permute-start | bytes 737288 | tf_op jit(solution)/shard_map/ppermute | solution.py:75
  115.5 1.6 %collective-permute-done.31.refs_1_ = f32[104,200]{1,0:T(8,128)S(1)} collective-permute-done((f32[104,200]{1,0:T(8,128)S(1)}, f32[104,200]{1,0:T(8,128)S(1)}, u32[]{:S(2)}, u32[]{:S(2)}) %collective-permute-start.31) | collective-permute-done | bytes 83232 | tf_op jit(solution)/shard_map/ppermute | solution.py:75
  117.2 1.3 %collective-permute-done.34.refs_2_ = f32[104,200]{1,0:T(8,128)S(1)} collective-permute-done((f32[104,200]{1,0:T(8,128)S(1)}, f32[104,200]{1,0:T(8,128)S(1)}, u32[]{:S(2)}, u32[]{:S(2)}) %collective-permute-start.34) | collective-permute-done | bytes 83232 | tf_op jit(solution)/shard_map/ppermute | solution.py:75
  118.5 0.9 shard_map.92.refs_7_.refs_1_
  119.6 2.3 %collective-permute-done.35.refs_6_ = f32[96,640]{1,0:T(8,128)S(1)} collective-permute-done((f32[96,640]{1,0:T(8,128)S(1)}, f32[96,640]{1,0:T(8,128)S(1)}, u32[]{:S(2)}, u32[]{:S(2)}) %collective-permute-start.35) | collective-permute-done | bytes 245792 | tf_op jit(solution)/shard_map/ppermute | solution.py:75
  121.9 0.8 shard_map.93.refs_2_.refs_5_
  122.8 0.9 copy.5
  123.7 0.6 collective-permute-done.37.refs_4_
  124.3 0.6 shard_map.94
  124.9 1.0 copy.6
  (64 shorter events, 6.8 us)
Async XLA Ops:
  0.7 1.2 copy-start
  1.9 9.2 %copy-start.1 = (f32[1024,200]{0,1:T(8,128)S(1)}, f32[1024,200]{0,1:T(8,128)}, u32[]{:S(2)}) copy-start(f32[1024,200]{0,1:T(8,128)} %param.4) | copy-start | bytes 2457604
  6.0 11.5 %collective-permute-start.3 = (f32[104,512]{1,0:T(8,128)S(1)}, f32[104,512]{1,0:T(8,128)S(1)}, u32[]{:S(2)}, u32[]{:S(2)}) collective-permute-start(f32[104,512]{1,0:T(8,128)S(1)} %get-tuple-element.33), channel_id=1, source_target_pairs={{0,1},{1,0},{2,3},{3,2},{4,5},{5,4},{6,7},{7,6},{8,9},{9,8},{10,11... | collective-permute-start | bytes 638984 | tf_op jit(solution)/shard_map/ppermute | solution.py:75
  9.1 8.4 %collective-permute-start = (f32[104,200]{1,0:T(8,128)S(1)}, f32[104,200]{1,0:T(8,128)S(1)}, u32[]{:S(2)}, u32[]{:S(2)}) collective-permute-start(f32[104,200]{1,0:T(8,128)S(1)} %get-tuple-element.25.refs_7_.refs_0_), channel_id=1, source_target_pairs={{0,1},{1,0},{2,3},{3,2},{4,5},{5,4},{6,7},{7,6},{8,9},{9,8},{10,11... | collective-permute-start | bytes 249608 | tf_op jit(solution)/shard_map/ppermute | solution.py:75
  9.2 12.6 %collective-permute-start.2 = (f32[96,512]{1,0:T(8,128)S(1)}, f32[96,512]{1,0:T(8,128)S(1)}, u32[]{:S(2)}, u32[]{:S(2)}) collective-permute-start(f32[96,512]{1,0:T(8,128)S(1)} %get-tuple-element.32), channel_id=1, source_target_pairs={{0,1},{1,0},{2,3},{3,2},{4,5},{5,4},{6,7},{7,6},{8,9},{9,8},{10,11... | collective-permute-start | bytes 589832 | tf_op jit(solution)/shard_map/ppermute | solution.py:75
  17.5 14.1 %collective-permute-start.5 = (f32[104,512]{1,0:T(8,128)S(1)}, f32[104,512]{1,0:T(8,128)S(1)}, u32[]{:S(2)}, u32[]{:S(2)}) collective-permute-start(f32[104,512]{1,0:T(8,128)S(1)} %shard_map.53.refs_2_.refs_5_), channel_id=1, source_target_pairs={{0,3},{1,2},{2,1},{3,0},{4,7},{5,6},{6,5},{7,4},{8,11},{9,10},{10,... | collective-permute-start | bytes 638984 | tf_op jit(solution)/shard_map/ppermute | solution.py:75
  21.7 8.3 %collective-permute-start.1 = (f32[104,200]{1,0:T(8,128)S(1)}, f32[104,200]{1,0:T(8,128)S(1)}, u32[]{:S(2)}, u32[]{:S(2)}) collective-permute-start(f32[104,200]{1,0:T(8,128)S(1)} %shard_map.52.refs_2_.refs_0_), channel_id=1, source_target_pairs={{0,3},{1,2},{2,1},{3,0},{4,7},{5,6},{6,5},{7,4},{8,11},{9,10},{10,... | collective-permute-start | bytes 249608 | tf_op jit(solution)/shard_map/ppermute | solution.py:75
  30.0 1.7 %collective-permute-start.4 = (f32[104,200]{1,0:T(8,128)S(1)}, f32[104,200]{1,0:T(8,128)S(1)}, u32[]{:S(2)}, u32[]{:S(2)}) collective-permute-start(f32[104,200]{1,0:T(8,128)S(1)} %shard_map.55.refs_1_.refs_7_), channel_id=1, source_target_pairs={{0,4},{4,0},{8,12},{12,8},{1,5},{5,1},{9,13},{13,9},{2,6},{6,2},{1... | collective-permute-start | bytes 249608 | tf_op jit(solution)/shard_map/ppermute | solution.py:75
  30.1 9.3 %collective-permute-start.6 = (f32[96,512]{1,0:T(8,128)S(1)}, f32[96,512]{1,0:T(8,128)S(1)}, u32[]{:S(2)}, u32[]{:S(2)}) collective-permute-start(f32[96,512]{1,0:T(8,128)S(1)} %shard_map.54.refs_2_.refs_5_), channel_id=1, source_target_pairs={{0,3},{1,2},{2,1},{3,0},{4,7},{5,6},{6,5},{7,4},{8,11},{9,10},{10,... | collective-permute-start | bytes 589832 | tf_op jit(solution)/shard_map/ppermute | solution.py:75
  32.5 12.4 %collective-permute-start.7 = (f32[104,512]{1,0:T(8,128)S(1)}, f32[104,512]{1,0:T(8,128)S(1)}, u32[]{:S(2)}, u32[]{:S(2)}) collective-permute-start(f32[104,512]{1,0:T(8,128)S(1)} %shard_map.56.refs_7_.refs_0_.refs_1_.refs_3_), channel_id=1, source_target_pairs={{0,1},{1,0},{2,3},{3,2},{4,5},{5,4},{6,7},{7,6},{8,9},{9,8},{10,11... | collective-permute-start | bytes 638984 | tf_op jit(solution)/shard_map/ppermute | solution.py:75
  40.2 9.8 %collective-permute-start.8 = (f32[96,512]{1,0:T(8,128)S(1)}, f32[96,512]{1,0:T(8,128)S(1)}, u32[]{:S(2)}, u32[]{:S(2)}) collective-permute-start(f32[96,512]{1,0:T(8,128)S(1)} %shard_map.57.refs_4_.refs_2_.refs_0_), channel_id=1, source_target_pairs={{0,1},{1,0},{2,3},{3,2},{4,5},{5,4},{6,7},{7,6},{8,9},{9,8},{10,11... | collective-permute-start | bytes 589832 | tf_op jit(solution)/shard_map/ppermute | solution.py:75
  45.5 1.6 %collective-permute-start.10 = (f32[56,640]{1,0:T(8,128)S(1)}, f32[56,640]{1,0:T(8,128)S(1)}, u32[]{:S(2)}, u32[]{:S(2)}) collective-permute-start(f32[56,640]{1,0:T(8,128)S(1)} %get-tuple-element.41), channel_id=1, source_target_pairs={{0,4},{4,0},{8,12},{12,8},{1,5},{5,1},{9,13},{13,9},{2,6},{6,2},{1... | collective-permute-start | bytes 430088 | tf_op jit(solution)/shard_map/ppermute | solution.py:75
  45.5 1.5 %collective-permute-start.9 = (f32[48,640]{1,0:T(8,128)S(1)}, f32[48,640]{1,0:T(8,128)S(1)}, u32[]{:S(2)}, u32[]{:S(2)}) collective-permute-start(f32[48,640]{1,0:T(8,128)S(1)} %get-tuple-element.40.refs_4_), channel_id=1, source_target_pairs={{0,4},{4,0},{8,12},{12,8},{1,5},{5,1},{9,13},{13,9},{2,6},{6,2},{1... | collective-permute-start | bytes 368648 | tf_op jit(solution)/shard_map/ppermute | solution.py:75
  47.1 8.7 %collective-permute-start.14 = (f32[104,640]{1,0:T(8,128)S(1)}, f32[104,640]{1,0:T(8,128)S(1)}, u32[]{:S(2)}, u32[]{:S(2)}) collective-permute-start(f32[104,640]{1,0:T(8,128)S(1)} %shard_map.60.refs_5_.refs_0_), channel_id=1, source_target_pairs={{0,8},{4,12},{8,0},{12,4},{1,9},{5,13},{9,1},{13,5},{2,10},{6,14},... | collective-permute-start | bytes 798728 | tf_op jit(solution)/shard_map/ppermute | solution.py:75
  51.7 4.1 %collective-permute-start.13 = (f32[96,640]{1,0:T(8,128)S(1)}, f32[96,640]{1,0:T(8,128)S(1)}, u32[]{:S(2)}, u32[]{:S(2)}) collective-permute-start(f32[96,640]{1,0:T(8,128)S(1)} %shard_map.62.refs_4_), channel_id=1, source_target_pairs={{0,4},{4,0},{8,12},{12,8},{1,5},{5,1},{9,13},{13,9},{2,6},{6,2},{1... | collective-permute-start | bytes 737288 | tf_op jit(solution)/shard_map/ppermute | solution.py:75
  51.8 1.7 %collective-permute-start.11 = (f32[104,200]{1,0:T(8,128)S(1)}, f32[104,200]{1,0:T(8,128)S(1)}, u32[]{:S(2)}, u32[]{:S(2)}) collective-permute-start(f32[104,200]{1,0:T(8,128)S(1)} %get-tuple-element.43.refs_4_), channel_id=1, source_target_pairs={{0,4},{4,0},{8,12},{12,8},{1,5},{5,1},{9,13},{13,9},{2,6},{6,2},{1... | collective-permute-start | bytes 249608 | tf_op jit(solution)/shard_map/ppermute | solution.py:75
  53.4 5.6 %collective-permute-start.12 = (f32[104,200]{1,0:T(8,128)S(1)}, f32[104,200]{1,0:T(8,128)S(1)}, u32[]{:S(2)}, u32[]{:S(2)}) collective-permute-start(f32[104,200]{1,0:T(8,128)S(1)} %shard_map.64.refs_2_.refs_0_), channel_id=1, source_target_pairs={{0,8},{4,12},{8,0},{12,4},{1,9},{5,13},{9,1},{13,5},{2,10},{6,14},... | collective-permute-start | bytes 249608 | tf_op jit(solution)/shard_map/ppermute | solution.py:75
  55.9 7.9 %collective-permute-start.16 = (f32[96,640]{1,0:T(8,128)S(1)}, f32[96,640]{1,0:T(8,128)S(1)}, u32[]{:S(2)}, u32[]{:S(2)}) collective-permute-start(f32[96,640]{1,0:T(8,128)S(1)} %shard_map.66.refs_2_.refs_5_), channel_id=1, source_target_pairs={{0,8},{4,12},{8,0},{12,4},{1,9},{5,13},{9,1},{13,5},{2,10},{6,14},... | collective-permute-start | bytes 737288 | tf_op jit(solution)/shard_map/ppermute | solution.py:75
  59.1 1.4 %collective-permute-start.15 = (f32[104,200]{1,0:T(8,128)S(1)}, f32[104,200]{1,0:T(8,128)S(1)}, u32[]{:S(2)}, u32[]{:S(2)}) collective-permute-start(f32[104,200]{1,0:T(8,128)S(1)} %shard_map.67.refs_1_.refs_6_), channel_id=1, source_target_pairs={{0,4},{4,0},{8,12},{12,8},{1,5},{5,1},{9,13},{13,9},{2,6},{6,2},{1... | collective-permute-start | bytes 249608 | tf_op jit(solution)/shard_map/ppermute | solution.py:75
  61.3 3.4 %collective-permute-start.17 = (f32[104,640]{1,0:T(8,128)S(1)}, f32[104,640]{1,0:T(8,128)S(1)}, u32[]{:S(2)}, u32[]{:S(2)}) collective-permute-start(f32[104,640]{1,0:T(8,128)S(1)} %shard_map.68.refs_7_.refs_0_.refs_1_.refs_3_), channel_id=1, source_target_pairs={{0,4},{4,0},{8,12},{12,8},{1,5},{5,1},{9,13},{13,9},{2,6},{6,2},{1... | collective-permute-start | bytes 798728 | tf_op jit(solution)/shard_map/ppermute | solution.py:75
  64.7 3.8 %collective-permute-start.18 = (f32[96,640]{1,0:T(8,128)S(1)}, f32[96,640]{1,0:T(8,128)S(1)}, u32[]{:S(2)}, u32[]{:S(2)}) collective-permute-start(f32[96,640]{1,0:T(8,128)S(1)} %shard_map.69.refs_4_.refs_2_.refs_0_), channel_id=1, source_target_pairs={{0,4},{4,0},{8,12},{12,8},{1,5},{5,1},{9,13},{13,9},{2,6},{6,2},{1... | collective-permute-start | bytes 737288 | tf_op jit(solution)/shard_map/ppermute | solution.py:75
  65.7 10.4 %collective-permute-start.22 = (f32[104,512]{1,0:T(8,128)S(1)}, f32[104,512]{1,0:T(8,128)S(1)}, u32[]{:S(2)}, u32[]{:S(2)}) collective-permute-start(f32[104,512]{1,0:T(8,128)S(1)} %shard_map.70.refs_4_), channel_id=1, source_target_pairs={{0,1},{1,0},{2,3},{3,2},{4,5},{5,4},{6,7},{7,6},{8,9},{9,8},{10,11... | collective-permute-start | bytes 638984 | tf_op jit(solution)/shard_map/ppermute | solution.py:75
  69.7 6.4 %collective-permute-start.19 = (f32[104,200]{1,0:T(8,128)S(1)}, f32[104,200]{1,0:T(8,128)S(1)}, u32[]{:S(2)}, u32[]{:S(2)}) collective-permute-start(f32[104,200]{1,0:T(8,128)S(1)} %shard_map.72.refs_4_.refs_0_), channel_id=1, source_target_pairs={{0,1},{1,0},{2,3},{3,2},{4,5},{5,4},{6,7},{7,6},{8,9},{9,8},{10,11... | collective-permute-start | bytes 249608 | tf_op jit(solution)/shard_map/ppermute | solution.py:75
  71.0 9.1 %collective-permute-start.21 = (f32[96,512]{1,0:T(8,128)S(1)}, f32[96,512]{1,0:T(8,128)S(1)}, u32[]{:S(2)}, u32[]{:S(2)}) collective-permute-start(f32[96,512]{1,0:T(8,128)S(1)} %shard_map.73.refs_4_), channel_id=1, source_target_pairs={{0,1},{1,0},{2,3},{3,2},{4,5},{5,4},{6,7},{7,6},{8,9},{9,8},{10,11... | collective-permute-start | bytes 589832 | tf_op jit(solution)/shard_map/ppermute | solution.py:75
  76.2 14.4 %collective-permute-start.24 = (f32[104,512]{1,0:T(8,128)S(1)}, f32[104,512]{1,0:T(8,128)S(1)}, u32[]{:S(2)}, u32[]{:S(2)}) collective-permute-start(f32[104,512]{1,0:T(8,128)S(1)} %shard_map.76.refs_2_.refs_5_), channel_id=1, source_target_pairs={{0,3},{1,2},{2,1},{3,0},{4,7},{5,6},{6,5},{7,4},{8,11},{9,10},{10,... | collective-permute-start | bytes 638984 | tf_op jit(solution)/shard_map/ppermute | solution.py:75
  77.7 10.4 %collective-permute-start.20 = (f32[104,200]{1,0:T(8,128)S(1)}, f32[104,200]{1,0:T(8,128)S(1)}, u32[]{:S(2)}, u32[]{:S(2)}) collective-permute-start(f32[104,200]{1,0:T(8,128)S(1)} %shard_map.75.refs_2_.refs_0_), channel_id=1, source_target_pairs={{0,3},{1,2},{2,1},{3,0},{4,7},{5,6},{6,5},{7,4},{8,11},{9,10},{10,... | collective-permute-start | bytes 249608 | tf_op jit(solution)/shard_map/ppermute | solution.py:75
  88.1 2.4 %collective-permute-start.23 = (f32[104,200]{1,0:T(8,128)S(1)}, f32[104,200]{1,0:T(8,128)S(1)}, u32[]{:S(2)}, u32[]{:S(2)}) collective-permute-start(f32[104,200]{1,0:T(8,128)S(1)} %shard_map.78.refs_1_.refs_7_), channel_id=1, source_target_pairs={{0,4},{4,0},{8,12},{12,8},{1,5},{5,1},{9,13},{13,9},{2,6},{6,2},{1... | collective-permute-start | bytes 249608 | tf_op jit(solution)/shard_map/ppermute | solution.py:75
  88.2 9.3 %collective-permute-start.25 = (f32[96,512]{1,0:T(8,128)S(1)}, f32[96,512]{1,0:T(8,128)S(1)}, u32[]{:S(2)}, u32[]{:S(2)}) collective-permute-start(f32[96,512]{1,0:T(8,128)S(1)} %shard_map.77.refs_2_.refs_5_), channel_id=1, source_target_pairs={{0,3},{1,2},{2,1},{3,0},{4,7},{5,6},{6,5},{7,4},{8,11},{9,10},{10,... | collective-permute-start | bytes 589832 | tf_op jit(solution)/shard_map/ppermute | solution.py:75
  91.4 11.6 %collective-permute-start.26 = (f32[104,512]{1,0:T(8,128)S(1)}, f32[104,512]{1,0:T(8,128)S(1)}, u32[]{:S(2)}, u32[]{:S(2)}) collective-permute-start(f32[104,512]{1,0:T(8,128)S(1)} %shard_map.79.refs_7_.refs_0_.refs_1_), channel_id=1, source_target_pairs={{0,1},{1,0},{2,3},{3,2},{4,5},{5,4},{6,7},{7,6},{8,9},{9,8},{10,11... | collective-permute-start | bytes 638984 | tf_op jit(solution)/shard_map/ppermute | solution.py:75
  98.3 9.8 %collective-permute-start.27 = (f32[96,512]{1,0:T(8,128)S(1)}, f32[96,512]{1,0:T(8,128)S(1)}, u32[]{:S(2)}, u32[]{:S(2)}) collective-permute-start(f32[96,512]{1,0:T(8,128)S(1)} %shard_map.80.refs_4_.refs_2_.refs_0_), channel_id=1, source_target_pairs={{0,1},{1,0},{2,3},{3,2},{4,5},{5,4},{6,7},{7,6},{8,9},{9,8},{10,11... | collective-permute-start | bytes 589832 | tf_op jit(solution)/shard_map/ppermute | solution.py:75
  103.5 1.6 %collective-permute-start.29 = (f32[56,640]{1,0:T(8,128)S(1)}, f32[56,640]{1,0:T(8,128)S(1)}, u32[]{:S(2)}, u32[]{:S(2)}) collective-permute-start(f32[56,640]{1,0:T(8,128)S(1)} %get-tuple-element.45), channel_id=1, source_target_pairs={{0,4},{4,0},{8,12},{12,8},{1,5},{5,1},{9,13},{13,9},{2,6},{6,2},{1... | collective-permute-start | bytes 430088 | tf_op jit(solution)/shard_map/ppermute | solution.py:75
  103.6 1.5 %collective-permute-start.28 = (f32[48,640]{1,0:T(8,128)S(1)}, f32[48,640]{1,0:T(8,128)S(1)}, u32[]{:S(2)}, u32[]{:S(2)}) collective-permute-start(f32[48,640]{1,0:T(8,128)S(1)} %get-tuple-element.44.refs_4_), channel_id=1, source_target_pairs={{0,4},{4,0},{8,12},{12,8},{1,5},{5,1},{9,13},{13,9},{2,6},{6,2},{1... | collective-permute-start | bytes 368648 | tf_op jit(solution)/shard_map/ppermute | solution.py:75
  105.2 8.7 %collective-permute-start.33 = (f32[104,640]{1,0:T(8,128)S(1)}, f32[104,640]{1,0:T(8,128)S(1)}, u32[]{:S(2)}, u32[]{:S(2)}) collective-permute-start(f32[104,640]{1,0:T(8,128)S(1)} %shard_map.83.refs_5_.refs_0_), channel_id=1, source_target_pairs={{0,8},{4,12},{8,0},{12,4},{1,9},{5,13},{9,1},{13,5},{2,10},{6,14},... | collective-permute-start | bytes 798728 | tf_op jit(solution)/shard_map/ppermute | solution.py:75
  109.8 4.1 %collective-permute-start.32 = (f32[96,640]{1,0:T(8,128)S(1)}, f32[96,640]{1,0:T(8,128)S(1)}, u32[]{:S(2)}, u32[]{:S(2)}) collective-permute-start(f32[96,640]{1,0:T(8,128)S(1)} %shard_map.85.refs_4_), channel_id=1, source_target_pairs={{0,4},{4,0},{8,12},{12,8},{1,5},{5,1},{9,13},{13,9},{2,6},{6,2},{1... | collective-permute-start | bytes 737288 | tf_op jit(solution)/shard_map/ppermute | solution.py:75
  109.8 1.7 %collective-permute-start.30 = (f32[104,200]{1,0:T(8,128)S(1)}, f32[104,200]{1,0:T(8,128)S(1)}, u32[]{:S(2)}, u32[]{:S(2)}) collective-permute-start(f32[104,200]{1,0:T(8,128)S(1)} %get-tuple-element.46.refs_4_), channel_id=1, source_target_pairs={{0,4},{4,0},{8,12},{12,8},{1,5},{5,1},{9,13},{13,9},{2,6},{6,2},{1... | collective-permute-start | bytes 249608 | tf_op jit(solution)/shard_map/ppermute | solution.py:75
  111.6 5.6 %collective-permute-start.31 = (f32[104,200]{1,0:T(8,128)S(1)}, f32[104,200]{1,0:T(8,128)S(1)}, u32[]{:S(2)}, u32[]{:S(2)}) collective-permute-start(f32[104,200]{1,0:T(8,128)S(1)} %shard_map.88.refs_2_.refs_0_), channel_id=1, source_target_pairs={{0,8},{4,12},{8,0},{12,4},{1,9},{5,13},{9,1},{13,5},{2,10},{6,14},... | collective-permute-start | bytes 249608 | tf_op jit(solution)/shard_map/ppermute | solution.py:75
  113.9 7.9 %collective-permute-start.35 = (f32[96,640]{1,0:T(8,128)S(1)}, f32[96,640]{1,0:T(8,128)S(1)}, u32[]{:S(2)}, u32[]{:S(2)}) collective-permute-start(f32[96,640]{1,0:T(8,128)S(1)} %shard_map.90.refs_2_.refs_5_), channel_id=1, source_target_pairs={{0,8},{4,12},{8,0},{12,4},{1,9},{5,13},{9,1},{13,5},{2,10},{6,14},... | collective-permute-start | bytes 737288 | tf_op jit(solution)/shard_map/ppermute | solution.py:75
  117.2 1.4 %collective-permute-start.34 = (f32[104,200]{1,0:T(8,128)S(1)}, f32[104,200]{1,0:T(8,128)S(1)}, u32[]{:S(2)}, u32[]{:S(2)}) collective-permute-start(f32[104,200]{1,0:T(8,128)S(1)} %shard_map.91.refs_1_.refs_6_), channel_id=1, source_target_pairs={{0,4},{4,0},{8,12},{12,8},{1,5},{5,1},{9,13},{13,9},{2,6},{6,2},{1... | collective-permute-start | bytes 249608 | tf_op jit(solution)/shard_map/ppermute | solution.py:75
  119.4 4.3 %collective-permute-start.36 = (f32[104,640]{1,0:T(8,128)S(1)}, f32[104,640]{1,0:T(8,128)S(1)}, u32[]{:S(2)}, u32[]{:S(2)}) collective-permute-start(f32[104,640]{1,0:T(8,128)S(1)} %shard_map.92.refs_7_.refs_1_), channel_id=1, source_target_pairs={{0,4},{4,0},{8,12},{12,8},{1,5},{5,1},{9,13},{13,9},{2,6},{6,2},{1... | collective-permute-start | bytes 798728 | tf_op jit(solution)/shard_map/ppermute | solution.py:75
  122.7 1.6 %collective-permute-start.37 = (f32[96,640]{1,0:T(8,128)S(1)}, f32[96,640]{1,0:T(8,128)S(1)}, u32[]{:S(2)}, u32[]{:S(2)}) collective-permute-start(f32[96,640]{1,0:T(8,128)S(1)} %shard_map.93.refs_2_.refs_5_), channel_id=1, source_target_pairs={{0,4},{4,0},{8,12},{12,8},{1,5},{5,1},{9,13},{13,9},{2,6},{6,2},{1... | collective-permute-start | bytes 737288 | tf_op jit(solution)/shard_map/ppermute | solution.py:75

commit v5 on v4

--- a/solution.py
+++ b/solution.py
@@ -9,7 +9,6 @@
 
 ITERS = 2
 FIRST_ROWS = 104
-GRAM_AT = 1
 WEIGHT = 12
 LAST_WEIGHT = 12
 VMEM = pl.BlockSpec(memory_space=pltpu.VMEM)
@@ -197,9 +196,9 @@
         def convert(copies, swap, x_refs, buffer):
             for i, copy in enumerate(copies):
                 copy.wait()
-                at = slice(i * piece, (i + 1) * piece)
-                own, other = halves(buffer[i].astype(F32), swap, columns)
-                x_refs[0][at, :], x_refs[1][at, :] = own.astype(BF16), other.astype(BF16)
+                for x_ref, start in zip(x_refs, (swap * columns, (1 - swap) * columns)):
+                    part = buffer[i, :, pl.ds(pl.multiple_of(start, 128), columns)]
+                    x_ref[i * piece : (i + 1) * piece, :] = part.astype(F32).astype(BF16)
 
         def prepare(where_ref, p_ref, counts_ref, g_ref, s0, s1, a0, a1, b0, b1, x0, x1, p, buffer, p_sem, sems):
             copy = pltpu.make_async_copy(p_ref, p, p_sem)
@@ -210,7 +209,7 @@
             for part, refs in ((own, (a0, a1)), (other, (b0, b1))):
                 refs[0][...], refs[1][...] = part[: sizes[0]], part[sizes[0] :]
             g_ref[...] = share(whole_gram([own, other]), where_ref[0] == 0)
-            convert(copies, where_ref[0] == 1, (x0, x1), buffer)
+            convert(copies, where_ref[0], (x0, x1), buffer)
             s = dot2(own, x0[...], 1, 1) + dot2(other, x1[...], 1, 1)
             s0[...], s1[...] = s[: sizes[0]], s[sizes[0] :]
 
@@ -218,7 +217,7 @@
             copies = load(where_ref[1] * rows, counts_ref, buffer, sems)
             mine, _ = halves(u_ref[...], where_ref[1] == 1, rows)
             u0[...], u1[...] = mine[: sizes[0]], mine[sizes[0] :]
-            convert(copies, where_ref[0] == 1, (x0, x1), buffer)
+            convert(copies, where_ref[0], (x0, x1), buffer)
             keep = dot2(stacked((a0, a1)), x0[...], 1, 1) + dot2(stacked((b0, b1)), x1[...], 1, 1)
             k0[...], k1[...] = keep[: sizes[0]], keep[sizes[0] :]
 
@@ -230,7 +229,7 @@
             prepare,
             [(grows, k)] + [(n, rows) for n in sizes] + [(n, columns) for n in sizes] * 2 + half_x,
             where,
-            program_init,
+            pltpu.with_memory_space_constraint(program_init, pltpu.HBM),
             pltpu.with_memory_space_constraint(counts, pltpu.HBM),
             flops=flops,
             any_args=(1, 2),
@@ -276,14 +275,13 @@
 
     for iteration in range(ITERS):
         if iteration:
-            nears, keeps = [], []
-            for i in range(2):
-                a, b = program_own[i : i + 1], program_other[i : i + 1]
-                if i == GRAM_AT:
-                    gram_p = gram(program_own, program_other, False)[0]
-                    gram_near = exchange(gram_p, "gene", genes, 1)
-                nears.append(exchange(product(a, b, *x[1], 1), "gene", genes, 1))
-                keeps.append(product(a, b, *x[0], 1))
+            a, b = program_own, program_other
+            nears = [exchange(product(a[:1], b[:1], *x[1], 1), "gene", genes, 1)]
+            keeps = [product(a[:1], b[:1], *x[0], 1)]
+            gram_p = gram(a, b, False)[0]
+            gram_near = exchange(gram_p, "gene", genes, 1)
+            nears.append(exchange(product(a[1:], b[1:], *x[1], 1), "gene", genes, 1))
+            keeps.append(product(a[1:], b[1:], *x[0], 1))
         gram_top = far(add(gram_p, gram_near), "gene", genes, True)
         tops = [far(add(keep, near), "gene", genes, True) for keep, near in zip(keeps, nears)]
         mine = add(*gram_top)
@@ -312,8 +310,9 @@
         mine = add(*gram_top)
         theirs = exchange(mine, "cell", cells, 1)
         new, other = [], []
+        last = iteration == ITERS - 1
         for i in range(2):
-            new.append(update(i, mine, theirs, program_own, tops[i], weight=LAST_WEIGHT if i == 0 and iteration == ITERS - 1 else 1))
+            new.append(update(i, mine, theirs, program_own, tops[i], weight=LAST_WEIGHT if last and i == 0 else 1))
             other.append(exchange(new[i], "cell", cells, 1))
         program_own, program_other = new, other
 

time: 126 us -> 125 us (level)
    unnamed x6 -> x4, local copies, waits for them, and re-layouts: 3.07 us -> 1.86 us
where the time goes in v5:
time: 125 us
  starting transfers between devices  51.2 us (41%)
  waiting for transfers between devices  43 us (34%)
  Pallas kernels  27.9 us (22%)
  local copies, waits for them, and re-layouts  1.86 us (1%)
    ppermute x38, starting transfers between devices, exchange(): return lax.ppermute(a, axis, [(i, i ^ flip) for i in range(size)])  51.2 us
    ppermute x38, waiting for transfers between devices, exchange(): return lax.ppermute(a, axis, [(i, i ^ flip) for i in range(size)])  43 us
    pallas_call x45, Pallas kernels, __call__(): pl.pallas_call(run, out_shape=[pltpu.VMEM(s.shape, s.dtype) for s in shap...  27.9 us
  transfers between devices with their start and end apart: 38, of which 20 were waited for; matrix products, arithmetic and copies ran while one was open for 1% of the time, Pallas kernels for 18%

profile of v5, /device:TPU:0, one launch (start us, length us, event | category | flops | bytes accessed | tf_op | source)
XLA Modules:
  0.0 125.1 jit_solution(7143200205768484710)
XLA Ops:
  0.7 4.5 %shard_map.50 = (f32[104,200]{1,0:T(8,128)S(1)}, f32[104,512]{1,0:T(8,128)S(1)}, f32[96,512]{1,0:T(8,128)S(1)}, f32[104,640]{1,0:T(8,128)S(1)}, f32[96,640]{1,0:...) custom-call(s32[2]{0:T(128)S(1)} %pad_add_fusion.refs_0_, ...), custom_call_target="tpu_custom_call" | custom-call | flops 524288000 | bytes 10405128 | tf_op jit(solution)/shard_map/pallas_call | solution.py:60
  5.3 3.1 %collective-permute-start.3 = (f32[104,512]{1,0:T(8,128)S(1)}, f32[104,512]{1,0:T(8,128)S(1)}, u32[]{:S(2)}, u32[]{:S(2)}) collective-permute-start(f32[104,512]{1,0:T(8,128)S(1)} %get-tuple-element.33), channel_id=1, source_target_pairs={{0,1},{1,0},{2,3},{3,2},{4,5},{5,4},{6,7},{7,6},{8,9},{9,8},{10,11... | collective-permute-start | bytes 638984 | tf_op jit(solution)/shard_map/ppermute | solution.py:74
  8.5 1.9 %collective-permute-start.2 = (f32[96,512]{1,0:T(8,128)S(1)}, f32[96,512]{1,0:T(8,128)S(1)}, u32[]{:S(2)}, u32[]{:S(2)}) collective-permute-start(f32[96,512]{1,0:T(8,128)S(1)} %get-tuple-element.32), channel_id=1, source_target_pairs={{0,1},{1,0},{2,3},{3,2},{4,5},{5,4},{6,7},{7,6},{8,9},{9,8},{10,11... | collective-permute-start | bytes 589832 | tf_op jit(solution)/shard_map/ppermute | solution.py:74
  10.4 3.3 %shard_map.51 = (f32[104,512]{1,0:T(8,128)S(1)}, f32[96,512]{1,0:T(8,128)S(1)}, bf16[512,640]{1,0:T(8,128)(2,1)S(1)}, bf16[512,640]{1,0:T(8,128)(2,1)S(1)}, f32[...) custom-call(s32[2]{0:T(128)S(1)} %pad_add_fusion.refs_0_, s32[1024,1280]{1,0:T(8,128)} %refs_1_.3, ...), custom_call_target="tpu_custom_call" | custom-call | flops 524288000 | bytes 10526728 | tf_op jit(solution)/shard_map/pallas_call | solution.py:60
  13.7 3.0 %collective-permute-done.refs_1_ = f32[104,200]{1,0:T(8,128)S(1)} collective-permute-done((f32[104,200]{1,0:T(8,128)S(1)}, f32[104,200]{1,0:T(8,128)S(1)}, u32[]{:S(2)}, u32[]{:S(2)}) %collective-permute-start) | collective-permute-done | bytes 83232 | tf_op jit(solution)/shard_map/ppermute | solution.py:74
  16.8 4.1 %collective-permute-start.5 = (f32[104,512]{1,0:T(8,128)S(1)}, f32[104,512]{1,0:T(8,128)S(1)}, u32[]{:S(2)}, u32[]{:S(2)}) collective-permute-start(f32[104,512]{1,0:T(8,128)S(1)} %shard_map.53.refs_2_.refs_5_), channel_id=1, source_target_pairs={{0,3},{1,2},{2,1},{3,0},{4,7},{5,6},{6,5},{7,4},{8,11},{9,10},{10,... | collective-permute-start | bytes 638984 | tf_op jit(solution)/shard_map/ppermute | solution.py:74
  21.1 8.2 %collective-permute-done.1.refs_1_ = f32[104,200]{1,0:T(8,128)S(1)} collective-permute-done((f32[104,200]{1,0:T(8,128)S(1)}, f32[104,200]{1,0:T(8,128)S(1)}, u32[]{:S(2)}, u32[]{:S(2)}) %collective-permute-start.1) | collective-permute-done | bytes 83232 | tf_op jit(solution)/shard_map/ppermute | solution.py:74
  29.4 1.6 %collective-permute-start.6 = (f32[96,512]{1,0:T(8,128)S(1)}, f32[96,512]{1,0:T(8,128)S(1)}, u32[]{:S(2)}, u32[]{:S(2)}) collective-permute-start(f32[96,512]{1,0:T(8,128)S(1)} %shard_map.54.refs_2_.refs_5_), channel_id=1, source_target_pairs={{0,3},{1,2},{2,1},{3,0},{4,7},{5,6},{6,5},{7,4},{8,11},{9,10},{10,... | collective-permute-start | bytes 589832 | tf_op jit(solution)/shard_map/ppermute | solution.py:74
  30.9 0.8 shard_map.56.refs_7_.refs_0_.refs_1_.refs_3_
  31.8 3.9 %collective-permute-start.7 = (f32[104,512]{1,0:T(8,128)S(1)}, f32[104,512]{1,0:T(8,128)S(1)}, u32[]{:S(2)}, u32[]{:S(2)}) collective-permute-start(f32[104,512]{1,0:T(8,128)S(1)} %shard_map.56.refs_7_.refs_0_.refs_1_.refs_3_), channel_id=1, source_target_pairs={{0,1},{1,0},{2,3},{3,2},{4,5},{5,4},{6,7},{7,6},{8,9},{9,8},{10,11... | collective-permute-start | bytes 638984 | tf_op jit(solution)/shard_map/ppermute | solution.py:74
  35.7 3.0 %collective-permute-done.6.refs_6_ = f32[96,512]{1,0:T(8,128)S(1)} collective-permute-done((f32[96,512]{1,0:T(8,128)S(1)}, f32[96,512]{1,0:T(8,128)S(1)}, u32[]{:S(2)}, u32[]{:S(2)}) %collective-permute-start.6) | collective-permute-done | bytes 196640 | tf_op jit(solution)/shard_map/ppermute | solution.py:74
  38.7 0.8 shard_map.57.refs_4_.refs_2_.refs_0_
  39.5 4.6 %collective-permute-start.8 = (f32[96,512]{1,0:T(8,128)S(1)}, f32[96,512]{1,0:T(8,128)S(1)}, u32[]{:S(2)}, u32[]{:S(2)}) collective-permute-start(f32[96,512]{1,0:T(8,128)S(1)} %shard_map.57.refs_4_.refs_2_.refs_0_), channel_id=1, source_target_pairs={{0,1},{1,0},{2,3},{3,2},{4,5},{5,4},{6,7},{7,6},{8,9},{9,8},{10,11... | collective-permute-start | bytes 589832 | tf_op jit(solution)/shard_map/ppermute | solution.py:74
  45.3 0.6 shard_map.59.refs_0_.refs_3_
  46.4 1.6 %collective-permute-start.14 = (f32[104,640]{1,0:T(8,128)S(1)}, f32[104,640]{1,0:T(8,128)S(1)}, u32[]{:S(2)}, u32[]{:S(2)}) collective-permute-start(f32[104,640]{1,0:T(8,128)S(1)} %shard_map.60.refs_5_.refs_0_), channel_id=1, source_target_pairs={{0,8},{4,12},{8,0},{12,4},{1,9},{5,13},{9,1},{13,5},{2,10},{6,14},... | collective-permute-start | bytes 798728 | tf_op jit(solution)/shard_map/ppermute | solution.py:74
  47.9 1.4 %collective-permute-done.8.refs_4_.refs_1_ = f32[96,512]{1,0:T(8,128)S(1)} collective-permute-done((f32[96,512]{1,0:T(8,128)S(1)}, f32[96,512]{1,0:T(8,128)S(1)}, u32[]{:S(2)}, u32[]{:S(2)}) %collective-permute-start.8) | collective-permute-done | bytes 196640 | tf_op jit(solution)/shard_map/ppermute | solution.py:74
  49.3 1.1 shard_map.61
  50.3 0.6 shard_map.62.refs_4_
  51.5 0.6 shard_map.63.refs_2_.refs_0_
  52.1 0.6 collective-permute-done.11.refs_1_
  52.7 1.6 %collective-permute-start.12 = (f32[104,200]{1,0:T(8,128)S(1)}, f32[104,200]{1,0:T(8,128)S(1)}, u32[]{:S(2)}, u32[]{:S(2)}) collective-permute-start(f32[104,200]{1,0:T(8,128)S(1)} %shard_map.64.refs_2_.refs_0_), channel_id=1, source_target_pairs={{0,8},{4,12},{8,0},{12,4},{1,9},{5,13},{9,1},{13,5},{2,10},{6,14},... | collective-permute-start | bytes 249608 | tf_op jit(solution)/shard_map/ppermute | solution.py:74
  54.3 0.8 collective-permute-done.14.refs_1_
  55.1 1.6 %collective-permute-start.16 = (f32[96,640]{1,0:T(8,128)S(1)}, f32[96,640]{1,0:T(8,128)S(1)}, u32[]{:S(2)}, u32[]{:S(2)}) collective-permute-start(f32[96,640]{1,0:T(8,128)S(1)} %shard_map.66.refs_2_.refs_5_), channel_id=1, source_target_pairs={{0,8},{4,12},{8,0},{12,4},{1,9},{5,13},{9,1},{13,5},{2,10},{6,14},... | collective-permute-start | bytes 737288 | tf_op jit(solution)/shard_map/ppermute | solution.py:74
  56.7 1.7 %collective-permute-done.12.refs_1_ = f32[104,200]{1,0:T(8,128)S(1)} collective-permute-done((f32[104,200]{1,0:T(8,128)S(1)}, f32[104,200]{1,0:T(8,128)S(1)}, u32[]{:S(2)}, u32[]{:S(2)}) %collective-permute-start.12) | collective-permute-done | bytes 83232 | tf_op jit(solution)/shard_map/ppermute | solution.py:74
  58.4 1.3 %collective-permute-done.15.refs_2_ = f32[104,200]{1,0:T(8,128)S(1)} collective-permute-done((f32[104,200]{1,0:T(8,128)S(1)}, f32[104,200]{1,0:T(8,128)S(1)}, u32[]{:S(2)}, u32[]{:S(2)}) %collective-permute-start.15) | collective-permute-done | bytes 83232 | tf_op jit(solution)/shard_map/ppermute | solution.py:74
  59.7 0.8 shard_map.68.refs_7_.refs_0_.refs_1_.refs_3_
  60.8 2.3 %collective-permute-done.16.refs_6_ = f32[96,640]{1,0:T(8,128)S(1)} collective-permute-done((f32[96,640]{1,0:T(8,128)S(1)}, f32[96,640]{1,0:T(8,128)S(1)}, u32[]{:S(2)}, u32[]{:S(2)}) %collective-permute-start.16) | collective-permute-done | bytes 245792 | tf_op jit(solution)/shard_map/ppermute | solution.py:74
  63.1 0.9 shard_map.69.refs_4_.refs_2_.refs_0_
  64.0 0.9 shard_map.70.refs_4_
  65.0 1.8 %collective-permute-start.22 = (f32[104,512]{1,0:T(8,128)S(1)}, f32[104,512]{1,0:T(8,128)S(1)}, u32[]{:S(2)}, u32[]{:S(2)}) collective-permute-start(f32[104,512]{1,0:T(8,128)S(1)} %shard_map.70.refs_4_), channel_id=1, source_target_pairs={{0,1},{1,0},{2,3},{3,2},{4,5},{5,4},{6,7},{7,6},{8,9},{9,8},{10,11... | collective-permute-start | bytes 638984 | tf_op jit(solution)/shard_map/ppermute | solution.py:74
  66.8 0.9 shard_map.71.refs_5_.refs_0_
  67.7 1.2 shard_map.72.refs_4_.refs_0_
  69.3 0.9 shard_map.73.refs_4_
  70.2 1.8 %collective-permute-start.21 = (f32[96,512]{1,0:T(8,128)S(1)}, f32[96,512]{1,0:T(8,128)S(1)}, u32[]{:S(2)}, u32[]{:S(2)}) collective-permute-start(f32[96,512]{1,0:T(8,128)S(1)} %shard_map.73.refs_4_), channel_id=1, source_target_pairs={{0,1},{1,0},{2,3},{3,2},{4,5},{5,4},{6,7},{7,6},{8,9},{9,8},{10,11... | collective-permute-start | bytes 589832 | tf_op jit(solution)/shard_map/ppermute | solution.py:74
  72.0 0.9 shard_map.74.refs_2_.refs_0_
  73.0 2.4 %collective-permute-done.19.refs_1_ = f32[104,200]{1,0:T(8,128)S(1)} collective-permute-done((f32[104,200]{1,0:T(8,128)S(1)}, f32[104,200]{1,0:T(8,128)S(1)}, u32[]{:S(2)}, u32[]{:S(2)}) %collective-permute-start.19) | collective-permute-done | bytes 83232 | tf_op jit(solution)/shard_map/ppermute | solution.py:74
  75.4 1.6 %collective-permute-start.24 = (f32[104,512]{1,0:T(8,128)S(1)}, f32[104,512]{1,0:T(8,128)S(1)}, u32[]{:S(2)}, u32[]{:S(2)}) collective-permute-start(f32[104,512]{1,0:T(8,128)S(1)} %shard_map.76.refs_2_.refs_5_), channel_id=1, source_target_pairs={{0,3},{1,2},{2,1},{3,0},{4,7},{5,6},{6,5},{7,4},{8,11},{9,10},{10,... | collective-permute-start | bytes 638984 | tf_op jit(solution)/shard_map/ppermute | solution.py:74
  77.0 2.3 %collective-permute-start.20 = (f32[104,200]{1,0:T(8,128)S(1)}, f32[104,200]{1,0:T(8,128)S(1)}, u32[]{:S(2)}, u32[]{:S(2)}) collective-permute-start(f32[104,200]{1,0:T(8,128)S(1)} %shard_map.75.refs_2_.refs_0_), channel_id=1, source_target_pairs={{0,3},{1,2},{2,1},{3,0},{4,7},{5,6},{6,5},{7,4},{8,11},{9,10},{10,... | collective-permute-start | bytes 249608 | tf_op jit(solution)/shard_map/ppermute | solution.py:74
  79.3 8.0 %collective-permute-done.20.refs_1_ = f32[104,200]{1,0:T(8,128)S(1)} collective-permute-done((f32[104,200]{1,0:T(8,128)S(1)}, f32[104,200]{1,0:T(8,128)S(1)}, u32[]{:S(2)}, u32[]{:S(2)}) %collective-permute-start.20) | collective-permute-done | bytes 83232 | tf_op jit(solution)/shard_map/ppermute | solution.py:74
  87.4 2.4 %collective-permute-start.25 = (f32[96,512]{1,0:T(8,128)S(1)}, f32[96,512]{1,0:T(8,128)S(1)}, u32[]{:S(2)}, u32[]{:S(2)}) collective-permute-start(f32[96,512]{1,0:T(8,128)S(1)} %shard_map.77.refs_2_.refs_5_), channel_id=1, source_target_pairs={{0,3},{1,2},{2,1},{3,0},{4,7},{5,6},{6,5},{7,4},{8,11},{9,10},{10,... | collective-permute-start | bytes 589832 | tf_op jit(solution)/shard_map/ppermute | solution.py:74
  89.8 0.8 shard_map.79.refs_7_.refs_0_.refs_1_
  90.6 4.5 %collective-permute-start.26 = (f32[104,512]{1,0:T(8,128)S(1)}, f32[104,512]{1,0:T(8,128)S(1)}, u32[]{:S(2)}, u32[]{:S(2)}) collective-permute-start(f32[104,512]{1,0:T(8,128)S(1)} %shard_map.79.refs_7_.refs_0_.refs_1_), channel_id=1, source_target_pairs={{0,1},{1,0},{2,3},{3,2},{4,5},{5,4},{6,7},{7,6},{8,9},{9,8},{10,11... | collective-permute-start | bytes 638984 | tf_op jit(solution)/shard_map/ppermute | solution.py:74
  95.1 1.6 %collective-permute-done.25.refs_6_ = f32[96,512]{1,0:T(8,128)S(1)} collective-permute-done((f32[96,512]{1,0:T(8,128)S(1)}, f32[96,512]{1,0:T(8,128)S(1)}, u32[]{:S(2)}, u32[]{:S(2)}) %collective-permute-start.25) | collective-permute-done | bytes 196640 | tf_op jit(solution)/shard_map/ppermute | solution.py:74
  96.7 0.8 shard_map.80.refs_4_.refs_2_.refs_0_
  97.5 4.7 %collective-permute-start.27 = (f32[96,512]{1,0:T(8,128)S(1)}, f32[96,512]{1,0:T(8,128)S(1)}, u32[]{:S(2)}, u32[]{:S(2)}) collective-permute-start(f32[96,512]{1,0:T(8,128)S(1)} %shard_map.80.refs_4_.refs_2_.refs_0_), channel_id=1, source_target_pairs={{0,1},{1,0},{2,3},{3,2},{4,5},{5,4},{6,7},{7,6},{8,9},{9,8},{10,11... | collective-permute-start | bytes 589832 | tf_op jit(solution)/shard_map/ppermute | solution.py:74
  103.4 0.6 shard_map.82.refs_0_.refs_3_
  104.4 1.6 %collective-permute-start.33 = (f32[104,640]{1,0:T(8,128)S(1)}, f32[104,640]{1,0:T(8,128)S(1)}, u32[]{:S(2)}, u32[]{:S(2)}) collective-permute-start(f32[104,640]{1,0:T(8,128)S(1)} %shard_map.83.refs_5_.refs_0_), channel_id=1, source_target_pairs={{0,8},{4,12},{8,0},{12,4},{1,9},{5,13},{9,1},{13,5},{2,10},{6,14},... | collective-permute-start | bytes 798728 | tf_op jit(solution)/shard_map/ppermute | solution.py:74
  106.0 1.4 %collective-permute-done.27.refs_4_.refs_1_ = f32[96,512]{1,0:T(8,128)S(1)} collective-permute-done((f32[96,512]{1,0:T(8,128)S(1)}, f32[96,512]{1,0:T(8,128)S(1)}, u32[]{:S(2)}, u32[]{:S(2)}) %collective-permute-start.27) | collective-permute-done | bytes 196640 | tf_op jit(solution)/shard_map/ppermute | solution.py:74
  107.3 1.1 shard_map.84
  108.4 0.6 shard_map.85.refs_4_
  109.6 0.6 shard_map.86.refs_5_.refs_0_
  110.2 0.6 shard_map.87.refs_2_
  110.8 1.6 %collective-permute-start.31 = (f32[104,200]{1,0:T(8,128)S(1)}, f32[104,200]{1,0:T(8,128)S(1)}, u32[]{:S(2)}, u32[]{:S(2)}) collective-permute-start(f32[104,200]{1,0:T(8,128)S(1)} %shard_map.88.refs_2_.refs_0_), channel_id=1, source_target_pairs={{0,8},{4,12},{8,0},{12,4},{1,9},{5,13},{9,1},{13,5},{2,10},{6,14},... | collective-permute-start | bytes 249608 | tf_op jit(solution)/shard_map/ppermute | solution.py:74
  112.4 0.7 collective-permute-done.33.refs_1_
  113.2 1.6 %collective-permute-start.35 = (f32[96,640]{1,0:T(8,128)S(1)}, f32[96,640]{1,0:T(8,128)S(1)}, u32[]{:S(2)}, u32[]{:S(2)}) collective-permute-start(f32[96,640]{1,0:T(8,128)S(1)} %shard_map.90.refs_2_.refs_5_), channel_id=1, source_target_pairs={{0,8},{4,12},{8,0},{12,4},{1,9},{5,13},{9,1},{13,5},{2,10},{6,14},... | collective-permute-start | bytes 737288 | tf_op jit(solution)/shard_map/ppermute | solution.py:74
  114.7 1.6 %collective-permute-done.31.refs_1_ = f32[104,200]{1,0:T(8,128)S(1)} collective-permute-done((f32[104,200]{1,0:T(8,128)S(1)}, f32[104,200]{1,0:T(8,128)S(1)}, u32[]{:S(2)}, u32[]{:S(2)}) %collective-permute-start.31) | collective-permute-done | bytes 83232 | tf_op jit(solution)/shard_map/ppermute | solution.py:74
  116.5 1.3 %collective-permute-done.34.refs_2_ = f32[104,200]{1,0:T(8,128)S(1)} collective-permute-done((f32[104,200]{1,0:T(8,128)S(1)}, f32[104,200]{1,0:T(8,128)S(1)}, u32[]{:S(2)}, u32[]{:S(2)}) %collective-permute-start.34) | collective-permute-done | bytes 83232 | tf_op jit(solution)/shard_map/ppermute | solution.py:74
  117.8 0.9 shard_map.92.refs_7_.refs_1_
  118.8 2.3 %collective-permute-done.35.refs_6_ = f32[96,640]{1,0:T(8,128)S(1)} collective-permute-done((f32[96,640]{1,0:T(8,128)S(1)}, f32[96,640]{1,0:T(8,128)S(1)}, u32[]{:S(2)}, u32[]{:S(2)}) %collective-permute-start.35) | collective-permute-done | bytes 245792 | tf_op jit(solution)/shard_map/ppermute | solution.py:74
  121.1 0.8 shard_map.93.refs_2_.refs_5_
  122.0 0.9 copy.5
  122.9 0.6 collective-permute-done.37.refs_4_
  123.5 0.6 shard_map.94
  124.2 1.0 copy.6
  (62 shorter events, 6.3 us)
Async XLA Ops:
  0.6 9.8 %copy-start = (f32[1024,200]{0,1:T(8,128)S(1)}, f32[1024,200]{0,1:T(8,128)}, u32[]{:S(2)}) copy-start(f32[1024,200]{0,1:T(8,128)} %param.4) | copy-start | bytes 2457604
  5.3 11.5 %collective-permute-start.3 = (f32[104,512]{1,0:T(8,128)S(1)}, f32[104,512]{1,0:T(8,128)S(1)}, u32[]{:S(2)}, u32[]{:S(2)}) collective-permute-start(f32[104,512]{1,0:T(8,128)S(1)} %get-tuple-element.33), channel_id=1, source_target_pairs={{0,1},{1,0},{2,3},{3,2},{4,5},{5,4},{6,7},{7,6},{8,9},{9,8},{10,11... | collective-permute-start | bytes 638984 | tf_op jit(solution)/shard_map/ppermute | solution.py:74
  8.4 8.4 %collective-permute-start = (f32[104,200]{1,0:T(8,128)S(1)}, f32[104,200]{1,0:T(8,128)S(1)}, u32[]{:S(2)}, u32[]{:S(2)}) collective-permute-start(f32[104,200]{1,0:T(8,128)S(1)} %get-tuple-element.25.refs_7_.refs_0_), channel_id=1, source_target_pairs={{0,1},{1,0},{2,3},{3,2},{4,5},{5,4},{6,7},{7,6},{8,9},{9,8},{10,11... | collective-permute-start | bytes 249608 | tf_op jit(solution)/shard_map/ppermute | solution.py:74
  8.5 12.6 %collective-permute-start.2 = (f32[96,512]{1,0:T(8,128)S(1)}, f32[96,512]{1,0:T(8,128)S(1)}, u32[]{:S(2)}, u32[]{:S(2)}) collective-permute-start(f32[96,512]{1,0:T(8,128)S(1)} %get-tuple-element.32), channel_id=1, source_target_pairs={{0,1},{1,0},{2,3},{3,2},{4,5},{5,4},{6,7},{7,6},{8,9},{9,8},{10,11... | collective-permute-start | bytes 589832 | tf_op jit(solution)/shard_map/ppermute | solution.py:74
  16.8 14.1 %collective-permute-start.5 = (f32[104,512]{1,0:T(8,128)S(1)}, f32[104,512]{1,0:T(8,128)S(1)}, u32[]{:S(2)}, u32[]{:S(2)}) collective-permute-start(f32[104,512]{1,0:T(8,128)S(1)} %shard_map.53.refs_2_.refs_5_), channel_id=1, source_target_pairs={{0,3},{1,2},{2,1},{3,0},{4,7},{5,6},{6,5},{7,4},{8,11},{9,10},{10,... | collective-permute-start | bytes 638984 | tf_op jit(solution)/shard_map/ppermute | solution.py:74
  20.9 8.3 %collective-permute-start.1 = (f32[104,200]{1,0:T(8,128)S(1)}, f32[104,200]{1,0:T(8,128)S(1)}, u32[]{:S(2)}, u32[]{:S(2)}) collective-permute-start(f32[104,200]{1,0:T(8,128)S(1)} %shard_map.52.refs_2_.refs_0_), channel_id=1, source_target_pairs={{0,3},{1,2},{2,1},{3,0},{4,7},{5,6},{6,5},{7,4},{8,11},{9,10},{10,... | collective-permute-start | bytes 249608 | tf_op jit(solution)/shard_map/ppermute | solution.py:74
  29.3 1.7 %collective-permute-start.4 = (f32[104,200]{1,0:T(8,128)S(1)}, f32[104,200]{1,0:T(8,128)S(1)}, u32[]{:S(2)}, u32[]{:S(2)}) collective-permute-start(f32[104,200]{1,0:T(8,128)S(1)} %shard_map.55.refs_1_.refs_7_), channel_id=1, source_target_pairs={{0,4},{4,0},{8,12},{12,8},{1,5},{5,1},{9,13},{13,9},{2,6},{6,2},{1... | collective-permute-start | bytes 249608 | tf_op jit(solution)/shard_map/ppermute | solution.py:74
  29.4 9.3 %collective-permute-start.6 = (f32[96,512]{1,0:T(8,128)S(1)}, f32[96,512]{1,0:T(8,128)S(1)}, u32[]{:S(2)}, u32[]{:S(2)}) collective-permute-start(f32[96,512]{1,0:T(8,128)S(1)} %shard_map.54.refs_2_.refs_5_), channel_id=1, source_target_pairs={{0,3},{1,2},{2,1},{3,0},{4,7},{5,6},{6,5},{7,4},{8,11},{9,10},{10,... | collective-permute-start | bytes 589832 | tf_op jit(solution)/shard_map/ppermute | solution.py:74
  31.8 12.4 %collective-permute-start.7 = (f32[104,512]{1,0:T(8,128)S(1)}, f32[104,512]{1,0:T(8,128)S(1)}, u32[]{:S(2)}, u32[]{:S(2)}) collective-permute-start(f32[104,512]{1,0:T(8,128)S(1)} %shard_map.56.refs_7_.refs_0_.refs_1_.refs_3_), channel_id=1, source_target_pairs={{0,1},{1,0},{2,3},{3,2},{4,5},{5,4},{6,7},{7,6},{8,9},{9,8},{10,11... | collective-permute-start | bytes 638984 | tf_op jit(solution)/shard_map/ppermute | solution.py:74
  39.5 9.8 %collective-permute-start.8 = (f32[96,512]{1,0:T(8,128)S(1)}, f32[96,512]{1,0:T(8,128)S(1)}, u32[]{:S(2)}, u32[]{:S(2)}) collective-permute-start(f32[96,512]{1,0:T(8,128)S(1)} %shard_map.57.refs_4_.refs_2_.refs_0_), channel_id=1, source_target_pairs={{0,1},{1,0},{2,3},{3,2},{4,5},{5,4},{6,7},{7,6},{8,9},{9,8},{10,11... | collective-permute-start | bytes 589832 | tf_op jit(solution)/shard_map/ppermute | solution.py:74
  44.7 1.6 %collective-permute-start.10 = (f32[56,640]{1,0:T(8,128)S(1)}, f32[56,640]{1,0:T(8,128)S(1)}, u32[]{:S(2)}, u32[]{:S(2)}) collective-permute-start(f32[56,640]{1,0:T(8,128)S(1)} %get-tuple-element.41), channel_id=1, source_target_pairs={{0,4},{4,0},{8,12},{12,8},{1,5},{5,1},{9,13},{13,9},{2,6},{6,2},{1... | collective-permute-start | bytes 430088 | tf_op jit(solution)/shard_map/ppermute | solution.py:74
  44.8 1.5 %collective-permute-start.9 = (f32[48,640]{1,0:T(8,128)S(1)}, f32[48,640]{1,0:T(8,128)S(1)}, u32[]{:S(2)}, u32[]{:S(2)}) collective-permute-start(f32[48,640]{1,0:T(8,128)S(1)} %get-tuple-element.40.refs_4_), channel_id=1, source_target_pairs={{0,4},{4,0},{8,12},{12,8},{1,5},{5,1},{9,13},{13,9},{2,6},{6,2},{1... | collective-permute-start | bytes 368648 | tf_op jit(solution)/shard_map/ppermute | solution.py:74
  46.4 8.7 %collective-permute-start.14 = (f32[104,640]{1,0:T(8,128)S(1)}, f32[104,640]{1,0:T(8,128)S(1)}, u32[]{:S(2)}, u32[]{:S(2)}) collective-permute-start(f32[104,640]{1,0:T(8,128)S(1)} %shard_map.60.refs_5_.refs_0_), channel_id=1, source_target_pairs={{0,8},{4,12},{8,0},{12,4},{1,9},{5,13},{9,1},{13,5},{2,10},{6,14},... | collective-permute-start | bytes 798728 | tf_op jit(solution)/shard_map/ppermute | solution.py:74
  51.0 4.1 %collective-permute-start.13 = (f32[96,640]{1,0:T(8,128)S(1)}, f32[96,640]{1,0:T(8,128)S(1)}, u32[]{:S(2)}, u32[]{:S(2)}) collective-permute-start(f32[96,640]{1,0:T(8,128)S(1)} %shard_map.62.refs_4_), channel_id=1, source_target_pairs={{0,4},{4,0},{8,12},{12,8},{1,5},{5,1},{9,13},{13,9},{2,6},{6,2},{1... | collective-permute-start | bytes 737288 | tf_op jit(solution)/shard_map/ppermute | solution.py:74
  51.0 1.7 %collective-permute-start.11 = (f32[104,200]{1,0:T(8,128)S(1)}, f32[104,200]{1,0:T(8,128)S(1)}, u32[]{:S(2)}, u32[]{:S(2)}) collective-permute-start(f32[104,200]{1,0:T(8,128)S(1)} %get-tuple-element.43.refs_4_), channel_id=1, source_target_pairs={{0,4},{4,0},{8,12},{12,8},{1,5},{5,1},{9,13},{13,9},{2,6},{6,2},{1... | collective-permute-start | bytes 249608 | tf_op jit(solution)/shard_map/ppermute | solution.py:74
  52.7 5.6 %collective-permute-start.12 = (f32[104,200]{1,0:T(8,128)S(1)}, f32[104,200]{1,0:T(8,128)S(1)}, u32[]{:S(2)}, u32[]{:S(2)}) collective-permute-start(f32[104,200]{1,0:T(8,128)S(1)} %shard_map.64.refs_2_.refs_0_), channel_id=1, source_target_pairs={{0,8},{4,12},{8,0},{12,4},{1,9},{5,13},{9,1},{13,5},{2,10},{6,14},... | collective-permute-start | bytes 249608 | tf_op jit(solution)/shard_map/ppermute | solution.py:74
  55.1 7.9 %collective-permute-start.16 = (f32[96,640]{1,0:T(8,128)S(1)}, f32[96,640]{1,0:T(8,128)S(1)}, u32[]{:S(2)}, u32[]{:S(2)}) collective-permute-start(f32[96,640]{1,0:T(8,128)S(1)} %shard_map.66.refs_2_.refs_5_), channel_id=1, source_target_pairs={{0,8},{4,12},{8,0},{12,4},{1,9},{5,13},{9,1},{13,5},{2,10},{6,14},... | collective-permute-start | bytes 737288 | tf_op jit(solution)/shard_map/ppermute | solution.py:74
  58.3 1.4 %collective-permute-start.15 = (f32[104,200]{1,0:T(8,128)S(1)}, f32[104,200]{1,0:T(8,128)S(1)}, u32[]{:S(2)}, u32[]{:S(2)}) collective-permute-start(f32[104,200]{1,0:T(8,128)S(1)} %shard_map.67.refs_1_.refs_6_), channel_id=1, source_target_pairs={{0,4},{4,0},{8,12},{12,8},{1,5},{5,1},{9,13},{13,9},{2,6},{6,2},{1... | collective-permute-start | bytes 249608 | tf_op jit(solution)/shard_map/ppermute | solution.py:74
  60.6 3.4 %collective-permute-start.17 = (f32[104,640]{1,0:T(8,128)S(1)}, f32[104,640]{1,0:T(8,128)S(1)}, u32[]{:S(2)}, u32[]{:S(2)}) collective-permute-start(f32[104,640]{1,0:T(8,128)S(1)} %shard_map.68.refs_7_.refs_0_.refs_1_.refs_3_), channel_id=1, source_target_pairs={{0,4},{4,0},{8,12},{12,8},{1,5},{5,1},{9,13},{13,9},{2,6},{6,2},{1... | collective-permute-start | bytes 798728 | tf_op jit(solution)/shard_map/ppermute | solution.py:74
  63.9 3.8 %collective-permute-start.18 = (f32[96,640]{1,0:T(8,128)S(1)}, f32[96,640]{1,0:T(8,128)S(1)}, u32[]{:S(2)}, u32[]{:S(2)}) collective-permute-start(f32[96,640]{1,0:T(8,128)S(1)} %shard_map.69.refs_4_.refs_2_.refs_0_), channel_id=1, source_target_pairs={{0,4},{4,0},{8,12},{12,8},{1,5},{5,1},{9,13},{13,9},{2,6},{6,2},{1... | collective-permute-start | bytes 737288 | tf_op jit(solution)/shard_map/ppermute | solution.py:74
  65.0 10.4 %collective-permute-start.22 = (f32[104,512]{1,0:T(8,128)S(1)}, f32[104,512]{1,0:T(8,128)S(1)}, u32[]{:S(2)}, u32[]{:S(2)}) collective-permute-start(f32[104,512]{1,0:T(8,128)S(1)} %shard_map.70.refs_4_), channel_id=1, source_target_pairs={{0,1},{1,0},{2,3},{3,2},{4,5},{5,4},{6,7},{7,6},{8,9},{9,8},{10,11... | collective-permute-start | bytes 638984 | tf_op jit(solution)/shard_map/ppermute | solution.py:74
  68.9 6.4 %collective-permute-start.19 = (f32[104,200]{1,0:T(8,128)S(1)}, f32[104,200]{1,0:T(8,128)S(1)}, u32[]{:S(2)}, u32[]{:S(2)}) collective-permute-start(f32[104,200]{1,0:T(8,128)S(1)} %shard_map.72.refs_4_.refs_0_), channel_id=1, source_target_pairs={{0,1},{1,0},{2,3},{3,2},{4,5},{5,4},{6,7},{7,6},{8,9},{9,8},{10,11... | collective-permute-start | bytes 249608 | tf_op jit(solution)/shard_map/ppermute | solution.py:74
  70.2 9.1 %collective-permute-start.21 = (f32[96,512]{1,0:T(8,128)S(1)}, f32[96,512]{1,0:T(8,128)S(1)}, u32[]{:S(2)}, u32[]{:S(2)}) collective-permute-start(f32[96,512]{1,0:T(8,128)S(1)} %shard_map.73.refs_4_), channel_id=1, source_target_pairs={{0,1},{1,0},{2,3},{3,2},{4,5},{5,4},{6,7},{7,6},{8,9},{9,8},{10,11... | collective-permute-start | bytes 589832 | tf_op jit(solution)/shard_map/ppermute | solution.py:74
  75.4 14.4 %collective-permute-start.24 = (f32[104,512]{1,0:T(8,128)S(1)}, f32[104,512]{1,0:T(8,128)S(1)}, u32[]{:S(2)}, u32[]{:S(2)}) collective-permute-start(f32[104,512]{1,0:T(8,128)S(1)} %shard_map.76.refs_2_.refs_5_), channel_id=1, source_target_pairs={{0,3},{1,2},{2,1},{3,0},{4,7},{5,6},{6,5},{7,4},{8,11},{9,10},{10,... | collective-permute-start | bytes 638984 | tf_op jit(solution)/shard_map/ppermute | solution.py:74
  77.0 10.4 %collective-permute-start.20 = (f32[104,200]{1,0:T(8,128)S(1)}, f32[104,200]{1,0:T(8,128)S(1)}, u32[]{:S(2)}, u32[]{:S(2)}) collective-permute-start(f32[104,200]{1,0:T(8,128)S(1)} %shard_map.75.refs_2_.refs_0_), channel_id=1, source_target_pairs={{0,3},{1,2},{2,1},{3,0},{4,7},{5,6},{6,5},{7,4},{8,11},{9,10},{10,... | collective-permute-start | bytes 249608 | tf_op jit(solution)/shard_map/ppermute | solution.py:74
  87.4 2.5 %collective-permute-start.23 = (f32[104,200]{1,0:T(8,128)S(1)}, f32[104,200]{1,0:T(8,128)S(1)}, u32[]{:S(2)}, u32[]{:S(2)}) collective-permute-start(f32[104,200]{1,0:T(8,128)S(1)} %shard_map.78.refs_1_.refs_7_), channel_id=1, source_target_pairs={{0,4},{4,0},{8,12},{12,8},{1,5},{5,1},{9,13},{13,9},{2,6},{6,2},{1... | collective-permute-start | bytes 249608 | tf_op jit(solution)/shard_map/ppermute | solution.py:74
  87.4 9.3 %collective-permute-start.25 = (f32[96,512]{1,0:T(8,128)S(1)}, f32[96,512]{1,0:T(8,128)S(1)}, u32[]{:S(2)}, u32[]{:S(2)}) collective-permute-start(f32[96,512]{1,0:T(8,128)S(1)} %shard_map.77.refs_2_.refs_5_), channel_id=1, source_target_pairs={{0,3},{1,2},{2,1},{3,0},{4,7},{5,6},{6,5},{7,4},{8,11},{9,10},{10,... | collective-permute-start | bytes 589832 | tf_op jit(solution)/shard_map/ppermute | solution.py:74
  90.6 11.6 %collective-permute-start.26 = (f32[104,512]{1,0:T(8,128)S(1)}, f32[104,512]{1,0:T(8,128)S(1)}, u32[]{:S(2)}, u32[]{:S(2)}) collective-permute-start(f32[104,512]{1,0:T(8,128)S(1)} %shard_map.79.refs_7_.refs_0_.refs_1_), channel_id=1, source_target_pairs={{0,1},{1,0},{2,3},{3,2},{4,5},{5,4},{6,7},{7,6},{8,9},{9,8},{10,11... | collective-permute-start | bytes 638984 | tf_op jit(solution)/shard_map/ppermute | solution.py:74
  97.5 9.8 %collective-permute-start.27 = (f32[96,512]{1,0:T(8,128)S(1)}, f32[96,512]{1,0:T(8,128)S(1)}, u32[]{:S(2)}, u32[]{:S(2)}) collective-permute-start(f32[96,512]{1,0:T(8,128)S(1)} %shard_map.80.refs_4_.refs_2_.refs_0_), channel_id=1, source_target_pairs={{0,1},{1,0},{2,3},{3,2},{4,5},{5,4},{6,7},{7,6},{8,9},{9,8},{10,11... | collective-permute-start | bytes 589832 | tf_op jit(solution)/shard_map/ppermute | solution.py:74
  102.8 1.6 %collective-permute-start.29 = (f32[56,640]{1,0:T(8,128)S(1)}, f32[56,640]{1,0:T(8,128)S(1)}, u32[]{:S(2)}, u32[]{:S(2)}) collective-permute-start(f32[56,640]{1,0:T(8,128)S(1)} %get-tuple-element.45), channel_id=1, source_target_pairs={{0,4},{4,0},{8,12},{12,8},{1,5},{5,1},{9,13},{13,9},{2,6},{6,2},{1... | collective-permute-start | bytes 430088 | tf_op jit(solution)/shard_map/ppermute | solution.py:74
  102.9 1.5 %collective-permute-start.28 = (f32[48,640]{1,0:T(8,128)S(1)}, f32[48,640]{1,0:T(8,128)S(1)}, u32[]{:S(2)}, u32[]{:S(2)}) collective-permute-start(f32[48,640]{1,0:T(8,128)S(1)} %get-tuple-element.44.refs_4_), channel_id=1, source_target_pairs={{0,4},{4,0},{8,12},{12,8},{1,5},{5,1},{9,13},{13,9},{2,6},{6,2},{1... | collective-permute-start | bytes 368648 | tf_op jit(solution)/shard_map/ppermute | solution.py:74
  104.4 8.7 %collective-permute-start.33 = (f32[104,640]{1,0:T(8,128)S(1)}, f32[104,640]{1,0:T(8,128)S(1)}, u32[]{:S(2)}, u32[]{:S(2)}) collective-permute-start(f32[104,640]{1,0:T(8,128)S(1)} %shard_map.83.refs_5_.refs_0_), channel_id=1, source_target_pairs={{0,8},{4,12},{8,0},{12,4},{1,9},{5,13},{9,1},{13,5},{2,10},{6,14},... | collective-permute-start | bytes 798728 | tf_op jit(solution)/shard_map/ppermute | solution.py:74
  109.0 4.1 %collective-permute-start.32 = (f32[96,640]{1,0:T(8,128)S(1)}, f32[96,640]{1,0:T(8,128)S(1)}, u32[]{:S(2)}, u32[]{:S(2)}) collective-permute-start(f32[96,640]{1,0:T(8,128)S(1)} %shard_map.85.refs_4_), channel_id=1, source_target_pairs={{0,4},{4,0},{8,12},{12,8},{1,5},{5,1},{9,13},{13,9},{2,6},{6,2},{1... | collective-permute-start | bytes 737288 | tf_op jit(solution)/shard_map/ppermute | solution.py:74
  109.1 1.7 %collective-permute-start.30 = (f32[104,200]{1,0:T(8,128)S(1)}, f32[104,200]{1,0:T(8,128)S(1)}, u32[]{:S(2)}, u32[]{:S(2)}) collective-permute-start(f32[104,200]{1,0:T(8,128)S(1)} %get-tuple-element.46.refs_4_), channel_id=1, source_target_pairs={{0,4},{4,0},{8,12},{12,8},{1,5},{5,1},{9,13},{13,9},{2,6},{6,2},{1... | collective-permute-start | bytes 249608 | tf_op jit(solution)/shard_map/ppermute | solution.py:74
  110.8 5.5 %collective-permute-start.31 = (f32[104,200]{1,0:T(8,128)S(1)}, f32[104,200]{1,0:T(8,128)S(1)}, u32[]{:S(2)}, u32[]{:S(2)}) collective-permute-start(f32[104,200]{1,0:T(8,128)S(1)} %shard_map.88.refs_2_.refs_0_), channel_id=1, source_target_pairs={{0,8},{4,12},{8,0},{12,4},{1,9},{5,13},{9,1},{13,5},{2,10},{6,14},... | collective-permute-start | bytes 249608 | tf_op jit(solution)/shard_map/ppermute | solution.py:74
  113.2 7.9 %collective-permute-start.35 = (f32[96,640]{1,0:T(8,128)S(1)}, f32[96,640]{1,0:T(8,128)S(1)}, u32[]{:S(2)}, u32[]{:S(2)}) collective-permute-start(f32[96,640]{1,0:T(8,128)S(1)} %shard_map.90.refs_2_.refs_5_), channel_id=1, source_target_pairs={{0,8},{4,12},{8,0},{12,4},{1,9},{5,13},{9,1},{13,5},{2,10},{6,14},... | collective-permute-start | bytes 737288 | tf_op jit(solution)/shard_map/ppermute | solution.py:74
  116.4 1.4 %collective-permute-start.34 = (f32[104,200]{1,0:T(8,128)S(1)}, f32[104,200]{1,0:T(8,128)S(1)}, u32[]{:S(2)}, u32[]{:S(2)}) collective-permute-start(f32[104,200]{1,0:T(8,128)S(1)} %shard_map.91.refs_1_.refs_6_), channel_id=1, source_target_pairs={{0,4},{4,0},{8,12},{12,8},{1,5},{5,1},{9,13},{13,9},{2,6},{6,2},{1... | collective-permute-start | bytes 249608 | tf_op jit(solution)/shard_map/ppermute | solution.py:74
  118.6 4.3 %collective-permute-start.36 = (f32[104,640]{1,0:T(8,128)S(1)}, f32[104,640]{1,0:T(8,128)S(1)}, u32[]{:S(2)}, u32[]{:S(2)}) collective-permute-start(f32[104,640]{1,0:T(8,128)S(1)} %shard_map.92.refs_7_.refs_1_), channel_id=1, source_target_pairs={{0,4},{4,0},{8,12},{12,8},{1,5},{5,1},{9,13},{13,9},{2,6},{6,2},{1... | collective-permute-start | bytes 798728 | tf_op jit(solution)/shard_map/ppermute | solution.py:74
  122.0 1.6 %collective-permute-start.37 = (f32[96,640]{1,0:T(8,128)S(1)}, f32[96,640]{1,0:T(8,128)S(1)}, u32[]{:S(2)}, u32[]{:S(2)}) collective-permute-start(f32[96,640]{1,0:T(8,128)S(1)} %shard_map.93.refs_2_.refs_5_), channel_id=1, source_target_pairs={{0,4},{4,0},{8,12},{12,8},{1,5},{5,1},{9,13},{13,9},{2,6},{6,2},{1... | collective-permute-start | bytes 737288 | tf_op jit(solution)/shard_map/ppermute | solution.py:74

commit v6 on v4

--- a/solution.py
+++ b/solution.py
@@ -8,10 +8,10 @@
 from jax.sharding import PartitionSpec as P
 
 ITERS = 2
-FIRST_ROWS = 104
+CHUNKS = (104, 96)
+USAGE_WEIGHTS = (1, 6, 1)
 GRAM_AT = 1
-WEIGHT = 12
-LAST_WEIGHT = 12
+PROGRAM_WEIGHTS = (1, 18)
 VMEM = pl.BlockSpec(memory_space=pltpu.VMEM)
 SMEM = pl.BlockSpec(memory_space=pltpu.SMEM)
 ANY = pl.BlockSpec(memory_space=pl.ANY)
@@ -82,31 +82,50 @@
     n_cells, n_genes = counts.shape
     k = program_init.shape[0]
     rows, columns = n_cells // 2, n_genes // 2
-    grows = -(-k // 16) * 8
-    first_size = FIRST_ROWS if k > FIRST_ROWS else grows
-    sizes = [first_size, k - first_size]
+    sizes = []
+    while sum(sizes) < k:
+        sizes.append(min(CHUNKS[len(sizes)] if len(sizes) < len(CHUNKS) else k, k - sum(sizes)))
+    n_chunks = len(sizes)
+    starts = [sum(sizes[:i]) for i in range(n_chunks)]
     where = jnp.stack([core, half]).astype(jnp.int32)
     chain = Chain()
 
     def stacked(refs):
         return jnp.concatenate([r[...] for r in refs], 0)
 
-    def whole_gram(parts):
-        return sum(dot3(a, a, 1, 1) for a in parts)
-
-    def share(g, first):
-        return jnp.where(first, g[:grows], g[k - grows :])
+    lane = 128
+    packs = lane < k <= 2 * lane and k % 8 == 0
+    packed = (2 * k - lane, lane) if packs else (-(-k // 16) * 16, k)
+    grows = packed[0] // 2
+
+    def packed_gram(parts):
+        g = sum(dot3(a, a, 1, 1) for a in parts)
+        if packs:
+            corner = jnp.concatenate([g[lane:, lane:], jnp.zeros((k - lane, 2 * lane - k), F32)], 1)
+            return jnp.concatenate([g[:, :lane], corner], 0)
+        return jnp.concatenate([g, jnp.zeros((packed[0] - k, k), F32)], 0) if packed[0] > k else g
+
+    def unpacked(t):
+        if packs:
+            upper = t[lane : 2 * lane].T[:, : k - lane]
+            right = jnp.concatenate([upper, t[k:, : k - lane]], 0)
+            return jnp.concatenate([t[:k], right], 1)
+        return t[:k]
+
+    def share(t, first):
+        return jnp.where(first, t[:grows], t[grows:])
 
     def gram(factor_a, factor_b, both):
-        def kernel(where_ref, a0, a1, b0, b1, *outs):
-            g = whole_gram([stacked((a0, a1)), stacked((b0, b1))])
+        def kernel(where_ref, *refs):
+            a_refs, b_refs, outs = refs[:n_chunks], refs[n_chunks : 2 * n_chunks], refs[2 * n_chunks :]
+            t = packed_gram([stacked(a_refs), stacked(b_refs)])
             first = where_ref[0] == 0
             if both:
-                outs[0][...] = share(g, jnp.logical_not(first))
-            outs[-1][...] = share(g, first)
+                outs[0][...] = share(t, jnp.logical_not(first))
+            outs[-1][...] = share(t, first)
 
         n = factor_a[0].shape[1] + factor_b[0].shape[1]
-        return chain(kernel, [(grows, k)] * (1 + both), where, *factor_a, *factor_b, flops=6 * k * k * n)
+        return chain(kernel, [(grows, packed[1])] * (1 + both), where, *factor_a, *factor_b, flops=6 * k * k * n)
 
     def product(a, b, xa, xb, dim, cut=0):
         parts = len(a)
@@ -132,19 +151,19 @@
         return chain(kernel, [a.shape], a, *b)[0]
 
     def update(index, mine, theirs, factor, tops, weight=1):
-        first = index * sizes[0]
+        first = starts[index]
 
         def rows_of(a):
             return a if a.shape[0] == sizes[index] else a[first : first + sizes[index]]
 
-        def kernel(where_ref, m_ref, t_ref, f0, f1, *refs):
-            *top_refs, o_ref = refs
+        def kernel(where_ref, m_ref, t_ref, *refs):
+            f_refs, (*top_refs, o_ref) = refs[:n_chunks], refs[n_chunks:]
             own = where_ref[0] == 0
             upper = jnp.where(own, m_ref[...], t_ref[...])
             lower = jnp.where(own, t_ref[...], m_ref[...])
-            g = rows_of(jnp.concatenate([upper, lower[2 * grows - k :]], 0))
-            f = stacked((f0, f1))
-            part = (f0, f1)[index][...]
+            g = rows_of(unpacked(jnp.concatenate([upper, lower], 0)))
+            f = stacked(f_refs)
+            part = f_refs[index][...]
             top = sum(rows_of(ref[...]) for ref in top_refs)
             o_ref[...] = part * top / dot3(g, f, 1, 0)
 
@@ -157,11 +176,12 @@
             mine, theirs = jnp.concatenate(mine, 0), jnp.concatenate(theirs, 0)
             return jnp.concatenate([jnp.where(which == 0, mine, theirs), jnp.where(which == 0, theirs, mine)], 1)
 
-        def kernel(where_ref, m0, m1, t0, t1, o_ref):
+        def kernel(where_ref, *refs):
+            *refs, o_ref = refs
             first = where_ref[index] == 0
-            for a, b, rows_at in ((m0, t0, slice(0, sizes[0])), (m1, t1, slice(sizes[0], k))):
-                o_ref[rows_at, :size] = jnp.where(first, a[...], b[...])
-                o_ref[rows_at, size:] = jnp.where(first, b[...], a[...])
+            for a, b, start, n in zip(refs[:n_chunks], refs[n_chunks:], starts, sizes):
+                o_ref[start : start + n, :size] = jnp.where(first, a[...], b[...])
+                o_ref[start : start + n, size:] = jnp.where(first, b[...], a[...])
 
         return chain(kernel, [(k, 2 * size)], where, *mine, *theirs)[0]
 
@@ -197,51 +217,60 @@
         def convert(copies, swap, x_refs, buffer):
             for i, copy in enumerate(copies):
                 copy.wait()
-                at = slice(i * piece, (i + 1) * piece)
-                own, other = halves(buffer[i].astype(F32), swap, columns)
-                x_refs[0][at, :], x_refs[1][at, :] = own.astype(BF16), other.astype(BF16)
-
-        def prepare(where_ref, p_ref, counts_ref, g_ref, s0, s1, a0, a1, b0, b1, x0, x1, p, buffer, p_sem, sems):
+                for x_ref, start in zip(x_refs, (swap * columns, (1 - swap) * columns)):
+                    part = buffer[i, :, pl.ds(pl.multiple_of(start, 128), columns)]
+                    x_ref[i * piece : (i + 1) * piece, :] = part.astype(F32).astype(BF16)
+
+        def scatter(a, refs):
+            for start, n, ref in zip(starts, sizes, refs):
+                ref[...] = a[start : start + n]
+
+        def prepare(where_ref, p_ref, counts_ref, g_ref, *refs):
+            s_refs, a_refs, b_refs = [refs[i * n_chunks : (i + 1) * n_chunks] for i in range(3)]
+            x0, x1, p, buffer, p_sem, sems = refs[3 * n_chunks :]
             copy = pltpu.make_async_copy(p_ref, p, p_sem)
             copy.start()
             copies = load((1 - where_ref[1]) * rows, counts_ref, buffer, sems)
             copy.wait()
             own, other = halves(p[...], where_ref[0] == 1, columns)
-            for part, refs in ((own, (a0, a1)), (other, (b0, b1))):
-                refs[0][...], refs[1][...] = part[: sizes[0]], part[sizes[0] :]
-            g_ref[...] = share(whole_gram([own, other]), where_ref[0] == 0)
-            convert(copies, where_ref[0] == 1, (x0, x1), buffer)
-            s = dot2(own, x0[...], 1, 1) + dot2(other, x1[...], 1, 1)
-            s0[...], s1[...] = s[: sizes[0]], s[sizes[0] :]
-
-        def load_own(where_ref, counts_ref, a0, a1, b0, b1, u_ref, k0, k1, x0, x1, u0, u1, buffer, sems):
+            scatter(own, a_refs)
+            scatter(other, b_refs)
+            g_ref[...] = share(packed_gram([own, other]), where_ref[0] == 0)
+            convert(copies, where_ref[0], (x0, x1), buffer)
+            scatter(dot2(own, x0[...], 1, 1) + dot2(other, x1[...], 1, 1), s_refs)
+
+        def load_own(where_ref, counts_ref, *refs):
+            a_refs, b_refs = refs[:n_chunks], refs[n_chunks : 2 * n_chunks]
+            u_ref, *refs = refs[2 * n_chunks :]
+            x0, x1, *refs = refs
+            k_refs, u_refs, (buffer, sems) = refs[:n_chunks], refs[n_chunks : 2 * n_chunks], refs[2 * n_chunks :]
             copies = load(where_ref[1] * rows, counts_ref, buffer, sems)
             mine, _ = halves(u_ref[...], where_ref[1] == 1, rows)
-            u0[...], u1[...] = mine[: sizes[0]], mine[sizes[0] :]
-            convert(copies, where_ref[0] == 1, (x0, x1), buffer)
-            keep = dot2(stacked((a0, a1)), x0[...], 1, 1) + dot2(stacked((b0, b1)), x1[...], 1, 1)
-            k0[...], k1[...] = keep[: sizes[0]], keep[sizes[0] :]
+            scatter(mine, u_refs)
+            convert(copies, where_ref[0], (x0, x1), buffer)
+            scatter(dot2(stacked(a_refs), x0[...], 1, 1) + dot2(stacked(b_refs), x1[...], 1, 1), k_refs)
 
         half_x = [jax.ShapeDtypeStruct((rows, columns), BF16)] * 2
         buffer = pltpu.VMEM((pieces, piece, n_genes), jnp.int32)
         sems = pltpu.SemaphoreType.DMA((pieces,))
         flops = 4 * k * rows * n_genes
-        gram_p, s0, s1, *rest = chain(
+        gram_p, *rest = chain(
             prepare,
-            [(grows, k)] + [(n, rows) for n in sizes] + [(n, columns) for n in sizes] * 2 + half_x,
+            [(grows, packed[1])] + [(n, rows) for n in sizes] + [(n, columns) for n in sizes] * 2 + half_x,
             where,
-            program_init,
+            pltpu.with_memory_space_constraint(program_init, pltpu.HBM),
             pltpu.with_memory_space_constraint(counts, pltpu.HBM),
             flops=flops,
             any_args=(1, 2),
             scratch=[pltpu.VMEM(program_init.shape, F32), buffer, pltpu.SemaphoreType.DMA, sems],
         )
-        program_own, program_other, x_other = list(rest[:2]), list(rest[2:4]), list(rest[4:])
+        sends, program_own, program_other = [list(rest[i * n_chunks : (i + 1) * n_chunks]) for i in range(3)]
+        x_other = list(rest[3 * n_chunks :])
         gram_near = exchange(gram_p, "gene", genes, 1)
-        nears = [exchange(a, "gene", genes, 1) for a in (s0, s1)]
-        keep0, keep1, x0, x1, u0, u1 = chain(
+        nears = [exchange(a, "gene", genes, 1) for a in sends]
+        x0, x1, *rest = chain(
             load_own,
-            [(n, rows) for n in sizes] + half_x + [(n, rows) for n in sizes],
+            half_x + [(n, rows) for n in sizes] * 2,
             where,
             pltpu.with_memory_space_constraint(counts, pltpu.HBM),
             *program_own,
@@ -252,8 +281,7 @@
             scratch=[buffer, sems],
         )
         x = [[x0, x1], x_other]
-        usage_own = [u0, u1]
-        keeps = [keep0, keep1]
+        keeps, usage_own = rest[:n_chunks], rest[n_chunks:]
     else:
 
         def at(a, which, axis):
@@ -261,7 +289,7 @@
             return [lax.dynamic_slice_in_dim(a, i * size, size, axis) for i in (which, 1 - which)]
 
         def chunked(a):
-            return [a[:first_size], a[first_size:]]
+            return [a[i : i + n] for i, n in zip(starts, sizes)]
 
         x = [at(part, core, 1) for part in at(counts.astype(BF16), half, 0)]
         program_own, program_other = [chunked(a) for a in at(program_init, core, 1)]
@@ -269,15 +297,16 @@
         gram_p = gram(program_own, program_other, False)[0]
         gram_near = exchange(gram_p, "gene", genes, 1)
         nears, keeps = [], []
-        for i in range(2):
+        for i in range(n_chunks):
             a, b = program_own[i : i + 1], program_other[i : i + 1]
             nears.append(exchange(product(a, b, *x[1], 1), "gene", genes, 1))
             keeps.append(product(a, b, *x[0], 1))
 
     for iteration in range(ITERS):
+        last = iteration == ITERS - 1
         if iteration:
             nears, keeps = [], []
-            for i in range(2):
+            for i in range(n_chunks):
                 a, b = program_own[i : i + 1], program_other[i : i + 1]
                 if i == GRAM_AT:
                     gram_p = gram(program_own, program_other, False)[0]
@@ -289,31 +318,34 @@
         mine = add(*gram_top)
         theirs = exchange(mine, "cell", cells, 1)
         new, other = [], []
-        for i in range(2):
-            new.append(update(i, mine, theirs, usage_own, tops[i], weight=WEIGHT if i else 1))
+        for i in range(n_chunks):
+            new.append(update(i, mine, theirs, usage_own, tops[i], weight=USAGE_WEIGHTS[min(i, 2)]))
             other.append(exchange(new[i], "gene", genes, 1))
         usage_own, usage_other = new, other
 
-        cut = sizes[0] // 16 * 8
-        send = product(new[:1], other[:1], x[0][1], x[1][1], 0, cut)
-        sends = [[exchange(a, "cell", cells, 1) for a in send]]
-        keeps = [product(new[:1], other[:1], x[0][0], x[1][0], 0)]
-        tops = [far(add(keeps[0], *sends[0]), "cell", cells, False)]
-        gram_send, gram_keep = gram(usage_own, usage_other, True)
-        gram_near = exchange(gram_send, "cell", cells, 1)
-        send = product(new[1:], other[1:], x[0][1], x[1][1], 0)
-        sends.append(exchange(send, "cell", cells, 1))
-        keeps.append(product(new[1:], other[1:], x[0][0], x[1][0], 0))
-        if iteration == ITERS - 1:
-            usage = join(usage_own, usage_other, 1, half)
-        gram_top = far(add(gram_keep, gram_near), "cell", cells, False)
-        tops[0] = (add(*tops[0]),)
-        tops.append(far(add(keeps[1], sends[1]), "cell", cells, False))
+        tops = []
+        for i in range(n_chunks):
+            a, b = new[i : i + 1], other[i : i + 1]
+            if i < n_chunks - 1:
+                cut = sizes[i] // 16 * 8
+                send = [exchange(part, "cell", cells, 1) for part in product(a, b, x[0][1], x[1][1], 0, cut)]
+                keep = product(a, b, x[0][0], x[1][0], 0)
+                tops.append(far(add(keep, *send), "cell", cells, False))
+                continue
+            gram_send, gram_keep = gram(usage_own, usage_other, True)
+            gram_near = exchange(gram_send, "cell", cells, 1)
+            send = exchange(product(a, b, x[0][1], x[1][1], 0), "cell", cells, 1)
+            keep = product(a, b, x[0][0], x[1][0], 0)
+            if last:
+                usage = join(usage_own, usage_other, 1, half)
+            gram_top = far(add(gram_keep, gram_near), "cell", cells, False)
+            tops = [(add(*top),) for top in tops]
+            tops.append(far(add(keep, send), "cell", cells, False))
         mine = add(*gram_top)
         theirs = exchange(mine, "cell", cells, 1)
         new, other = [], []
-        for i in range(2):
-            new.append(update(i, mine, theirs, program_own, tops[i], weight=LAST_WEIGHT if i == 0 and iteration == ITERS - 1 else 1))
+        for i in range(n_chunks):
+            new.append(update(i, mine, theirs, program_own, tops[i], weight=PROGRAM_WEIGHTS[last] if i == 0 else 1))
             other.append(exchange(new[i], "cell", cells, 1))
         program_own, program_other = new, other
 

time: 126 us -> 121 us (0.960)
  waiting for transfers between devices: 43 us -> 40.7 us
  starting transfers between devices: 51.2 us -> 49 us
    ppermute x38, starting transfers between devices: 51.2 us -> 49 us  [exchange(): return lax.ppermute(a, axis, [(i, i ^ flip) for i in range(size)])]
    ppermute x38, waiting for transfers between devices: 43 us -> 40.7 us  [exchange(): return lax.ppermute(a, axis, [(i, i ^ flip) for i in range(size)])]
    unnamed x6 -> x4, local copies, waits for them, and re-layouts: 3.07 us -> 1.86 us
  transfers between devices with their start and end apart: 38 -> 38, of which waited for: 20 -> 20; matrix products, arithmetic and copies ran while one was open for 1% -> 1% of each run, Pallas kernels for 18% -> 19%
where the time goes in v6:
time: 121 us
  starting transfers between devices  49 us (40%)
  waiting for transfers between devices  40.7 us (34%)
  Pallas kernels  28.3 us (23%)
  local copies, waits for them, and re-layouts  1.86 us (2%)
    ppermute x38, starting transfers between devices, exchange(): return lax.ppermute(a, axis, [(i, i ^ flip) for i in range(size)])  49 us
    ppermute x38, waiting for transfers between devices, exchange(): return lax.ppermute(a, axis, [(i, i ^ flip) for i in range(size)])  40.7 us
    pallas_call x45, Pallas kernels, __call__(): pl.pallas_call(run, out_shape=[pltpu.VMEM(s.shape, s.dtype) for s in shap...  28.3 us
  transfers between devices with their start and end apart: 38, of which 20 were waited for; matrix products, arithmetic and copies ran while one was open for 1% of the time, Pallas kernels for 19%

profile of v6, /device:TPU:0, one launch (start us, length us, event | category | flops | bytes accessed | tf_op | source)
XLA Modules:
  0.0 120.9 jit_solution(11387279515533368980)
XLA Ops:
  0.7 4.5 %shard_map.50 = (f32[136,128]{1,0:T(8,128)S(1)}, f32[104,512]{1,0:T(8,128)S(1)}, f32[96,512]{1,0:T(8,128)S(1)}, f32[104,640]{1,0:T(8,128)S(1)}, f32[96,640]{1,0:...) custom-call(s32[2]{0:T(128)S(1)} %pad_add_fusion.refs_0_, ...), custom_call_target="tpu_custom_call" | custom-call | flops 524288000 | bytes 10391560 | tf_op jit(solution)/shard_map/pallas_call | solution.py:61
  5.3 3.1 %collective-permute-start.3 = (f32[104,512]{1,0:T(8,128)S(1)}, f32[104,512]{1,0:T(8,128)S(1)}, u32[]{:S(2)}, u32[]{:S(2)}) collective-permute-start(f32[104,512]{1,0:T(8,128)S(1)} %get-tuple-element.34), channel_id=1, source_target_pairs={{0,1},{1,0},{2,3},{3,2},{4,5},{5,4},{6,7},{7,6},{8,9},{9,8},{10,11... | collective-permute-start | bytes 638984 | tf_op jit(solution)/shard_map/ppermute | solution.py:75
  8.4 1.9 %collective-permute-start.2 = (f32[96,512]{1,0:T(8,128)S(1)}, f32[96,512]{1,0:T(8,128)S(1)}, u32[]{:S(2)}, u32[]{:S(2)}) collective-permute-start(f32[96,512]{1,0:T(8,128)S(1)} %get-tuple-element.32), channel_id=1, source_target_pairs={{0,1},{1,0},{2,3},{3,2},{4,5},{5,4},{6,7},{7,6},{8,9},{9,8},{10,11... | collective-permute-start | bytes 589832 | tf_op jit(solution)/shard_map/ppermute | solution.py:75
  10.4 3.3 %shard_map.51 = (bf16[512,640]{1,0:T(8,128)(2,1)S(1)}, bf16[512,640]{1,0:T(8,128)(2,1)S(1)}, f32[104,512]{1,0:T(8,128)S(1)}, f32[96,512]{1,0:T(8,128)S(1)}, f32[...) custom-call(s32[2]{0:T(128)S(1)} %pad_add_fusion.refs_0_, s32[1024,1280]{1,0:T(8,128)} %refs_1_.3, ...), custom_call_target="tpu_custom_call" | custom-call | flops 524288000 | bytes 10526728 | tf_op jit(solution)/shard_map/pallas_call | solution.py:61
  13.7 2.2 %collective-permute-done.refs_1_ = f32[136,128]{1,0:T(8,128)S(1)} collective-permute-done((f32[136,128]{1,0:T(8,128)S(1)}, f32[136,128]{1,0:T(8,128)S(1)}, u32[]{:S(2)}, u32[]{:S(2)}) %collective-permute-start) | collective-permute-done | bytes 69664 | tf_op jit(solution)/shard_map/ppermute | solution.py:75
  16.0 4.1 %collective-permute-start.5 = (f32[104,512]{1,0:T(8,128)S(1)}, f32[104,512]{1,0:T(8,128)S(1)}, u32[]{:S(2)}, u32[]{:S(2)}) collective-permute-start(f32[104,512]{1,0:T(8,128)S(1)} %shard_map.53.refs_2_.refs_5_), channel_id=1, source_target_pairs={{0,3},{1,2},{2,1},{3,0},{4,7},{5,6},{6,5},{7,4},{8,11},{9,10},{10,... | collective-permute-start | bytes 638984 | tf_op jit(solution)/shard_map/ppermute | solution.py:75
  20.3 7.4 %collective-permute-done.1.refs_1_ = f32[136,128]{1,0:T(8,128)S(1)} collective-permute-done((f32[136,128]{1,0:T(8,128)S(1)}, f32[136,128]{1,0:T(8,128)S(1)}, u32[]{:S(2)}, u32[]{:S(2)}) %collective-permute-start.1) | collective-permute-done | bytes 69664 | tf_op jit(solution)/shard_map/ppermute | solution.py:75
  27.8 1.6 %collective-permute-start.6 = (f32[96,512]{1,0:T(8,128)S(1)}, f32[96,512]{1,0:T(8,128)S(1)}, u32[]{:S(2)}, u32[]{:S(2)}) collective-permute-start(f32[96,512]{1,0:T(8,128)S(1)} %shard_map.54.refs_2_.refs_5_), channel_id=1, source_target_pairs={{0,3},{1,2},{2,1},{3,0},{4,7},{5,6},{6,5},{7,4},{8,11},{9,10},{10,... | collective-permute-start | bytes 589832 | tf_op jit(solution)/shard_map/ppermute | solution.py:75
  29.3 0.8 shard_map.56.refs_7_.refs_0_.refs_1_.refs_3_
  30.2 3.1 %collective-permute-start.7 = (f32[104,512]{1,0:T(8,128)S(1)}, f32[104,512]{1,0:T(8,128)S(1)}, u32[]{:S(2)}, u32[]{:S(2)}) collective-permute-start(f32[104,512]{1,0:T(8,128)S(1)} %shard_map.56.refs_7_.refs_0_.refs_1_.refs_3_), channel_id=1, source_target_pairs={{0,1},{1,0},{2,3},{3,2},{4,5},{5,4},{6,7},{7,6},{8,9},{9,8},{10,11... | collective-permute-start | bytes 638984 | tf_op jit(solution)/shard_map/ppermute | solution.py:75
  33.3 4.1 %collective-permute-done.6.refs_6_ = f32[96,512]{1,0:T(8,128)S(1)} collective-permute-done((f32[96,512]{1,0:T(8,128)S(1)}, f32[96,512]{1,0:T(8,128)S(1)}, u32[]{:S(2)}, u32[]{:S(2)}) %collective-permute-start.6) | collective-permute-done | bytes 196640 | tf_op jit(solution)/shard_map/ppermute | solution.py:75
  37.4 0.9 shard_map.57.refs_4_.refs_2_.refs_0_
  38.2 4.3 %collective-permute-start.8 = (f32[96,512]{1,0:T(8,128)S(1)}, f32[96,512]{1,0:T(8,128)S(1)}, u32[]{:S(2)}, u32[]{:S(2)}) collective-permute-start(f32[96,512]{1,0:T(8,128)S(1)} %shard_map.57.refs_4_.refs_2_.refs_0_), channel_id=1, source_target_pairs={{0,1},{1,0},{2,3},{3,2},{4,5},{5,4},{6,7},{7,6},{8,9},{9,8},{10,11... | collective-permute-start | bytes 589832 | tf_op jit(solution)/shard_map/ppermute | solution.py:75
  42.6 0.6 shard_map.58
  43.7 0.6 shard_map.59.refs_0_.refs_3_
  44.8 1.6 %collective-permute-start.14 = (f32[104,640]{1,0:T(8,128)S(1)}, f32[104,640]{1,0:T(8,128)S(1)}, u32[]{:S(2)}, u32[]{:S(2)}) collective-permute-start(f32[104,640]{1,0:T(8,128)S(1)} %shard_map.60.refs_5_.refs_0_), channel_id=1, source_target_pairs={{0,8},{4,12},{8,0},{12,4},{1,9},{5,13},{9,1},{13,5},{2,10},{6,14},... | collective-permute-start | bytes 798728 | tf_op jit(solution)/shard_map/ppermute | solution.py:75
  46.4 1.4 %collective-permute-done.8.refs_4_.refs_1_ = f32[96,512]{1,0:T(8,128)S(1)} collective-permute-done((f32[96,512]{1,0:T(8,128)S(1)}, f32[96,512]{1,0:T(8,128)S(1)}, u32[]{:S(2)}, u32[]{:S(2)}) %collective-permute-start.8) | collective-permute-done | bytes 196640 | tf_op jit(solution)/shard_map/ppermute | solution.py:75
  47.7 1.1 shard_map.61
  48.8 0.6 shard_map.62.refs_4_
  50.0 0.6 shard_map.63.refs_2_.refs_0_
  51.1 1.6 %collective-permute-start.12 = (f32[136,128]{1,0:T(8,128)S(1)}, f32[136,128]{1,0:T(8,128)S(1)}, u32[]{:S(2)}, u32[]{:S(2)}) collective-permute-start(f32[136,128]{1,0:T(8,128)S(1)} %shard_map.64.refs_2_.refs_0_), channel_id=1, source_target_pairs={{0,8},{4,12},{8,0},{12,4},{1,9},{5,13},{9,1},{13,5},{2,10},{6,14},... | collective-permute-start | bytes 208904 | tf_op jit(solution)/shard_map/ppermute | solution.py:75
  52.7 0.8 collective-permute-done.14.refs_1_
  53.6 1.6 %collective-permute-start.16 = (f32[96,640]{1,0:T(8,128)S(1)}, f32[96,640]{1,0:T(8,128)S(1)}, u32[]{:S(2)}, u32[]{:S(2)}) collective-permute-start(f32[96,640]{1,0:T(8,128)S(1)} %shard_map.66.refs_2_.refs_5_), channel_id=1, source_target_pairs={{0,8},{4,12},{8,0},{12,4},{1,9},{5,13},{9,1},{13,5},{2,10},{6,14},... | collective-permute-start | bytes 737288 | tf_op jit(solution)/shard_map/ppermute | solution.py:75
  55.6 1.2 %collective-permute-done.15.refs_2_ = f32[136,128]{1,0:T(8,128)S(1)} collective-permute-done((f32[136,128]{1,0:T(8,128)S(1)}, f32[136,128]{1,0:T(8,128)S(1)}, u32[]{:S(2)}, u32[]{:S(2)}) %collective-permute-start.15) | collective-permute-done | bytes 69664 | tf_op jit(solution)/shard_map/ppermute | solution.py:75
  56.8 0.9 shard_map.68.refs_7_.refs_0_.refs_1_.refs_3_
  57.9 3.0 %collective-permute-done.16.refs_6_ = f32[96,640]{1,0:T(8,128)S(1)} collective-permute-done((f32[96,640]{1,0:T(8,128)S(1)}, f32[96,640]{1,0:T(8,128)S(1)}, u32[]{:S(2)}, u32[]{:S(2)}) %collective-permute-start.16) | collective-permute-done | bytes 245792 | tf_op jit(solution)/shard_map/ppermute | solution.py:75
  61.0 0.9 shard_map.69.refs_4_.refs_2_.refs_0_
  62.0 0.9 shard_map.70.refs_4_
  63.0 1.5 %collective-permute-start.22 = (f32[104,512]{1,0:T(8,128)S(1)}, f32[104,512]{1,0:T(8,128)S(1)}, u32[]{:S(2)}, u32[]{:S(2)}) collective-permute-start(f32[104,512]{1,0:T(8,128)S(1)} %shard_map.70.refs_4_), channel_id=1, source_target_pairs={{0,1},{1,0},{2,3},{3,2},{4,5},{5,4},{6,7},{7,6},{8,9},{9,8},{10,11... | collective-permute-start | bytes 638984 | tf_op jit(solution)/shard_map/ppermute | solution.py:75
  64.5 0.9 shard_map.71.refs_5_.refs_0_
  65.5 1.2 %shard_map.72.refs_4_.refs_0_ = f32[136,128]{1,0:T(8,128)S(1)} custom-call(s32[2]{0:T(128)S(1)} %pad_add_fusion.refs_0_, f32[104,640]{1,0:T(8,128)S(1)} %shard_map.68.refs_7_.refs_0_.refs_1_.refs_3_, f32[96,640]{1,0:T(8,128)S(1)} %shard_map.69.refs_4_.refs_2_.refs_0_, f32[104,640]{1,0:T(8,128)S(1)} %collective-permute-done.17.refs_1_.refs_3_, ...), custom_call_target="tpu_custom_call" | custom-call | flops 307200000 | bytes 1093640 | tf_op jit(solution)/shard_map/pallas_call | solution.py:61
  66.7 0.6 collective-permute-start.19
  67.3 0.9 shard_map.73.refs_4_
  68.2 1.5 %collective-permute-start.21 = (f32[96,512]{1,0:T(8,128)S(1)}, f32[96,512]{1,0:T(8,128)S(1)}, u32[]{:S(2)}, u32[]{:S(2)}) collective-permute-start(f32[96,512]{1,0:T(8,128)S(1)} %shard_map.73.refs_4_), channel_id=1, source_target_pairs={{0,1},{1,0},{2,3},{3,2},{4,5},{5,4},{6,7},{7,6},{8,9},{9,8},{10,11... | collective-permute-start | bytes 589832 | tf_op jit(solution)/shard_map/ppermute | solution.py:75
  69.8 0.9 shard_map.74.refs_2_.refs_0_
  70.7 1.9 %collective-permute-done.19.refs_1_ = f32[136,128]{1,0:T(8,128)S(1)} collective-permute-done((f32[136,128]{1,0:T(8,128)S(1)}, f32[136,128]{1,0:T(8,128)S(1)}, u32[]{:S(2)}, u32[]{:S(2)}) %collective-permute-start.19) | collective-permute-done | bytes 69664 | tf_op jit(solution)/shard_map/ppermute | solution.py:75
  72.6 1.6 %collective-permute-start.24 = (f32[104,512]{1,0:T(8,128)S(1)}, f32[104,512]{1,0:T(8,128)S(1)}, u32[]{:S(2)}, u32[]{:S(2)}) collective-permute-start(f32[104,512]{1,0:T(8,128)S(1)} %shard_map.76.refs_2_.refs_5_), channel_id=1, source_target_pairs={{0,3},{1,2},{2,1},{3,0},{4,7},{5,6},{6,5},{7,4},{8,11},{9,10},{10,... | collective-permute-start | bytes 638984 | tf_op jit(solution)/shard_map/ppermute | solution.py:75
  74.2 2.3 %collective-permute-start.20 = (f32[136,128]{1,0:T(8,128)S(1)}, f32[136,128]{1,0:T(8,128)S(1)}, u32[]{:S(2)}, u32[]{:S(2)}) collective-permute-start(f32[136,128]{1,0:T(8,128)S(1)} %shard_map.75.refs_2_.refs_0_), channel_id=1, source_target_pairs={{0,3},{1,2},{2,1},{3,0},{4,7},{5,6},{6,5},{7,4},{8,11},{9,10},{10,... | collective-permute-start | bytes 208904 | tf_op jit(solution)/shard_map/ppermute | solution.py:75
  76.5 7.0 %collective-permute-done.20.refs_1_ = f32[136,128]{1,0:T(8,128)S(1)} collective-permute-done((f32[136,128]{1,0:T(8,128)S(1)}, f32[136,128]{1,0:T(8,128)S(1)}, u32[]{:S(2)}, u32[]{:S(2)}) %collective-permute-start.20) | collective-permute-done | bytes 69664 | tf_op jit(solution)/shard_map/ppermute | solution.py:75
  83.6 2.4 %collective-permute-start.25 = (f32[96,512]{1,0:T(8,128)S(1)}, f32[96,512]{1,0:T(8,128)S(1)}, u32[]{:S(2)}, u32[]{:S(2)}) collective-permute-start(f32[96,512]{1,0:T(8,128)S(1)} %shard_map.77.refs_2_.refs_5_), channel_id=1, source_target_pairs={{0,3},{1,2},{2,1},{3,0},{4,7},{5,6},{6,5},{7,4},{8,11},{9,10},{10,... | collective-permute-start | bytes 589832 | tf_op jit(solution)/shard_map/ppermute | solution.py:75
  86.0 0.9 shard_map.79.refs_7_.refs_0_.refs_1_
  86.8 3.6 %collective-permute-start.26 = (f32[104,512]{1,0:T(8,128)S(1)}, f32[104,512]{1,0:T(8,128)S(1)}, u32[]{:S(2)}, u32[]{:S(2)}) collective-permute-start(f32[104,512]{1,0:T(8,128)S(1)} %shard_map.79.refs_7_.refs_0_.refs_1_), channel_id=1, source_target_pairs={{0,1},{1,0},{2,3},{3,2},{4,5},{5,4},{6,7},{7,6},{8,9},{9,8},{10,11... | collective-permute-start | bytes 638984 | tf_op jit(solution)/shard_map/ppermute | solution.py:75
  90.4 2.4 %collective-permute-done.25.refs_6_ = f32[96,512]{1,0:T(8,128)S(1)} collective-permute-done((f32[96,512]{1,0:T(8,128)S(1)}, f32[96,512]{1,0:T(8,128)S(1)}, u32[]{:S(2)}, u32[]{:S(2)}) %collective-permute-start.25) | collective-permute-done | bytes 196640 | tf_op jit(solution)/shard_map/ppermute | solution.py:75
  92.9 0.9 shard_map.80.refs_4_.refs_2_.refs_0_
  93.8 4.7 %collective-permute-start.27 = (f32[96,512]{1,0:T(8,128)S(1)}, f32[96,512]{1,0:T(8,128)S(1)}, u32[]{:S(2)}, u32[]{:S(2)}) collective-permute-start(f32[96,512]{1,0:T(8,128)S(1)} %shard_map.80.refs_4_.refs_2_.refs_0_), channel_id=1, source_target_pairs={{0,1},{1,0},{2,3},{3,2},{4,5},{5,4},{6,7},{7,6},{8,9},{9,8},{10,11... | collective-permute-start | bytes 589832 | tf_op jit(solution)/shard_map/ppermute | solution.py:75
  98.4 0.6 shard_map.81
  99.6 0.6 shard_map.82.refs_0_.refs_3_
  100.6 1.5 %collective-permute-start.33 = (f32[104,640]{1,0:T(8,128)S(1)}, f32[104,640]{1,0:T(8,128)S(1)}, u32[]{:S(2)}, u32[]{:S(2)}) collective-permute-start(f32[104,640]{1,0:T(8,128)S(1)} %shard_map.83.refs_5_.refs_0_), channel_id=1, source_target_pairs={{0,8},{4,12},{8,0},{12,4},{1,9},{5,13},{9,1},{13,5},{2,10},{6,14},... | collective-permute-start | bytes 798728 | tf_op jit(solution)/shard_map/ppermute | solution.py:75
  102.2 1.4 %collective-permute-done.27.refs_4_.refs_1_ = f32[96,512]{1,0:T(8,128)S(1)} collective-permute-done((f32[96,512]{1,0:T(8,128)S(1)}, f32[96,512]{1,0:T(8,128)S(1)}, u32[]{:S(2)}, u32[]{:S(2)}) %collective-permute-start.27) | collective-permute-done | bytes 196640 | tf_op jit(solution)/shard_map/ppermute | solution.py:75
  103.6 1.1 shard_map.84
  104.6 0.6 shard_map.85.refs_4_
  105.8 0.6 shard_map.86.refs_5_.refs_0_
  106.4 0.6 shard_map.87.refs_2_
  107.0 1.5 %collective-permute-start.31 = (f32[136,128]{1,0:T(8,128)S(1)}, f32[136,128]{1,0:T(8,128)S(1)}, u32[]{:S(2)}, u32[]{:S(2)}) collective-permute-start(f32[136,128]{1,0:T(8,128)S(1)} %shard_map.88.refs_2_.refs_0_), channel_id=1, source_target_pairs={{0,8},{4,12},{8,0},{12,4},{1,9},{5,13},{9,1},{13,5},{2,10},{6,14},... | collective-permute-start | bytes 208904 | tf_op jit(solution)/shard_map/ppermute | solution.py:75
  108.6 0.8 collective-permute-done.33.refs_1_
  109.4 1.5 %collective-permute-start.35 = (f32[96,640]{1,0:T(8,128)S(1)}, f32[96,640]{1,0:T(8,128)S(1)}, u32[]{:S(2)}, u32[]{:S(2)}) collective-permute-start(f32[96,640]{1,0:T(8,128)S(1)} %shard_map.90.refs_2_.refs_5_), channel_id=1, source_target_pairs={{0,8},{4,12},{8,0},{12,4},{1,9},{5,13},{9,1},{13,5},{2,10},{6,14},... | collective-permute-start | bytes 737288 | tf_op jit(solution)/shard_map/ppermute | solution.py:75
  111.5 1.2 %collective-permute-done.34.refs_2_ = f32[136,128]{1,0:T(8,128)S(1)} collective-permute-done((f32[136,128]{1,0:T(8,128)S(1)}, f32[136,128]{1,0:T(8,128)S(1)}, u32[]{:S(2)}, u32[]{:S(2)}) %collective-permute-start.34) | collective-permute-done | bytes 69664 | tf_op jit(solution)/shard_map/ppermute | solution.py:75
  112.8 0.9 shard_map.92.refs_7_.refs_1_
  113.9 2.9 %collective-permute-done.35.refs_6_ = f32[96,640]{1,0:T(8,128)S(1)} collective-permute-done((f32[96,640]{1,0:T(8,128)S(1)}, f32[96,640]{1,0:T(8,128)S(1)}, u32[]{:S(2)}, u32[]{:S(2)}) %collective-permute-start.35) | collective-permute-done | bytes 245792 | tf_op jit(solution)/shard_map/ppermute | solution.py:75
  116.8 0.9 shard_map.93.refs_2_.refs_5_
  117.8 0.9 copy.5
  118.7 0.6 collective-permute-done.37.refs_4_
  119.3 0.6 shard_map.94
  119.9 1.0 copy.6
  (62 shorter events, 6.1 us)
Async XLA Ops:
  0.6 9.8 %copy-start = (f32[1024,200]{0,1:T(8,128)S(1)}, f32[1024,200]{0,1:T(8,128)}, u32[]{:S(2)}) copy-start(f32[1024,200]{0,1:T(8,128)} %param.4) | copy-start | bytes 2457604
  5.3 10.7 %collective-permute-start.3 = (f32[104,512]{1,0:T(8,128)S(1)}, f32[104,512]{1,0:T(8,128)S(1)}, u32[]{:S(2)}, u32[]{:S(2)}) collective-permute-start(f32[104,512]{1,0:T(8,128)S(1)} %get-tuple-element.34), channel_id=1, source_target_pairs={{0,1},{1,0},{2,3},{3,2},{4,5},{5,4},{6,7},{7,6},{8,9},{9,8},{10,11... | collective-permute-start | bytes 638984 | tf_op jit(solution)/shard_map/ppermute | solution.py:75
  8.4 7.6 %collective-permute-start = (f32[136,128]{1,0:T(8,128)S(1)}, f32[136,128]{1,0:T(8,128)S(1)}, u32[]{:S(2)}, u32[]{:S(2)}) collective-permute-start(f32[136,128]{1,0:T(8,128)S(1)} %get-tuple-element.25.refs_7_.refs_0_), channel_id=1, source_target_pairs={{0,1},{1,0},{2,3},{3,2},{4,5},{5,4},{6,7},{7,6},{8,9},{9,8},{10,11... | collective-permute-start | bytes 208904 | tf_op jit(solution)/shard_map/ppermute | solution.py:75
  8.4 11.8 %collective-permute-start.2 = (f32[96,512]{1,0:T(8,128)S(1)}, f32[96,512]{1,0:T(8,128)S(1)}, u32[]{:S(2)}, u32[]{:S(2)}) collective-permute-start(f32[96,512]{1,0:T(8,128)S(1)} %get-tuple-element.32), channel_id=1, source_target_pairs={{0,1},{1,0},{2,3},{3,2},{4,5},{5,4},{6,7},{7,6},{8,9},{9,8},{10,11... | collective-permute-start | bytes 589832 | tf_op jit(solution)/shard_map/ppermute | solution.py:75
  16.0 13.3 %collective-permute-start.5 = (f32[104,512]{1,0:T(8,128)S(1)}, f32[104,512]{1,0:T(8,128)S(1)}, u32[]{:S(2)}, u32[]{:S(2)}) collective-permute-start(f32[104,512]{1,0:T(8,128)S(1)} %shard_map.53.refs_2_.refs_5_), channel_id=1, source_target_pairs={{0,3},{1,2},{2,1},{3,0},{4,7},{5,6},{6,5},{7,4},{8,11},{9,10},{10,... | collective-permute-start | bytes 638984 | tf_op jit(solution)/shard_map/ppermute | solution.py:75
  20.1 7.5 %collective-permute-start.1 = (f32[136,128]{1,0:T(8,128)S(1)}, f32[136,128]{1,0:T(8,128)S(1)}, u32[]{:S(2)}, u32[]{:S(2)}) collective-permute-start(f32[136,128]{1,0:T(8,128)S(1)} %shard_map.52.refs_2_.refs_0_), channel_id=1, source_target_pairs={{0,3},{1,2},{2,1},{3,0},{4,7},{5,6},{6,5},{7,4},{8,11},{9,10},{10,... | collective-permute-start | bytes 208904 | tf_op jit(solution)/shard_map/ppermute | solution.py:75
  27.7 1.7 %collective-permute-start.4 = (f32[136,128]{1,0:T(8,128)S(1)}, f32[136,128]{1,0:T(8,128)S(1)}, u32[]{:S(2)}, u32[]{:S(2)}) collective-permute-start(f32[136,128]{1,0:T(8,128)S(1)} %shard_map.55.refs_1_.refs_7_), channel_id=1, source_target_pairs={{0,4},{4,0},{8,12},{12,8},{1,5},{5,1},{9,13},{13,9},{2,6},{6,2},{1... | collective-permute-start | bytes 208904 | tf_op jit(solution)/shard_map/ppermute | solution.py:75
  27.8 9.6 %collective-permute-start.6 = (f32[96,512]{1,0:T(8,128)S(1)}, f32[96,512]{1,0:T(8,128)S(1)}, u32[]{:S(2)}, u32[]{:S(2)}) collective-permute-start(f32[96,512]{1,0:T(8,128)S(1)} %shard_map.54.refs_2_.refs_5_), channel_id=1, source_target_pairs={{0,3},{1,2},{2,1},{3,0},{4,7},{5,6},{6,5},{7,4},{8,11},{9,10},{10,... | collective-permute-start | bytes 589832 | tf_op jit(solution)/shard_map/ppermute | solution.py:75
  30.2 12.4 %collective-permute-start.7 = (f32[104,512]{1,0:T(8,128)S(1)}, f32[104,512]{1,0:T(8,128)S(1)}, u32[]{:S(2)}, u32[]{:S(2)}) collective-permute-start(f32[104,512]{1,0:T(8,128)S(1)} %shard_map.56.refs_7_.refs_0_.refs_1_.refs_3_), channel_id=1, source_target_pairs={{0,1},{1,0},{2,3},{3,2},{4,5},{5,4},{6,7},{7,6},{8,9},{9,8},{10,11... | collective-permute-start | bytes 638984 | tf_op jit(solution)/shard_map/ppermute | solution.py:75
  38.2 9.5 %collective-permute-start.8 = (f32[96,512]{1,0:T(8,128)S(1)}, f32[96,512]{1,0:T(8,128)S(1)}, u32[]{:S(2)}, u32[]{:S(2)}) collective-permute-start(f32[96,512]{1,0:T(8,128)S(1)} %shard_map.57.refs_4_.refs_2_.refs_0_), channel_id=1, source_target_pairs={{0,1},{1,0},{2,3},{3,2},{4,5},{5,4},{6,7},{7,6},{8,9},{9,8},{10,11... | collective-permute-start | bytes 589832 | tf_op jit(solution)/shard_map/ppermute | solution.py:75
  43.2 1.6 %collective-permute-start.10 = (f32[56,640]{1,0:T(8,128)S(1)}, f32[56,640]{1,0:T(8,128)S(1)}, u32[]{:S(2)}, u32[]{:S(2)}) collective-permute-start(f32[56,640]{1,0:T(8,128)S(1)} %get-tuple-element.41), channel_id=1, source_target_pairs={{0,4},{4,0},{8,12},{12,8},{1,5},{5,1},{9,13},{13,9},{2,6},{6,2},{1... | collective-permute-start | bytes 430088 | tf_op jit(solution)/shard_map/ppermute | solution.py:75
  43.2 1.5 %collective-permute-start.9 = (f32[48,640]{1,0:T(8,128)S(1)}, f32[48,640]{1,0:T(8,128)S(1)}, u32[]{:S(2)}, u32[]{:S(2)}) collective-permute-start(f32[48,640]{1,0:T(8,128)S(1)} %get-tuple-element.40.refs_4_), channel_id=1, source_target_pairs={{0,4},{4,0},{8,12},{12,8},{1,5},{5,1},{9,13},{13,9},{2,6},{6,2},{1... | collective-permute-start | bytes 368648 | tf_op jit(solution)/shard_map/ppermute | solution.py:75
  44.8 8.7 %collective-permute-start.14 = (f32[104,640]{1,0:T(8,128)S(1)}, f32[104,640]{1,0:T(8,128)S(1)}, u32[]{:S(2)}, u32[]{:S(2)}) collective-permute-start(f32[104,640]{1,0:T(8,128)S(1)} %shard_map.60.refs_5_.refs_0_), channel_id=1, source_target_pairs={{0,8},{4,12},{8,0},{12,4},{1,9},{5,13},{9,1},{13,5},{2,10},{6,14},... | collective-permute-start | bytes 798728 | tf_op jit(solution)/shard_map/ppermute | solution.py:75
  49.4 4.1 %collective-permute-start.13 = (f32[96,640]{1,0:T(8,128)S(1)}, f32[96,640]{1,0:T(8,128)S(1)}, u32[]{:S(2)}, u32[]{:S(2)}) collective-permute-start(f32[96,640]{1,0:T(8,128)S(1)} %shard_map.62.refs_4_), channel_id=1, source_target_pairs={{0,4},{4,0},{8,12},{12,8},{1,5},{5,1},{9,13},{13,9},{2,6},{6,2},{1... | collective-permute-start | bytes 737288 | tf_op jit(solution)/shard_map/ppermute | solution.py:75
  49.5 1.6 %collective-permute-start.11 = (f32[136,128]{1,0:T(8,128)S(1)}, f32[136,128]{1,0:T(8,128)S(1)}, u32[]{:S(2)}, u32[]{:S(2)}) collective-permute-start(f32[136,128]{1,0:T(8,128)S(1)} %get-tuple-element.43.refs_4_), channel_id=1, source_target_pairs={{0,4},{4,0},{8,12},{12,8},{1,5},{5,1},{9,13},{13,9},{2,6},{6,2},{1... | collective-permute-start | bytes 208904 | tf_op jit(solution)/shard_map/ppermute | solution.py:75
  51.1 4.4 %collective-permute-start.12 = (f32[136,128]{1,0:T(8,128)S(1)}, f32[136,128]{1,0:T(8,128)S(1)}, u32[]{:S(2)}, u32[]{:S(2)}) collective-permute-start(f32[136,128]{1,0:T(8,128)S(1)} %shard_map.64.refs_2_.refs_0_), channel_id=1, source_target_pairs={{0,8},{4,12},{8,0},{12,4},{1,9},{5,13},{9,1},{13,5},{2,10},{6,14},... | collective-permute-start | bytes 208904 | tf_op jit(solution)/shard_map/ppermute | solution.py:75
  53.6 7.4 %collective-permute-start.16 = (f32[96,640]{1,0:T(8,128)S(1)}, f32[96,640]{1,0:T(8,128)S(1)}, u32[]{:S(2)}, u32[]{:S(2)}) collective-permute-start(f32[96,640]{1,0:T(8,128)S(1)} %shard_map.66.refs_2_.refs_5_), channel_id=1, source_target_pairs={{0,8},{4,12},{8,0},{12,4},{1,9},{5,13},{9,1},{13,5},{2,10},{6,14},... | collective-permute-start | bytes 737288 | tf_op jit(solution)/shard_map/ppermute | solution.py:75
  55.5 1.3 %collective-permute-start.15 = (f32[136,128]{1,0:T(8,128)S(1)}, f32[136,128]{1,0:T(8,128)S(1)}, u32[]{:S(2)}, u32[]{:S(2)}) collective-permute-start(f32[136,128]{1,0:T(8,128)S(1)} %shard_map.67.refs_1_.refs_6_), channel_id=1, source_target_pairs={{0,4},{4,0},{8,12},{12,8},{1,5},{5,1},{9,13},{13,9},{2,6},{6,2},{1... | collective-permute-start | bytes 208904 | tf_op jit(solution)/shard_map/ppermute | solution.py:75
  57.7 4.3 %collective-permute-start.17 = (f32[104,640]{1,0:T(8,128)S(1)}, f32[104,640]{1,0:T(8,128)S(1)}, u32[]{:S(2)}, u32[]{:S(2)}) collective-permute-start(f32[104,640]{1,0:T(8,128)S(1)} %shard_map.68.refs_7_.refs_0_.refs_1_.refs_3_), channel_id=1, source_target_pairs={{0,4},{4,0},{8,12},{12,8},{1,5},{5,1},{9,13},{13,9},{2,6},{6,2},{1... | collective-permute-start | bytes 798728 | tf_op jit(solution)/shard_map/ppermute | solution.py:75
  61.9 3.5 %collective-permute-start.18 = (f32[96,640]{1,0:T(8,128)S(1)}, f32[96,640]{1,0:T(8,128)S(1)}, u32[]{:S(2)}, u32[]{:S(2)}) collective-permute-start(f32[96,640]{1,0:T(8,128)S(1)} %shard_map.69.refs_4_.refs_2_.refs_0_), channel_id=1, source_target_pairs={{0,4},{4,0},{8,12},{12,8},{1,5},{5,1},{9,13},{13,9},{2,6},{6,2},{1... | collective-permute-start | bytes 737288 | tf_op jit(solution)/shard_map/ppermute | solution.py:75
  63.0 9.6 %collective-permute-start.22 = (f32[104,512]{1,0:T(8,128)S(1)}, f32[104,512]{1,0:T(8,128)S(1)}, u32[]{:S(2)}, u32[]{:S(2)}) collective-permute-start(f32[104,512]{1,0:T(8,128)S(1)} %shard_map.70.refs_4_), channel_id=1, source_target_pairs={{0,1},{1,0},{2,3},{3,2},{4,5},{5,4},{6,7},{7,6},{8,9},{9,8},{10,11... | collective-permute-start | bytes 638984 | tf_op jit(solution)/shard_map/ppermute | solution.py:75
  66.7 5.9 %collective-permute-start.19 = (f32[136,128]{1,0:T(8,128)S(1)}, f32[136,128]{1,0:T(8,128)S(1)}, u32[]{:S(2)}, u32[]{:S(2)}) collective-permute-start(f32[136,128]{1,0:T(8,128)S(1)} %shard_map.72.refs_4_.refs_0_), channel_id=1, source_target_pairs={{0,1},{1,0},{2,3},{3,2},{4,5},{5,4},{6,7},{7,6},{8,9},{9,8},{10,11... | collective-permute-start | bytes 208904 | tf_op jit(solution)/shard_map/ppermute | solution.py:75
  68.2 8.3 %collective-permute-start.21 = (f32[96,512]{1,0:T(8,128)S(1)}, f32[96,512]{1,0:T(8,128)S(1)}, u32[]{:S(2)}, u32[]{:S(2)}) collective-permute-start(f32[96,512]{1,0:T(8,128)S(1)} %shard_map.73.refs_4_), channel_id=1, source_target_pairs={{0,1},{1,0},{2,3},{3,2},{4,5},{5,4},{6,7},{7,6},{8,9},{9,8},{10,11... | collective-permute-start | bytes 589832 | tf_op jit(solution)/shard_map/ppermute | solution.py:75
  72.6 13.4 %collective-permute-start.24 = (f32[104,512]{1,0:T(8,128)S(1)}, f32[104,512]{1,0:T(8,128)S(1)}, u32[]{:S(2)}, u32[]{:S(2)}) collective-permute-start(f32[104,512]{1,0:T(8,128)S(1)} %shard_map.76.refs_2_.refs_5_), channel_id=1, source_target_pairs={{0,3},{1,2},{2,1},{3,0},{4,7},{5,6},{6,5},{7,4},{8,11},{9,10},{10,... | collective-permute-start | bytes 638984 | tf_op jit(solution)/shard_map/ppermute | solution.py:75
  74.2 9.3 %collective-permute-start.20 = (f32[136,128]{1,0:T(8,128)S(1)}, f32[136,128]{1,0:T(8,128)S(1)}, u32[]{:S(2)}, u32[]{:S(2)}) collective-permute-start(f32[136,128]{1,0:T(8,128)S(1)} %shard_map.75.refs_2_.refs_0_), channel_id=1, source_target_pairs={{0,3},{1,2},{2,1},{3,0},{4,7},{5,6},{6,5},{7,4},{8,11},{9,10},{10,... | collective-permute-start | bytes 208904 | tf_op jit(solution)/shard_map/ppermute | solution.py:75
  83.5 2.5 %collective-permute-start.23 = (f32[136,128]{1,0:T(8,128)S(1)}, f32[136,128]{1,0:T(8,128)S(1)}, u32[]{:S(2)}, u32[]{:S(2)}) collective-permute-start(f32[136,128]{1,0:T(8,128)S(1)} %shard_map.78.refs_1_.refs_7_), channel_id=1, source_target_pairs={{0,4},{4,0},{8,12},{12,8},{1,5},{5,1},{9,13},{13,9},{2,6},{6,2},{1... | collective-permute-start | bytes 208904 | tf_op jit(solution)/shard_map/ppermute | solution.py:75
  83.6 9.3 %collective-permute-start.25 = (f32[96,512]{1,0:T(8,128)S(1)}, f32[96,512]{1,0:T(8,128)S(1)}, u32[]{:S(2)}, u32[]{:S(2)}) collective-permute-start(f32[96,512]{1,0:T(8,128)S(1)} %shard_map.77.refs_2_.refs_5_), channel_id=1, source_target_pairs={{0,3},{1,2},{2,1},{3,0},{4,7},{5,6},{6,5},{7,4},{8,11},{9,10},{10,... | collective-permute-start | bytes 589832 | tf_op jit(solution)/shard_map/ppermute | solution.py:75
  86.8 11.6 %collective-permute-start.26 = (f32[104,512]{1,0:T(8,128)S(1)}, f32[104,512]{1,0:T(8,128)S(1)}, u32[]{:S(2)}, u32[]{:S(2)}) collective-permute-start(f32[104,512]{1,0:T(8,128)S(1)} %shard_map.79.refs_7_.refs_0_.refs_1_), channel_id=1, source_target_pairs={{0,1},{1,0},{2,3},{3,2},{4,5},{5,4},{6,7},{7,6},{8,9},{9,8},{10,11... | collective-permute-start | bytes 638984 | tf_op jit(solution)/shard_map/ppermute | solution.py:75
  93.8 9.8 %collective-permute-start.27 = (f32[96,512]{1,0:T(8,128)S(1)}, f32[96,512]{1,0:T(8,128)S(1)}, u32[]{:S(2)}, u32[]{:S(2)}) collective-permute-start(f32[96,512]{1,0:T(8,128)S(1)} %shard_map.80.refs_4_.refs_2_.refs_0_), channel_id=1, source_target_pairs={{0,1},{1,0},{2,3},{3,2},{4,5},{5,4},{6,7},{7,6},{8,9},{9,8},{10,11... | collective-permute-start | bytes 589832 | tf_op jit(solution)/shard_map/ppermute | solution.py:75
  99.0 1.6 %collective-permute-start.29 = (f32[56,640]{1,0:T(8,128)S(1)}, f32[56,640]{1,0:T(8,128)S(1)}, u32[]{:S(2)}, u32[]{:S(2)}) collective-permute-start(f32[56,640]{1,0:T(8,128)S(1)} %get-tuple-element.45), channel_id=1, source_target_pairs={{0,4},{4,0},{8,12},{12,8},{1,5},{5,1},{9,13},{13,9},{2,6},{6,2},{1... | collective-permute-start | bytes 430088 | tf_op jit(solution)/shard_map/ppermute | solution.py:75
  99.1 1.5 %collective-permute-start.28 = (f32[48,640]{1,0:T(8,128)S(1)}, f32[48,640]{1,0:T(8,128)S(1)}, u32[]{:S(2)}, u32[]{:S(2)}) collective-permute-start(f32[48,640]{1,0:T(8,128)S(1)} %get-tuple-element.44.refs_4_), channel_id=1, source_target_pairs={{0,4},{4,0},{8,12},{12,8},{1,5},{5,1},{9,13},{13,9},{2,6},{6,2},{1... | collective-permute-start | bytes 368648 | tf_op jit(solution)/shard_map/ppermute | solution.py:75
  100.6 8.7 %collective-permute-start.33 = (f32[104,640]{1,0:T(8,128)S(1)}, f32[104,640]{1,0:T(8,128)S(1)}, u32[]{:S(2)}, u32[]{:S(2)}) collective-permute-start(f32[104,640]{1,0:T(8,128)S(1)} %shard_map.83.refs_5_.refs_0_), channel_id=1, source_target_pairs={{0,8},{4,12},{8,0},{12,4},{1,9},{5,13},{9,1},{13,5},{2,10},{6,14},... | collective-permute-start | bytes 798728 | tf_op jit(solution)/shard_map/ppermute | solution.py:75
  105.2 4.1 %collective-permute-start.32 = (f32[96,640]{1,0:T(8,128)S(1)}, f32[96,640]{1,0:T(8,128)S(1)}, u32[]{:S(2)}, u32[]{:S(2)}) collective-permute-start(f32[96,640]{1,0:T(8,128)S(1)} %shard_map.85.refs_4_), channel_id=1, source_target_pairs={{0,4},{4,0},{8,12},{12,8},{1,5},{5,1},{9,13},{13,9},{2,6},{6,2},{1... | collective-permute-start | bytes 737288 | tf_op jit(solution)/shard_map/ppermute | solution.py:75
  105.3 1.7 %collective-permute-start.30 = (f32[136,128]{1,0:T(8,128)S(1)}, f32[136,128]{1,0:T(8,128)S(1)}, u32[]{:S(2)}, u32[]{:S(2)}) collective-permute-start(f32[136,128]{1,0:T(8,128)S(1)} %get-tuple-element.46.refs_4_), channel_id=1, source_target_pairs={{0,4},{4,0},{8,12},{12,8},{1,5},{5,1},{9,13},{13,9},{2,6},{6,2},{1... | collective-permute-start | bytes 208904 | tf_op jit(solution)/shard_map/ppermute | solution.py:75
  107.0 4.4 %collective-permute-start.31 = (f32[136,128]{1,0:T(8,128)S(1)}, f32[136,128]{1,0:T(8,128)S(1)}, u32[]{:S(2)}, u32[]{:S(2)}) collective-permute-start(f32[136,128]{1,0:T(8,128)S(1)} %shard_map.88.refs_2_.refs_0_), channel_id=1, source_target_pairs={{0,8},{4,12},{8,0},{12,4},{1,9},{5,13},{9,1},{13,5},{2,10},{6,14},... | collective-permute-start | bytes 208904 | tf_op jit(solution)/shard_map/ppermute | solution.py:75
  109.4 7.4 %collective-permute-start.35 = (f32[96,640]{1,0:T(8,128)S(1)}, f32[96,640]{1,0:T(8,128)S(1)}, u32[]{:S(2)}, u32[]{:S(2)}) collective-permute-start(f32[96,640]{1,0:T(8,128)S(1)} %shard_map.90.refs_2_.refs_5_), channel_id=1, source_target_pairs={{0,8},{4,12},{8,0},{12,4},{1,9},{5,13},{9,1},{13,5},{2,10},{6,14},... | collective-permute-start | bytes 737288 | tf_op jit(solution)/shard_map/ppermute | solution.py:75
  111.4 1.3 %collective-permute-start.34 = (f32[136,128]{1,0:T(8,128)S(1)}, f32[136,128]{1,0:T(8,128)S(1)}, u32[]{:S(2)}, u32[]{:S(2)}) collective-permute-start(f32[136,128]{1,0:T(8,128)S(1)} %shard_map.91.refs_1_.refs_6_), channel_id=1, source_target_pairs={{0,4},{4,0},{8,12},{12,8},{1,5},{5,1},{9,13},{13,9},{2,6},{6,2},{1... | collective-permute-start | bytes 208904 | tf_op jit(solution)/shard_map/ppermute | solution.py:75
  113.7 5.1 %collective-permute-start.36 = (f32[104,640]{1,0:T(8,128)S(1)}, f32[104,640]{1,0:T(8,128)S(1)}, u32[]{:S(2)}, u32[]{:S(2)}) collective-permute-start(f32[104,640]{1,0:T(8,128)S(1)} %shard_map.92.refs_7_.refs_1_), channel_id=1, source_target_pairs={{0,4},{4,0},{8,12},{12,8},{1,5},{5,1},{9,13},{13,9},{2,6},{6,2},{1... | collective-permute-start | bytes 798728 | tf_op jit(solution)/shard_map/ppermute | solution.py:75
  117.8 1.6 %collective-permute-start.37 = (f32[96,640]{1,0:T(8,128)S(1)}, f32[96,640]{1,0:T(8,128)S(1)}, u32[]{:S(2)}, u32[]{:S(2)}) collective-permute-start(f32[96,640]{1,0:T(8,128)S(1)} %shard_map.93.refs_2_.refs_5_), channel_id=1, source_target_pairs={{0,4},{4,0},{8,12},{12,8},{1,5},{5,1},{9,13},{13,9},{2,6},{6,2},{1... | collective-permute-start | bytes 737288 | tf_op jit(solution)/shard_map/ppermute | solution.py:75

commit v7 on v6

--- a/solution.py
+++ b/solution.py
@@ -11,7 +11,7 @@
 CHUNKS = (104, 96)
 USAGE_WEIGHTS = (1, 6, 1)
 GRAM_AT = 1
-PROGRAM_WEIGHTS = (1, 18)
+PROGRAM_WEIGHTS = (1, 16)
 VMEM = pl.BlockSpec(memory_space=pltpu.VMEM)
 SMEM = pl.BlockSpec(memory_space=pltpu.SMEM)
 ANY = pl.BlockSpec(memory_space=pl.ANY)
@@ -150,25 +150,42 @@
 
         return chain(kernel, [a.shape], a, *b)[0]
 
-    def update(index, mine, theirs, factor, tops, weight=1):
-        first = starts[index]
-
-        def rows_of(a):
-            return a if a.shape[0] == sizes[index] else a[first : first + sizes[index]]
-
-        def kernel(where_ref, m_ref, t_ref, *refs):
+    def rows_of(a, index):
+        return a[starts[index] : starts[index] + sizes[index]]
+
+    def denominator(where_ref, m_ref, t_ref, f_refs, index):
+        own = where_ref[0] == 0
+        upper = jnp.where(own, m_ref[...], t_ref[...])
+        lower = jnp.where(own, t_ref[...], m_ref[...])
+        g = unpacked(jnp.concatenate([upper, lower], 0))
+        return dot3(rows_of(g, index), stacked(f_refs), 1, 0)
+
+    def update(mine, theirs, factor, tops, axis, size, flip, weights):
+        def first(where_ref, m_ref, t_ref, *refs):
             f_refs, (*top_refs, o_ref) = refs[:n_chunks], refs[n_chunks:]
-            own = where_ref[0] == 0
-            upper = jnp.where(own, m_ref[...], t_ref[...])
-            lower = jnp.where(own, t_ref[...], m_ref[...])
-            g = rows_of(unpacked(jnp.concatenate([upper, lower], 0)))
-            f = stacked(f_refs)
-            part = f_refs[index][...]
-            top = sum(rows_of(ref[...]) for ref in top_refs)
-            o_ref[...] = part * top / dot3(g, f, 1, 0)
-
-        n, m = factor[index].shape
-        return chain(kernel, [(n, m)], where, mine, theirs, *factor, *tops, flops=6 * n * k * m * weight)[0]
+            below = denominator(where_ref, m_ref, t_ref, f_refs, 0)
+            o_ref[...] = f_refs[0][...] * sum(ref[...] for ref in top_refs) / below
+
+        def below(index, where_ref, m_ref, t_ref, *refs):
+            refs[-1][...] = denominator(where_ref, m_ref, t_ref, refs[:n_chunks], index)
+
+        def rest(f_ref, d_ref, *refs):
+            *top_refs, o_ref = refs
+            o_ref[...] = f_ref[...] * sum(ref[...] for ref in top_refs) / d_ref[...]
+
+        m = factor[0].shape[1]
+        shapes = [(n, m) for n in sizes]
+        flops = [6 * n * k * m * weight for n, weight in zip(sizes, weights)]
+        new = [chain(first, shapes[:1], where, mine, theirs, *factor, *tops[0], flops=flops[0])[0]]
+        other = [exchange(new[0], axis, size, flip)]
+        divisors = [
+            chain(functools.partial(below, i), shapes[i : i + 1], where, mine, theirs, *factor)[0]
+            for i in range(1, n_chunks)
+        ]
+        for i in range(1, n_chunks):
+            new.append(chain(rest, shapes[i : i + 1], factor[i], divisors[i - 1], *tops[i], flops=flops[i])[0])
+            other.append(exchange(new[i], axis, size, flip))
+        return new, other
 
     def join(mine, theirs, index, which):
         size = mine[0].shape[1]
@@ -317,10 +334,7 @@
         tops = [far(add(keep, near), "gene", genes, True) for keep, near in zip(keeps, nears)]
         mine = add(*gram_top)
         theirs = exchange(mine, "cell", cells, 1)
-        new, other = [], []
-        for i in range(n_chunks):
-            new.append(update(i, mine, theirs, usage_own, tops[i], weight=USAGE_WEIGHTS[min(i, 2)]))
-            other.append(exchange(new[i], "gene", genes, 1))
+        new, other = update(mine, theirs, usage_own, tops, "gene", genes, 1, USAGE_WEIGHTS)
         usage_own, usage_other = new, other
 
         tops = []
@@ -343,11 +357,8 @@
             tops.append(far(add(keep, send), "cell", cells, False))
         mine = add(*gram_top)
         theirs = exchange(mine, "cell", cells, 1)
-        new, other = [], []
-        for i in range(n_chunks):
-            new.append(update(i, mine, theirs, program_own, tops[i], weight=PROGRAM_WEIGHTS[last] if i == 0 else 1))
-            other.append(exchange(new[i], "cell", cells, 1))
-        program_own, program_other = new, other
+        weights = (PROGRAM_WEIGHTS[last], 1, 1)
+        program_own, program_other = update(mine, theirs, program_own, tops, "cell", cells, 1, weights)
 
     return usage.T, join(program_own, program_other, 0, core)
 

time: 121 us -> 118 us (0.975)
  waiting for transfers between devices: 40.7 us -> 37.2 us
    ppermute x38, waiting for transfers between devices: 40.7 us -> 37.2 us  [exchange(): return lax.ppermute(a, axis, [(i, i ^ flip) for i in range(size)])]
    pallas_call x45 -> x49, Pallas kernels: 28.3 us -> 28.5 us  [__call__(): pl.pallas_call(run, out_shape=[pltpu.VMEM(s.shape, s.dtype) for s in shap...]
  transfers between devices with their start and end apart: 38 -> 38, of which waited for: 20 -> 20; matrix products, arithmetic and copies ran while one was open for 1% -> 1% of each run, Pallas kernels for 19% -> 20%
where the time goes in v7:
time: 118 us
  starting transfers between devices  48.9 us (41%)
  waiting for transfers between devices  37.2 us (32%)
  Pallas kernels  28.5 us (24%)
  local copies, waits for them, and re-layouts  1.86 us (2%)
    ppermute x38, starting transfers between devices, exchange(): return lax.ppermute(a, axis, [(i, i ^ flip) for i in range(size)])  48.9 us
    ppermute x38, waiting for transfers between devices, exchange(): return lax.ppermute(a, axis, [(i, i ^ flip) for i in range(size)])  37.2 us
    pallas_call x49, Pallas kernels, __call__(): pl.pallas_call(run, out_shape=[pltpu.VMEM(s.shape, s.dtype) for s in shap...  28.5 us
  transfers between devices with their start and end apart: 38, of which 20 were waited for; matrix products, arithmetic and copies ran while one was open for 1% of the time, Pallas kernels for 20%

profile of v7, /device:TPU:0, one launch (start us, length us, event | category | flops | bytes accessed | tf_op | source)
XLA Modules:
  0.0 117.6 jit_solution(15375437319912532812)
XLA Ops:
  0.7 4.5 %shard_map.50 = (f32[136,128]{1,0:T(8,128)S(1)}, f32[104,512]{1,0:T(8,128)S(1)}, f32[96,512]{1,0:T(8,128)S(1)}, f32[104,640]{1,0:T(8,128)S(1)}, f32[96,640]{1,0:...) custom-call(s32[2]{0:T(128)S(1)} %pad_add_fusion.refs_0_, ...), custom_call_target="tpu_custom_call" | custom-call | flops 524288000 | bytes 10391560 | tf_op jit(solution)/shard_map/pallas_call | solution.py:61
  5.3 3.1 %collective-permute-start.3 = (f32[104,512]{1,0:T(8,128)S(1)}, f32[104,512]{1,0:T(8,128)S(1)}, u32[]{:S(2)}, u32[]{:S(2)}) collective-permute-start(f32[104,512]{1,0:T(8,128)S(1)} %get-tuple-element.34), channel_id=1, source_target_pairs={{0,1},{1,0},{2,3},{3,2},{4,5},{5,4},{6,7},{7,6},{8,9},{9,8},{10,11... | collective-permute-start | bytes 638984 | tf_op jit(solution)/shard_map/ppermute | solution.py:75
  8.4 1.9 %collective-permute-start.2 = (f32[96,512]{1,0:T(8,128)S(1)}, f32[96,512]{1,0:T(8,128)S(1)}, u32[]{:S(2)}, u32[]{:S(2)}) collective-permute-start(f32[96,512]{1,0:T(8,128)S(1)} %get-tuple-element.32), channel_id=1, source_target_pairs={{0,1},{1,0},{2,3},{3,2},{4,5},{5,4},{6,7},{7,6},{8,9},{9,8},{10,11... | collective-permute-start | bytes 589832 | tf_op jit(solution)/shard_map/ppermute | solution.py:75
  10.4 3.3 %shard_map.51 = (bf16[512,640]{1,0:T(8,128)(2,1)S(1)}, bf16[512,640]{1,0:T(8,128)(2,1)S(1)}, f32[104,512]{1,0:T(8,128)S(1)}, f32[96,512]{1,0:T(8,128)S(1)}, f32[...) custom-call(s32[2]{0:T(128)S(1)} %pad_add_fusion.refs_0_, s32[1024,1280]{1,0:T(8,128)} %refs_1_.3, ...), custom_call_target="tpu_custom_call" | custom-call | flops 524288000 | bytes 10526728 | tf_op jit(solution)/shard_map/pallas_call | solution.py:61
  13.7 2.2 %collective-permute-done.refs_1_ = f32[136,128]{1,0:T(8,128)S(1)} collective-permute-done((f32[136,128]{1,0:T(8,128)S(1)}, f32[136,128]{1,0:T(8,128)S(1)}, u32[]{:S(2)}, u32[]{:S(2)}) %collective-permute-start) | collective-permute-done | bytes 69664 | tf_op jit(solution)/shard_map/ppermute | solution.py:75
  16.0 4.1 %collective-permute-start.5 = (f32[104,512]{1,0:T(8,128)S(1)}, f32[104,512]{1,0:T(8,128)S(1)}, u32[]{:S(2)}, u32[]{:S(2)}) collective-permute-start(f32[104,512]{1,0:T(8,128)S(1)} %shard_map.53.refs_2_.refs_5_), channel_id=1, source_target_pairs={{0,3},{1,2},{2,1},{3,0},{4,7},{5,6},{6,5},{7,4},{8,11},{9,10},{10,... | collective-permute-start | bytes 638984 | tf_op jit(solution)/shard_map/ppermute | solution.py:75
  20.2 7.4 %collective-permute-done.1.refs_1_ = f32[136,128]{1,0:T(8,128)S(1)} collective-permute-done((f32[136,128]{1,0:T(8,128)S(1)}, f32[136,128]{1,0:T(8,128)S(1)}, u32[]{:S(2)}, u32[]{:S(2)}) %collective-permute-start.1) | collective-permute-done | bytes 69664 | tf_op jit(solution)/shard_map/ppermute | solution.py:75
  27.8 1.6 %collective-permute-start.6 = (f32[96,512]{1,0:T(8,128)S(1)}, f32[96,512]{1,0:T(8,128)S(1)}, u32[]{:S(2)}, u32[]{:S(2)}) collective-permute-start(f32[96,512]{1,0:T(8,128)S(1)} %shard_map.54.refs_2_), channel_id=1, source_target_pairs={{0,3},{1,2},{2,1},{3,0},{4,7},{5,6},{6,5},{7,4},{8,11},{9,10},{10,... | collective-permute-start | bytes 589832 | tf_op jit(solution)/shard_map/ppermute | solution.py:75
  29.3 0.9 shard_map.56.refs_5_.refs_0_.refs_1_.refs_3_
  30.2 3.1 %collective-permute-start.7 = (f32[104,512]{1,0:T(8,128)S(1)}, f32[104,512]{1,0:T(8,128)S(1)}, u32[]{:S(2)}, u32[]{:S(2)}) collective-permute-start(f32[104,512]{1,0:T(8,128)S(1)} %shard_map.56.refs_5_.refs_0_.refs_1_.refs_3_), channel_id=1, source_target_pairs={{0,1},{1,0},{2,3},{3,2},{4,5},{5,4},{6,7},{7,6},{8,9},{9,8},{10,11... | collective-permute-start | bytes 638984 | tf_op jit(solution)/shard_map/ppermute | solution.py:75
  33.3 0.8 shard_map.57.refs_1_.refs_4_
  34.2 3.2 %collective-permute-done.6.refs_3_ = f32[96,512]{1,0:T(8,128)S(1)} collective-permute-done((f32[96,512]{1,0:T(8,128)S(1)}, f32[96,512]{1,0:T(8,128)S(1)}, u32[]{:S(2)}, u32[]{:S(2)}) %collective-permute-start.6) | collective-permute-done | bytes 196640 | tf_op jit(solution)/shard_map/ppermute | solution.py:75
  37.4 4.3 %collective-permute-start.8 = (f32[96,512]{1,0:T(8,128)S(1)}, f32[96,512]{1,0:T(8,128)S(1)}, u32[]{:S(2)}, u32[]{:S(2)}) collective-permute-start(f32[96,512]{1,0:T(8,128)S(1)} %shard_map.58.refs_4_.refs_2_.refs_0_), channel_id=1, source_target_pairs={{0,1},{1,0},{2,3},{3,2},{4,5},{5,4},{6,7},{7,6},{8,9},{9,8},{10,11... | collective-permute-start | bytes 589832 | tf_op jit(solution)/shard_map/ppermute | solution.py:75
  41.8 0.6 shard_map.59
  42.9 0.6 shard_map.60.refs_0_.refs_3_
  44.0 1.6 %collective-permute-start.14 = (f32[104,640]{1,0:T(8,128)S(1)}, f32[104,640]{1,0:T(8,128)S(1)}, u32[]{:S(2)}, u32[]{:S(2)}) collective-permute-start(f32[104,640]{1,0:T(8,128)S(1)} %shard_map.61.refs_5_.refs_0_), channel_id=1, source_target_pairs={{0,8},{4,12},{8,0},{12,4},{1,9},{5,13},{9,1},{13,5},{2,10},{6,14},... | collective-permute-start | bytes 798728 | tf_op jit(solution)/shard_map/ppermute | solution.py:75
  45.6 1.4 %collective-permute-done.8.refs_4_.refs_1_ = f32[96,512]{1,0:T(8,128)S(1)} collective-permute-done((f32[96,512]{1,0:T(8,128)S(1)}, f32[96,512]{1,0:T(8,128)S(1)}, u32[]{:S(2)}, u32[]{:S(2)}) %collective-permute-start.8) | collective-permute-done | bytes 196640 | tf_op jit(solution)/shard_map/ppermute | solution.py:75
  46.9 1.1 shard_map.62
  48.0 0.6 shard_map.63.refs_4_
  49.2 0.6 shard_map.64.refs_2_.refs_0_
  50.3 1.6 %collective-permute-start.12 = (f32[136,128]{1,0:T(8,128)S(1)}, f32[136,128]{1,0:T(8,128)S(1)}, u32[]{:S(2)}, u32[]{:S(2)}) collective-permute-start(f32[136,128]{1,0:T(8,128)S(1)} %shard_map.65.refs_2_.refs_0_), channel_id=1, source_target_pairs={{0,8},{4,12},{8,0},{12,4},{1,9},{5,13},{9,1},{13,5},{2,10},{6,14},... | collective-permute-start | bytes 208904 | tf_op jit(solution)/shard_map/ppermute | solution.py:75
  51.8 0.8 collective-permute-done.14.refs_1_
  52.8 1.6 %collective-permute-start.16 = (f32[96,640]{1,0:T(8,128)S(1)}, f32[96,640]{1,0:T(8,128)S(1)}, u32[]{:S(2)}, u32[]{:S(2)}) collective-permute-start(f32[96,640]{1,0:T(8,128)S(1)} %shard_map.67.refs_2_), channel_id=1, source_target_pairs={{0,8},{4,12},{8,0},{12,4},{1,9},{5,13},{9,1},{13,5},{2,10},{6,14},... | collective-permute-start | bytes 737288 | tf_op jit(solution)/shard_map/ppermute | solution.py:75
  54.7 1.2 %collective-permute-done.15.refs_2_ = f32[136,128]{1,0:T(8,128)S(1)} collective-permute-done((f32[136,128]{1,0:T(8,128)S(1)}, f32[136,128]{1,0:T(8,128)S(1)}, u32[]{:S(2)}, u32[]{:S(2)}) %collective-permute-start.15) | collective-permute-done | bytes 69664 | tf_op jit(solution)/shard_map/ppermute | solution.py:75
  56.0 0.9 shard_map.69.refs_5_.refs_0_.refs_1_.refs_3_
  57.1 0.9 shard_map.70.refs_1_.refs_4_
  58.0 2.1 %collective-permute-done.16.refs_3_ = f32[96,640]{1,0:T(8,128)S(1)} collective-permute-done((f32[96,640]{1,0:T(8,128)S(1)}, f32[96,640]{1,0:T(8,128)S(1)}, u32[]{:S(2)}, u32[]{:S(2)}) %collective-permute-start.16) | collective-permute-done | bytes 245792 | tf_op jit(solution)/shard_map/ppermute | solution.py:75
  60.3 0.9 shard_map.72.refs_4_
  61.3 1.6 %collective-permute-start.22 = (f32[104,512]{1,0:T(8,128)S(1)}, f32[104,512]{1,0:T(8,128)S(1)}, u32[]{:S(2)}, u32[]{:S(2)}) collective-permute-start(f32[104,512]{1,0:T(8,128)S(1)} %shard_map.72.refs_4_), channel_id=1, source_target_pairs={{0,1},{1,0},{2,3},{3,2},{4,5},{5,4},{6,7},{7,6},{8,9},{9,8},{10,11... | collective-permute-start | bytes 638984 | tf_op jit(solution)/shard_map/ppermute | solution.py:75
  62.8 0.9 shard_map.73.refs_5_.refs_0_
  63.8 1.2 %shard_map.74.refs_4_.refs_0_ = f32[136,128]{1,0:T(8,128)S(1)} custom-call(s32[2]{0:T(128)S(1)} %pad_add_fusion.refs_0_, f32[104,640]{1,0:T(8,128)S(1)} %shard_map.69.refs_5_.refs_0_.refs_1_.refs_3_, f32[96,640]{1,0:T(8,128)S(1)} %shard_map.71.refs_4_.refs_2_.refs_0_, f32[104,640]{1,0:T(8,128)S(1)} %collective-permute-done.17.refs_1_.refs_3_, ...), custom_call_target="tpu_custom_call" | custom-call | flops 307200000 | bytes 1093640 | tf_op jit(solution)/shard_map/pallas_call | solution.py:61
  65.1 0.6 collective-permute-start.19
  65.7 0.9 shard_map.75.refs_4_
  66.6 1.6 %collective-permute-start.21 = (f32[96,512]{1,0:T(8,128)S(1)}, f32[96,512]{1,0:T(8,128)S(1)}, u32[]{:S(2)}, u32[]{:S(2)}) collective-permute-start(f32[96,512]{1,0:T(8,128)S(1)} %shard_map.75.refs_4_), channel_id=1, source_target_pairs={{0,1},{1,0},{2,3},{3,2},{4,5},{5,4},{6,7},{7,6},{8,9},{9,8},{10,11... | collective-permute-start | bytes 589832 | tf_op jit(solution)/shard_map/ppermute | solution.py:75
  68.1 0.9 shard_map.76.refs_2_.refs_0_
  69.1 1.8 %collective-permute-done.19.refs_1_ = f32[136,128]{1,0:T(8,128)S(1)} collective-permute-done((f32[136,128]{1,0:T(8,128)S(1)}, f32[136,128]{1,0:T(8,128)S(1)}, u32[]{:S(2)}, u32[]{:S(2)}) %collective-permute-start.19) | collective-permute-done | bytes 69664 | tf_op jit(solution)/shard_map/ppermute | solution.py:75
  71.0 1.6 %collective-permute-start.24 = (f32[104,512]{1,0:T(8,128)S(1)}, f32[104,512]{1,0:T(8,128)S(1)}, u32[]{:S(2)}, u32[]{:S(2)}) collective-permute-start(f32[104,512]{1,0:T(8,128)S(1)} %shard_map.78.refs_2_.refs_5_), channel_id=1, source_target_pairs={{0,3},{1,2},{2,1},{3,0},{4,7},{5,6},{6,5},{7,4},{8,11},{9,10},{10,... | collective-permute-start | bytes 638984 | tf_op jit(solution)/shard_map/ppermute | solution.py:75
  72.5 2.3 %collective-permute-start.20 = (f32[136,128]{1,0:T(8,128)S(1)}, f32[136,128]{1,0:T(8,128)S(1)}, u32[]{:S(2)}, u32[]{:S(2)}) collective-permute-start(f32[136,128]{1,0:T(8,128)S(1)} %shard_map.77.refs_2_.refs_0_), channel_id=1, source_target_pairs={{0,3},{1,2},{2,1},{3,0},{4,7},{5,6},{6,5},{7,4},{8,11},{9,10},{10,... | collective-permute-start | bytes 208904 | tf_op jit(solution)/shard_map/ppermute | solution.py:75
  74.9 7.0 %collective-permute-done.20.refs_1_ = f32[136,128]{1,0:T(8,128)S(1)} collective-permute-done((f32[136,128]{1,0:T(8,128)S(1)}, f32[136,128]{1,0:T(8,128)S(1)}, u32[]{:S(2)}, u32[]{:S(2)}) %collective-permute-start.20) | collective-permute-done | bytes 69664 | tf_op jit(solution)/shard_map/ppermute | solution.py:75
  81.9 2.4 %collective-permute-start.25 = (f32[96,512]{1,0:T(8,128)S(1)}, f32[96,512]{1,0:T(8,128)S(1)}, u32[]{:S(2)}, u32[]{:S(2)}) collective-permute-start(f32[96,512]{1,0:T(8,128)S(1)} %shard_map.79.refs_2_), channel_id=1, source_target_pairs={{0,3},{1,2},{2,1},{3,0},{4,7},{5,6},{6,5},{7,4},{8,11},{9,10},{10,... | collective-permute-start | bytes 589832 | tf_op jit(solution)/shard_map/ppermute | solution.py:75
  84.3 0.9 shard_map.81.refs_5_.refs_0_.refs_1_
  85.2 3.6 %collective-permute-start.26 = (f32[104,512]{1,0:T(8,128)S(1)}, f32[104,512]{1,0:T(8,128)S(1)}, u32[]{:S(2)}, u32[]{:S(2)}) collective-permute-start(f32[104,512]{1,0:T(8,128)S(1)} %shard_map.81.refs_5_.refs_0_.refs_1_), channel_id=1, source_target_pairs={{0,1},{1,0},{2,3},{3,2},{4,5},{5,4},{6,7},{7,6},{8,9},{9,8},{10,11... | collective-permute-start | bytes 638984 | tf_op jit(solution)/shard_map/ppermute | solution.py:75
  88.8 0.8 shard_map.82.refs_1_.refs_4_
  89.6 1.6 %collective-permute-done.25.refs_3_ = f32[96,512]{1,0:T(8,128)S(1)} collective-permute-done((f32[96,512]{1,0:T(8,128)S(1)}, f32[96,512]{1,0:T(8,128)S(1)}, u32[]{:S(2)}, u32[]{:S(2)}) %collective-permute-start.25) | collective-permute-done | bytes 196640 | tf_op jit(solution)/shard_map/ppermute | solution.py:75
  91.3 4.7 %collective-permute-start.27 = (f32[96,512]{1,0:T(8,128)S(1)}, f32[96,512]{1,0:T(8,128)S(1)}, u32[]{:S(2)}, u32[]{:S(2)}) collective-permute-start(f32[96,512]{1,0:T(8,128)S(1)} %shard_map.83.refs_4_.refs_2_.refs_0_), channel_id=1, source_target_pairs={{0,1},{1,0},{2,3},{3,2},{4,5},{5,4},{6,7},{7,6},{8,9},{9,8},{10,11... | collective-permute-start | bytes 589832 | tf_op jit(solution)/shard_map/ppermute | solution.py:75
  95.9 0.6 shard_map.84
  97.1 0.6 shard_map.85.refs_0_.refs_3_
  98.2 1.5 %collective-permute-start.33 = (f32[104,640]{1,0:T(8,128)S(1)}, f32[104,640]{1,0:T(8,128)S(1)}, u32[]{:S(2)}, u32[]{:S(2)}) collective-permute-start(f32[104,640]{1,0:T(8,128)S(1)} %shard_map.86.refs_5_.refs_0_), channel_id=1, source_target_pairs={{0,8},{4,12},{8,0},{12,4},{1,9},{5,13},{9,1},{13,5},{2,10},{6,14},... | collective-permute-start | bytes 798728 | tf_op jit(solution)/shard_map/ppermute | solution.py:75
  99.7 1.4 %collective-permute-done.27.refs_4_.refs_1_ = f32[96,512]{1,0:T(8,128)S(1)} collective-permute-done((f32[96,512]{1,0:T(8,128)S(1)}, f32[96,512]{1,0:T(8,128)S(1)}, u32[]{:S(2)}, u32[]{:S(2)}) %collective-permute-start.27) | collective-permute-done | bytes 196640 | tf_op jit(solution)/shard_map/ppermute | solution.py:75
  101.1 1.1 shard_map.87
  102.2 0.6 shard_map.88.refs_4_
  103.3 0.6 shard_map.89.refs_5_.refs_0_
  103.9 0.6 shard_map.90.refs_2_
  104.6 1.5 %collective-permute-start.31 = (f32[136,128]{1,0:T(8,128)S(1)}, f32[136,128]{1,0:T(8,128)S(1)}, u32[]{:S(2)}, u32[]{:S(2)}) collective-permute-start(f32[136,128]{1,0:T(8,128)S(1)} %shard_map.91.refs_2_.refs_0_), channel_id=1, source_target_pairs={{0,8},{4,12},{8,0},{12,4},{1,9},{5,13},{9,1},{13,5},{2,10},{6,14},... | collective-permute-start | bytes 208904 | tf_op jit(solution)/shard_map/ppermute | solution.py:75
  106.1 0.8 collective-permute-done.33.refs_1_
  106.9 1.5 %collective-permute-start.35 = (f32[96,640]{1,0:T(8,128)S(1)}, f32[96,640]{1,0:T(8,128)S(1)}, u32[]{:S(2)}, u32[]{:S(2)}) collective-permute-start(f32[96,640]{1,0:T(8,128)S(1)} %shard_map.93.refs_2_), channel_id=1, source_target_pairs={{0,8},{4,12},{8,0},{12,4},{1,9},{5,13},{9,1},{13,5},{2,10},{6,14},... | collective-permute-start | bytes 737288 | tf_op jit(solution)/shard_map/ppermute | solution.py:75
  109.0 1.2 %collective-permute-done.34.refs_2_ = f32[136,128]{1,0:T(8,128)S(1)} collective-permute-done((f32[136,128]{1,0:T(8,128)S(1)}, f32[136,128]{1,0:T(8,128)S(1)}, u32[]{:S(2)}, u32[]{:S(2)}) %collective-permute-start.34) | collective-permute-done | bytes 69664 | tf_op jit(solution)/shard_map/ppermute | solution.py:75
  110.3 0.9 shard_map.95.refs_5_.refs_1_
  111.4 0.9 shard_map.96.refs_1_.refs_4_
  112.3 2.0 %collective-permute-done.35.refs_3_ = f32[96,640]{1,0:T(8,128)S(1)} collective-permute-done((f32[96,640]{1,0:T(8,128)S(1)}, f32[96,640]{1,0:T(8,128)S(1)}, u32[]{:S(2)}, u32[]{:S(2)}) %collective-permute-start.35) | collective-permute-done | bytes 245792 | tf_op jit(solution)/shard_map/ppermute | solution.py:75
  114.5 0.9 copy.5
  115.4 0.6 collective-permute-done.37.refs_4_
  116.0 0.6 shard_map.98
  116.6 1.0 copy.6
  (66 shorter events, 6.4 us)
Async XLA Ops:
  0.6 9.8 %copy-start = (f32[1024,200]{0,1:T(8,128)S(1)}, f32[1024,200]{0,1:T(8,128)}, u32[]{:S(2)}) copy-start(f32[1024,200]{0,1:T(8,128)} %param.4) | copy-start | bytes 2457604
  5.3 10.7 %collective-permute-start.3 = (f32[104,512]{1,0:T(8,128)S(1)}, f32[104,512]{1,0:T(8,128)S(1)}, u32[]{:S(2)}, u32[]{:S(2)}) collective-permute-start(f32[104,512]{1,0:T(8,128)S(1)} %get-tuple-element.34), channel_id=1, source_target_pairs={{0,1},{1,0},{2,3},{3,2},{4,5},{5,4},{6,7},{7,6},{8,9},{9,8},{10,11... | collective-permute-start | bytes 638984 | tf_op jit(solution)/shard_map/ppermute | solution.py:75
  8.4 7.6 %collective-permute-start = (f32[136,128]{1,0:T(8,128)S(1)}, f32[136,128]{1,0:T(8,128)S(1)}, u32[]{:S(2)}, u32[]{:S(2)}) collective-permute-start(f32[136,128]{1,0:T(8,128)S(1)} %get-tuple-element.25.refs_7_.refs_0_), channel_id=1, source_target_pairs={{0,1},{1,0},{2,3},{3,2},{4,5},{5,4},{6,7},{7,6},{8,9},{9,8},{10,11... | collective-permute-start | bytes 208904 | tf_op jit(solution)/shard_map/ppermute | solution.py:75
  8.4 11.8 %collective-permute-start.2 = (f32[96,512]{1,0:T(8,128)S(1)}, f32[96,512]{1,0:T(8,128)S(1)}, u32[]{:S(2)}, u32[]{:S(2)}) collective-permute-start(f32[96,512]{1,0:T(8,128)S(1)} %get-tuple-element.32), channel_id=1, source_target_pairs={{0,1},{1,0},{2,3},{3,2},{4,5},{5,4},{6,7},{7,6},{8,9},{9,8},{10,11... | collective-permute-start | bytes 589832 | tf_op jit(solution)/shard_map/ppermute | solution.py:75
  16.0 13.3 %collective-permute-start.5 = (f32[104,512]{1,0:T(8,128)S(1)}, f32[104,512]{1,0:T(8,128)S(1)}, u32[]{:S(2)}, u32[]{:S(2)}) collective-permute-start(f32[104,512]{1,0:T(8,128)S(1)} %shard_map.53.refs_2_.refs_5_), channel_id=1, source_target_pairs={{0,3},{1,2},{2,1},{3,0},{4,7},{5,6},{6,5},{7,4},{8,11},{9,10},{10,... | collective-permute-start | bytes 638984 | tf_op jit(solution)/shard_map/ppermute | solution.py:75
  20.1 7.5 %collective-permute-start.1 = (f32[136,128]{1,0:T(8,128)S(1)}, f32[136,128]{1,0:T(8,128)S(1)}, u32[]{:S(2)}, u32[]{:S(2)}) collective-permute-start(f32[136,128]{1,0:T(8,128)S(1)} %shard_map.52.refs_2_.refs_0_), channel_id=1, source_target_pairs={{0,3},{1,2},{2,1},{3,0},{4,7},{5,6},{6,5},{7,4},{8,11},{9,10},{10,... | collective-permute-start | bytes 208904 | tf_op jit(solution)/shard_map/ppermute | solution.py:75
  27.7 1.7 %collective-permute-start.4 = (f32[136,128]{1,0:T(8,128)S(1)}, f32[136,128]{1,0:T(8,128)S(1)}, u32[]{:S(2)}, u32[]{:S(2)}) collective-permute-start(f32[136,128]{1,0:T(8,128)S(1)} %shard_map.55.refs_1_.refs_7_), channel_id=1, source_target_pairs={{0,4},{4,0},{8,12},{12,8},{1,5},{5,1},{9,13},{13,9},{2,6},{6,2},{1... | collective-permute-start | bytes 208904 | tf_op jit(solution)/shard_map/ppermute | solution.py:75
  27.8 9.6 %collective-permute-start.6 = (f32[96,512]{1,0:T(8,128)S(1)}, f32[96,512]{1,0:T(8,128)S(1)}, u32[]{:S(2)}, u32[]{:S(2)}) collective-permute-start(f32[96,512]{1,0:T(8,128)S(1)} %shard_map.54.refs_2_), channel_id=1, source_target_pairs={{0,3},{1,2},{2,1},{3,0},{4,7},{5,6},{6,5},{7,4},{8,11},{9,10},{10,... | collective-permute-start | bytes 589832 | tf_op jit(solution)/shard_map/ppermute | solution.py:75
  30.2 11.6 %collective-permute-start.7 = (f32[104,512]{1,0:T(8,128)S(1)}, f32[104,512]{1,0:T(8,128)S(1)}, u32[]{:S(2)}, u32[]{:S(2)}) collective-permute-start(f32[104,512]{1,0:T(8,128)S(1)} %shard_map.56.refs_5_.refs_0_.refs_1_.refs_3_), channel_id=1, source_target_pairs={{0,1},{1,0},{2,3},{3,2},{4,5},{5,4},{6,7},{7,6},{8,9},{9,8},{10,11... | collective-permute-start | bytes 638984 | tf_op jit(solution)/shard_map/ppermute | solution.py:75
  37.4 9.5 %collective-permute-start.8 = (f32[96,512]{1,0:T(8,128)S(1)}, f32[96,512]{1,0:T(8,128)S(1)}, u32[]{:S(2)}, u32[]{:S(2)}) collective-permute-start(f32[96,512]{1,0:T(8,128)S(1)} %shard_map.58.refs_4_.refs_2_.refs_0_), channel_id=1, source_target_pairs={{0,1},{1,0},{2,3},{3,2},{4,5},{5,4},{6,7},{7,6},{8,9},{9,8},{10,11... | collective-permute-start | bytes 589832 | tf_op jit(solution)/shard_map/ppermute | solution.py:75
  42.4 1.6 %collective-permute-start.10 = (f32[56,640]{1,0:T(8,128)S(1)}, f32[56,640]{1,0:T(8,128)S(1)}, u32[]{:S(2)}, u32[]{:S(2)}) collective-permute-start(f32[56,640]{1,0:T(8,128)S(1)} %get-tuple-element.41), channel_id=1, source_target_pairs={{0,4},{4,0},{8,12},{12,8},{1,5},{5,1},{9,13},{13,9},{2,6},{6,2},{1... | collective-permute-start | bytes 430088 | tf_op jit(solution)/shard_map/ppermute | solution.py:75
  42.4 1.5 %collective-permute-start.9 = (f32[48,640]{1,0:T(8,128)S(1)}, f32[48,640]{1,0:T(8,128)S(1)}, u32[]{:S(2)}, u32[]{:S(2)}) collective-permute-start(f32[48,640]{1,0:T(8,128)S(1)} %get-tuple-element.40.refs_4_), channel_id=1, source_target_pairs={{0,4},{4,0},{8,12},{12,8},{1,5},{5,1},{9,13},{13,9},{2,6},{6,2},{1... | collective-permute-start | bytes 368648 | tf_op jit(solution)/shard_map/ppermute | solution.py:75
  44.0 8.7 %collective-permute-start.14 = (f32[104,640]{1,0:T(8,128)S(1)}, f32[104,640]{1,0:T(8,128)S(1)}, u32[]{:S(2)}, u32[]{:S(2)}) collective-permute-start(f32[104,640]{1,0:T(8,128)S(1)} %shard_map.61.refs_5_.refs_0_), channel_id=1, source_target_pairs={{0,8},{4,12},{8,0},{12,4},{1,9},{5,13},{9,1},{13,5},{2,10},{6,14},... | collective-permute-start | bytes 798728 | tf_op jit(solution)/shard_map/ppermute | solution.py:75
  48.6 4.1 %collective-permute-start.13 = (f32[96,640]{1,0:T(8,128)S(1)}, f32[96,640]{1,0:T(8,128)S(1)}, u32[]{:S(2)}, u32[]{:S(2)}) collective-permute-start(f32[96,640]{1,0:T(8,128)S(1)} %shard_map.63.refs_4_), channel_id=1, source_target_pairs={{0,4},{4,0},{8,12},{12,8},{1,5},{5,1},{9,13},{13,9},{2,6},{6,2},{1... | collective-permute-start | bytes 737288 | tf_op jit(solution)/shard_map/ppermute | solution.py:75
  48.7 1.6 %collective-permute-start.11 = (f32[136,128]{1,0:T(8,128)S(1)}, f32[136,128]{1,0:T(8,128)S(1)}, u32[]{:S(2)}, u32[]{:S(2)}) collective-permute-start(f32[136,128]{1,0:T(8,128)S(1)} %get-tuple-element.43.refs_4_), channel_id=1, source_target_pairs={{0,4},{4,0},{8,12},{12,8},{1,5},{5,1},{9,13},{13,9},{2,6},{6,2},{1... | collective-permute-start | bytes 208904 | tf_op jit(solution)/shard_map/ppermute | solution.py:75
  50.3 4.4 %collective-permute-start.12 = (f32[136,128]{1,0:T(8,128)S(1)}, f32[136,128]{1,0:T(8,128)S(1)}, u32[]{:S(2)}, u32[]{:S(2)}) collective-permute-start(f32[136,128]{1,0:T(8,128)S(1)} %shard_map.65.refs_2_.refs_0_), channel_id=1, source_target_pairs={{0,8},{4,12},{8,0},{12,4},{1,9},{5,13},{9,1},{13,5},{2,10},{6,14},... | collective-permute-start | bytes 208904 | tf_op jit(solution)/shard_map/ppermute | solution.py:75
  52.8 7.4 %collective-permute-start.16 = (f32[96,640]{1,0:T(8,128)S(1)}, f32[96,640]{1,0:T(8,128)S(1)}, u32[]{:S(2)}, u32[]{:S(2)}) collective-permute-start(f32[96,640]{1,0:T(8,128)S(1)} %shard_map.67.refs_2_), channel_id=1, source_target_pairs={{0,8},{4,12},{8,0},{12,4},{1,9},{5,13},{9,1},{13,5},{2,10},{6,14},... | collective-permute-start | bytes 737288 | tf_op jit(solution)/shard_map/ppermute | solution.py:75
  54.7 1.3 %collective-permute-start.15 = (f32[136,128]{1,0:T(8,128)S(1)}, f32[136,128]{1,0:T(8,128)S(1)}, u32[]{:S(2)}, u32[]{:S(2)}) collective-permute-start(f32[136,128]{1,0:T(8,128)S(1)} %shard_map.68.refs_1_.refs_6_), channel_id=1, source_target_pairs={{0,4},{4,0},{8,12},{12,8},{1,5},{5,1},{9,13},{13,9},{2,6},{6,2},{1... | collective-permute-start | bytes 208904 | tf_op jit(solution)/shard_map/ppermute | solution.py:75
  56.9 3.4 %collective-permute-start.17 = (f32[104,640]{1,0:T(8,128)S(1)}, f32[104,640]{1,0:T(8,128)S(1)}, u32[]{:S(2)}, u32[]{:S(2)}) collective-permute-start(f32[104,640]{1,0:T(8,128)S(1)} %shard_map.69.refs_5_.refs_0_.refs_1_.refs_3_), channel_id=1, source_target_pairs={{0,4},{4,0},{8,12},{12,8},{1,5},{5,1},{9,13},{13,9},{2,6},{6,2},{1... | collective-permute-start | bytes 798728 | tf_op jit(solution)/shard_map/ppermute | solution.py:75
  60.3 3.5 %collective-permute-start.18 = (f32[96,640]{1,0:T(8,128)S(1)}, f32[96,640]{1,0:T(8,128)S(1)}, u32[]{:S(2)}, u32[]{:S(2)}) collective-permute-start(f32[96,640]{1,0:T(8,128)S(1)} %shard_map.71.refs_4_.refs_2_.refs_0_), channel_id=1, source_target_pairs={{0,4},{4,0},{8,12},{12,8},{1,5},{5,1},{9,13},{13,9},{2,6},{6,2},{1... | collective-permute-start | bytes 737288 | tf_op jit(solution)/shard_map/ppermute | solution.py:75
  61.3 9.6 %collective-permute-start.22 = (f32[104,512]{1,0:T(8,128)S(1)}, f32[104,512]{1,0:T(8,128)S(1)}, u32[]{:S(2)}, u32[]{:S(2)}) collective-permute-start(f32[104,512]{1,0:T(8,128)S(1)} %shard_map.72.refs_4_), channel_id=1, source_target_pairs={{0,1},{1,0},{2,3},{3,2},{4,5},{5,4},{6,7},{7,6},{8,9},{9,8},{10,11... | collective-permute-start | bytes 638984 | tf_op jit(solution)/shard_map/ppermute | solution.py:75
  65.1 5.8 %collective-permute-start.19 = (f32[136,128]{1,0:T(8,128)S(1)}, f32[136,128]{1,0:T(8,128)S(1)}, u32[]{:S(2)}, u32[]{:S(2)}) collective-permute-start(f32[136,128]{1,0:T(8,128)S(1)} %shard_map.74.refs_4_.refs_0_), channel_id=1, source_target_pairs={{0,1},{1,0},{2,3},{3,2},{4,5},{5,4},{6,7},{7,6},{8,9},{9,8},{10,11... | collective-permute-start | bytes 208904 | tf_op jit(solution)/shard_map/ppermute | solution.py:75
  66.6 8.3 %collective-permute-start.21 = (f32[96,512]{1,0:T(8,128)S(1)}, f32[96,512]{1,0:T(8,128)S(1)}, u32[]{:S(2)}, u32[]{:S(2)}) collective-permute-start(f32[96,512]{1,0:T(8,128)S(1)} %shard_map.75.refs_4_), channel_id=1, source_target_pairs={{0,1},{1,0},{2,3},{3,2},{4,5},{5,4},{6,7},{7,6},{8,9},{9,8},{10,11... | collective-permute-start | bytes 589832 | tf_op jit(solution)/shard_map/ppermute | solution.py:75
  71.0 13.4 %collective-permute-start.24 = (f32[104,512]{1,0:T(8,128)S(1)}, f32[104,512]{1,0:T(8,128)S(1)}, u32[]{:S(2)}, u32[]{:S(2)}) collective-permute-start(f32[104,512]{1,0:T(8,128)S(1)} %shard_map.78.refs_2_.refs_5_), channel_id=1, source_target_pairs={{0,3},{1,2},{2,1},{3,0},{4,7},{5,6},{6,5},{7,4},{8,11},{9,10},{10,... | collective-permute-start | bytes 638984 | tf_op jit(solution)/shard_map/ppermute | solution.py:75
  72.5 9.3 %collective-permute-start.20 = (f32[136,128]{1,0:T(8,128)S(1)}, f32[136,128]{1,0:T(8,128)S(1)}, u32[]{:S(2)}, u32[]{:S(2)}) collective-permute-start(f32[136,128]{1,0:T(8,128)S(1)} %shard_map.77.refs_2_.refs_0_), channel_id=1, source_target_pairs={{0,3},{1,2},{2,1},{3,0},{4,7},{5,6},{6,5},{7,4},{8,11},{9,10},{10,... | collective-permute-start | bytes 208904 | tf_op jit(solution)/shard_map/ppermute | solution.py:75
  81.9 2.5 %collective-permute-start.23 = (f32[136,128]{1,0:T(8,128)S(1)}, f32[136,128]{1,0:T(8,128)S(1)}, u32[]{:S(2)}, u32[]{:S(2)}) collective-permute-start(f32[136,128]{1,0:T(8,128)S(1)} %shard_map.80.refs_1_.refs_7_), channel_id=1, source_target_pairs={{0,4},{4,0},{8,12},{12,8},{1,5},{5,1},{9,13},{13,9},{2,6},{6,2},{1... | collective-permute-start | bytes 208904 | tf_op jit(solution)/shard_map/ppermute | solution.py:75
  81.9 9.3 %collective-permute-start.25 = (f32[96,512]{1,0:T(8,128)S(1)}, f32[96,512]{1,0:T(8,128)S(1)}, u32[]{:S(2)}, u32[]{:S(2)}) collective-permute-start(f32[96,512]{1,0:T(8,128)S(1)} %shard_map.79.refs_2_), channel_id=1, source_target_pairs={{0,3},{1,2},{2,1},{3,0},{4,7},{5,6},{6,5},{7,4},{8,11},{9,10},{10,... | collective-permute-start | bytes 589832 | tf_op jit(solution)/shard_map/ppermute | solution.py:75
  85.2 10.8 %collective-permute-start.26 = (f32[104,512]{1,0:T(8,128)S(1)}, f32[104,512]{1,0:T(8,128)S(1)}, u32[]{:S(2)}, u32[]{:S(2)}) collective-permute-start(f32[104,512]{1,0:T(8,128)S(1)} %shard_map.81.refs_5_.refs_0_.refs_1_), channel_id=1, source_target_pairs={{0,1},{1,0},{2,3},{3,2},{4,5},{5,4},{6,7},{7,6},{8,9},{9,8},{10,11... | collective-permute-start | bytes 638984 | tf_op jit(solution)/shard_map/ppermute | solution.py:75
  91.3 9.8 %collective-permute-start.27 = (f32[96,512]{1,0:T(8,128)S(1)}, f32[96,512]{1,0:T(8,128)S(1)}, u32[]{:S(2)}, u32[]{:S(2)}) collective-permute-start(f32[96,512]{1,0:T(8,128)S(1)} %shard_map.83.refs_4_.refs_2_.refs_0_), channel_id=1, source_target_pairs={{0,1},{1,0},{2,3},{3,2},{4,5},{5,4},{6,7},{7,6},{8,9},{9,8},{10,11... | collective-permute-start | bytes 589832 | tf_op jit(solution)/shard_map/ppermute | solution.py:75
  96.5 1.6 %collective-permute-start.29 = (f32[56,640]{1,0:T(8,128)S(1)}, f32[56,640]{1,0:T(8,128)S(1)}, u32[]{:S(2)}, u32[]{:S(2)}) collective-permute-start(f32[56,640]{1,0:T(8,128)S(1)} %get-tuple-element.45), channel_id=1, source_target_pairs={{0,4},{4,0},{8,12},{12,8},{1,5},{5,1},{9,13},{13,9},{2,6},{6,2},{1... | collective-permute-start | bytes 430088 | tf_op jit(solution)/shard_map/ppermute | solution.py:75
  96.6 1.5 %collective-permute-start.28 = (f32[48,640]{1,0:T(8,128)S(1)}, f32[48,640]{1,0:T(8,128)S(1)}, u32[]{:S(2)}, u32[]{:S(2)}) collective-permute-start(f32[48,640]{1,0:T(8,128)S(1)} %get-tuple-element.44.refs_4_), channel_id=1, source_target_pairs={{0,4},{4,0},{8,12},{12,8},{1,5},{5,1},{9,13},{13,9},{2,6},{6,2},{1... | collective-permute-start | bytes 368648 | tf_op jit(solution)/shard_map/ppermute | solution.py:75
  98.2 8.7 %collective-permute-start.33 = (f32[104,640]{1,0:T(8,128)S(1)}, f32[104,640]{1,0:T(8,128)S(1)}, u32[]{:S(2)}, u32[]{:S(2)}) collective-permute-start(f32[104,640]{1,0:T(8,128)S(1)} %shard_map.86.refs_5_.refs_0_), channel_id=1, source_target_pairs={{0,8},{4,12},{8,0},{12,4},{1,9},{5,13},{9,1},{13,5},{2,10},{6,14},... | collective-permute-start | bytes 798728 | tf_op jit(solution)/shard_map/ppermute | solution.py:75
  102.8 4.1 %collective-permute-start.32 = (f32[96,640]{1,0:T(8,128)S(1)}, f32[96,640]{1,0:T(8,128)S(1)}, u32[]{:S(2)}, u32[]{:S(2)}) collective-permute-start(f32[96,640]{1,0:T(8,128)S(1)} %shard_map.88.refs_4_), channel_id=1, source_target_pairs={{0,4},{4,0},{8,12},{12,8},{1,5},{5,1},{9,13},{13,9},{2,6},{6,2},{1... | collective-permute-start | bytes 737288 | tf_op jit(solution)/shard_map/ppermute | solution.py:75
  102.8 1.7 %collective-permute-start.30 = (f32[136,128]{1,0:T(8,128)S(1)}, f32[136,128]{1,0:T(8,128)S(1)}, u32[]{:S(2)}, u32[]{:S(2)}) collective-permute-start(f32[136,128]{1,0:T(8,128)S(1)} %get-tuple-element.46.refs_4_), channel_id=1, source_target_pairs={{0,4},{4,0},{8,12},{12,8},{1,5},{5,1},{9,13},{13,9},{2,6},{6,2},{1... | collective-permute-start | bytes 208904 | tf_op jit(solution)/shard_map/ppermute | solution.py:75
  104.6 4.4 %collective-permute-start.31 = (f32[136,128]{1,0:T(8,128)S(1)}, f32[136,128]{1,0:T(8,128)S(1)}, u32[]{:S(2)}, u32[]{:S(2)}) collective-permute-start(f32[136,128]{1,0:T(8,128)S(1)} %shard_map.91.refs_2_.refs_0_), channel_id=1, source_target_pairs={{0,8},{4,12},{8,0},{12,4},{1,9},{5,13},{9,1},{13,5},{2,10},{6,14},... | collective-permute-start | bytes 208904 | tf_op jit(solution)/shard_map/ppermute | solution.py:75
  106.9 7.4 %collective-permute-start.35 = (f32[96,640]{1,0:T(8,128)S(1)}, f32[96,640]{1,0:T(8,128)S(1)}, u32[]{:S(2)}, u32[]{:S(2)}) collective-permute-start(f32[96,640]{1,0:T(8,128)S(1)} %shard_map.93.refs_2_), channel_id=1, source_target_pairs={{0,8},{4,12},{8,0},{12,4},{1,9},{5,13},{9,1},{13,5},{2,10},{6,14},... | collective-permute-start | bytes 737288 | tf_op jit(solution)/shard_map/ppermute | solution.py:75
  109.0 1.3 %collective-permute-start.34 = (f32[136,128]{1,0:T(8,128)S(1)}, f32[136,128]{1,0:T(8,128)S(1)}, u32[]{:S(2)}, u32[]{:S(2)}) collective-permute-start(f32[136,128]{1,0:T(8,128)S(1)} %shard_map.94.refs_1_.refs_6_), channel_id=1, source_target_pairs={{0,4},{4,0},{8,12},{12,8},{1,5},{5,1},{9,13},{13,9},{2,6},{6,2},{1... | collective-permute-start | bytes 208904 | tf_op jit(solution)/shard_map/ppermute | solution.py:75
  111.2 4.2 %collective-permute-start.36 = (f32[104,640]{1,0:T(8,128)S(1)}, f32[104,640]{1,0:T(8,128)S(1)}, u32[]{:S(2)}, u32[]{:S(2)}) collective-permute-start(f32[104,640]{1,0:T(8,128)S(1)} %shard_map.95.refs_5_.refs_1_), channel_id=1, source_target_pairs={{0,4},{4,0},{8,12},{12,8},{1,5},{5,1},{9,13},{13,9},{2,6},{6,2},{1... | collective-permute-start | bytes 798728 | tf_op jit(solution)/shard_map/ppermute | solution.py:75
  114.4 1.6 %collective-permute-start.37 = (f32[96,640]{1,0:T(8,128)S(1)}, f32[96,640]{1,0:T(8,128)S(1)}, u32[]{:S(2)}, u32[]{:S(2)}) collective-permute-start(f32[96,640]{1,0:T(8,128)S(1)} %shard_map.97.refs_2_.refs_5_), channel_id=1, source_target_pairs={{0,4},{4,0},{8,12},{12,8},{1,5},{5,1},{9,13},{13,9},{2,6},{6,2},{1... | collective-permute-start | bytes 737288 | tf_op jit(solution)/shard_map/ppermute | solution.py:75

commit v8 on v7

--- a/solution.py
+++ b/solution.py
@@ -242,7 +242,7 @@
             for start, n, ref in zip(starts, sizes, refs):
                 ref[...] = a[start : start + n]
 
-        def prepare(where_ref, p_ref, counts_ref, g_ref, *refs):
+        def prepare(where_ref, p_ref, counts_ref, *refs):
             s_refs, a_refs, b_refs = [refs[i * n_chunks : (i + 1) * n_chunks] for i in range(3)]
             x0, x1, p, buffer, p_sem, sems = refs[3 * n_chunks :]
             copy = pltpu.make_async_copy(p_ref, p, p_sem)
@@ -252,28 +252,29 @@
             own, other = halves(p[...], where_ref[0] == 1, columns)
             scatter(own, a_refs)
             scatter(other, b_refs)
-            g_ref[...] = share(packed_gram([own, other]), where_ref[0] == 0)
             convert(copies, where_ref[0], (x0, x1), buffer)
             scatter(dot2(own, x0[...], 1, 1) + dot2(other, x1[...], 1, 1), s_refs)
 
         def load_own(where_ref, counts_ref, *refs):
             a_refs, b_refs = refs[:n_chunks], refs[n_chunks : 2 * n_chunks]
             u_ref, *refs = refs[2 * n_chunks :]
-            x0, x1, *refs = refs
+            g_ref, x0, x1, *refs = refs
             k_refs, u_refs, (buffer, sems) = refs[:n_chunks], refs[n_chunks : 2 * n_chunks], refs[2 * n_chunks :]
             copies = load(where_ref[1] * rows, counts_ref, buffer, sems)
+            own, other = stacked(a_refs), stacked(b_refs)
+            g_ref[...] = share(packed_gram([own, other]), where_ref[0] == 0)
             mine, _ = halves(u_ref[...], where_ref[1] == 1, rows)
             scatter(mine, u_refs)
             convert(copies, where_ref[0], (x0, x1), buffer)
-            scatter(dot2(stacked(a_refs), x0[...], 1, 1) + dot2(stacked(b_refs), x1[...], 1, 1), k_refs)
+            scatter(dot2(own, x0[...], 1, 1) + dot2(other, x1[...], 1, 1), k_refs)
 
         half_x = [jax.ShapeDtypeStruct((rows, columns), BF16)] * 2
         buffer = pltpu.VMEM((pieces, piece, n_genes), jnp.int32)
         sems = pltpu.SemaphoreType.DMA((pieces,))
         flops = 4 * k * rows * n_genes
-        gram_p, *rest = chain(
+        rest = chain(
             prepare,
-            [(grows, packed[1])] + [(n, rows) for n in sizes] + [(n, columns) for n in sizes] * 2 + half_x,
+            [(n, rows) for n in sizes] + [(n, columns) for n in sizes] * 2 + half_x,
             where,
             pltpu.with_memory_space_constraint(program_init, pltpu.HBM),
             pltpu.with_memory_space_constraint(counts, pltpu.HBM),
@@ -283,11 +284,10 @@
         )
         sends, program_own, program_other = [list(rest[i * n_chunks : (i + 1) * n_chunks]) for i in range(3)]
         x_other = list(rest[3 * n_chunks :])
-        gram_near = exchange(gram_p, "gene", genes, 1)
         nears = [exchange(a, "gene", genes, 1) for a in sends]
-        x0, x1, *rest = chain(
+        gram_p, x0, x1, *rest = chain(
             load_own,
-            half_x + [(n, rows) for n in sizes] * 2,
+            [(grows, packed[1])] + half_x + [(n, rows) for n in sizes] * 2,
             where,
             pltpu.with_memory_space_constraint(counts, pltpu.HBM),
             *program_own,
@@ -299,6 +299,7 @@
         )
         x = [[x0, x1], x_other]
         keeps, usage_own = rest[:n_chunks], rest[n_chunks:]
+        gram_near = exchange(gram_p, "gene", genes, 1)
     else:
 
         def at(a, which, axis):

time: 118 us -> 117 us (level)
  transfers between devices with their start and end apart: 38 -> 38, of which waited for: 20 -> 21; matrix products, arithmetic and copies ran while one was open for 1% -> 1% of each run, Pallas kernels for 20% -> 21%
where the time goes in v8:
time: 117 us
  starting transfers between devices  49.4 us (42%)
  waiting for transfers between devices  36.2 us (31%)
  Pallas kernels  28.7 us (25%)
  local copies, waits for them, and re-layouts  1.86 us (2%)
    ppermute x38, starting transfers between devices, exchange(): return lax.ppermute(a, axis, [(i, i ^ flip) for i in range(size)])  49.4 us
    ppermute x38, waiting for transfers between devices, exchange(): return lax.ppermute(a, axis, [(i, i ^ flip) for i in range(size)])  36.2 us
    pallas_call x49, Pallas kernels, __call__(): pl.pallas_call(run, out_shape=[pltpu.VMEM(s.shape, s.dtype) for s in shap...  28.7 us
  transfers between devices with their start and end apart: 38, of which 21 were waited for; matrix products, arithmetic and copies ran while one was open for 1% of the time, Pallas kernels for 21%

profile of v8, /device:TPU:0, one launch (start us, length us, event | category | flops | bytes accessed | tf_op | source)
XLA Modules:
  0.0 117.3 jit_solution(11402116873442618890)
XLA Ops:
  0.7 3.6 %shard_map.50 = (f32[104,512]{1,0:T(8,128)S(1)}, f32[96,512]{1,0:T(8,128)S(1)}, f32[104,640]{1,0:T(8,128)S(1)}, f32[96,640]{1,0:T(8,128)S(1)}, f32[104,640]{1,0:...) custom-call(s32[2]{0:T(128)S(1)} %pad_add_fusion.refs_0_, ...), custom_call_target="tpu_custom_call" | custom-call | flops 524288000 | bytes 10321928 | tf_op jit(solution)/shard_map/pallas_call | solution.py:61
  4.4 3.1 %collective-permute-start.3 = (f32[104,512]{1,0:T(8,128)S(1)}, f32[104,512]{1,0:T(8,128)S(1)}, u32[]{:S(2)}, u32[]{:S(2)}) collective-permute-start(f32[104,512]{1,0:T(8,128)S(1)} %get-tuple-element.29.refs_7_), channel_id=1, source_target_pairs={{0,1},{1,0},{2,3},{3,2},{4,5},{5,4},{6,7},{7,6},{8,9},{9,8},{10,11... | collective-permute-start | bytes 638984 | tf_op jit(solution)/shard_map/ppermute | solution.py:75
  7.5 4.3 %shard_map.51 = (f32[136,128]{1,0:T(8,128)S(1)}, bf16[512,640]{1,0:T(8,128)(2,1)S(1)}, bf16[512,640]{1,0:T(8,128)(2,1)S(1)}, f32[104,512]{1,0:T(8,128)S(1)}, f32...) custom-call(s32[2]{0:T(128)S(1)} %pad_add_fusion.refs_0_, s32[1024,1280]{1,0:T(8,128)} %refs_1_.3, ...), custom_call_target="tpu_custom_call" | custom-call | flops 524288000 | bytes 10596360 | tf_op jit(solution)/shard_map/pallas_call | solution.py:61
  11.9 2.0 %collective-permute-start.2 = (f32[96,512]{1,0:T(8,128)S(1)}, f32[96,512]{1,0:T(8,128)S(1)}, u32[]{:S(2)}, u32[]{:S(2)}) collective-permute-start(f32[96,512]{1,0:T(8,128)S(1)} %get-tuple-element.32), channel_id=1, source_target_pairs={{0,1},{1,0},{2,3},{3,2},{4,5},{5,4},{6,7},{7,6},{8,9},{9,8},{10,11... | collective-permute-start | bytes 589832 | tf_op jit(solution)/shard_map/ppermute | solution.py:75
  13.9 3.1 %collective-permute-done.refs_1_ = f32[136,128]{1,0:T(8,128)S(1)} collective-permute-done((f32[136,128]{1,0:T(8,128)S(1)}, f32[136,128]{1,0:T(8,128)S(1)}, u32[]{:S(2)}, u32[]{:S(2)}) %collective-permute-start) | collective-permute-done | bytes 69664 | tf_op jit(solution)/shard_map/ppermute | solution.py:75
  17.1 2.5 %collective-permute-start.5 = (f32[104,512]{1,0:T(8,128)S(1)}, f32[104,512]{1,0:T(8,128)S(1)}, u32[]{:S(2)}, u32[]{:S(2)}) collective-permute-start(f32[104,512]{1,0:T(8,128)S(1)} %shard_map.53.refs_2_.refs_5_), channel_id=1, source_target_pairs={{0,3},{1,2},{2,1},{3,0},{4,7},{5,6},{6,5},{7,4},{8,11},{9,10},{10,... | collective-permute-start | bytes 638984 | tf_op jit(solution)/shard_map/ppermute | solution.py:75
  19.5 1.4 %collective-permute-start.1 = (f32[136,128]{1,0:T(8,128)S(1)}, f32[136,128]{1,0:T(8,128)S(1)}, u32[]{:S(2)}, u32[]{:S(2)}) collective-permute-start(f32[136,128]{1,0:T(8,128)S(1)} %shard_map.52.refs_2_.refs_0_), channel_id=1, source_target_pairs={{0,3},{1,2},{2,1},{3,0},{4,7},{5,6},{6,5},{7,4},{8,11},{9,10},{10,... | collective-permute-start | bytes 208904 | tf_op jit(solution)/shard_map/ppermute | solution.py:75
  21.0 7.0 %collective-permute-done.1.refs_1_ = f32[136,128]{1,0:T(8,128)S(1)} collective-permute-done((f32[136,128]{1,0:T(8,128)S(1)}, f32[136,128]{1,0:T(8,128)S(1)}, u32[]{:S(2)}, u32[]{:S(2)}) %collective-permute-start.1) | collective-permute-done | bytes 69664 | tf_op jit(solution)/shard_map/ppermute | solution.py:75
  28.1 1.0 collective-permute-start.6
  29.3 0.9 shard_map.56.refs_5_.refs_0_.refs_1_.refs_3_
  30.2 3.5 %collective-permute-start.7 = (f32[104,512]{1,0:T(8,128)S(1)}, f32[104,512]{1,0:T(8,128)S(1)}, u32[]{:S(2)}, u32[]{:S(2)}) collective-permute-start(f32[104,512]{1,0:T(8,128)S(1)} %shard_map.56.refs_5_.refs_0_.refs_1_.refs_3_), channel_id=1, source_target_pairs={{0,1},{1,0},{2,3},{3,2},{4,5},{5,4},{6,7},{7,6},{8,9},{9,8},{10,11... | collective-permute-start | bytes 638984 | tf_op jit(solution)/shard_map/ppermute | solution.py:75
  33.7 0.8 shard_map.57.refs_1_.refs_4_
  34.6 3.1 %collective-permute-done.6.refs_3_ = f32[96,512]{1,0:T(8,128)S(1)} collective-permute-done((f32[96,512]{1,0:T(8,128)S(1)}, f32[96,512]{1,0:T(8,128)S(1)}, u32[]{:S(2)}, u32[]{:S(2)}) %collective-permute-start.6) | collective-permute-done | bytes 196640 | tf_op jit(solution)/shard_map/ppermute | solution.py:75
  37.7 4.3 %collective-permute-start.8 = (f32[96,512]{1,0:T(8,128)S(1)}, f32[96,512]{1,0:T(8,128)S(1)}, u32[]{:S(2)}, u32[]{:S(2)}) collective-permute-start(f32[96,512]{1,0:T(8,128)S(1)} %shard_map.58.refs_4_.refs_2_.refs_0_), channel_id=1, source_target_pairs={{0,1},{1,0},{2,3},{3,2},{4,5},{5,4},{6,7},{7,6},{8,9},{9,8},{10,11... | collective-permute-start | bytes 589832 | tf_op jit(solution)/shard_map/ppermute | solution.py:75
  42.1 0.6 shard_map.59
  44.3 1.5 %collective-permute-start.14 = (f32[104,640]{1,0:T(8,128)S(1)}, f32[104,640]{1,0:T(8,128)S(1)}, u32[]{:S(2)}, u32[]{:S(2)}) collective-permute-start(f32[104,640]{1,0:T(8,128)S(1)} %shard_map.61.refs_5_.refs_0_), channel_id=1, source_target_pairs={{0,8},{4,12},{8,0},{12,4},{1,9},{5,13},{9,1},{13,5},{2,10},{6,14},... | collective-permute-start | bytes 798728 | tf_op jit(solution)/shard_map/ppermute | solution.py:75
  45.9 1.4 %collective-permute-done.8.refs_4_.refs_1_ = f32[96,512]{1,0:T(8,128)S(1)} collective-permute-done((f32[96,512]{1,0:T(8,128)S(1)}, f32[96,512]{1,0:T(8,128)S(1)}, u32[]{:S(2)}, u32[]{:S(2)}) %collective-permute-start.8) | collective-permute-done | bytes 196640 | tf_op jit(solution)/shard_map/ppermute | solution.py:75
  47.2 1.1 shard_map.62
  48.3 0.6 shard_map.63.refs_4_
  49.5 0.6 shard_map.64.refs_2_.refs_0_
  50.6 1.6 %collective-permute-start.12 = (f32[136,128]{1,0:T(8,128)S(1)}, f32[136,128]{1,0:T(8,128)S(1)}, u32[]{:S(2)}, u32[]{:S(2)}) collective-permute-start(f32[136,128]{1,0:T(8,128)S(1)} %shard_map.65.refs_2_.refs_0_), channel_id=1, source_target_pairs={{0,8},{4,12},{8,0},{12,4},{1,9},{5,13},{9,1},{13,5},{2,10},{6,14},... | collective-permute-start | bytes 208904 | tf_op jit(solution)/shard_map/ppermute | solution.py:75
  52.1 0.8 collective-permute-done.14.refs_1_
  53.1 1.6 %collective-permute-start.16 = (f32[96,640]{1,0:T(8,128)S(1)}, f32[96,640]{1,0:T(8,128)S(1)}, u32[]{:S(2)}, u32[]{:S(2)}) collective-permute-start(f32[96,640]{1,0:T(8,128)S(1)} %shard_map.67.refs_2_), channel_id=1, source_target_pairs={{0,8},{4,12},{8,0},{12,4},{1,9},{5,13},{9,1},{13,5},{2,10},{6,14},... | collective-permute-start | bytes 737288 | tf_op jit(solution)/shard_map/ppermute | solution.py:75
  55.0 1.2 %collective-permute-done.15.refs_2_ = f32[136,128]{1,0:T(8,128)S(1)} collective-permute-done((f32[136,128]{1,0:T(8,128)S(1)}, f32[136,128]{1,0:T(8,128)S(1)}, u32[]{:S(2)}, u32[]{:S(2)}) %collective-permute-start.15) | collective-permute-done | bytes 69664 | tf_op jit(solution)/shard_map/ppermute | solution.py:75
  56.3 0.9 shard_map.69.refs_5_.refs_0_.refs_1_.refs_3_
  57.4 0.9 shard_map.70.refs_1_.refs_4_
  58.3 2.2 %collective-permute-done.16.refs_3_ = f32[96,640]{1,0:T(8,128)S(1)} collective-permute-done((f32[96,640]{1,0:T(8,128)S(1)}, f32[96,640]{1,0:T(8,128)S(1)}, u32[]{:S(2)}, u32[]{:S(2)}) %collective-permute-start.16) | collective-permute-done | bytes 245792 | tf_op jit(solution)/shard_map/ppermute | solution.py:75
  60.7 0.9 shard_map.72.refs_4_
  61.6 1.6 %collective-permute-start.22 = (f32[104,512]{1,0:T(8,128)S(1)}, f32[104,512]{1,0:T(8,128)S(1)}, u32[]{:S(2)}, u32[]{:S(2)}) collective-permute-start(f32[104,512]{1,0:T(8,128)S(1)} %shard_map.72.refs_4_), channel_id=1, source_target_pairs={{0,1},{1,0},{2,3},{3,2},{4,5},{5,4},{6,7},{7,6},{8,9},{9,8},{10,11... | collective-permute-start | bytes 638984 | tf_op jit(solution)/shard_map/ppermute | solution.py:75
  63.2 0.9 shard_map.73.refs_5_.refs_0_
  64.1 1.2 %shard_map.74.refs_4_.refs_0_ = f32[136,128]{1,0:T(8,128)S(1)} custom-call(s32[2]{0:T(128)S(1)} %pad_add_fusion.refs_0_, f32[104,640]{1,0:T(8,128)S(1)} %shard_map.69.refs_5_.refs_0_.refs_1_.refs_3_, f32[96,640]{1,0:T(8,128)S(1)} %shard_map.71.refs_4_.refs_2_.refs_0_, f32[104,640]{1,0:T(8,128)S(1)} %collective-permute-done.17.refs_1_.refs_3_, ...), custom_call_target="tpu_custom_call" | custom-call | flops 307200000 | bytes 1093640 | tf_op jit(solution)/shard_map/pallas_call | solution.py:61
  65.4 0.6 collective-permute-start.19
  66.0 0.9 shard_map.75.refs_4_
  66.9 1.6 %collective-permute-start.21 = (f32[96,512]{1,0:T(8,128)S(1)}, f32[96,512]{1,0:T(8,128)S(1)}, u32[]{:S(2)}, u32[]{:S(2)}) collective-permute-start(f32[96,512]{1,0:T(8,128)S(1)} %shard_map.75.refs_4_), channel_id=1, source_target_pairs={{0,1},{1,0},{2,3},{3,2},{4,5},{5,4},{6,7},{7,6},{8,9},{9,8},{10,11... | collective-permute-start | bytes 589832 | tf_op jit(solution)/shard_map/ppermute | solution.py:75
  68.4 0.9 shard_map.76.refs_2_.refs_0_
  69.4 1.8 %collective-permute-done.19.refs_1_ = f32[136,128]{1,0:T(8,128)S(1)} collective-permute-done((f32[136,128]{1,0:T(8,128)S(1)}, f32[136,128]{1,0:T(8,128)S(1)}, u32[]{:S(2)}, u32[]{:S(2)}) %collective-permute-start.19) | collective-permute-done | bytes 69664 | tf_op jit(solution)/shard_map/ppermute | solution.py:75
  71.3 1.0 collective-permute-start.24
  72.3 2.9 %collective-permute-start.20 = (f32[136,128]{1,0:T(8,128)S(1)}, f32[136,128]{1,0:T(8,128)S(1)}, u32[]{:S(2)}, u32[]{:S(2)}) collective-permute-start(f32[136,128]{1,0:T(8,128)S(1)} %shard_map.77.refs_2_.refs_0_), channel_id=1, source_target_pairs={{0,3},{1,2},{2,1},{3,0},{4,7},{5,6},{6,5},{7,4},{8,11},{9,10},{10,... | collective-permute-start | bytes 208904 | tf_op jit(solution)/shard_map/ppermute | solution.py:75
  75.2 6.4 %collective-permute-done.20.refs_1_ = f32[136,128]{1,0:T(8,128)S(1)} collective-permute-done((f32[136,128]{1,0:T(8,128)S(1)}, f32[136,128]{1,0:T(8,128)S(1)}, u32[]{:S(2)}, u32[]{:S(2)}) %collective-permute-start.20) | collective-permute-done | bytes 69664 | tf_op jit(solution)/shard_map/ppermute | solution.py:75
  81.6 3.0 %collective-permute-start.25 = (f32[96,512]{1,0:T(8,128)S(1)}, f32[96,512]{1,0:T(8,128)S(1)}, u32[]{:S(2)}, u32[]{:S(2)}) collective-permute-start(f32[96,512]{1,0:T(8,128)S(1)} %shard_map.79.refs_2_), channel_id=1, source_target_pairs={{0,3},{1,2},{2,1},{3,0},{4,7},{5,6},{6,5},{7,4},{8,11},{9,10},{10,... | collective-permute-start | bytes 589832 | tf_op jit(solution)/shard_map/ppermute | solution.py:75
  84.6 0.9 shard_map.81.refs_5_.refs_0_.refs_1_
  85.5 3.6 %collective-permute-start.26 = (f32[104,512]{1,0:T(8,128)S(1)}, f32[104,512]{1,0:T(8,128)S(1)}, u32[]{:S(2)}, u32[]{:S(2)}) collective-permute-start(f32[104,512]{1,0:T(8,128)S(1)} %shard_map.81.refs_5_.refs_0_.refs_1_), channel_id=1, source_target_pairs={{0,1},{1,0},{2,3},{3,2},{4,5},{5,4},{6,7},{7,6},{8,9},{9,8},{10,11... | collective-permute-start | bytes 638984 | tf_op jit(solution)/shard_map/ppermute | solution.py:75
  89.1 0.8 shard_map.82.refs_1_.refs_4_
  90.0 1.0 collective-permute-done.25.refs_3_
  91.0 4.7 %collective-permute-start.27 = (f32[96,512]{1,0:T(8,128)S(1)}, f32[96,512]{1,0:T(8,128)S(1)}, u32[]{:S(2)}, u32[]{:S(2)}) collective-permute-start(f32[96,512]{1,0:T(8,128)S(1)} %shard_map.83.refs_4_.refs_2_.refs_0_), channel_id=1, source_target_pairs={{0,1},{1,0},{2,3},{3,2},{4,5},{5,4},{6,7},{7,6},{8,9},{9,8},{10,11... | collective-permute-start | bytes 589832 | tf_op jit(solution)/shard_map/ppermute | solution.py:75
  95.7 0.6 shard_map.84
  96.8 0.6 shard_map.85.refs_0_.refs_3_
  97.9 1.6 %collective-permute-start.33 = (f32[104,640]{1,0:T(8,128)S(1)}, f32[104,640]{1,0:T(8,128)S(1)}, u32[]{:S(2)}, u32[]{:S(2)}) collective-permute-start(f32[104,640]{1,0:T(8,128)S(1)} %shard_map.86.refs_5_.refs_0_), channel_id=1, source_target_pairs={{0,8},{4,12},{8,0},{12,4},{1,9},{5,13},{9,1},{13,5},{2,10},{6,14},... | collective-permute-start | bytes 798728 | tf_op jit(solution)/shard_map/ppermute | solution.py:75
  99.5 1.3 %collective-permute-done.27.refs_4_.refs_1_ = f32[96,512]{1,0:T(8,128)S(1)} collective-permute-done((f32[96,512]{1,0:T(8,128)S(1)}, f32[96,512]{1,0:T(8,128)S(1)}, u32[]{:S(2)}, u32[]{:S(2)}) %collective-permute-start.27) | collective-permute-done | bytes 196640 | tf_op jit(solution)/shard_map/ppermute | solution.py:75
  100.8 1.1 shard_map.87
  101.9 0.6 shard_map.88.refs_4_
  103.1 0.6 shard_map.89.refs_5_.refs_0_
  103.7 0.6 shard_map.90.refs_2_
  104.3 1.6 %collective-permute-start.31 = (f32[136,128]{1,0:T(8,128)S(1)}, f32[136,128]{1,0:T(8,128)S(1)}, u32[]{:S(2)}, u32[]{:S(2)}) collective-permute-start(f32[136,128]{1,0:T(8,128)S(1)} %shard_map.91.refs_2_.refs_0_), channel_id=1, source_target_pairs={{0,8},{4,12},{8,0},{12,4},{1,9},{5,13},{9,1},{13,5},{2,10},{6,14},... | collective-permute-start | bytes 208904 | tf_op jit(solution)/shard_map/ppermute | solution.py:75
  105.9 0.6 collective-permute-done.33.refs_1_
  106.6 1.6 %collective-permute-start.35 = (f32[96,640]{1,0:T(8,128)S(1)}, f32[96,640]{1,0:T(8,128)S(1)}, u32[]{:S(2)}, u32[]{:S(2)}) collective-permute-start(f32[96,640]{1,0:T(8,128)S(1)} %shard_map.93.refs_2_), channel_id=1, source_target_pairs={{0,8},{4,12},{8,0},{12,4},{1,9},{5,13},{9,1},{13,5},{2,10},{6,14},... | collective-permute-start | bytes 737288 | tf_op jit(solution)/shard_map/ppermute | solution.py:75
  108.8 1.2 %collective-permute-done.34.refs_2_ = f32[136,128]{1,0:T(8,128)S(1)} collective-permute-done((f32[136,128]{1,0:T(8,128)S(1)}, f32[136,128]{1,0:T(8,128)S(1)}, u32[]{:S(2)}, u32[]{:S(2)}) %collective-permute-start.34) | collective-permute-done | bytes 69664 | tf_op jit(solution)/shard_map/ppermute | solution.py:75
  110.0 0.9 shard_map.95.refs_5_.refs_1_
  111.2 0.9 shard_map.96.refs_1_.refs_4_
  112.1 2.0 %collective-permute-done.35.refs_3_ = f32[96,640]{1,0:T(8,128)S(1)} collective-permute-done((f32[96,640]{1,0:T(8,128)S(1)}, f32[96,640]{1,0:T(8,128)S(1)}, u32[]{:S(2)}, u32[]{:S(2)}) %collective-permute-start.35) | collective-permute-done | bytes 245792 | tf_op jit(solution)/shard_map/ppermute | solution.py:75
  114.2 0.9 copy.5
  115.1 0.6 collective-permute-done.37.refs_4_
  115.7 0.6 shard_map.98
  116.4 1.0 copy.6
  (66 shorter events, 7.1 us)
Async XLA Ops:
  0.6 6.8 %copy-start = (f32[1024,200]{0,1:T(8,128)S(1)}, f32[1024,200]{0,1:T(8,128)}, u32[]{:S(2)}) copy-start(f32[1024,200]{0,1:T(8,128)} %param.4) | copy-start | bytes 2457604
  4.4 12.6 %collective-permute-start.3 = (f32[104,512]{1,0:T(8,128)S(1)}, f32[104,512]{1,0:T(8,128)S(1)}, u32[]{:S(2)}, u32[]{:S(2)}) collective-permute-start(f32[104,512]{1,0:T(8,128)S(1)} %get-tuple-element.29.refs_7_), channel_id=1, source_target_pairs={{0,1},{1,0},{2,3},{3,2},{4,5},{5,4},{6,7},{7,6},{8,9},{9,8},{10,11... | collective-permute-start | bytes 638984 | tf_op jit(solution)/shard_map/ppermute | solution.py:75
  11.8 5.2 %collective-permute-start = (f32[136,128]{1,0:T(8,128)S(1)}, f32[136,128]{1,0:T(8,128)S(1)}, u32[]{:S(2)}, u32[]{:S(2)}) collective-permute-start(f32[136,128]{1,0:T(8,128)S(1)} %get-tuple-element.30.refs_0_.refs_2_), channel_id=1, source_target_pairs={{0,1},{1,0},{2,3},{3,2},{4,5},{5,4},{6,7},{7,6},{8,9},{9,8},{10,11... | collective-permute-start | bytes 208904 | tf_op jit(solution)/shard_map/ppermute | solution.py:75
  11.9 9.0 %collective-permute-start.2 = (f32[96,512]{1,0:T(8,128)S(1)}, f32[96,512]{1,0:T(8,128)S(1)}, u32[]{:S(2)}, u32[]{:S(2)}) collective-permute-start(f32[96,512]{1,0:T(8,128)S(1)} %get-tuple-element.32), channel_id=1, source_target_pairs={{0,1},{1,0},{2,3},{3,2},{4,5},{5,4},{6,7},{7,6},{8,9},{9,8},{10,11... | collective-permute-start | bytes 589832 | tf_op jit(solution)/shard_map/ppermute | solution.py:75
  17.1 12.2 %collective-permute-start.5 = (f32[104,512]{1,0:T(8,128)S(1)}, f32[104,512]{1,0:T(8,128)S(1)}, u32[]{:S(2)}, u32[]{:S(2)}) collective-permute-start(f32[104,512]{1,0:T(8,128)S(1)} %shard_map.53.refs_2_.refs_5_), channel_id=1, source_target_pairs={{0,3},{1,2},{2,1},{3,0},{4,7},{5,6},{6,5},{7,4},{8,11},{9,10},{10,... | collective-permute-start | bytes 638984 | tf_op jit(solution)/shard_map/ppermute | solution.py:75
  19.5 8.4 %collective-permute-start.1 = (f32[136,128]{1,0:T(8,128)S(1)}, f32[136,128]{1,0:T(8,128)S(1)}, u32[]{:S(2)}, u32[]{:S(2)}) collective-permute-start(f32[136,128]{1,0:T(8,128)S(1)} %shard_map.52.refs_2_.refs_0_), channel_id=1, source_target_pairs={{0,3},{1,2},{2,1},{3,0},{4,7},{5,6},{6,5},{7,4},{8,11},{9,10},{10,... | collective-permute-start | bytes 208904 | tf_op jit(solution)/shard_map/ppermute | solution.py:75
  28.0 1.3 %collective-permute-start.4 = (f32[136,128]{1,0:T(8,128)S(1)}, f32[136,128]{1,0:T(8,128)S(1)}, u32[]{:S(2)}, u32[]{:S(2)}) collective-permute-start(f32[136,128]{1,0:T(8,128)S(1)} %shard_map.55.refs_1_.refs_7_), channel_id=1, source_target_pairs={{0,4},{4,0},{8,12},{12,8},{1,5},{5,1},{9,13},{13,9},{2,6},{6,2},{1... | collective-permute-start | bytes 208904 | tf_op jit(solution)/shard_map/ppermute | solution.py:75
  28.1 9.6 %collective-permute-start.6 = (f32[96,512]{1,0:T(8,128)S(1)}, f32[96,512]{1,0:T(8,128)S(1)}, u32[]{:S(2)}, u32[]{:S(2)}) collective-permute-start(f32[96,512]{1,0:T(8,128)S(1)} %shard_map.54.refs_2_), channel_id=1, source_target_pairs={{0,3},{1,2},{2,1},{3,0},{4,7},{5,6},{6,5},{7,4},{8,11},{9,10},{10,... | collective-permute-start | bytes 589832 | tf_op jit(solution)/shard_map/ppermute | solution.py:75
  30.2 11.9 %collective-permute-start.7 = (f32[104,512]{1,0:T(8,128)S(1)}, f32[104,512]{1,0:T(8,128)S(1)}, u32[]{:S(2)}, u32[]{:S(2)}) collective-permute-start(f32[104,512]{1,0:T(8,128)S(1)} %shard_map.56.refs_5_.refs_0_.refs_1_.refs_3_), channel_id=1, source_target_pairs={{0,1},{1,0},{2,3},{3,2},{4,5},{5,4},{6,7},{7,6},{8,9},{9,8},{10,11... | collective-permute-start | bytes 638984 | tf_op jit(solution)/shard_map/ppermute | solution.py:75
  37.7 9.5 %collective-permute-start.8 = (f32[96,512]{1,0:T(8,128)S(1)}, f32[96,512]{1,0:T(8,128)S(1)}, u32[]{:S(2)}, u32[]{:S(2)}) collective-permute-start(f32[96,512]{1,0:T(8,128)S(1)} %shard_map.58.refs_4_.refs_2_.refs_0_), channel_id=1, source_target_pairs={{0,1},{1,0},{2,3},{3,2},{4,5},{5,4},{6,7},{7,6},{8,9},{9,8},{10,11... | collective-permute-start | bytes 589832 | tf_op jit(solution)/shard_map/ppermute | solution.py:75
  42.7 1.6 %collective-permute-start.10 = (f32[56,640]{1,0:T(8,128)S(1)}, f32[56,640]{1,0:T(8,128)S(1)}, u32[]{:S(2)}, u32[]{:S(2)}) collective-permute-start(f32[56,640]{1,0:T(8,128)S(1)} %get-tuple-element.41), channel_id=1, source_target_pairs={{0,4},{4,0},{8,12},{12,8},{1,5},{5,1},{9,13},{13,9},{2,6},{6,2},{1... | collective-permute-start | bytes 430088 | tf_op jit(solution)/shard_map/ppermute | solution.py:75
  42.7 1.5 %collective-permute-start.9 = (f32[48,640]{1,0:T(8,128)S(1)}, f32[48,640]{1,0:T(8,128)S(1)}, u32[]{:S(2)}, u32[]{:S(2)}) collective-permute-start(f32[48,640]{1,0:T(8,128)S(1)} %get-tuple-element.40.refs_4_), channel_id=1, source_target_pairs={{0,4},{4,0},{8,12},{12,8},{1,5},{5,1},{9,13},{13,9},{2,6},{6,2},{1... | collective-permute-start | bytes 368648 | tf_op jit(solution)/shard_map/ppermute | solution.py:75
  44.3 8.7 %collective-permute-start.14 = (f32[104,640]{1,0:T(8,128)S(1)}, f32[104,640]{1,0:T(8,128)S(1)}, u32[]{:S(2)}, u32[]{:S(2)}) collective-permute-start(f32[104,640]{1,0:T(8,128)S(1)} %shard_map.61.refs_5_.refs_0_), channel_id=1, source_target_pairs={{0,8},{4,12},{8,0},{12,4},{1,9},{5,13},{9,1},{13,5},{2,10},{6,14},... | collective-permute-start | bytes 798728 | tf_op jit(solution)/shard_map/ppermute | solution.py:75
  48.9 4.1 %collective-permute-start.13 = (f32[96,640]{1,0:T(8,128)S(1)}, f32[96,640]{1,0:T(8,128)S(1)}, u32[]{:S(2)}, u32[]{:S(2)}) collective-permute-start(f32[96,640]{1,0:T(8,128)S(1)} %shard_map.63.refs_4_), channel_id=1, source_target_pairs={{0,4},{4,0},{8,12},{12,8},{1,5},{5,1},{9,13},{13,9},{2,6},{6,2},{1... | collective-permute-start | bytes 737288 | tf_op jit(solution)/shard_map/ppermute | solution.py:75
  49.0 1.6 %collective-permute-start.11 = (f32[136,128]{1,0:T(8,128)S(1)}, f32[136,128]{1,0:T(8,128)S(1)}, u32[]{:S(2)}, u32[]{:S(2)}) collective-permute-start(f32[136,128]{1,0:T(8,128)S(1)} %get-tuple-element.43.refs_4_), channel_id=1, source_target_pairs={{0,4},{4,0},{8,12},{12,8},{1,5},{5,1},{9,13},{13,9},{2,6},{6,2},{1... | collective-permute-start | bytes 208904 | tf_op jit(solution)/shard_map/ppermute | solution.py:75
  50.6 4.4 %collective-permute-start.12 = (f32[136,128]{1,0:T(8,128)S(1)}, f32[136,128]{1,0:T(8,128)S(1)}, u32[]{:S(2)}, u32[]{:S(2)}) collective-permute-start(f32[136,128]{1,0:T(8,128)S(1)} %shard_map.65.refs_2_.refs_0_), channel_id=1, source_target_pairs={{0,8},{4,12},{8,0},{12,4},{1,9},{5,13},{9,1},{13,5},{2,10},{6,14},... | collective-permute-start | bytes 208904 | tf_op jit(solution)/shard_map/ppermute | solution.py:75
  53.1 7.4 %collective-permute-start.16 = (f32[96,640]{1,0:T(8,128)S(1)}, f32[96,640]{1,0:T(8,128)S(1)}, u32[]{:S(2)}, u32[]{:S(2)}) collective-permute-start(f32[96,640]{1,0:T(8,128)S(1)} %shard_map.67.refs_2_), channel_id=1, source_target_pairs={{0,8},{4,12},{8,0},{12,4},{1,9},{5,13},{9,1},{13,5},{2,10},{6,14},... | collective-permute-start | bytes 737288 | tf_op jit(solution)/shard_map/ppermute | solution.py:75
  55.0 1.3 %collective-permute-start.15 = (f32[136,128]{1,0:T(8,128)S(1)}, f32[136,128]{1,0:T(8,128)S(1)}, u32[]{:S(2)}, u32[]{:S(2)}) collective-permute-start(f32[136,128]{1,0:T(8,128)S(1)} %shard_map.68.refs_1_.refs_6_), channel_id=1, source_target_pairs={{0,4},{4,0},{8,12},{12,8},{1,5},{5,1},{9,13},{13,9},{2,6},{6,2},{1... | collective-permute-start | bytes 208904 | tf_op jit(solution)/shard_map/ppermute | solution.py:75
  57.2 3.5 %collective-permute-start.17 = (f32[104,640]{1,0:T(8,128)S(1)}, f32[104,640]{1,0:T(8,128)S(1)}, u32[]{:S(2)}, u32[]{:S(2)}) collective-permute-start(f32[104,640]{1,0:T(8,128)S(1)} %shard_map.69.refs_5_.refs_0_.refs_1_.refs_3_), channel_id=1, source_target_pairs={{0,4},{4,0},{8,12},{12,8},{1,5},{5,1},{9,13},{13,9},{2,6},{6,2},{1... | collective-permute-start | bytes 798728 | tf_op jit(solution)/shard_map/ppermute | solution.py:75
  60.6 3.5 %collective-permute-start.18 = (f32[96,640]{1,0:T(8,128)S(1)}, f32[96,640]{1,0:T(8,128)S(1)}, u32[]{:S(2)}, u32[]{:S(2)}) collective-permute-start(f32[96,640]{1,0:T(8,128)S(1)} %shard_map.71.refs_4_.refs_2_.refs_0_), channel_id=1, source_target_pairs={{0,4},{4,0},{8,12},{12,8},{1,5},{5,1},{9,13},{13,9},{2,6},{6,2},{1... | collective-permute-start | bytes 737288 | tf_op jit(solution)/shard_map/ppermute | solution.py:75
  61.6 9.6 %collective-permute-start.22 = (f32[104,512]{1,0:T(8,128)S(1)}, f32[104,512]{1,0:T(8,128)S(1)}, u32[]{:S(2)}, u32[]{:S(2)}) collective-permute-start(f32[104,512]{1,0:T(8,128)S(1)} %shard_map.72.refs_4_), channel_id=1, source_target_pairs={{0,1},{1,0},{2,3},{3,2},{4,5},{5,4},{6,7},{7,6},{8,9},{9,8},{10,11... | collective-permute-start | bytes 638984 | tf_op jit(solution)/shard_map/ppermute | solution.py:75
  65.4 5.9 %collective-permute-start.19 = (f32[136,128]{1,0:T(8,128)S(1)}, f32[136,128]{1,0:T(8,128)S(1)}, u32[]{:S(2)}, u32[]{:S(2)}) collective-permute-start(f32[136,128]{1,0:T(8,128)S(1)} %shard_map.74.refs_4_.refs_0_), channel_id=1, source_target_pairs={{0,1},{1,0},{2,3},{3,2},{4,5},{5,4},{6,7},{7,6},{8,9},{9,8},{10,11... | collective-permute-start | bytes 208904 | tf_op jit(solution)/shard_map/ppermute | solution.py:75
  66.9 8.3 %collective-permute-start.21 = (f32[96,512]{1,0:T(8,128)S(1)}, f32[96,512]{1,0:T(8,128)S(1)}, u32[]{:S(2)}, u32[]{:S(2)}) collective-permute-start(f32[96,512]{1,0:T(8,128)S(1)} %shard_map.75.refs_4_), channel_id=1, source_target_pairs={{0,1},{1,0},{2,3},{3,2},{4,5},{5,4},{6,7},{7,6},{8,9},{9,8},{10,11... | collective-permute-start | bytes 589832 | tf_op jit(solution)/shard_map/ppermute | solution.py:75
  71.3 13.4 %collective-permute-start.24 = (f32[104,512]{1,0:T(8,128)S(1)}, f32[104,512]{1,0:T(8,128)S(1)}, u32[]{:S(2)}, u32[]{:S(2)}) collective-permute-start(f32[104,512]{1,0:T(8,128)S(1)} %shard_map.78.refs_2_.refs_5_), channel_id=1, source_target_pairs={{0,3},{1,2},{2,1},{3,0},{4,7},{5,6},{6,5},{7,4},{8,11},{9,10},{10,... | collective-permute-start | bytes 638984 | tf_op jit(solution)/shard_map/ppermute | solution.py:75
  72.3 9.3 %collective-permute-start.20 = (f32[136,128]{1,0:T(8,128)S(1)}, f32[136,128]{1,0:T(8,128)S(1)}, u32[]{:S(2)}, u32[]{:S(2)}) collective-permute-start(f32[136,128]{1,0:T(8,128)S(1)} %shard_map.77.refs_2_.refs_0_), channel_id=1, source_target_pairs={{0,3},{1,2},{2,1},{3,0},{4,7},{5,6},{6,5},{7,4},{8,11},{9,10},{10,... | collective-permute-start | bytes 208904 | tf_op jit(solution)/shard_map/ppermute | solution.py:75
  81.6 3.1 %collective-permute-start.23 = (f32[136,128]{1,0:T(8,128)S(1)}, f32[136,128]{1,0:T(8,128)S(1)}, u32[]{:S(2)}, u32[]{:S(2)}) collective-permute-start(f32[136,128]{1,0:T(8,128)S(1)} %shard_map.80.refs_1_.refs_7_), channel_id=1, source_target_pairs={{0,4},{4,0},{8,12},{12,8},{1,5},{5,1},{9,13},{13,9},{2,6},{6,2},{1... | collective-permute-start | bytes 208904 | tf_op jit(solution)/shard_map/ppermute | solution.py:75
  81.6 9.3 %collective-permute-start.25 = (f32[96,512]{1,0:T(8,128)S(1)}, f32[96,512]{1,0:T(8,128)S(1)}, u32[]{:S(2)}, u32[]{:S(2)}) collective-permute-start(f32[96,512]{1,0:T(8,128)S(1)} %shard_map.79.refs_2_), channel_id=1, source_target_pairs={{0,3},{1,2},{2,1},{3,0},{4,7},{5,6},{6,5},{7,4},{8,11},{9,10},{10,... | collective-permute-start | bytes 589832 | tf_op jit(solution)/shard_map/ppermute | solution.py:75
  85.5 10.2 %collective-permute-start.26 = (f32[104,512]{1,0:T(8,128)S(1)}, f32[104,512]{1,0:T(8,128)S(1)}, u32[]{:S(2)}, u32[]{:S(2)}) collective-permute-start(f32[104,512]{1,0:T(8,128)S(1)} %shard_map.81.refs_5_.refs_0_.refs_1_), channel_id=1, source_target_pairs={{0,1},{1,0},{2,3},{3,2},{4,5},{5,4},{6,7},{7,6},{8,9},{9,8},{10,11... | collective-permute-start | bytes 638984 | tf_op jit(solution)/shard_map/ppermute | solution.py:75
  91.0 9.8 %collective-permute-start.27 = (f32[96,512]{1,0:T(8,128)S(1)}, f32[96,512]{1,0:T(8,128)S(1)}, u32[]{:S(2)}, u32[]{:S(2)}) collective-permute-start(f32[96,512]{1,0:T(8,128)S(1)} %shard_map.83.refs_4_.refs_2_.refs_0_), channel_id=1, source_target_pairs={{0,1},{1,0},{2,3},{3,2},{4,5},{5,4},{6,7},{7,6},{8,9},{9,8},{10,11... | collective-permute-start | bytes 589832 | tf_op jit(solution)/shard_map/ppermute | solution.py:75
  96.2 1.6 %collective-permute-start.29 = (f32[56,640]{1,0:T(8,128)S(1)}, f32[56,640]{1,0:T(8,128)S(1)}, u32[]{:S(2)}, u32[]{:S(2)}) collective-permute-start(f32[56,640]{1,0:T(8,128)S(1)} %get-tuple-element.45), channel_id=1, source_target_pairs={{0,4},{4,0},{8,12},{12,8},{1,5},{5,1},{9,13},{13,9},{2,6},{6,2},{1... | collective-permute-start | bytes 430088 | tf_op jit(solution)/shard_map/ppermute | solution.py:75
  96.3 1.5 %collective-permute-start.28 = (f32[48,640]{1,0:T(8,128)S(1)}, f32[48,640]{1,0:T(8,128)S(1)}, u32[]{:S(2)}, u32[]{:S(2)}) collective-permute-start(f32[48,640]{1,0:T(8,128)S(1)} %get-tuple-element.44.refs_4_), channel_id=1, source_target_pairs={{0,4},{4,0},{8,12},{12,8},{1,5},{5,1},{9,13},{13,9},{2,6},{6,2},{1... | collective-permute-start | bytes 368648 | tf_op jit(solution)/shard_map/ppermute | solution.py:75
  97.9 8.7 %collective-permute-start.33 = (f32[104,640]{1,0:T(8,128)S(1)}, f32[104,640]{1,0:T(8,128)S(1)}, u32[]{:S(2)}, u32[]{:S(2)}) collective-permute-start(f32[104,640]{1,0:T(8,128)S(1)} %shard_map.86.refs_5_.refs_0_), channel_id=1, source_target_pairs={{0,8},{4,12},{8,0},{12,4},{1,9},{5,13},{9,1},{13,5},{2,10},{6,14},... | collective-permute-start | bytes 798728 | tf_op jit(solution)/shard_map/ppermute | solution.py:75
  102.5 4.1 %collective-permute-start.32 = (f32[96,640]{1,0:T(8,128)S(1)}, f32[96,640]{1,0:T(8,128)S(1)}, u32[]{:S(2)}, u32[]{:S(2)}) collective-permute-start(f32[96,640]{1,0:T(8,128)S(1)} %shard_map.88.refs_4_), channel_id=1, source_target_pairs={{0,4},{4,0},{8,12},{12,8},{1,5},{5,1},{9,13},{13,9},{2,6},{6,2},{1... | collective-permute-start | bytes 737288 | tf_op jit(solution)/shard_map/ppermute | solution.py:75
  102.6 1.7 %collective-permute-start.30 = (f32[136,128]{1,0:T(8,128)S(1)}, f32[136,128]{1,0:T(8,128)S(1)}, u32[]{:S(2)}, u32[]{:S(2)}) collective-permute-start(f32[136,128]{1,0:T(8,128)S(1)} %get-tuple-element.46.refs_4_), channel_id=1, source_target_pairs={{0,4},{4,0},{8,12},{12,8},{1,5},{5,1},{9,13},{13,9},{2,6},{6,2},{1... | collective-permute-start | bytes 208904 | tf_op jit(solution)/shard_map/ppermute | solution.py:75
  104.3 4.4 %collective-permute-start.31 = (f32[136,128]{1,0:T(8,128)S(1)}, f32[136,128]{1,0:T(8,128)S(1)}, u32[]{:S(2)}, u32[]{:S(2)}) collective-permute-start(f32[136,128]{1,0:T(8,128)S(1)} %shard_map.91.refs_2_.refs_0_), channel_id=1, source_target_pairs={{0,8},{4,12},{8,0},{12,4},{1,9},{5,13},{9,1},{13,5},{2,10},{6,14},... | collective-permute-start | bytes 208904 | tf_op jit(solution)/shard_map/ppermute | solution.py:75
  106.6 7.4 %collective-permute-start.35 = (f32[96,640]{1,0:T(8,128)S(1)}, f32[96,640]{1,0:T(8,128)S(1)}, u32[]{:S(2)}, u32[]{:S(2)}) collective-permute-start(f32[96,640]{1,0:T(8,128)S(1)} %shard_map.93.refs_2_), channel_id=1, source_target_pairs={{0,8},{4,12},{8,0},{12,4},{1,9},{5,13},{9,1},{13,5},{2,10},{6,14},... | collective-permute-start | bytes 737288 | tf_op jit(solution)/shard_map/ppermute | solution.py:75
  108.7 1.3 %collective-permute-start.34 = (f32[136,128]{1,0:T(8,128)S(1)}, f32[136,128]{1,0:T(8,128)S(1)}, u32[]{:S(2)}, u32[]{:S(2)}) collective-permute-start(f32[136,128]{1,0:T(8,128)S(1)} %shard_map.94.refs_1_.refs_6_), channel_id=1, source_target_pairs={{0,4},{4,0},{8,12},{12,8},{1,5},{5,1},{9,13},{13,9},{2,6},{6,2},{1... | collective-permute-start | bytes 208904 | tf_op jit(solution)/shard_map/ppermute | solution.py:75
  111.0 4.2 %collective-permute-start.36 = (f32[104,640]{1,0:T(8,128)S(1)}, f32[104,640]{1,0:T(8,128)S(1)}, u32[]{:S(2)}, u32[]{:S(2)}) collective-permute-start(f32[104,640]{1,0:T(8,128)S(1)} %shard_map.95.refs_5_.refs_1_), channel_id=1, source_target_pairs={{0,4},{4,0},{8,12},{12,8},{1,5},{5,1},{9,13},{13,9},{2,6},{6,2},{1... | collective-permute-start | bytes 798728 | tf_op jit(solution)/shard_map/ppermute | solution.py:75
  114.1 1.6 %collective-permute-start.37 = (f32[96,640]{1,0:T(8,128)S(1)}, f32[96,640]{1,0:T(8,128)S(1)}, u32[]{:S(2)}, u32[]{:S(2)}) collective-permute-start(f32[96,640]{1,0:T(8,128)S(1)} %shard_map.97.refs_2_.refs_5_), channel_id=1, source_target_pairs={{0,4},{4,0},{8,12},{12,8},{1,5},{5,1},{9,13},{13,9},{2,6},{6,2},{1... | collective-permute-start | bytes 737288 | tf_op jit(solution)/shard_map/ppermute | solution.py:75

commit v9 on v8

--- a/solution.py
+++ b/solution.py
@@ -127,6 +127,23 @@
         n = factor_a[0].shape[1] + factor_b[0].shape[1]
         return chain(kernel, [(grows, packed[1])] * (1 + both), where, *factor_a, *factor_b, flops=6 * k * k * n)
 
+    def partial(a, xa, dim):
+        def kernel(a_ref, xa_ref, o_ref):
+            o_ref[...] = dot2(a_ref[...], xa_ref[...], 1, dim)
+
+        return chain(kernel, [(a.shape[0], xa.shape[1 - dim])], a, xa)[0]
+
+    def rest_of_product(base, b, xb, dim, cut=0):
+        n, m = base.shape
+
+        def kernel(base_ref, b_ref, xb_ref, *o_refs):
+            o = base_ref[...] + dot2(b_ref[...], xb_ref[...], 1, dim)
+            for ref, part in zip(o_refs, (o[:cut], o[cut:]) if cut else (o,)):
+                ref[...] = part
+
+        outs = [(cut, m), (n - cut, m)] if cut else [(n, m)]
+        return chain(kernel, outs, base, b, xb, flops=8 * n * b.shape[1] * m)
+
     def product(a, b, xa, xb, dim, cut=0):
         parts = len(a)
 
@@ -160,7 +177,7 @@
         g = unpacked(jnp.concatenate([upper, lower], 0))
         return dot3(rows_of(g, index), stacked(f_refs), 1, 0)
 
-    def update(mine, theirs, factor, tops, axis, size, flip, weights):
+    def update(mine, theirs, factor, tops, axis, size, flip, weights, x_next, dim):
         def first(where_ref, m_ref, t_ref, *refs):
             f_refs, (*top_refs, o_ref) = refs[:n_chunks], refs[n_chunks:]
             below = denominator(where_ref, m_ref, t_ref, f_refs, 0)
@@ -182,10 +199,11 @@
             chain(functools.partial(below, i), shapes[i : i + 1], where, mine, theirs, *factor)[0]
             for i in range(1, n_chunks)
         ]
+        base = None if x_next is None else partial(new[0], x_next, dim)
         for i in range(1, n_chunks):
             new.append(chain(rest, shapes[i : i + 1], factor[i], divisors[i - 1], *tops[i], flops=flops[i])[0])
             other.append(exchange(new[i], axis, size, flip))
-        return new, other
+        return new, other, base
 
     def join(mine, theirs, index, which):
         size = mine[0].shape[1]
@@ -329,13 +347,14 @@
                 if i == GRAM_AT:
                     gram_p = gram(program_own, program_other, False)[0]
                     gram_near = exchange(gram_p, "gene", genes, 1)
-                nears.append(exchange(product(a, b, *x[1], 1), "gene", genes, 1))
+                send = product(a, b, *x[1], 1) if i else rest_of_product(base, b[0], x[1][1], 1)[0]
+                nears.append(exchange(send, "gene", genes, 1))
                 keeps.append(product(a, b, *x[0], 1))
         gram_top = far(add(gram_p, gram_near), "gene", genes, True)
         tops = [far(add(keep, near), "gene", genes, True) for keep, near in zip(keeps, nears)]
         mine = add(*gram_top)
         theirs = exchange(mine, "cell", cells, 1)
-        new, other = update(mine, theirs, usage_own, tops, "gene", genes, 1, USAGE_WEIGHTS)
+        new, other, base = update(mine, theirs, usage_own, tops, "gene", genes, 1, USAGE_WEIGHTS, x[0][1], 0)
         usage_own, usage_other = new, other
 
         tops = []
@@ -343,7 +362,11 @@
             a, b = new[i : i + 1], other[i : i + 1]
             if i < n_chunks - 1:
                 cut = sizes[i] // 16 * 8
-                send = [exchange(part, "cell", cells, 1) for part in product(a, b, x[0][1], x[1][1], 0, cut)]
+                if i:
+                    send = product(a, b, x[0][1], x[1][1], 0, cut)
+                else:
+                    send = rest_of_product(base, b[0], x[1][1], 0, cut)
+                send = [exchange(part, "cell", cells, 1) for part in send]
                 keep = product(a, b, x[0][0], x[1][0], 0)
                 tops.append(far(add(keep, *send), "cell", cells, False))
                 continue
@@ -359,7 +382,10 @@
         mine = add(*gram_top)
         theirs = exchange(mine, "cell", cells, 1)
         weights = (PROGRAM_WEIGHTS[last], 1, 1)
-        program_own, program_other = update(mine, theirs, program_own, tops, "cell", cells, 1, weights)
+        x_next = None if last else x[1][0]
+        program_own, program_other, base = update(
+            mine, theirs, program_own, tops, "cell", cells, 1, weights, x_next, 1
+        )
 
     return usage.T, join(program_own, program_other, 0, core)
 

time: 117 us -> 117 us (level)
    pallas_call x49 -> x52, Pallas kernels: 28.7 us -> 29.2 us  [__call__(): pl.pallas_call(run, out_shape=[pltpu.VMEM(s.shape, s.dtype) for s in shap...]
where the time goes in v9:
time: 117 us
  starting transfers between devices  49.4 us (42%)
  waiting for transfers between devices  35.2 us (30%)
  Pallas kernels  29.2 us (25%)
  local copies, waits for them, and re-layouts  1.86 us (2%)
    ppermute x38, starting transfers between devices, exchange(): return lax.ppermute(a, axis, [(i, i ^ flip) for i in range(size)])  49.4 us
    ppermute x38, waiting for transfers between devices, exchange(): return lax.ppermute(a, axis, [(i, i ^ flip) for i in range(size)])  35.2 us
    pallas_call x52, Pallas kernels, __call__(): pl.pallas_call(run, out_shape=[pltpu.VMEM(s.shape, s.dtype) for s in shap...  29.2 us
  transfers between devices with their start and end apart: 38, of which 21 were waited for; matrix products, arithmetic and copies ran while one was open for 1% of the time, Pallas kernels for 21%

profile of v9, /device:TPU:0, one launch (start us, length us, event | category | flops | bytes accessed | tf_op | source)
XLA Modules:
  0.0 116.9 jit_solution(10855605399830180488)
XLA Ops:
  0.7 3.6 %shard_map.50 = (f32[104,512]{1,0:T(8,128)S(1)}, f32[96,512]{1,0:T(8,128)S(1)}, f32[104,640]{1,0:T(8,128)S(1)}, f32[96,640]{1,0:T(8,128)S(1)}, f32[104,640]{1,0:...) custom-call(s32[2]{0:T(128)S(1)} %pad_add_fusion.refs_0_, ...), custom_call_target="tpu_custom_call" | custom-call | flops 524288000 | bytes 10321928 | tf_op jit(solution)/shard_map/pallas_call | solution.py:61
  4.4 3.1 %collective-permute-start.3 = (f32[104,512]{1,0:T(8,128)S(1)}, f32[104,512]{1,0:T(8,128)S(1)}, u32[]{:S(2)}, u32[]{:S(2)}) collective-permute-start(f32[104,512]{1,0:T(8,128)S(1)} %get-tuple-element.29.refs_7_), channel_id=1, source_target_pairs={{0,1},{1,0},{2,3},{3,2},{4,5},{5,4},{6,7},{7,6},{8,9},{9,8},{10,11... | collective-permute-start | bytes 638984 | tf_op jit(solution)/shard_map/ppermute | solution.py:75
  7.5 4.3 %shard_map.51 = (f32[136,128]{1,0:T(8,128)S(1)}, bf16[512,640]{1,0:T(8,128)(2,1)S(1)}, bf16[512,640]{1,0:T(8,128)(2,1)S(1)}, f32[104,512]{1,0:T(8,128)S(1)}, f32...) custom-call(s32[2]{0:T(128)S(1)} %pad_add_fusion.refs_0_, s32[1024,1280]{1,0:T(8,128)} %refs_1_.3, ...), custom_call_target="tpu_custom_call" | custom-call | flops 524288000 | bytes 10596360 | tf_op jit(solution)/shard_map/pallas_call | solution.py:61
  11.9 2.0 %collective-permute-start.2 = (f32[96,512]{1,0:T(8,128)S(1)}, f32[96,512]{1,0:T(8,128)S(1)}, u32[]{:S(2)}, u32[]{:S(2)}) collective-permute-start(f32[96,512]{1,0:T(8,128)S(1)} %get-tuple-element.32), channel_id=1, source_target_pairs={{0,1},{1,0},{2,3},{3,2},{4,5},{5,4},{6,7},{7,6},{8,9},{9,8},{10,11... | collective-permute-start | bytes 589832 | tf_op jit(solution)/shard_map/ppermute | solution.py:75
  13.9 3.1 %collective-permute-done.refs_1_ = f32[136,128]{1,0:T(8,128)S(1)} collective-permute-done((f32[136,128]{1,0:T(8,128)S(1)}, f32[136,128]{1,0:T(8,128)S(1)}, u32[]{:S(2)}, u32[]{:S(2)}) %collective-permute-start) | collective-permute-done | bytes 69664 | tf_op jit(solution)/shard_map/ppermute | solution.py:75
  17.1 2.5 %collective-permute-start.5 = (f32[104,512]{1,0:T(8,128)S(1)}, f32[104,512]{1,0:T(8,128)S(1)}, u32[]{:S(2)}, u32[]{:S(2)}) collective-permute-start(f32[104,512]{1,0:T(8,128)S(1)} %shard_map.53.refs_2_.refs_5_), channel_id=1, source_target_pairs={{0,3},{1,2},{2,1},{3,0},{4,7},{5,6},{6,5},{7,4},{8,11},{9,10},{10,... | collective-permute-start | bytes 638984 | tf_op jit(solution)/shard_map/ppermute | solution.py:75
  19.6 1.4 %collective-permute-start.1 = (f32[136,128]{1,0:T(8,128)S(1)}, f32[136,128]{1,0:T(8,128)S(1)}, u32[]{:S(2)}, u32[]{:S(2)}) collective-permute-start(f32[136,128]{1,0:T(8,128)S(1)} %shard_map.52.refs_2_.refs_0_), channel_id=1, source_target_pairs={{0,3},{1,2},{2,1},{3,0},{4,7},{5,6},{6,5},{7,4},{8,11},{9,10},{10,... | collective-permute-start | bytes 208904 | tf_op jit(solution)/shard_map/ppermute | solution.py:75
  21.0 7.0 %collective-permute-done.1.refs_1_ = f32[136,128]{1,0:T(8,128)S(1)} collective-permute-done((f32[136,128]{1,0:T(8,128)S(1)}, f32[136,128]{1,0:T(8,128)S(1)}, u32[]{:S(2)}, u32[]{:S(2)}) %collective-permute-start.1) | collective-permute-done | bytes 69664 | tf_op jit(solution)/shard_map/ppermute | solution.py:75
  28.1 1.0 collective-permute-start.6
  29.3 0.9 shard_map.56.refs_5_.refs_0_.refs_1_.refs_3_
  30.2 3.5 %collective-permute-start.7 = (f32[104,512]{1,0:T(8,128)S(1)}, f32[104,512]{1,0:T(8,128)S(1)}, u32[]{:S(2)}, u32[]{:S(2)}) collective-permute-start(f32[104,512]{1,0:T(8,128)S(1)} %shard_map.56.refs_5_.refs_0_.refs_1_.refs_3_), channel_id=1, source_target_pairs={{0,1},{1,0},{2,3},{3,2},{4,5},{5,4},{6,7},{7,6},{8,9},{9,8},{10,11... | collective-permute-start | bytes 638984 | tf_op jit(solution)/shard_map/ppermute | solution.py:75
  33.7 0.8 shard_map.57.refs_2_.refs_1_
  34.9 2.7 %collective-permute-done.6.refs_3_ = f32[96,512]{1,0:T(8,128)S(1)} collective-permute-done((f32[96,512]{1,0:T(8,128)S(1)}, f32[96,512]{1,0:T(8,128)S(1)}, u32[]{:S(2)}, u32[]{:S(2)}) %collective-permute-start.6) | collective-permute-done | bytes 196640 | tf_op jit(solution)/shard_map/ppermute | solution.py:75
  37.7 4.3 %collective-permute-start.8 = (f32[96,512]{1,0:T(8,128)S(1)}, f32[96,512]{1,0:T(8,128)S(1)}, u32[]{:S(2)}, u32[]{:S(2)}) collective-permute-start(f32[96,512]{1,0:T(8,128)S(1)} %shard_map.59.refs_3_.refs_2_.refs_0_.refs_4_), channel_id=1, source_target_pairs={{0,1},{1,0},{2,3},{3,2},{4,5},{5,4},{6,7},{7,6},{8,9},{9,8},{10,11... | collective-permute-start | bytes 589832 | tf_op jit(solution)/shard_map/ppermute | solution.py:75
  43.0 0.6 shard_map.61.refs_0_.refs_3_
  44.1 1.6 %collective-permute-start.14 = (f32[104,640]{1,0:T(8,128)S(1)}, f32[104,640]{1,0:T(8,128)S(1)}, u32[]{:S(2)}, u32[]{:S(2)}) collective-permute-start(f32[104,640]{1,0:T(8,128)S(1)} %shard_map.62.refs_5_.refs_0_), channel_id=1, source_target_pairs={{0,8},{4,12},{8,0},{12,4},{1,9},{5,13},{9,1},{13,5},{2,10},{6,14},... | collective-permute-start | bytes 798728 | tf_op jit(solution)/shard_map/ppermute | solution.py:75
  45.6 1.6 %collective-permute-done.8.refs_4_.refs_1_ = f32[96,512]{1,0:T(8,128)S(1)} collective-permute-done((f32[96,512]{1,0:T(8,128)S(1)}, f32[96,512]{1,0:T(8,128)S(1)}, u32[]{:S(2)}, u32[]{:S(2)}) %collective-permute-start.8) | collective-permute-done | bytes 196640 | tf_op jit(solution)/shard_map/ppermute | solution.py:75
  47.2 1.1 shard_map.63
  48.3 0.6 shard_map.64.refs_4_
  49.4 0.6 shard_map.65.refs_2_.refs_0_
  50.6 1.6 %collective-permute-start.12 = (f32[136,128]{1,0:T(8,128)S(1)}, f32[136,128]{1,0:T(8,128)S(1)}, u32[]{:S(2)}, u32[]{:S(2)}) collective-permute-start(f32[136,128]{1,0:T(8,128)S(1)} %shard_map.66.refs_2_.refs_0_), channel_id=1, source_target_pairs={{0,8},{4,12},{8,0},{12,4},{1,9},{5,13},{9,1},{13,5},{2,10},{6,14},... | collective-permute-start | bytes 208904 | tf_op jit(solution)/shard_map/ppermute | solution.py:75
  52.1 0.6 collective-permute-done.14.refs_1_
  52.8 1.6 %collective-permute-start.16 = (f32[96,640]{1,0:T(8,128)S(1)}, f32[96,640]{1,0:T(8,128)S(1)}, u32[]{:S(2)}, u32[]{:S(2)}) collective-permute-start(f32[96,640]{1,0:T(8,128)S(1)} %shard_map.68.refs_2_), channel_id=1, source_target_pairs={{0,8},{4,12},{8,0},{12,4},{1,9},{5,13},{9,1},{13,5},{2,10},{6,14},... | collective-permute-start | bytes 737288 | tf_op jit(solution)/shard_map/ppermute | solution.py:75
  54.4 0.5 collective-permute-done.12.refs_1_
  55.0 1.2 %collective-permute-done.15.refs_2_ = f32[136,128]{1,0:T(8,128)S(1)} collective-permute-done((f32[136,128]{1,0:T(8,128)S(1)}, f32[136,128]{1,0:T(8,128)S(1)}, u32[]{:S(2)}, u32[]{:S(2)}) %collective-permute-start.15) | collective-permute-done | bytes 69664 | tf_op jit(solution)/shard_map/ppermute | solution.py:75
  56.3 0.9 shard_map.70.refs_5_.refs_0_.refs_1_.refs_3_
  57.4 0.9 shard_map.71.refs_2_.refs_1_
  58.9 1.4 %collective-permute-done.16.refs_3_ = f32[96,640]{1,0:T(8,128)S(1)} collective-permute-done((f32[96,640]{1,0:T(8,128)S(1)}, f32[96,640]{1,0:T(8,128)S(1)}, u32[]{:S(2)}, u32[]{:S(2)}) %collective-permute-start.16) | collective-permute-done | bytes 245792 | tf_op jit(solution)/shard_map/ppermute | solution.py:75
  60.4 0.5 shard_map.74.refs_4_
  61.0 1.7 %collective-permute-start.22 = (f32[104,512]{1,0:T(8,128)S(1)}, f32[104,512]{1,0:T(8,128)S(1)}, u32[]{:S(2)}, u32[]{:S(2)}) collective-permute-start(f32[104,512]{1,0:T(8,128)S(1)} %shard_map.74.refs_4_), channel_id=1, source_target_pairs={{0,1},{1,0},{2,3},{3,2},{4,5},{5,4},{6,7},{7,6},{8,9},{9,8},{10,11... | collective-permute-start | bytes 638984 | tf_op jit(solution)/shard_map/ppermute | solution.py:75
  62.7 0.9 shard_map.75.refs_5_.refs_0_
  63.7 1.2 %shard_map.76.refs_4_.refs_0_ = f32[136,128]{1,0:T(8,128)S(1)} custom-call(s32[2]{0:T(128)S(1)} %pad_add_fusion.refs_0_, f32[104,640]{1,0:T(8,128)S(1)} %shard_map.70.refs_5_.refs_0_.refs_1_.refs_3_, f32[96,640]{1,0:T(8,128)S(1)} %shard_map.73.refs_3_.refs_2_.refs_0_.refs_4_, f32[104,640]{1,0:T(8,128)S(1)} %collective-permute-done.17.refs_1_.refs_3_, ...), custom_call_target="tpu_custom_call" | custom-call | flops 307200000 | bytes 1093640 | tf_op jit(solution)/shard_map/pallas_call | solution.py:61
  65.3 0.9 shard_map.77.refs_4_
  66.3 1.7 %collective-permute-start.21 = (f32[96,512]{1,0:T(8,128)S(1)}, f32[96,512]{1,0:T(8,128)S(1)}, u32[]{:S(2)}, u32[]{:S(2)}) collective-permute-start(f32[96,512]{1,0:T(8,128)S(1)} %shard_map.77.refs_4_), channel_id=1, source_target_pairs={{0,1},{1,0},{2,3},{3,2},{4,5},{5,4},{6,7},{7,6},{8,9},{9,8},{10,11... | collective-permute-start | bytes 589832 | tf_op jit(solution)/shard_map/ppermute | solution.py:75
  68.0 0.9 shard_map.78.refs_2_.refs_0_
  68.9 1.6 %collective-permute-done.19.refs_1_ = f32[136,128]{1,0:T(8,128)S(1)} collective-permute-done((f32[136,128]{1,0:T(8,128)S(1)}, f32[136,128]{1,0:T(8,128)S(1)}, u32[]{:S(2)}, u32[]{:S(2)}) %collective-permute-start.19) | collective-permute-done | bytes 69664 | tf_op jit(solution)/shard_map/ppermute | solution.py:75
  70.6 1.0 collective-permute-start.24
  71.6 2.9 %collective-permute-start.20 = (f32[136,128]{1,0:T(8,128)S(1)}, f32[136,128]{1,0:T(8,128)S(1)}, u32[]{:S(2)}, u32[]{:S(2)}) collective-permute-start(f32[136,128]{1,0:T(8,128)S(1)} %shard_map.79.refs_2_.refs_0_), channel_id=1, source_target_pairs={{0,3},{1,2},{2,1},{3,0},{4,7},{5,6},{6,5},{7,4},{8,11},{9,10},{10,... | collective-permute-start | bytes 208904 | tf_op jit(solution)/shard_map/ppermute | solution.py:75
  74.6 6.6 %collective-permute-done.20.refs_1_ = f32[136,128]{1,0:T(8,128)S(1)} collective-permute-done((f32[136,128]{1,0:T(8,128)S(1)}, f32[136,128]{1,0:T(8,128)S(1)}, u32[]{:S(2)}, u32[]{:S(2)}) %collective-permute-start.20) | collective-permute-done | bytes 69664 | tf_op jit(solution)/shard_map/ppermute | solution.py:75
  81.2 3.0 %collective-permute-start.25 = (f32[96,512]{1,0:T(8,128)S(1)}, f32[96,512]{1,0:T(8,128)S(1)}, u32[]{:S(2)}, u32[]{:S(2)}) collective-permute-start(f32[96,512]{1,0:T(8,128)S(1)} %shard_map.81.refs_2_), channel_id=1, source_target_pairs={{0,3},{1,2},{2,1},{3,0},{4,7},{5,6},{6,5},{7,4},{8,11},{9,10},{10,... | collective-permute-start | bytes 589832 | tf_op jit(solution)/shard_map/ppermute | solution.py:75
  84.2 0.9 shard_map.83.refs_5_.refs_0_.refs_1_
  85.1 3.6 %collective-permute-start.26 = (f32[104,512]{1,0:T(8,128)S(1)}, f32[104,512]{1,0:T(8,128)S(1)}, u32[]{:S(2)}, u32[]{:S(2)}) collective-permute-start(f32[104,512]{1,0:T(8,128)S(1)} %shard_map.83.refs_5_.refs_0_.refs_1_), channel_id=1, source_target_pairs={{0,1},{1,0},{2,3},{3,2},{4,5},{5,4},{6,7},{7,6},{8,9},{9,8},{10,11... | collective-permute-start | bytes 638984 | tf_op jit(solution)/shard_map/ppermute | solution.py:75
  88.7 0.8 shard_map.84.refs_2_.refs_1_
  89.9 0.6 collective-permute-done.25.refs_3_
  90.6 4.7 %collective-permute-start.27 = (f32[96,512]{1,0:T(8,128)S(1)}, f32[96,512]{1,0:T(8,128)S(1)}, u32[]{:S(2)}, u32[]{:S(2)}) collective-permute-start(f32[96,512]{1,0:T(8,128)S(1)} %shard_map.86.refs_3_.refs_2_.refs_0_), channel_id=1, source_target_pairs={{0,1},{1,0},{2,3},{3,2},{4,5},{5,4},{6,7},{7,6},{8,9},{9,8},{10,11... | collective-permute-start | bytes 589832 | tf_op jit(solution)/shard_map/ppermute | solution.py:75
  96.2 0.6 shard_map.88.refs_0_.refs_3_
  97.3 1.7 %collective-permute-start.33 = (f32[104,640]{1,0:T(8,128)S(1)}, f32[104,640]{1,0:T(8,128)S(1)}, u32[]{:S(2)}, u32[]{:S(2)}) collective-permute-start(f32[104,640]{1,0:T(8,128)S(1)} %shard_map.89.refs_5_.refs_0_), channel_id=1, source_target_pairs={{0,8},{4,12},{8,0},{12,4},{1,9},{5,13},{9,1},{13,5},{2,10},{6,14},... | collective-permute-start | bytes 798728 | tf_op jit(solution)/shard_map/ppermute | solution.py:75
  99.0 1.4 %collective-permute-done.27.refs_4_.refs_1_ = f32[96,512]{1,0:T(8,128)S(1)} collective-permute-done((f32[96,512]{1,0:T(8,128)S(1)}, f32[96,512]{1,0:T(8,128)S(1)}, u32[]{:S(2)}, u32[]{:S(2)}) %collective-permute-start.27) | collective-permute-done | bytes 196640 | tf_op jit(solution)/shard_map/ppermute | solution.py:75
  100.4 1.1 shard_map.90
  101.5 0.6 shard_map.91.refs_4_
  102.7 0.6 shard_map.92.refs_5_.refs_0_
  103.3 0.6 shard_map.93.refs_2_
  103.9 1.5 %collective-permute-start.31 = (f32[136,128]{1,0:T(8,128)S(1)}, f32[136,128]{1,0:T(8,128)S(1)}, u32[]{:S(2)}, u32[]{:S(2)}) collective-permute-start(f32[136,128]{1,0:T(8,128)S(1)} %shard_map.94.refs_2_.refs_0_), channel_id=1, source_target_pairs={{0,8},{4,12},{8,0},{12,4},{1,9},{5,13},{9,1},{13,5},{2,10},{6,14},... | collective-permute-start | bytes 208904 | tf_op jit(solution)/shard_map/ppermute | solution.py:75
  105.4 0.7 collective-permute-done.33.refs_1_
  106.2 1.5 %collective-permute-start.35 = (f32[96,640]{1,0:T(8,128)S(1)}, f32[96,640]{1,0:T(8,128)S(1)}, u32[]{:S(2)}, u32[]{:S(2)}) collective-permute-start(f32[96,640]{1,0:T(8,128)S(1)} %shard_map.96.refs_2_), channel_id=1, source_target_pairs={{0,8},{4,12},{8,0},{12,4},{1,9},{5,13},{9,1},{13,5},{2,10},{6,14},... | collective-permute-start | bytes 737288 | tf_op jit(solution)/shard_map/ppermute | solution.py:75
  107.7 0.6 collective-permute-done.31.refs_1_
  108.4 1.2 %collective-permute-done.34.refs_2_ = f32[136,128]{1,0:T(8,128)S(1)} collective-permute-done((f32[136,128]{1,0:T(8,128)S(1)}, f32[136,128]{1,0:T(8,128)S(1)}, u32[]{:S(2)}, u32[]{:S(2)}) %collective-permute-start.34) | collective-permute-done | bytes 69664 | tf_op jit(solution)/shard_map/ppermute | solution.py:75
  109.6 0.9 shard_map.98.refs_5_.refs_1_
  110.8 0.9 shard_map.99.refs_1_.refs_4_
  111.7 2.0 %collective-permute-done.35.refs_3_ = f32[96,640]{1,0:T(8,128)S(1)} collective-permute-done((f32[96,640]{1,0:T(8,128)S(1)}, f32[96,640]{1,0:T(8,128)S(1)}, u32[]{:S(2)}, u32[]{:S(2)}) %collective-permute-start.35) | collective-permute-done | bytes 245792 | tf_op jit(solution)/shard_map/ppermute | solution.py:75
  113.8 0.9 copy.5
  114.7 0.6 collective-permute-done.37.refs_4_
  115.3 0.6 shard_map.101
  115.9 1.0 copy.6
  (69 shorter events, 8.1 us)
Async XLA Ops:
  0.6 6.9 %copy-start = (f32[1024,200]{0,1:T(8,128)S(1)}, f32[1024,200]{0,1:T(8,128)}, u32[]{:S(2)}) copy-start(f32[1024,200]{0,1:T(8,128)} %param.4) | copy-start | bytes 2457604
  4.4 12.6 %collective-permute-start.3 = (f32[104,512]{1,0:T(8,128)S(1)}, f32[104,512]{1,0:T(8,128)S(1)}, u32[]{:S(2)}, u32[]{:S(2)}) collective-permute-start(f32[104,512]{1,0:T(8,128)S(1)} %get-tuple-element.29.refs_7_), channel_id=1, source_target_pairs={{0,1},{1,0},{2,3},{3,2},{4,5},{5,4},{6,7},{7,6},{8,9},{9,8},{10,11... | collective-permute-start | bytes 638984 | tf_op jit(solution)/shard_map/ppermute | solution.py:75
  11.8 5.2 %collective-permute-start = (f32[136,128]{1,0:T(8,128)S(1)}, f32[136,128]{1,0:T(8,128)S(1)}, u32[]{:S(2)}, u32[]{:S(2)}) collective-permute-start(f32[136,128]{1,0:T(8,128)S(1)} %get-tuple-element.30.refs_0_.refs_2_), channel_id=1, source_target_pairs={{0,1},{1,0},{2,3},{3,2},{4,5},{5,4},{6,7},{7,6},{8,9},{9,8},{10,11... | collective-permute-start | bytes 208904 | tf_op jit(solution)/shard_map/ppermute | solution.py:75
  11.9 9.0 %collective-permute-start.2 = (f32[96,512]{1,0:T(8,128)S(1)}, f32[96,512]{1,0:T(8,128)S(1)}, u32[]{:S(2)}, u32[]{:S(2)}) collective-permute-start(f32[96,512]{1,0:T(8,128)S(1)} %get-tuple-element.32), channel_id=1, source_target_pairs={{0,1},{1,0},{2,3},{3,2},{4,5},{5,4},{6,7},{7,6},{8,9},{9,8},{10,11... | collective-permute-start | bytes 589832 | tf_op jit(solution)/shard_map/ppermute | solution.py:75
  17.1 12.2 %collective-permute-start.5 = (f32[104,512]{1,0:T(8,128)S(1)}, f32[104,512]{1,0:T(8,128)S(1)}, u32[]{:S(2)}, u32[]{:S(2)}) collective-permute-start(f32[104,512]{1,0:T(8,128)S(1)} %shard_map.53.refs_2_.refs_5_), channel_id=1, source_target_pairs={{0,3},{1,2},{2,1},{3,0},{4,7},{5,6},{6,5},{7,4},{8,11},{9,10},{10,... | collective-permute-start | bytes 638984 | tf_op jit(solution)/shard_map/ppermute | solution.py:75
  19.6 8.4 %collective-permute-start.1 = (f32[136,128]{1,0:T(8,128)S(1)}, f32[136,128]{1,0:T(8,128)S(1)}, u32[]{:S(2)}, u32[]{:S(2)}) collective-permute-start(f32[136,128]{1,0:T(8,128)S(1)} %shard_map.52.refs_2_.refs_0_), channel_id=1, source_target_pairs={{0,3},{1,2},{2,1},{3,0},{4,7},{5,6},{6,5},{7,4},{8,11},{9,10},{10,... | collective-permute-start | bytes 208904 | tf_op jit(solution)/shard_map/ppermute | solution.py:75
  28.0 1.3 %collective-permute-start.4 = (f32[136,128]{1,0:T(8,128)S(1)}, f32[136,128]{1,0:T(8,128)S(1)}, u32[]{:S(2)}, u32[]{:S(2)}) collective-permute-start(f32[136,128]{1,0:T(8,128)S(1)} %shard_map.55.refs_1_.refs_7_), channel_id=1, source_target_pairs={{0,4},{4,0},{8,12},{12,8},{1,5},{5,1},{9,13},{13,9},{2,6},{6,2},{1... | collective-permute-start | bytes 208904 | tf_op jit(solution)/shard_map/ppermute | solution.py:75
  28.1 9.6 %collective-permute-start.6 = (f32[96,512]{1,0:T(8,128)S(1)}, f32[96,512]{1,0:T(8,128)S(1)}, u32[]{:S(2)}, u32[]{:S(2)}) collective-permute-start(f32[96,512]{1,0:T(8,128)S(1)} %shard_map.54.refs_2_), channel_id=1, source_target_pairs={{0,3},{1,2},{2,1},{3,0},{4,7},{5,6},{6,5},{7,4},{8,11},{9,10},{10,... | collective-permute-start | bytes 589832 | tf_op jit(solution)/shard_map/ppermute | solution.py:75
  30.2 11.9 %collective-permute-start.7 = (f32[104,512]{1,0:T(8,128)S(1)}, f32[104,512]{1,0:T(8,128)S(1)}, u32[]{:S(2)}, u32[]{:S(2)}) collective-permute-start(f32[104,512]{1,0:T(8,128)S(1)} %shard_map.56.refs_5_.refs_0_.refs_1_.refs_3_), channel_id=1, source_target_pairs={{0,1},{1,0},{2,3},{3,2},{4,5},{5,4},{6,7},{7,6},{8,9},{9,8},{10,11... | collective-permute-start | bytes 638984 | tf_op jit(solution)/shard_map/ppermute | solution.py:75
  37.7 9.5 %collective-permute-start.8 = (f32[96,512]{1,0:T(8,128)S(1)}, f32[96,512]{1,0:T(8,128)S(1)}, u32[]{:S(2)}, u32[]{:S(2)}) collective-permute-start(f32[96,512]{1,0:T(8,128)S(1)} %shard_map.59.refs_3_.refs_2_.refs_0_.refs_4_), channel_id=1, source_target_pairs={{0,1},{1,0},{2,3},{3,2},{4,5},{5,4},{6,7},{7,6},{8,9},{9,8},{10,11... | collective-permute-start | bytes 589832 | tf_op jit(solution)/shard_map/ppermute | solution.py:75
  42.4 1.6 %collective-permute-start.10 = (f32[56,640]{1,0:T(8,128)S(1)}, f32[56,640]{1,0:T(8,128)S(1)}, u32[]{:S(2)}, u32[]{:S(2)}) collective-permute-start(f32[56,640]{1,0:T(8,128)S(1)} %get-tuple-element.41), channel_id=1, source_target_pairs={{0,4},{4,0},{8,12},{12,8},{1,5},{5,1},{9,13},{13,9},{2,6},{6,2},{1... | collective-permute-start | bytes 430088 | tf_op jit(solution)/shard_map/ppermute | solution.py:75
  42.5 1.5 %collective-permute-start.9 = (f32[48,640]{1,0:T(8,128)S(1)}, f32[48,640]{1,0:T(8,128)S(1)}, u32[]{:S(2)}, u32[]{:S(2)}) collective-permute-start(f32[48,640]{1,0:T(8,128)S(1)} %get-tuple-element.40.refs_4_), channel_id=1, source_target_pairs={{0,4},{4,0},{8,12},{12,8},{1,5},{5,1},{9,13},{13,9},{2,6},{6,2},{1... | collective-permute-start | bytes 368648 | tf_op jit(solution)/shard_map/ppermute | solution.py:75
  44.1 8.7 %collective-permute-start.14 = (f32[104,640]{1,0:T(8,128)S(1)}, f32[104,640]{1,0:T(8,128)S(1)}, u32[]{:S(2)}, u32[]{:S(2)}) collective-permute-start(f32[104,640]{1,0:T(8,128)S(1)} %shard_map.62.refs_5_.refs_0_), channel_id=1, source_target_pairs={{0,8},{4,12},{8,0},{12,4},{1,9},{5,13},{9,1},{13,5},{2,10},{6,14},... | collective-permute-start | bytes 798728 | tf_op jit(solution)/shard_map/ppermute | solution.py:75
  48.9 3.9 %collective-permute-start.13 = (f32[96,640]{1,0:T(8,128)S(1)}, f32[96,640]{1,0:T(8,128)S(1)}, u32[]{:S(2)}, u32[]{:S(2)}) collective-permute-start(f32[96,640]{1,0:T(8,128)S(1)} %shard_map.64.refs_4_), channel_id=1, source_target_pairs={{0,4},{4,0},{8,12},{12,8},{1,5},{5,1},{9,13},{13,9},{2,6},{6,2},{1... | collective-permute-start | bytes 737288 | tf_op jit(solution)/shard_map/ppermute | solution.py:75
  48.9 1.6 %collective-permute-start.11 = (f32[136,128]{1,0:T(8,128)S(1)}, f32[136,128]{1,0:T(8,128)S(1)}, u32[]{:S(2)}, u32[]{:S(2)}) collective-permute-start(f32[136,128]{1,0:T(8,128)S(1)} %get-tuple-element.43.refs_4_), channel_id=1, source_target_pairs={{0,4},{4,0},{8,12},{12,8},{1,5},{5,1},{9,13},{13,9},{2,6},{6,2},{1... | collective-permute-start | bytes 208904 | tf_op jit(solution)/shard_map/ppermute | solution.py:75
  50.6 4.4 %collective-permute-start.12 = (f32[136,128]{1,0:T(8,128)S(1)}, f32[136,128]{1,0:T(8,128)S(1)}, u32[]{:S(2)}, u32[]{:S(2)}) collective-permute-start(f32[136,128]{1,0:T(8,128)S(1)} %shard_map.66.refs_2_.refs_0_), channel_id=1, source_target_pairs={{0,8},{4,12},{8,0},{12,4},{1,9},{5,13},{9,1},{13,5},{2,10},{6,14},... | collective-permute-start | bytes 208904 | tf_op jit(solution)/shard_map/ppermute | solution.py:75
  52.8 7.4 %collective-permute-start.16 = (f32[96,640]{1,0:T(8,128)S(1)}, f32[96,640]{1,0:T(8,128)S(1)}, u32[]{:S(2)}, u32[]{:S(2)}) collective-permute-start(f32[96,640]{1,0:T(8,128)S(1)} %shard_map.68.refs_2_), channel_id=1, source_target_pairs={{0,8},{4,12},{8,0},{12,4},{1,9},{5,13},{9,1},{13,5},{2,10},{6,14},... | collective-permute-start | bytes 737288 | tf_op jit(solution)/shard_map/ppermute | solution.py:75
  54.9 1.3 %collective-permute-start.15 = (f32[136,128]{1,0:T(8,128)S(1)}, f32[136,128]{1,0:T(8,128)S(1)}, u32[]{:S(2)}, u32[]{:S(2)}) collective-permute-start(f32[136,128]{1,0:T(8,128)S(1)} %shard_map.69.refs_1_.refs_6_), channel_id=1, source_target_pairs={{0,4},{4,0},{8,12},{12,8},{1,5},{5,1},{9,13},{13,9},{2,6},{6,2},{1... | collective-permute-start | bytes 208904 | tf_op jit(solution)/shard_map/ppermute | solution.py:75
  57.2 3.2 %collective-permute-start.17 = (f32[104,640]{1,0:T(8,128)S(1)}, f32[104,640]{1,0:T(8,128)S(1)}, u32[]{:S(2)}, u32[]{:S(2)}) collective-permute-start(f32[104,640]{1,0:T(8,128)S(1)} %shard_map.70.refs_5_.refs_0_.refs_1_.refs_3_), channel_id=1, source_target_pairs={{0,4},{4,0},{8,12},{12,8},{1,5},{5,1},{9,13},{13,9},{2,6},{6,2},{1... | collective-permute-start | bytes 798728 | tf_op jit(solution)/shard_map/ppermute | solution.py:75
  60.3 3.3 %collective-permute-start.18 = (f32[96,640]{1,0:T(8,128)S(1)}, f32[96,640]{1,0:T(8,128)S(1)}, u32[]{:S(2)}, u32[]{:S(2)}) collective-permute-start(f32[96,640]{1,0:T(8,128)S(1)} %shard_map.73.refs_3_.refs_2_.refs_0_.refs_4_), channel_id=1, source_target_pairs={{0,4},{4,0},{8,12},{12,8},{1,5},{5,1},{9,13},{13,9},{2,6},{6,2},{1... | collective-permute-start | bytes 737288 | tf_op jit(solution)/shard_map/ppermute | solution.py:75
  61.0 9.6 %collective-permute-start.22 = (f32[104,512]{1,0:T(8,128)S(1)}, f32[104,512]{1,0:T(8,128)S(1)}, u32[]{:S(2)}, u32[]{:S(2)}) collective-permute-start(f32[104,512]{1,0:T(8,128)S(1)} %shard_map.74.refs_4_), channel_id=1, source_target_pairs={{0,1},{1,0},{2,3},{3,2},{4,5},{5,4},{6,7},{7,6},{8,9},{9,8},{10,11... | collective-permute-start | bytes 638984 | tf_op jit(solution)/shard_map/ppermute | solution.py:75
  64.9 5.7 %collective-permute-start.19 = (f32[136,128]{1,0:T(8,128)S(1)}, f32[136,128]{1,0:T(8,128)S(1)}, u32[]{:S(2)}, u32[]{:S(2)}) collective-permute-start(f32[136,128]{1,0:T(8,128)S(1)} %shard_map.76.refs_4_.refs_0_), channel_id=1, source_target_pairs={{0,1},{1,0},{2,3},{3,2},{4,5},{5,4},{6,7},{7,6},{8,9},{9,8},{10,11... | collective-permute-start | bytes 208904 | tf_op jit(solution)/shard_map/ppermute | solution.py:75
  66.3 8.3 %collective-permute-start.21 = (f32[96,512]{1,0:T(8,128)S(1)}, f32[96,512]{1,0:T(8,128)S(1)}, u32[]{:S(2)}, u32[]{:S(2)}) collective-permute-start(f32[96,512]{1,0:T(8,128)S(1)} %shard_map.77.refs_4_), channel_id=1, source_target_pairs={{0,1},{1,0},{2,3},{3,2},{4,5},{5,4},{6,7},{7,6},{8,9},{9,8},{10,11... | collective-permute-start | bytes 589832 | tf_op jit(solution)/shard_map/ppermute | solution.py:75
  70.6 13.6 %collective-permute-start.24 = (f32[104,512]{1,0:T(8,128)S(1)}, f32[104,512]{1,0:T(8,128)S(1)}, u32[]{:S(2)}, u32[]{:S(2)}) collective-permute-start(f32[104,512]{1,0:T(8,128)S(1)} %shard_map.80.refs_2_.refs_5_), channel_id=1, source_target_pairs={{0,3},{1,2},{2,1},{3,0},{4,7},{5,6},{6,5},{7,4},{8,11},{9,10},{10,... | collective-permute-start | bytes 638984 | tf_op jit(solution)/shard_map/ppermute | solution.py:75
  71.6 9.5 %collective-permute-start.20 = (f32[136,128]{1,0:T(8,128)S(1)}, f32[136,128]{1,0:T(8,128)S(1)}, u32[]{:S(2)}, u32[]{:S(2)}) collective-permute-start(f32[136,128]{1,0:T(8,128)S(1)} %shard_map.79.refs_2_.refs_0_), channel_id=1, source_target_pairs={{0,3},{1,2},{2,1},{3,0},{4,7},{5,6},{6,5},{7,4},{8,11},{9,10},{10,... | collective-permute-start | bytes 208904 | tf_op jit(solution)/shard_map/ppermute | solution.py:75
  81.2 3.0 %collective-permute-start.23 = (f32[136,128]{1,0:T(8,128)S(1)}, f32[136,128]{1,0:T(8,128)S(1)}, u32[]{:S(2)}, u32[]{:S(2)}) collective-permute-start(f32[136,128]{1,0:T(8,128)S(1)} %shard_map.82.refs_1_.refs_7_), channel_id=1, source_target_pairs={{0,4},{4,0},{8,12},{12,8},{1,5},{5,1},{9,13},{13,9},{2,6},{6,2},{1... | collective-permute-start | bytes 208904 | tf_op jit(solution)/shard_map/ppermute | solution.py:75
  81.2 9.3 %collective-permute-start.25 = (f32[96,512]{1,0:T(8,128)S(1)}, f32[96,512]{1,0:T(8,128)S(1)}, u32[]{:S(2)}, u32[]{:S(2)}) collective-permute-start(f32[96,512]{1,0:T(8,128)S(1)} %shard_map.81.refs_2_), channel_id=1, source_target_pairs={{0,3},{1,2},{2,1},{3,0},{4,7},{5,6},{6,5},{7,4},{8,11},{9,10},{10,... | collective-permute-start | bytes 589832 | tf_op jit(solution)/shard_map/ppermute | solution.py:75
  85.1 10.2 %collective-permute-start.26 = (f32[104,512]{1,0:T(8,128)S(1)}, f32[104,512]{1,0:T(8,128)S(1)}, u32[]{:S(2)}, u32[]{:S(2)}) collective-permute-start(f32[104,512]{1,0:T(8,128)S(1)} %shard_map.83.refs_5_.refs_0_.refs_1_), channel_id=1, source_target_pairs={{0,1},{1,0},{2,3},{3,2},{4,5},{5,4},{6,7},{7,6},{8,9},{9,8},{10,11... | collective-permute-start | bytes 638984 | tf_op jit(solution)/shard_map/ppermute | solution.py:75
  90.6 9.8 %collective-permute-start.27 = (f32[96,512]{1,0:T(8,128)S(1)}, f32[96,512]{1,0:T(8,128)S(1)}, u32[]{:S(2)}, u32[]{:S(2)}) collective-permute-start(f32[96,512]{1,0:T(8,128)S(1)} %shard_map.86.refs_3_.refs_2_.refs_0_), channel_id=1, source_target_pairs={{0,1},{1,0},{2,3},{3,2},{4,5},{5,4},{6,7},{7,6},{8,9},{9,8},{10,11... | collective-permute-start | bytes 589832 | tf_op jit(solution)/shard_map/ppermute | solution.py:75
  95.6 1.6 %collective-permute-start.29 = (f32[56,640]{1,0:T(8,128)S(1)}, f32[56,640]{1,0:T(8,128)S(1)}, u32[]{:S(2)}, u32[]{:S(2)}) collective-permute-start(f32[56,640]{1,0:T(8,128)S(1)} %get-tuple-element.45), channel_id=1, source_target_pairs={{0,4},{4,0},{8,12},{12,8},{1,5},{5,1},{9,13},{13,9},{2,6},{6,2},{1... | collective-permute-start | bytes 430088 | tf_op jit(solution)/shard_map/ppermute | solution.py:75
  95.7 1.5 %collective-permute-start.28 = (f32[48,640]{1,0:T(8,128)S(1)}, f32[48,640]{1,0:T(8,128)S(1)}, u32[]{:S(2)}, u32[]{:S(2)}) collective-permute-start(f32[48,640]{1,0:T(8,128)S(1)} %get-tuple-element.44.refs_4_), channel_id=1, source_target_pairs={{0,4},{4,0},{8,12},{12,8},{1,5},{5,1},{9,13},{13,9},{2,6},{6,2},{1... | collective-permute-start | bytes 368648 | tf_op jit(solution)/shard_map/ppermute | solution.py:75
  97.3 8.8 %collective-permute-start.33 = (f32[104,640]{1,0:T(8,128)S(1)}, f32[104,640]{1,0:T(8,128)S(1)}, u32[]{:S(2)}, u32[]{:S(2)}) collective-permute-start(f32[104,640]{1,0:T(8,128)S(1)} %shard_map.89.refs_5_.refs_0_), channel_id=1, source_target_pairs={{0,8},{4,12},{8,0},{12,4},{1,9},{5,13},{9,1},{13,5},{2,10},{6,14},... | collective-permute-start | bytes 798728 | tf_op jit(solution)/shard_map/ppermute | solution.py:75
  102.1 4.1 %collective-permute-start.32 = (f32[96,640]{1,0:T(8,128)S(1)}, f32[96,640]{1,0:T(8,128)S(1)}, u32[]{:S(2)}, u32[]{:S(2)}) collective-permute-start(f32[96,640]{1,0:T(8,128)S(1)} %shard_map.91.refs_4_), channel_id=1, source_target_pairs={{0,4},{4,0},{8,12},{12,8},{1,5},{5,1},{9,13},{13,9},{2,6},{6,2},{1... | collective-permute-start | bytes 737288 | tf_op jit(solution)/shard_map/ppermute | solution.py:75
  102.2 1.7 %collective-permute-start.30 = (f32[136,128]{1,0:T(8,128)S(1)}, f32[136,128]{1,0:T(8,128)S(1)}, u32[]{:S(2)}, u32[]{:S(2)}) collective-permute-start(f32[136,128]{1,0:T(8,128)S(1)} %get-tuple-element.46.refs_4_), channel_id=1, source_target_pairs={{0,4},{4,0},{8,12},{12,8},{1,5},{5,1},{9,13},{13,9},{2,6},{6,2},{1... | collective-permute-start | bytes 208904 | tf_op jit(solution)/shard_map/ppermute | solution.py:75
  103.9 4.4 %collective-permute-start.31 = (f32[136,128]{1,0:T(8,128)S(1)}, f32[136,128]{1,0:T(8,128)S(1)}, u32[]{:S(2)}, u32[]{:S(2)}) collective-permute-start(f32[136,128]{1,0:T(8,128)S(1)} %shard_map.94.refs_2_.refs_0_), channel_id=1, source_target_pairs={{0,8},{4,12},{8,0},{12,4},{1,9},{5,13},{9,1},{13,5},{2,10},{6,14},... | collective-permute-start | bytes 208904 | tf_op jit(solution)/shard_map/ppermute | solution.py:75
  106.2 7.4 %collective-permute-start.35 = (f32[96,640]{1,0:T(8,128)S(1)}, f32[96,640]{1,0:T(8,128)S(1)}, u32[]{:S(2)}, u32[]{:S(2)}) collective-permute-start(f32[96,640]{1,0:T(8,128)S(1)} %shard_map.96.refs_2_), channel_id=1, source_target_pairs={{0,8},{4,12},{8,0},{12,4},{1,9},{5,13},{9,1},{13,5},{2,10},{6,14},... | collective-permute-start | bytes 737288 | tf_op jit(solution)/shard_map/ppermute | solution.py:75
  108.3 1.3 %collective-permute-start.34 = (f32[136,128]{1,0:T(8,128)S(1)}, f32[136,128]{1,0:T(8,128)S(1)}, u32[]{:S(2)}, u32[]{:S(2)}) collective-permute-start(f32[136,128]{1,0:T(8,128)S(1)} %shard_map.97.refs_1_.refs_6_), channel_id=1, source_target_pairs={{0,4},{4,0},{8,12},{12,8},{1,5},{5,1},{9,13},{13,9},{2,6},{6,2},{1... | collective-permute-start | bytes 208904 | tf_op jit(solution)/shard_map/ppermute | solution.py:75
  110.5 4.2 %collective-permute-start.36 = (f32[104,640]{1,0:T(8,128)S(1)}, f32[104,640]{1,0:T(8,128)S(1)}, u32[]{:S(2)}, u32[]{:S(2)}) collective-permute-start(f32[104,640]{1,0:T(8,128)S(1)} %shard_map.98.refs_5_.refs_1_), channel_id=1, source_target_pairs={{0,4},{4,0},{8,12},{12,8},{1,5},{5,1},{9,13},{13,9},{2,6},{6,2},{1... | collective-permute-start | bytes 798728 | tf_op jit(solution)/shard_map/ppermute | solution.py:75
  113.7 1.6 %collective-permute-start.37 = (f32[96,640]{1,0:T(8,128)S(1)}, f32[96,640]{1,0:T(8,128)S(1)}, u32[]{:S(2)}, u32[]{:S(2)}) collective-permute-start(f32[96,640]{1,0:T(8,128)S(1)} %shard_map.100.refs_2_.refs_5_), channel_id=1, source_target_pairs={{0,4},{4,0},{8,12},{12,8},{1,5},{5,1},{9,13},{13,9},{2,6},{6,2},{1... | collective-permute-start | bytes 737288 | tf_op jit(solution)/shard_map/ppermute | solution.py:75

commit v10 on v9

--- a/solution.py
+++ b/solution.py
@@ -341,7 +341,7 @@
     for iteration in range(ITERS):
         last = iteration == ITERS - 1
         if iteration:
-            nears, keeps = [], []
+            nears = []
             for i in range(n_chunks):
                 a, b = program_own[i : i + 1], program_other[i : i + 1]
                 if i == GRAM_AT:
@@ -349,7 +349,7 @@
                     gram_near = exchange(gram_p, "gene", genes, 1)
                 send = product(a, b, *x[1], 1) if i else rest_of_product(base, b[0], x[1][1], 1)[0]
                 nears.append(exchange(send, "gene", genes, 1))
-                keeps.append(product(a, b, *x[0], 1))
+            keeps = [product(program_own[i : i + 1], program_other[i : i + 1], *x[0], 1) for i in range(n_chunks)]
         gram_top = far(add(gram_p, gram_near), "gene", genes, True)
         tops = [far(add(keep, near), "gene", genes, True) for keep, near in zip(keeps, nears)]
         mine = add(*gram_top)

time: 117 us -> 117 us (level)
  no operation moved by 1% of the time
where the time goes in v10:
time: 117 us
  starting transfers between devices  49.4 us (42%)
  waiting for transfers between devices  35.2 us (30%)
  Pallas kernels  29.3 us (25%)
  local copies, waits for them, and re-layouts  1.86 us (2%)
    ppermute x38, starting transfers between devices, exchange(): return lax.ppermute(a, axis, [(i, i ^ flip) for i in range(size)])  49.4 us
    ppermute x38, waiting for transfers between devices, exchange(): return lax.ppermute(a, axis, [(i, i ^ flip) for i in range(size)])  35.2 us
    pallas_call x52, Pallas kernels, __call__(): pl.pallas_call(run, out_shape=[pltpu.VMEM(s.shape, s.dtype) for s in shap...  29.3 us
  transfers between devices with their start and end apart: 38, of which 21 were waited for; matrix products, arithmetic and copies ran while one was open for 1% of the time, Pallas kernels for 21%

profile of v10, /device:TPU:0, one launch (start us, length us, event | category | flops | bytes accessed | tf_op | source)
XLA Modules:
  0.0 117.0 jit_solution(15538558369168391490)
XLA Ops:
  0.7 3.6 %shard_map.50 = (f32[104,512]{1,0:T(8,128)S(1)}, f32[96,512]{1,0:T(8,128)S(1)}, f32[104,640]{1,0:T(8,128)S(1)}, f32[96,640]{1,0:T(8,128)S(1)}, f32[104,640]{1,0:...) custom-call(s32[2]{0:T(128)S(1)} %pad_add_fusion.refs_0_, ...), custom_call_target="tpu_custom_call" | custom-call | flops 524288000 | bytes 10321928 | tf_op jit(solution)/shard_map/pallas_call | solution.py:61
  4.4 3.1 %collective-permute-start.3 = (f32[104,512]{1,0:T(8,128)S(1)}, f32[104,512]{1,0:T(8,128)S(1)}, u32[]{:S(2)}, u32[]{:S(2)}) collective-permute-start(f32[104,512]{1,0:T(8,128)S(1)} %get-tuple-element.29.refs_7_), channel_id=1, source_target_pairs={{0,1},{1,0},{2,3},{3,2},{4,5},{5,4},{6,7},{7,6},{8,9},{9,8},{10,11... | collective-permute-start | bytes 638984 | tf_op jit(solution)/shard_map/ppermute | solution.py:75
  7.5 4.3 %shard_map.51 = (f32[136,128]{1,0:T(8,128)S(1)}, bf16[512,640]{1,0:T(8,128)(2,1)S(1)}, bf16[512,640]{1,0:T(8,128)(2,1)S(1)}, f32[104,512]{1,0:T(8,128)S(1)}, f32...) custom-call(s32[2]{0:T(128)S(1)} %pad_add_fusion.refs_0_, s32[1024,1280]{1,0:T(8,128)} %refs_1_.3, ...), custom_call_target="tpu_custom_call" | custom-call | flops 524288000 | bytes 10596360 | tf_op jit(solution)/shard_map/pallas_call | solution.py:61
  11.9 2.0 %collective-permute-start.2 = (f32[96,512]{1,0:T(8,128)S(1)}, f32[96,512]{1,0:T(8,128)S(1)}, u32[]{:S(2)}, u32[]{:S(2)}) collective-permute-start(f32[96,512]{1,0:T(8,128)S(1)} %get-tuple-element.32), channel_id=1, source_target_pairs={{0,1},{1,0},{2,3},{3,2},{4,5},{5,4},{6,7},{7,6},{8,9},{9,8},{10,11... | collective-permute-start | bytes 589832 | tf_op jit(solution)/shard_map/ppermute | solution.py:75
  13.9 3.1 %collective-permute-done.refs_1_ = f32[136,128]{1,0:T(8,128)S(1)} collective-permute-done((f32[136,128]{1,0:T(8,128)S(1)}, f32[136,128]{1,0:T(8,128)S(1)}, u32[]{:S(2)}, u32[]{:S(2)}) %collective-permute-start) | collective-permute-done | bytes 69664 | tf_op jit(solution)/shard_map/ppermute | solution.py:75
  17.1 2.5 %collective-permute-start.5 = (f32[104,512]{1,0:T(8,128)S(1)}, f32[104,512]{1,0:T(8,128)S(1)}, u32[]{:S(2)}, u32[]{:S(2)}) collective-permute-start(f32[104,512]{1,0:T(8,128)S(1)} %shard_map.53.refs_2_.refs_5_), channel_id=1, source_target_pairs={{0,3},{1,2},{2,1},{3,0},{4,7},{5,6},{6,5},{7,4},{8,11},{9,10},{10,... | collective-permute-start | bytes 638984 | tf_op jit(solution)/shard_map/ppermute | solution.py:75
  19.6 1.4 %collective-permute-start.1 = (f32[136,128]{1,0:T(8,128)S(1)}, f32[136,128]{1,0:T(8,128)S(1)}, u32[]{:S(2)}, u32[]{:S(2)}) collective-permute-start(f32[136,128]{1,0:T(8,128)S(1)} %shard_map.52.refs_2_.refs_0_), channel_id=1, source_target_pairs={{0,3},{1,2},{2,1},{3,0},{4,7},{5,6},{6,5},{7,4},{8,11},{9,10},{10,... | collective-permute-start | bytes 208904 | tf_op jit(solution)/shard_map/ppermute | solution.py:75
  21.0 7.0 %collective-permute-done.1.refs_1_ = f32[136,128]{1,0:T(8,128)S(1)} collective-permute-done((f32[136,128]{1,0:T(8,128)S(1)}, f32[136,128]{1,0:T(8,128)S(1)}, u32[]{:S(2)}, u32[]{:S(2)}) %collective-permute-start.1) | collective-permute-done | bytes 69664 | tf_op jit(solution)/shard_map/ppermute | solution.py:75
  28.1 1.0 collective-permute-start.6
  29.3 0.9 shard_map.56.refs_5_.refs_0_.refs_1_.refs_3_
  30.2 3.5 %collective-permute-start.7 = (f32[104,512]{1,0:T(8,128)S(1)}, f32[104,512]{1,0:T(8,128)S(1)}, u32[]{:S(2)}, u32[]{:S(2)}) collective-permute-start(f32[104,512]{1,0:T(8,128)S(1)} %shard_map.56.refs_5_.refs_0_.refs_1_.refs_3_), channel_id=1, source_target_pairs={{0,1},{1,0},{2,3},{3,2},{4,5},{5,4},{6,7},{7,6},{8,9},{9,8},{10,11... | collective-permute-start | bytes 638984 | tf_op jit(solution)/shard_map/ppermute | solution.py:75
  33.7 0.8 shard_map.57.refs_2_.refs_1_
  34.9 2.7 %collective-permute-done.6.refs_3_ = f32[96,512]{1,0:T(8,128)S(1)} collective-permute-done((f32[96,512]{1,0:T(8,128)S(1)}, f32[96,512]{1,0:T(8,128)S(1)}, u32[]{:S(2)}, u32[]{:S(2)}) %collective-permute-start.6) | collective-permute-done | bytes 196640 | tf_op jit(solution)/shard_map/ppermute | solution.py:75
  37.7 4.3 %collective-permute-start.8 = (f32[96,512]{1,0:T(8,128)S(1)}, f32[96,512]{1,0:T(8,128)S(1)}, u32[]{:S(2)}, u32[]{:S(2)}) collective-permute-start(f32[96,512]{1,0:T(8,128)S(1)} %shard_map.59.refs_3_.refs_2_.refs_0_.refs_4_), channel_id=1, source_target_pairs={{0,1},{1,0},{2,3},{3,2},{4,5},{5,4},{6,7},{7,6},{8,9},{9,8},{10,11... | collective-permute-start | bytes 589832 | tf_op jit(solution)/shard_map/ppermute | solution.py:75
  43.0 0.6 shard_map.61.refs_0_.refs_3_
  44.1 1.6 %collective-permute-start.14 = (f32[104,640]{1,0:T(8,128)S(1)}, f32[104,640]{1,0:T(8,128)S(1)}, u32[]{:S(2)}, u32[]{:S(2)}) collective-permute-start(f32[104,640]{1,0:T(8,128)S(1)} %shard_map.62.refs_5_.refs_0_), channel_id=1, source_target_pairs={{0,8},{4,12},{8,0},{12,4},{1,9},{5,13},{9,1},{13,5},{2,10},{6,14},... | collective-permute-start | bytes 798728 | tf_op jit(solution)/shard_map/ppermute | solution.py:75
  45.7 1.5 %collective-permute-done.8.refs_4_.refs_1_ = f32[96,512]{1,0:T(8,128)S(1)} collective-permute-done((f32[96,512]{1,0:T(8,128)S(1)}, f32[96,512]{1,0:T(8,128)S(1)}, u32[]{:S(2)}, u32[]{:S(2)}) %collective-permute-start.8) | collective-permute-done | bytes 196640 | tf_op jit(solution)/shard_map/ppermute | solution.py:75
  47.2 1.1 shard_map.63
  48.3 0.6 shard_map.64.refs_4_
  49.5 0.6 shard_map.65.refs_2_.refs_0_
  50.6 1.6 %collective-permute-start.12 = (f32[136,128]{1,0:T(8,128)S(1)}, f32[136,128]{1,0:T(8,128)S(1)}, u32[]{:S(2)}, u32[]{:S(2)}) collective-permute-start(f32[136,128]{1,0:T(8,128)S(1)} %shard_map.66.refs_2_.refs_0_), channel_id=1, source_target_pairs={{0,8},{4,12},{8,0},{12,4},{1,9},{5,13},{9,1},{13,5},{2,10},{6,14},... | collective-permute-start | bytes 208904 | tf_op jit(solution)/shard_map/ppermute | solution.py:75
  52.1 0.7 collective-permute-done.14.refs_1_
  52.9 1.6 %collective-permute-start.16 = (f32[96,640]{1,0:T(8,128)S(1)}, f32[96,640]{1,0:T(8,128)S(1)}, u32[]{:S(2)}, u32[]{:S(2)}) collective-permute-start(f32[96,640]{1,0:T(8,128)S(1)} %shard_map.68.refs_2_), channel_id=1, source_target_pairs={{0,8},{4,12},{8,0},{12,4},{1,9},{5,13},{9,1},{13,5},{2,10},{6,14},... | collective-permute-start | bytes 737288 | tf_op jit(solution)/shard_map/ppermute | solution.py:75
  55.0 1.2 %collective-permute-done.15.refs_2_ = f32[136,128]{1,0:T(8,128)S(1)} collective-permute-done((f32[136,128]{1,0:T(8,128)S(1)}, f32[136,128]{1,0:T(8,128)S(1)}, u32[]{:S(2)}, u32[]{:S(2)}) %collective-permute-start.15) | collective-permute-done | bytes 69664 | tf_op jit(solution)/shard_map/ppermute | solution.py:75
  56.3 0.9 shard_map.70.refs_5_.refs_0_.refs_1_.refs_3_
  57.4 0.9 shard_map.71.refs_2_.refs_1_
  58.3 0.5 shard_map.72.refs_4_.refs_0_
  58.9 1.4 %collective-permute-done.16.refs_3_ = f32[96,640]{1,0:T(8,128)S(1)} collective-permute-done((f32[96,640]{1,0:T(8,128)S(1)}, f32[96,640]{1,0:T(8,128)S(1)}, u32[]{:S(2)}, u32[]{:S(2)}) %collective-permute-start.16) | collective-permute-done | bytes 245792 | tf_op jit(solution)/shard_map/ppermute | solution.py:75
  60.5 0.5 shard_map.74.refs_5_
  61.0 1.7 %collective-permute-start.22 = (f32[104,512]{1,0:T(8,128)S(1)}, f32[104,512]{1,0:T(8,128)S(1)}, u32[]{:S(2)}, u32[]{:S(2)}) collective-permute-start(f32[104,512]{1,0:T(8,128)S(1)} %shard_map.74.refs_5_), channel_id=1, source_target_pairs={{0,1},{1,0},{2,3},{3,2},{4,5},{5,4},{6,7},{7,6},{8,9},{9,8},{10,11... | collective-permute-start | bytes 638984 | tf_op jit(solution)/shard_map/ppermute | solution.py:75
  62.7 1.2 %shard_map.75.refs_4_.refs_0_ = f32[136,128]{1,0:T(8,128)S(1)} custom-call(s32[2]{0:T(128)S(1)} %pad_add_fusion.refs_0_, f32[104,640]{1,0:T(8,128)S(1)} %shard_map.70.refs_5_.refs_0_.refs_1_.refs_3_, f32[96,640]{1,0:T(8,128)S(1)} %shard_map.73.refs_3_.refs_2_.refs_0_.refs_4_, f32[104,640]{1,0:T(8,128)S(1)} %collective-permute-done.17.refs_1_.refs_3_, ...), custom_call_target="tpu_custom_call" | custom-call | flops 307200000 | bytes 1093640 | tf_op jit(solution)/shard_map/pallas_call | solution.py:61
  64.0 0.9 collective-permute-start.19
  64.9 0.9 shard_map.76.refs_4_
  65.8 1.2 %collective-permute-start.21 = (f32[96,512]{1,0:T(8,128)S(1)}, f32[96,512]{1,0:T(8,128)S(1)}, u32[]{:S(2)}, u32[]{:S(2)}) collective-permute-start(f32[96,512]{1,0:T(8,128)S(1)} %shard_map.76.refs_4_), channel_id=1, source_target_pairs={{0,1},{1,0},{2,3},{3,2},{4,5},{5,4},{6,7},{7,6},{8,9},{9,8},{10,11... | collective-permute-start | bytes 589832 | tf_op jit(solution)/shard_map/ppermute | solution.py:75
  67.1 0.9 shard_map.77.refs_4_.refs_0_
  68.0 0.9 shard_map.78.refs_2_.refs_0_
  68.9 1.7 %collective-permute-done.19.refs_1_ = f32[136,128]{1,0:T(8,128)S(1)} collective-permute-done((f32[136,128]{1,0:T(8,128)S(1)}, f32[136,128]{1,0:T(8,128)S(1)}, u32[]{:S(2)}, u32[]{:S(2)}) %collective-permute-start.19) | collective-permute-done | bytes 69664 | tf_op jit(solution)/shard_map/ppermute | solution.py:75
  70.7 1.0 collective-permute-start.24
  71.7 2.9 %collective-permute-start.20 = (f32[136,128]{1,0:T(8,128)S(1)}, f32[136,128]{1,0:T(8,128)S(1)}, u32[]{:S(2)}, u32[]{:S(2)}) collective-permute-start(f32[136,128]{1,0:T(8,128)S(1)} %shard_map.79.refs_2_.refs_0_), channel_id=1, source_target_pairs={{0,3},{1,2},{2,1},{3,0},{4,7},{5,6},{6,5},{7,4},{8,11},{9,10},{10,... | collective-permute-start | bytes 208904 | tf_op jit(solution)/shard_map/ppermute | solution.py:75
  74.6 6.6 %collective-permute-done.20.refs_1_ = f32[136,128]{1,0:T(8,128)S(1)} collective-permute-done((f32[136,128]{1,0:T(8,128)S(1)}, f32[136,128]{1,0:T(8,128)S(1)}, u32[]{:S(2)}, u32[]{:S(2)}) %collective-permute-start.20) | collective-permute-done | bytes 69664 | tf_op jit(solution)/shard_map/ppermute | solution.py:75
  81.2 3.0 %collective-permute-start.25 = (f32[96,512]{1,0:T(8,128)S(1)}, f32[96,512]{1,0:T(8,128)S(1)}, u32[]{:S(2)}, u32[]{:S(2)}) collective-permute-start(f32[96,512]{1,0:T(8,128)S(1)} %shard_map.81.refs_2_), channel_id=1, source_target_pairs={{0,3},{1,2},{2,1},{3,0},{4,7},{5,6},{6,5},{7,4},{8,11},{9,10},{10,... | collective-permute-start | bytes 589832 | tf_op jit(solution)/shard_map/ppermute | solution.py:75
  84.2 0.9 shard_map.83.refs_5_.refs_0_.refs_1_
  85.1 3.6 %collective-permute-start.26 = (f32[104,512]{1,0:T(8,128)S(1)}, f32[104,512]{1,0:T(8,128)S(1)}, u32[]{:S(2)}, u32[]{:S(2)}) collective-permute-start(f32[104,512]{1,0:T(8,128)S(1)} %shard_map.83.refs_5_.refs_0_.refs_1_), channel_id=1, source_target_pairs={{0,1},{1,0},{2,3},{3,2},{4,5},{5,4},{6,7},{7,6},{8,9},{9,8},{10,11... | collective-permute-start | bytes 638984 | tf_op jit(solution)/shard_map/ppermute | solution.py:75
  88.7 0.8 shard_map.84.refs_2_.refs_1_
  89.9 0.6 collective-permute-done.25.refs_3_
  90.6 4.7 %collective-permute-start.27 = (f32[96,512]{1,0:T(8,128)S(1)}, f32[96,512]{1,0:T(8,128)S(1)}, u32[]{:S(2)}, u32[]{:S(2)}) collective-permute-start(f32[96,512]{1,0:T(8,128)S(1)} %shard_map.86.refs_3_.refs_2_.refs_0_), channel_id=1, source_target_pairs={{0,1},{1,0},{2,3},{3,2},{4,5},{5,4},{6,7},{7,6},{8,9},{9,8},{10,11... | collective-permute-start | bytes 589832 | tf_op jit(solution)/shard_map/ppermute | solution.py:75
  96.3 0.6 shard_map.88.refs_0_.refs_3_
  97.3 1.7 %collective-permute-start.33 = (f32[104,640]{1,0:T(8,128)S(1)}, f32[104,640]{1,0:T(8,128)S(1)}, u32[]{:S(2)}, u32[]{:S(2)}) collective-permute-start(f32[104,640]{1,0:T(8,128)S(1)} %shard_map.89.refs_5_.refs_0_), channel_id=1, source_target_pairs={{0,8},{4,12},{8,0},{12,4},{1,9},{5,13},{9,1},{13,5},{2,10},{6,14},... | collective-permute-start | bytes 798728 | tf_op jit(solution)/shard_map/ppermute | solution.py:75
  99.0 1.4 %collective-permute-done.27.refs_4_.refs_1_ = f32[96,512]{1,0:T(8,128)S(1)} collective-permute-done((f32[96,512]{1,0:T(8,128)S(1)}, f32[96,512]{1,0:T(8,128)S(1)}, u32[]{:S(2)}, u32[]{:S(2)}) %collective-permute-start.27) | collective-permute-done | bytes 196640 | tf_op jit(solution)/shard_map/ppermute | solution.py:75
  100.4 1.1 shard_map.90
  101.5 0.6 shard_map.91.refs_4_
  102.7 0.6 shard_map.92.refs_5_.refs_0_
  103.3 0.6 shard_map.93.refs_2_
  103.9 1.5 %collective-permute-start.31 = (f32[136,128]{1,0:T(8,128)S(1)}, f32[136,128]{1,0:T(8,128)S(1)}, u32[]{:S(2)}, u32[]{:S(2)}) collective-permute-start(f32[136,128]{1,0:T(8,128)S(1)} %shard_map.94.refs_2_.refs_0_), channel_id=1, source_target_pairs={{0,8},{4,12},{8,0},{12,4},{1,9},{5,13},{9,1},{13,5},{2,10},{6,14},... | collective-permute-start | bytes 208904 | tf_op jit(solution)/shard_map/ppermute | solution.py:75
  105.4 0.8 collective-permute-done.33.refs_1_
  106.3 1.5 %collective-permute-start.35 = (f32[96,640]{1,0:T(8,128)S(1)}, f32[96,640]{1,0:T(8,128)S(1)}, u32[]{:S(2)}, u32[]{:S(2)}) collective-permute-start(f32[96,640]{1,0:T(8,128)S(1)} %shard_map.96.refs_2_), channel_id=1, source_target_pairs={{0,8},{4,12},{8,0},{12,4},{1,9},{5,13},{9,1},{13,5},{2,10},{6,14},... | collective-permute-start | bytes 737288 | tf_op jit(solution)/shard_map/ppermute | solution.py:75
  108.4 1.2 %collective-permute-done.34.refs_2_ = f32[136,128]{1,0:T(8,128)S(1)} collective-permute-done((f32[136,128]{1,0:T(8,128)S(1)}, f32[136,128]{1,0:T(8,128)S(1)}, u32[]{:S(2)}, u32[]{:S(2)}) %collective-permute-start.34) | collective-permute-done | bytes 69664 | tf_op jit(solution)/shard_map/ppermute | solution.py:75
  109.6 0.9 shard_map.98.refs_5_.refs_1_
  110.8 0.9 shard_map.99.refs_1_.refs_4_
  111.7 2.0 %collective-permute-done.35.refs_3_ = f32[96,640]{1,0:T(8,128)S(1)} collective-permute-done((f32[96,640]{1,0:T(8,128)S(1)}, f32[96,640]{1,0:T(8,128)S(1)}, u32[]{:S(2)}, u32[]{:S(2)}) %collective-permute-start.35) | collective-permute-done | bytes 245792 | tf_op jit(solution)/shard_map/ppermute | solution.py:75
  113.9 0.9 copy.5
  114.8 0.6 collective-permute-done.37.refs_4_
  115.4 0.6 shard_map.101
  116.0 1.0 copy.6
  (69 shorter events, 8.3 us)
Async XLA Ops:
  0.6 6.9 %copy-start = (f32[1024,200]{0,1:T(8,128)S(1)}, f32[1024,200]{0,1:T(8,128)}, u32[]{:S(2)}) copy-start(f32[1024,200]{0,1:T(8,128)} %param.4) | copy-start | bytes 2457604
  4.4 12.6 %collective-permute-start.3 = (f32[104,512]{1,0:T(8,128)S(1)}, f32[104,512]{1,0:T(8,128)S(1)}, u32[]{:S(2)}, u32[]{:S(2)}) collective-permute-start(f32[104,512]{1,0:T(8,128)S(1)} %get-tuple-element.29.refs_7_), channel_id=1, source_target_pairs={{0,1},{1,0},{2,3},{3,2},{4,5},{5,4},{6,7},{7,6},{8,9},{9,8},{10,11... | collective-permute-start | bytes 638984 | tf_op jit(solution)/shard_map/ppermute | solution.py:75
  11.8 5.2 %collective-permute-start = (f32[136,128]{1,0:T(8,128)S(1)}, f32[136,128]{1,0:T(8,128)S(1)}, u32[]{:S(2)}, u32[]{:S(2)}) collective-permute-start(f32[136,128]{1,0:T(8,128)S(1)} %get-tuple-element.30.refs_0_.refs_2_), channel_id=1, source_target_pairs={{0,1},{1,0},{2,3},{3,2},{4,5},{5,4},{6,7},{7,6},{8,9},{9,8},{10,11... | collective-permute-start | bytes 208904 | tf_op jit(solution)/shard_map/ppermute | solution.py:75
  11.9 9.0 %collective-permute-start.2 = (f32[96,512]{1,0:T(8,128)S(1)}, f32[96,512]{1,0:T(8,128)S(1)}, u32[]{:S(2)}, u32[]{:S(2)}) collective-permute-start(f32[96,512]{1,0:T(8,128)S(1)} %get-tuple-element.32), channel_id=1, source_target_pairs={{0,1},{1,0},{2,3},{3,2},{4,5},{5,4},{6,7},{7,6},{8,9},{9,8},{10,11... | collective-permute-start | bytes 589832 | tf_op jit(solution)/shard_map/ppermute | solution.py:75
  17.1 12.2 %collective-permute-start.5 = (f32[104,512]{1,0:T(8,128)S(1)}, f32[104,512]{1,0:T(8,128)S(1)}, u32[]{:S(2)}, u32[]{:S(2)}) collective-permute-start(f32[104,512]{1,0:T(8,128)S(1)} %shard_map.53.refs_2_.refs_5_), channel_id=1, source_target_pairs={{0,3},{1,2},{2,1},{3,0},{4,7},{5,6},{6,5},{7,4},{8,11},{9,10},{10,... | collective-permute-start | bytes 638984 | tf_op jit(solution)/shard_map/ppermute | solution.py:75
  19.6 8.4 %collective-permute-start.1 = (f32[136,128]{1,0:T(8,128)S(1)}, f32[136,128]{1,0:T(8,128)S(1)}, u32[]{:S(2)}, u32[]{:S(2)}) collective-permute-start(f32[136,128]{1,0:T(8,128)S(1)} %shard_map.52.refs_2_.refs_0_), channel_id=1, source_target_pairs={{0,3},{1,2},{2,1},{3,0},{4,7},{5,6},{6,5},{7,4},{8,11},{9,10},{10,... | collective-permute-start | bytes 208904 | tf_op jit(solution)/shard_map/ppermute | solution.py:75
  28.0 1.3 %collective-permute-start.4 = (f32[136,128]{1,0:T(8,128)S(1)}, f32[136,128]{1,0:T(8,128)S(1)}, u32[]{:S(2)}, u32[]{:S(2)}) collective-permute-start(f32[136,128]{1,0:T(8,128)S(1)} %shard_map.55.refs_1_.refs_7_), channel_id=1, source_target_pairs={{0,4},{4,0},{8,12},{12,8},{1,5},{5,1},{9,13},{13,9},{2,6},{6,2},{1... | collective-permute-start | bytes 208904 | tf_op jit(solution)/shard_map/ppermute | solution.py:75
  28.1 9.6 %collective-permute-start.6 = (f32[96,512]{1,0:T(8,128)S(1)}, f32[96,512]{1,0:T(8,128)S(1)}, u32[]{:S(2)}, u32[]{:S(2)}) collective-permute-start(f32[96,512]{1,0:T(8,128)S(1)} %shard_map.54.refs_2_), channel_id=1, source_target_pairs={{0,3},{1,2},{2,1},{3,0},{4,7},{5,6},{6,5},{7,4},{8,11},{9,10},{10,... | collective-permute-start | bytes 589832 | tf_op jit(solution)/shard_map/ppermute | solution.py:75
  30.2 11.9 %collective-permute-start.7 = (f32[104,512]{1,0:T(8,128)S(1)}, f32[104,512]{1,0:T(8,128)S(1)}, u32[]{:S(2)}, u32[]{:S(2)}) collective-permute-start(f32[104,512]{1,0:T(8,128)S(1)} %shard_map.56.refs_5_.refs_0_.refs_1_.refs_3_), channel_id=1, source_target_pairs={{0,1},{1,0},{2,3},{3,2},{4,5},{5,4},{6,7},{7,6},{8,9},{9,8},{10,11... | collective-permute-start | bytes 638984 | tf_op jit(solution)/shard_map/ppermute | solution.py:75
  37.7 9.5 %collective-permute-start.8 = (f32[96,512]{1,0:T(8,128)S(1)}, f32[96,512]{1,0:T(8,128)S(1)}, u32[]{:S(2)}, u32[]{:S(2)}) collective-permute-start(f32[96,512]{1,0:T(8,128)S(1)} %shard_map.59.refs_3_.refs_2_.refs_0_.refs_4_), channel_id=1, source_target_pairs={{0,1},{1,0},{2,3},{3,2},{4,5},{5,4},{6,7},{7,6},{8,9},{9,8},{10,11... | collective-permute-start | bytes 589832 | tf_op jit(solution)/shard_map/ppermute | solution.py:75
  42.5 1.6 %collective-permute-start.10 = (f32[56,640]{1,0:T(8,128)S(1)}, f32[56,640]{1,0:T(8,128)S(1)}, u32[]{:S(2)}, u32[]{:S(2)}) collective-permute-start(f32[56,640]{1,0:T(8,128)S(1)} %get-tuple-element.41), channel_id=1, source_target_pairs={{0,4},{4,0},{8,12},{12,8},{1,5},{5,1},{9,13},{13,9},{2,6},{6,2},{1... | collective-permute-start | bytes 430088 | tf_op jit(solution)/shard_map/ppermute | solution.py:75
  42.6 1.5 %collective-permute-start.9 = (f32[48,640]{1,0:T(8,128)S(1)}, f32[48,640]{1,0:T(8,128)S(1)}, u32[]{:S(2)}, u32[]{:S(2)}) collective-permute-start(f32[48,640]{1,0:T(8,128)S(1)} %get-tuple-element.40.refs_4_), channel_id=1, source_target_pairs={{0,4},{4,0},{8,12},{12,8},{1,5},{5,1},{9,13},{13,9},{2,6},{6,2},{1... | collective-permute-start | bytes 368648 | tf_op jit(solution)/shard_map/ppermute | solution.py:75
  44.1 8.7 %collective-permute-start.14 = (f32[104,640]{1,0:T(8,128)S(1)}, f32[104,640]{1,0:T(8,128)S(1)}, u32[]{:S(2)}, u32[]{:S(2)}) collective-permute-start(f32[104,640]{1,0:T(8,128)S(1)} %shard_map.62.refs_5_.refs_0_), channel_id=1, source_target_pairs={{0,8},{4,12},{8,0},{12,4},{1,9},{5,13},{9,1},{13,5},{2,10},{6,14},... | collective-permute-start | bytes 798728 | tf_op jit(solution)/shard_map/ppermute | solution.py:75
  48.9 3.9 %collective-permute-start.13 = (f32[96,640]{1,0:T(8,128)S(1)}, f32[96,640]{1,0:T(8,128)S(1)}, u32[]{:S(2)}, u32[]{:S(2)}) collective-permute-start(f32[96,640]{1,0:T(8,128)S(1)} %shard_map.64.refs_4_), channel_id=1, source_target_pairs={{0,4},{4,0},{8,12},{12,8},{1,5},{5,1},{9,13},{13,9},{2,6},{6,2},{1... | collective-permute-start | bytes 737288 | tf_op jit(solution)/shard_map/ppermute | solution.py:75
  49.0 1.6 %collective-permute-start.11 = (f32[136,128]{1,0:T(8,128)S(1)}, f32[136,128]{1,0:T(8,128)S(1)}, u32[]{:S(2)}, u32[]{:S(2)}) collective-permute-start(f32[136,128]{1,0:T(8,128)S(1)} %get-tuple-element.43.refs_4_), channel_id=1, source_target_pairs={{0,4},{4,0},{8,12},{12,8},{1,5},{5,1},{9,13},{13,9},{2,6},{6,2},{1... | collective-permute-start | bytes 208904 | tf_op jit(solution)/shard_map/ppermute | solution.py:75
  50.6 4.4 %collective-permute-start.12 = (f32[136,128]{1,0:T(8,128)S(1)}, f32[136,128]{1,0:T(8,128)S(1)}, u32[]{:S(2)}, u32[]{:S(2)}) collective-permute-start(f32[136,128]{1,0:T(8,128)S(1)} %shard_map.66.refs_2_.refs_0_), channel_id=1, source_target_pairs={{0,8},{4,12},{8,0},{12,4},{1,9},{5,13},{9,1},{13,5},{2,10},{6,14},... | collective-permute-start | bytes 208904 | tf_op jit(solution)/shard_map/ppermute | solution.py:75
  52.9 7.4 %collective-permute-start.16 = (f32[96,640]{1,0:T(8,128)S(1)}, f32[96,640]{1,0:T(8,128)S(1)}, u32[]{:S(2)}, u32[]{:S(2)}) collective-permute-start(f32[96,640]{1,0:T(8,128)S(1)} %shard_map.68.refs_2_), channel_id=1, source_target_pairs={{0,8},{4,12},{8,0},{12,4},{1,9},{5,13},{9,1},{13,5},{2,10},{6,14},... | collective-permute-start | bytes 737288 | tf_op jit(solution)/shard_map/ppermute | solution.py:75
  55.0 1.3 %collective-permute-start.15 = (f32[136,128]{1,0:T(8,128)S(1)}, f32[136,128]{1,0:T(8,128)S(1)}, u32[]{:S(2)}, u32[]{:S(2)}) collective-permute-start(f32[136,128]{1,0:T(8,128)S(1)} %shard_map.69.refs_1_.refs_6_), channel_id=1, source_target_pairs={{0,4},{4,0},{8,12},{12,8},{1,5},{5,1},{9,13},{13,9},{2,6},{6,2},{1... | collective-permute-start | bytes 208904 | tf_op jit(solution)/shard_map/ppermute | solution.py:75
  57.2 3.3 %collective-permute-start.17 = (f32[104,640]{1,0:T(8,128)S(1)}, f32[104,640]{1,0:T(8,128)S(1)}, u32[]{:S(2)}, u32[]{:S(2)}) collective-permute-start(f32[104,640]{1,0:T(8,128)S(1)} %shard_map.70.refs_5_.refs_0_.refs_1_.refs_3_), channel_id=1, source_target_pairs={{0,4},{4,0},{8,12},{12,8},{1,5},{5,1},{9,13},{13,9},{2,6},{6,2},{1... | collective-permute-start | bytes 798728 | tf_op jit(solution)/shard_map/ppermute | solution.py:75
  60.4 2.4 %collective-permute-start.18 = (f32[96,640]{1,0:T(8,128)S(1)}, f32[96,640]{1,0:T(8,128)S(1)}, u32[]{:S(2)}, u32[]{:S(2)}) collective-permute-start(f32[96,640]{1,0:T(8,128)S(1)} %shard_map.73.refs_3_.refs_2_.refs_0_.refs_4_), channel_id=1, source_target_pairs={{0,4},{4,0},{8,12},{12,8},{1,5},{5,1},{9,13},{13,9},{2,6},{6,2},{1... | collective-permute-start | bytes 737288 | tf_op jit(solution)/shard_map/ppermute | solution.py:75
  61.0 9.6 %collective-permute-start.22 = (f32[104,512]{1,0:T(8,128)S(1)}, f32[104,512]{1,0:T(8,128)S(1)}, u32[]{:S(2)}, u32[]{:S(2)}) collective-permute-start(f32[104,512]{1,0:T(8,128)S(1)} %shard_map.74.refs_5_), channel_id=1, source_target_pairs={{0,1},{1,0},{2,3},{3,2},{4,5},{5,4},{6,7},{7,6},{8,9},{9,8},{10,11... | collective-permute-start | bytes 638984 | tf_op jit(solution)/shard_map/ppermute | solution.py:75
  64.0 6.6 %collective-permute-start.19 = (f32[136,128]{1,0:T(8,128)S(1)}, f32[136,128]{1,0:T(8,128)S(1)}, u32[]{:S(2)}, u32[]{:S(2)}) collective-permute-start(f32[136,128]{1,0:T(8,128)S(1)} %shard_map.75.refs_4_.refs_0_), channel_id=1, source_target_pairs={{0,1},{1,0},{2,3},{3,2},{4,5},{5,4},{6,7},{7,6},{8,9},{9,8},{10,11... | collective-permute-start | bytes 208904 | tf_op jit(solution)/shard_map/ppermute | solution.py:75
  65.8 8.7 %collective-permute-start.21 = (f32[96,512]{1,0:T(8,128)S(1)}, f32[96,512]{1,0:T(8,128)S(1)}, u32[]{:S(2)}, u32[]{:S(2)}) collective-permute-start(f32[96,512]{1,0:T(8,128)S(1)} %shard_map.76.refs_4_), channel_id=1, source_target_pairs={{0,1},{1,0},{2,3},{3,2},{4,5},{5,4},{6,7},{7,6},{8,9},{9,8},{10,11... | collective-permute-start | bytes 589832 | tf_op jit(solution)/shard_map/ppermute | solution.py:75
  70.7 13.5 %collective-permute-start.24 = (f32[104,512]{1,0:T(8,128)S(1)}, f32[104,512]{1,0:T(8,128)S(1)}, u32[]{:S(2)}, u32[]{:S(2)}) collective-permute-start(f32[104,512]{1,0:T(8,128)S(1)} %shard_map.80.refs_2_.refs_5_), channel_id=1, source_target_pairs={{0,3},{1,2},{2,1},{3,0},{4,7},{5,6},{6,5},{7,4},{8,11},{9,10},{10,... | collective-permute-start | bytes 638984 | tf_op jit(solution)/shard_map/ppermute | solution.py:75
  71.7 9.5 %collective-permute-start.20 = (f32[136,128]{1,0:T(8,128)S(1)}, f32[136,128]{1,0:T(8,128)S(1)}, u32[]{:S(2)}, u32[]{:S(2)}) collective-permute-start(f32[136,128]{1,0:T(8,128)S(1)} %shard_map.79.refs_2_.refs_0_), channel_id=1, source_target_pairs={{0,3},{1,2},{2,1},{3,0},{4,7},{5,6},{6,5},{7,4},{8,11},{9,10},{10,... | collective-permute-start | bytes 208904 | tf_op jit(solution)/shard_map/ppermute | solution.py:75
  81.2 3.0 %collective-permute-start.23 = (f32[136,128]{1,0:T(8,128)S(1)}, f32[136,128]{1,0:T(8,128)S(1)}, u32[]{:S(2)}, u32[]{:S(2)}) collective-permute-start(f32[136,128]{1,0:T(8,128)S(1)} %shard_map.82.refs_1_.refs_7_), channel_id=1, source_target_pairs={{0,4},{4,0},{8,12},{12,8},{1,5},{5,1},{9,13},{13,9},{2,6},{6,2},{1... | collective-permute-start | bytes 208904 | tf_op jit(solution)/shard_map/ppermute | solution.py:75
  81.2 9.3 %collective-permute-start.25 = (f32[96,512]{1,0:T(8,128)S(1)}, f32[96,512]{1,0:T(8,128)S(1)}, u32[]{:S(2)}, u32[]{:S(2)}) collective-permute-start(f32[96,512]{1,0:T(8,128)S(1)} %shard_map.81.refs_2_), channel_id=1, source_target_pairs={{0,3},{1,2},{2,1},{3,0},{4,7},{5,6},{6,5},{7,4},{8,11},{9,10},{10,... | collective-permute-start | bytes 589832 | tf_op jit(solution)/shard_map/ppermute | solution.py:75
  85.1 10.2 %collective-permute-start.26 = (f32[104,512]{1,0:T(8,128)S(1)}, f32[104,512]{1,0:T(8,128)S(1)}, u32[]{:S(2)}, u32[]{:S(2)}) collective-permute-start(f32[104,512]{1,0:T(8,128)S(1)} %shard_map.83.refs_5_.refs_0_.refs_1_), channel_id=1, source_target_pairs={{0,1},{1,0},{2,3},{3,2},{4,5},{5,4},{6,7},{7,6},{8,9},{9,8},{10,11... | collective-permute-start | bytes 638984 | tf_op jit(solution)/shard_map/ppermute | solution.py:75
  90.6 9.8 %collective-permute-start.27 = (f32[96,512]{1,0:T(8,128)S(1)}, f32[96,512]{1,0:T(8,128)S(1)}, u32[]{:S(2)}, u32[]{:S(2)}) collective-permute-start(f32[96,512]{1,0:T(8,128)S(1)} %shard_map.86.refs_3_.refs_2_.refs_0_), channel_id=1, source_target_pairs={{0,1},{1,0},{2,3},{3,2},{4,5},{5,4},{6,7},{7,6},{8,9},{9,8},{10,11... | collective-permute-start | bytes 589832 | tf_op jit(solution)/shard_map/ppermute | solution.py:75
  95.7 1.6 %collective-permute-start.29 = (f32[56,640]{1,0:T(8,128)S(1)}, f32[56,640]{1,0:T(8,128)S(1)}, u32[]{:S(2)}, u32[]{:S(2)}) collective-permute-start(f32[56,640]{1,0:T(8,128)S(1)} %get-tuple-element.45), channel_id=1, source_target_pairs={{0,4},{4,0},{8,12},{12,8},{1,5},{5,1},{9,13},{13,9},{2,6},{6,2},{1... | collective-permute-start | bytes 430088 | tf_op jit(solution)/shard_map/ppermute | solution.py:75
  95.8 1.5 %collective-permute-start.28 = (f32[48,640]{1,0:T(8,128)S(1)}, f32[48,640]{1,0:T(8,128)S(1)}, u32[]{:S(2)}, u32[]{:S(2)}) collective-permute-start(f32[48,640]{1,0:T(8,128)S(1)} %get-tuple-element.44.refs_4_), channel_id=1, source_target_pairs={{0,4},{4,0},{8,12},{12,8},{1,5},{5,1},{9,13},{13,9},{2,6},{6,2},{1... | collective-permute-start | bytes 368648 | tf_op jit(solution)/shard_map/ppermute | solution.py:75
  97.3 8.8 %collective-permute-start.33 = (f32[104,640]{1,0:T(8,128)S(1)}, f32[104,640]{1,0:T(8,128)S(1)}, u32[]{:S(2)}, u32[]{:S(2)}) collective-permute-start(f32[104,640]{1,0:T(8,128)S(1)} %shard_map.89.refs_5_.refs_0_), channel_id=1, source_target_pairs={{0,8},{4,12},{8,0},{12,4},{1,9},{5,13},{9,1},{13,5},{2,10},{6,14},... | collective-permute-start | bytes 798728 | tf_op jit(solution)/shard_map/ppermute | solution.py:75
  102.1 4.1 %collective-permute-start.32 = (f32[96,640]{1,0:T(8,128)S(1)}, f32[96,640]{1,0:T(8,128)S(1)}, u32[]{:S(2)}, u32[]{:S(2)}) collective-permute-start(f32[96,640]{1,0:T(8,128)S(1)} %shard_map.91.refs_4_), channel_id=1, source_target_pairs={{0,4},{4,0},{8,12},{12,8},{1,5},{5,1},{9,13},{13,9},{2,6},{6,2},{1... | collective-permute-start | bytes 737288 | tf_op jit(solution)/shard_map/ppermute | solution.py:75
  102.2 1.7 %collective-permute-start.30 = (f32[136,128]{1,0:T(8,128)S(1)}, f32[136,128]{1,0:T(8,128)S(1)}, u32[]{:S(2)}, u32[]{:S(2)}) collective-permute-start(f32[136,128]{1,0:T(8,128)S(1)} %get-tuple-element.46.refs_4_), channel_id=1, source_target_pairs={{0,4},{4,0},{8,12},{12,8},{1,5},{5,1},{9,13},{13,9},{2,6},{6,2},{1... | collective-permute-start | bytes 208904 | tf_op jit(solution)/shard_map/ppermute | solution.py:75
  103.9 4.4 %collective-permute-start.31 = (f32[136,128]{1,0:T(8,128)S(1)}, f32[136,128]{1,0:T(8,128)S(1)}, u32[]{:S(2)}, u32[]{:S(2)}) collective-permute-start(f32[136,128]{1,0:T(8,128)S(1)} %shard_map.94.refs_2_.refs_0_), channel_id=1, source_target_pairs={{0,8},{4,12},{8,0},{12,4},{1,9},{5,13},{9,1},{13,5},{2,10},{6,14},... | collective-permute-start | bytes 208904 | tf_op jit(solution)/shard_map/ppermute | solution.py:75
  106.3 7.4 %collective-permute-start.35 = (f32[96,640]{1,0:T(8,128)S(1)}, f32[96,640]{1,0:T(8,128)S(1)}, u32[]{:S(2)}, u32[]{:S(2)}) collective-permute-start(f32[96,640]{1,0:T(8,128)S(1)} %shard_map.96.refs_2_), channel_id=1, source_target_pairs={{0,8},{4,12},{8,0},{12,4},{1,9},{5,13},{9,1},{13,5},{2,10},{6,14},... | collective-permute-start | bytes 737288 | tf_op jit(solution)/shard_map/ppermute | solution.py:75
  108.3 1.3 %collective-permute-start.34 = (f32[136,128]{1,0:T(8,128)S(1)}, f32[136,128]{1,0:T(8,128)S(1)}, u32[]{:S(2)}, u32[]{:S(2)}) collective-permute-start(f32[136,128]{1,0:T(8,128)S(1)} %shard_map.97.refs_1_.refs_6_), channel_id=1, source_target_pairs={{0,4},{4,0},{8,12},{12,8},{1,5},{5,1},{9,13},{13,9},{2,6},{6,2},{1... | collective-permute-start | bytes 208904 | tf_op jit(solution)/shard_map/ppermute | solution.py:75
  110.6 4.2 %collective-permute-start.36 = (f32[104,640]{1,0:T(8,128)S(1)}, f32[104,640]{1,0:T(8,128)S(1)}, u32[]{:S(2)}, u32[]{:S(2)}) collective-permute-start(f32[104,640]{1,0:T(8,128)S(1)} %shard_map.98.refs_5_.refs_1_), channel_id=1, source_target_pairs={{0,4},{4,0},{8,12},{12,8},{1,5},{5,1},{9,13},{13,9},{2,6},{6,2},{1... | collective-permute-start | bytes 798728 | tf_op jit(solution)/shard_map/ppermute | solution.py:75
  113.8 1.6 %collective-permute-start.37 = (f32[96,640]{1,0:T(8,128)S(1)}, f32[96,640]{1,0:T(8,128)S(1)}, u32[]{:S(2)}, u32[]{:S(2)}) collective-permute-start(f32[96,640]{1,0:T(8,128)S(1)} %shard_map.100.refs_2_.refs_5_), channel_id=1, source_target_pairs={{0,4},{4,0},{8,12},{12,8},{1,5},{5,1},{9,13},{13,9},{2,6},{6,2},{1... | collective-permute-start | bytes 737288 | tf_op jit(solution)/shard_map/ppermute | solution.py:75
